TPU v7x, 32 devices: a whole 2x2x4 slice. The times are simulated.
32 devices in a mesh: req: 8 (over z, y), head: 4 (over x, core).
Axes of the slice: x: 2, y: 2, z: 4, core: 2. Of those that a mesh axis runs over, the one named last changes fastest.
Arguments:
- hidden_in: bfloat16 [16, 2048], P(None, 'head'), may hold values from -1.5 to 1.5
- attention_gain: float32 [2048], replicated, may hold values from 0.1 to 1.9
- query_gain: float32 [64], replicated, may hold values from 0.5 to 2
- key_gain: float32 [64], replicated, may hold values from 1.5 to 4
- feedforward_gain: float32 [2048], replicated, may hold values from 0.1 to 1.9
- input_weight: bfloat16 [2048, 1920], P('req', 'head'), may hold values from -0.125 to 0.125
- output_weight: bfloat16 [1280, 2048], P('req', 'head'), may hold values from -0.15625 to 0.15625
- gate_weight: bfloat16 [2048, 5120], P('req', 'head'), may hold values from -0.125 to 0.125
- up_weight: bfloat16 [2048, 5120], P('req', 'head'), may hold values from -0.125 to 0.125
- down_weight: bfloat16 [5120, 2048], P('req', 'head'), may hold values from -0.078125 to 0.078125
- old_cache: bfloat16 [256, 128, 640], P(('req', 'head')), may hold values from -400 to 400
- keep_rows: int32 [256, 64], P(('req', 'head')), may hold values from -1 to 127, as said below
- drop_weights: float32 [256, 128], P(('req', 'head')), may hold values from 0.1 to 1
- dest_slots: int32 [32, 8], P(('req', 'head')), may hold values from 0 to 7, each once within a row
- lengths: int32 [16], replicated, may hold values from 1 to 16, 128 in all
- page_table: int32 [16, 16], P('req'), may hold values from 0 to 7, as said below
- source: int32 [8], replicated, may hold values from 0 to 7, each once
Outputs:
- compact_cache: bfloat16 [128, 128, 640], P(('req', 'head'))
- summary_rows: bfloat16 [256, 640], P(('req', 'head'))
- hidden_out: bfloat16 [16, 2048], P(None, 'head')
Inputs may be any that keep to these rules, and one draw needn't show every extreme that they name: `keep_rows`: row p lists kept rows of page p in ascending order, from 32 to 64 of them, then -1 to the end; some page keeps 64. `page_table`: row g * 2 + k belongs to the k-th request held by index g of req; entry j is the slot, on the device with req index g and head index j % 4, of that request's j-th page. On every device the entries that point to it form a permutation of its 8 slots. `source`: A permutation of the continued requests over the held slots. `dest_slots`: each row is a permutation. `lengths`: they sum to 128 and the largest is 16.
All inputs are finite; a program needn't handle non-finite values.
Results may differ from a plain program's by a relative error of at most 0.015.
The roundings to bfloat16 on the way count: a program that leaves them out, or rounds other values in their place, can miss the bound.
Values may be sent and summed in bfloat16 or wider, within the bound.
No kernel may reach another device: no remote copies, remote signals or barrier semaphores. Data moves between devices by JAX's collectives and lax.ppermute only.
A program may use at most 64 MiB of HBM per device.

v0:
```python
import jax
import jax.numpy as jnp
from jax import lax
from jax.sharding import PartitionSpec as P

D = 2048
HEADS = 20
KVH = 5
HD = 64
FF = 5120
PAGE = 128
KEEP = 64
NP = 16
R_DEV = 2
KVW = 640


epsilon = 1e-06
negative = -1e30


def joined(part, axis, combine):
    gathered = jax.tree.map(lambda a: lax.all_gather(a, axis), part)

    def take(source):
        return jax.tree.map(lambda a: lax.dynamic_index_in_dim(a, source, 0, False), gathered)

    return lax.fori_loop(
        1, lax.axis_size(axis), lambda source, state: combine(state, take(source)), take(0)
    )


def rms_rows(values, gain):
    mean_square = jnp.mean(values * values, axis=-1, keepdims=True)
    return values * lax.rsqrt(mean_square + epsilon) * gain


def rotate(vectors, positions):
    half = vectors.shape[-1] // 2
    frequency = 10000.0 ** (-jnp.arange(half, dtype=jnp.float32) / half)
    angles = positions.astype(jnp.float32)[:, None] * frequency[None, :]
    cosine = jnp.cos(angles)[:, None, :]
    sine = jnp.sin(angles)[:, None, :]
    first = vectors[..., :half]
    second = vectors[..., half:]
    return jnp.concatenate(
        [first * cosine - second * sine, second * cosine + first * sine], axis=-1
    )


def compact_pages(pages, keep, weights):
    rows = jnp.arange(pages.shape[1], dtype=jnp.int32)
    picks = keep[:, :, None] == rows[None, None, :]
    kept = jnp.einsum(
        "pkr,prc->pkc", picks.astype(jnp.bfloat16), pages, preferred_element_type=jnp.float32
    ).astype(jnp.bfloat16)
    dropped = weights * (1.0 - jnp.sum(picks.astype(jnp.float32), axis=1))
    total = jnp.sum(dropped, axis=1)
    means = (
        jnp.einsum(
            "pr,prc->pc", dropped, pages.astype(jnp.float32), precision=lax.Precision.HIGHEST
        )
        / total[:, None]
    )
    return (kept, means.astype(jnp.bfloat16), jnp.log(total))


def merge_parts(first, second):
    top_first, mass_first, sum_first = first
    top_second, mass_second, sum_second = second
    top = jnp.maximum(top_first, top_second)
    scale_first = jnp.exp(top_first - top)
    scale_second = jnp.exp(top_second - top)
    mass = mass_first * scale_first + mass_second * scale_second
    summed = sum_first * scale_first[..., None] + sum_second * scale_second[..., None]
    return (top, mass, summed)


def held_request(rows, source):
    half = R_DEV // 2
    position = rows % R_DEV
    slot = rows // R_DEV * half + position - half
    continued = jnp.arange(source.shape[0], dtype=jnp.int32)
    matches = source[None, :] == slot[:, None]
    owner_cont = jnp.sum(jnp.where(matches, continued[None, :], 0), axis=1)
    carried = owner_cont // half * R_DEV + half + owner_cont % half
    return jnp.where(position < half, rows, carried)


def full_rows(values):
    return lax.all_gather(values, "head", axis=1, tiled=True)


def feature_block(rows, count):
    return lax.dynamic_slice_in_dim(rows, lax.axis_index("req") * count, count, 1)


def normed_block(rows, gain, count):
    whole = full_rows(rows)
    normed = rms_rows(whole.astype(jnp.float32), gain).astype(jnp.bfloat16)
    return feature_block(normed, count)


def input_block(rows, count):
    return feature_block(full_rows(rows), count)


def project(inputs, weight):
    return lax.psum(jnp.dot(inputs, weight, preferred_element_type=jnp.float32), "req")


def on_device(
    hidden_in,
    attention_gain,
    query_gain,
    key_gain,
    feedforward_gain,
    input_weight,
    output_weight,
    gate_weight,
    up_weight,
    down_weight,
    old_cache,
    keep_rows,
    drop_weights,
    dest_slots,
    lengths,
    page_table,
    source,
):
    groups = lax.axis_size("req")
    lanes = lax.axis_size("head")
    group = lax.axis_index("req")
    lane = lax.axis_index("head")
    requests = hidden_in.shape[0]
    half = R_DEV // 2
    split = KVH * HD
    ratio = HEADS // KVH
    scale = HD ** (-0.5)
    pages_here = old_cache.shape[0]
    slots = jnp.arange(R_DEV, dtype=jnp.int32)
    held = held_request(group * R_DEV + slots, source)
    held_len = lengths[held]
    positions = held_len * PAGE
    inputs = normed_block(hidden_in, attention_gain, D // groups)
    partial_qkv = jnp.dot(inputs, input_weight, preferred_element_type=jnp.float32)
    mixed = lax.psum(partial_qkv, "req").astype(jnp.bfloat16)
    qkv = lax.all_gather(mixed, "head", axis=1, tiled=True)
    held_qkv = qkv[held].astype(jnp.float32)
    query = rotate(
        rms_rows(held_qkv[:, : HEADS * HD].reshape(R_DEV, HEADS, HD), query_gain), positions
    ).astype(jnp.bfloat16)
    key_new = rotate(
        rms_rows(held_qkv[:, HEADS * HD : (HEADS + KVH) * HD].reshape(R_DEV, KVH, HD), key_gain),
        positions,
    ).astype(jnp.bfloat16)
    value_new = held_qkv[:, (HEADS + KVH) * HD :].reshape(R_DEV, KVH, HD)
    kept, means, bias = compact_pages(old_cache, keep_rows, drop_weights)
    destination = dest_slots[0]
    fresh_ids = jnp.arange(pages_here, dtype=jnp.int32)
    inverse = jnp.sum(
        jnp.where(destination[None, :] == fresh_ids[:, None], fresh_ids[None, :], 0), axis=1
    )
    compact = kept[inverse].reshape(pages_here // 2, PAGE, KVW)
    summaries = means[inverse]
    per_lane = NP // lanes
    table = page_table.reshape(R_DEV, per_lane, lanes)
    mine = lax.dynamic_slice_in_dim(table, lane, 1, 2)[:, :, 0]
    logical = jnp.arange(per_lane, dtype=jnp.int32) * lanes + lane
    live = logical[None, :] < held_len[:, None]
    owner = jnp.any((mine[:, :, None] == fresh_ids[None, None, :]) & live[:, :, None], axis=1)
    query_groups = query.reshape(R_DEV, KVH, ratio, HD)
    row_keys = kept[:, :, :split].reshape(pages_here, KEEP, KVH, HD)
    row_values = kept[:, :, split:].reshape(pages_here, KEEP, KVH, HD)
    row_live = keep_rows >= 0
    allowed = owner[:, None, None, :, None] & row_live[None, None, None, :, :]
    scores = (
        jnp.einsum("rngd,pmnd->rngpm", query_groups, row_keys, preferred_element_type=jnp.float32)
        * scale
    )
    scores = jnp.where(allowed, scores, negative)
    mean_keys = means[:, :split].reshape(pages_here, KVH, HD)
    mean_values = means[:, split:].reshape(pages_here, KVH, HD)
    mean_scores = (
        jnp.einsum("rngd,pnd->rngp", query_groups, mean_keys, preferred_element_type=jnp.float32)
        * scale
        + bias[None, None, None, :]
    )
    mean_allowed = owner[:, None, None, :]
    mean_scores = jnp.where(mean_allowed, mean_scores, negative)
    top = jnp.maximum(jnp.max(scores, axis=(3, 4)), jnp.max(mean_scores, axis=3))
    row_weight = jnp.where(allowed, jnp.exp(scores - top[..., None, None]), 0.0)
    mean_weight = jnp.where(mean_allowed, jnp.exp(mean_scores - top[..., None]), 0.0)
    mass = jnp.sum(row_weight, axis=(3, 4)) + jnp.sum(mean_weight, axis=3)
    total = jnp.einsum(
        "rngpm,pmnd->rngd",
        row_weight,
        row_values.astype(jnp.float32),
        precision=lax.Precision.HIGHEST,
    )
    total = total + jnp.einsum(
        "rngp,pnd->rngd",
        mean_weight,
        mean_values.astype(jnp.float32),
        precision=lax.Precision.HIGHEST,
    )
    top, mass, total = joined((top, mass, total), "head", merge_parts)
    own_score = (
        jnp.einsum("rngd,rnd->rng", query_groups, key_new, preferred_element_type=jnp.float32)
        * scale
    )
    final_top = jnp.maximum(top, own_score)
    earlier = jnp.exp(top - final_top)
    own_weight = jnp.exp(own_score - final_top)
    mass = mass * earlier + own_weight
    total = total * earlier[..., None] + own_weight[..., None] * value_new[:, :, None, :]
    attention = (total / mass[..., None]).reshape(R_DEV, HEADS * HD).astype(jnp.bfloat16)
    moved = lax.all_to_all(attention, "req", split_axis=1, concat_axis=0, tiled=True)
    everyone = jnp.arange(requests, dtype=jnp.int32)
    position = everyone % R_DEV
    cont_index = everyone // R_DEV * half + position - half
    slot_of = source[jnp.clip(cont_index, 0, source.shape[0] - 1)]
    held_row = slot_of // half * R_DEV + half + slot_of % half
    row_of = jnp.where(position < half, everyone, held_row)
    attention_rows = moved[row_of]
    projected = project(attention_rows, output_weight)
    mid = (hidden_in.astype(jnp.float32) + projected).astype(jnp.bfloat16)
    inputs_mid = normed_block(mid, feedforward_gain, D // groups)
    both = jnp.concatenate([gate_weight, up_weight], axis=1)
    local_units = gate_weight.shape[1]
    sums = lax.psum(jnp.dot(inputs_mid, both, preferred_element_type=jnp.float32), "req")
    active = (jax.nn.silu(sums[:, :local_units]) * sums[:, local_units:]).astype(jnp.bfloat16)
    down = project(input_block(active, FF // groups), down_weight)
    residual = lax.optimization_barrier(mid).astype(jnp.float32)
    result = (residual + down).astype(jnp.bfloat16)
    return (compact, summaries, result)


def solution(mesh):
    placed = (
        P(None, "head"),
        P(),
        P(),
        P(),
        P(),
        P("req", "head"),
        P("req", "head"),
        P("req", "head"),
        P("req", "head"),
        P("req", "head"),
        P(("req", "head"), None, None),
        P(("req", "head"), None),
        P(("req", "head"), None),
        P(("req", "head"), None),
        P(),
        P("req", None),
        P(),
    )
    return jax.shard_map(
        on_device,
        mesh=mesh,
        in_specs=placed,
        out_specs=(P(("req", "head"), None, None), P(("req", "head"), None), P(None, "head")),
        check_vma=False,
    )
```

profile of v0, /device:TPU:0, one launch (start us, length us, event | category | flops | bytes accessed | tf_op | source)
XLA Modules:
  0.0 254.6 jit_solution(17800833804854793408)
XLA Ops:
  7.2 6.6 %all_gather.26 = bf16[16,2048]{1,0:T(8,128)(2,1)S(1)} all-gather(bf16[16,512]{1,0:T(8,128)(2,1)} %param.19), channel_id=1, replica_groups=mesh['req'=8,'head'=4] {'head'}, dimensions={1}, use_global_device_ids=true | all-gather | bytes 81920 | tf_op jit(solution)/shard_map/all_gather | solution.py:91
  14.6 0.8 convert_reduce_fusion
  15.5 0.8 dynamic-slice
  16.3 1.1 fusion.36
  17.4 37.9 %psum.28 = bf16[16,480]{1,0:T(8,128)(2,1)S(1)} all-reduce(f32[16,480]{1,0:T(8,128)S(1)} %fusion.36), channel_id=1, replica_groups=mesh['req'=8,'head'=4] {'req'}, use_global_device_ids=true, to_apply=%region_6.7 | all-reduce | flops 7680 | bytes 46080 | tf_op jit(solution)/shard_map/psum | solution.py:147
  55.3 5.2 %all-gather.3 = bf16[4,480,16]{1,2,0:T(8,128)(2,1)S(1)} all-gather(bf16[1,480,16]{1,2,0:T(8,128)(2,1)S(1)} %bitcast.115), channel_id=1, replica_groups=mesh['req'=8,'head'=4] {'head'}, dimensions={0}, use_global_device_ids=true | all-gather | bytes 76800 | tf_op jit(solution)/shard_map/all_gather | solution.py:148
  60.7 0.8 fusion.48
  65.2 0.7 fusion.72
  68.7 5.3 %all-gather.2 = f32[8,5,4,64]{3,2,0,1:T(4,128)S(1)} all-gather(f32[2,5,4,64]{3,2,0,1:T(4,128)S(1)} %fusion.10), channel_id=4, replica_groups=mesh['req'=8,'head'=4] {'head'}, dimensions={0}, use_global_device_ids=true | all-gather | bytes 51200 | tf_op jit(solution)/shard_map/all_gather | solution.py:23
  74.1 5.2 %all-gather.1 = f32[8,5,4]{1,2,0:T(4,128)S(1)} all-gather(f32[2,5,4]{1,2,0:T(4,128)S(1)} %copy.92), channel_id=3, replica_groups=mesh['req'=8,'head'=4] {'head'}, dimensions={0}, use_global_device_ids=true | all-gather | bytes 800 | tf_op jit(solution)/shard_map/all_gather | solution.py:23
  79.3 5.2 %all-gather = f32[8,5,4]{1,2,0:T(4,128)S(1)} all-gather(f32[2,5,4]{1,2,0:T(4,128)S(1)} %copy.91), channel_id=2, replica_groups=mesh['req'=8,'head'=4] {'head'}, dimensions={0}, use_global_device_ids=true | all-gather | bytes 800 | tf_op jit(solution)/shard_map/all_gather | solution.py:23
  84.5 1.0 while.19
  87.4 3.3 %all-to-all-start = ((bf16[2,8,160]{2,0,1:T(2,128)(2,1)}), bf16[2,8,160]{2,0,1:T(2,128)(2,1)S(1)}, u32[]{:S(2)}, u32[]{:S(2)}) async-start(bf16[2,8,160]{2,0,1:T(2,128)(2,1)} %copy.102), calls=%async_computation | async-start | bytes 16384 | tf_op jit(solution)/shard_map/all_to_all | solution.py:218
  91.6 0.8 dynamic-slice.1
  92.4 4.8 %all-to-all-done = bf16[2,8,160]{2,0,1:T(2,128)(2,1)S(1)} async-done(((bf16[2,8,160]{2,0,1:T(2,128)(2,1)}), bf16[2,8,160]{2,0,1:T(2,128)(2,1)S(1)}, u32[]{:S(2)}, u32[]{:S(2)}) %all-to-all-start) | async-done | bytes 5152 | tf_op jit(solution)/shard_map/all_to_all | solution.py:218
  97.9 33.4 %psum.29 = f32[16,512]{1,0:T(8,128)S(1)} all-reduce(f32[16,512]{1,0:T(8,128)S(1)} %fusion.73), channel_id=1, replica_groups=mesh['req'=8,'head'=4] {'req'}, use_global_device_ids=true, to_apply=%region_15.16 | all-reduce | flops 8192 | bytes 65536 | tf_op jit(solution)/shard_map/psum | solution.py:109
  131.3 5.2 %all_gather.32 = bf16[16,2048]{1,0:T(8,128)(2,1)S(1)} all-gather(bf16[16,512]{1,0:T(8,128)(2,1)S(1)} %add_convert_fusion.1), channel_id=1, replica_groups=mesh['req'=8,'head'=4] {'head'}, dimensions={1}, use_global_device_ids=true | all-gather | bytes 81920 | tf_op jit(solution)/shard_map/all_gather | solution.py:91
  136.8 1.0 fusion.4
  137.8 1.2 gather_fusion.1
  139.0 1.5 gather_fusion
  140.4 64.2 %all-reduce.2.cloned.1.call-done = f32[16,2560]{1,0:T(8,128)} async-done(((f32[16,2560]{1,0:T(8,128)}), f32[16,2560]{1,0:T(8,128)}) %all-reduce.2.cloned.1.call-update) | async-done | bytes 163856 | tf_op jit(solution)/shard_map/psum | solution.py:231
  204.6 1.0 fusion.18
  205.5 5.5 %all_gather.33 = bf16[16,5120]{1,0:T(8,128)(2,1)S(1)} all-gather(bf16[16,1280]{1,0:T(8,128)(2,1)S(1)} %fusion.18), channel_id=1, replica_groups=mesh['req'=8,'head'=4] {'head'}, dimensions={1}, use_global_device_ids=true | all-gather | bytes 204800 | tf_op jit(solution)/shard_map/all_gather | solution.py:91
  211.3 35.9 %psum.31 = f32[16,512]{1,0:T(8,128)S(1)} all-reduce(f32[16,512]{1,0:T(8,128)S(1)} %fusion.20), channel_id=1, replica_groups=mesh['req'=8,'head'=4] {'req'}, use_global_device_ids=true, to_apply=%region_18.19 | all-reduce | flops 8192 | bytes 65536 | tf_op jit(solution)/shard_map/psum | solution.py:109
  (132 shorter events, 12.9 us)
Async XLA Ops:
  7.2 56.8 %copy-start = (bf16[8,128,640]{2,1,0:T(8,128)(2,1)S(1)}, bf16[8,128,640]{2,1,0:T(8,128)(2,1)}, u32[]{:S(2)}) copy-start(bf16[8,128,640]{2,1,0:T(8,128)(2,1)} %param.29) | copy-start | bytes 3932164
  7.2 56.8 %copy-start.6 = (s32[8,64]{1,0:T(8,128)S(1)}, s32[8,64]{1,0:T(8,128)}, u32[]{:S(2)}) copy-start(s32[8,64]{1,0:T(8,128)} %param.30) | copy-start | bytes 6148
  7.2 55.2 %copy-start.1 = (s32[16]{0:T(128)S(1)}, s32[16]{0:T(128)}, u32[]{:S(2)}) copy-start(s32[16]{0:T(128)} %param.33) | copy-start | bytes 196
  7.2 55.9 %copy-start.9 = (f32[64]{0:T(128)S(1)}, f32[64]{0:T(128)}, u32[]{:S(2)}) copy-start(f32[64]{0:T(128)} %param.21) | copy-start | bytes 772
  7.2 56.3 %copy-start.8 = (s32[2,16]{1,0:T(2,128)S(1)}, s32[2,16]{1,0:T(2,128)}, u32[]{:S(2)}) copy-start(s32[2,16]{1,0:T(2,128)} %param.34) | copy-start | bytes 388
  64.4 0.7 copy-start.7
  67.6 18.1 %copy-start.10 = (f32[64]{0:T(128)S(1)}, f32[64]{0:T(128)}, u32[]{:S(2)}) copy-start(f32[64]{0:T(128)} %param.22) | copy-start | bytes 772
  67.8 23.0 %copy-start.2 = (s32[8]{0:T(128)S(1)}, s32[8]{0:T(128)}, u32[]{:S(2)}) copy-start(s32[8]{0:T(128)} %param.35) | copy-start | bytes 100
  68.5 23.0 %copy-start.13 = (s32[1,8]{1,0:T(1,128)S(1)}, s32[1,8]{1,0:T(1,128)}, u32[]{:S(2)}) copy-start(s32[1,8]{1,0:T(1,128)} %param.32) | copy-start | bytes 100
  68.5 29.3 %copy-start.4 = (bf16[160,512]{1,0:T(8,128)(2,1)S(1)}, bf16[160,512]{1,0:T(8,128)(2,1)}, u32[]{:S(2)}) copy-start(bf16[160,512]{1,0:T(8,128)(2,1)} %param.25) | copy-start | bytes 491524
  68.5 62.9 %copy-start.5 = (bf16[16,512]{1,0:T(8,128)(2,1)S(1)}, bf16[16,512]{1,0:T(8,128)(2,1)}, u32[]{:S(2)}) copy-start(bf16[16,512]{1,0:T(8,128)(2,1)} %param.19) | copy-start | bytes 49156
  84.5 52.3 %copy-start.11 = (bf16[256,1280]{1,0:T(8,128)(2,1)S(1)}, bf16[256,1280]{1,0:T(8,128)(2,1)}, u32[]{:S(2)}) copy-start(bf16[256,1280]{1,0:T(8,128)(2,1)} %param.27) | copy-start | bytes 1966084
  85.5 51.2 %copy-start.12 = (bf16[256,1280]{1,0:T(8,128)(2,1)S(1)}, bf16[256,1280]{1,0:T(8,128)(2,1)}, u32[]{:S(2)}) copy-start(bf16[256,1280]{1,0:T(8,128)(2,1)} %param.26) | copy-start | bytes 1966084
  87.4 9.8 %all-to-all-start = ((bf16[2,8,160]{2,0,1:T(2,128)(2,1)}), bf16[2,8,160]{2,0,1:T(2,128)(2,1)S(1)}, u32[]{:S(2)}, u32[]{:S(2)}) async-start(bf16[2,8,160]{2,0,1:T(2,128)(2,1)} %copy.102), calls=%async_computation | async-start | bytes 16384 | tf_op jit(solution)/shard_map/all_to_all | solution.py:218
  90.7 113.9 %all-reduce.2.cloned.1.call-start = ((), (), s32[]{:S(2)}) async-start(), calls=%async_computation.1 | async-start | bytes 327680 | tf_op jit(solution)/shard_map/psum | solution.py:231
  137.7 73.3 %copy-start.3 = (bf16[640,512]{1,0:T(8,128)(2,1)S(1)}, bf16[640,512]{1,0:T(8,128)(2,1)}, u32[]{:S(2)}) copy-start(bf16[640,512]{1,0:T(8,128)(2,1)} %param.28) | copy-start | bytes 1966084
Sparse Core Ops, SparseCore 0:
  137.9 66.6 all-reduce.1
where the time goes:
time: 255 us
  blocking collectives  145 us (57%)
  waiting for transfers between devices  69 us (27%)
  between operations  14.4 us (6%)
  local copies, waits for them, and re-layouts  10.8 us (4%)
  other arithmetic  6.62 us (3%)
  matrix products  5.03 us (2%)
  starting transfers between devices  3.37 us (1%)
    psum x2, blocking collectives, project(): lax.psum(jnp.dot(inputs, weight, preferred_element_type=jnp.float32), 'req')  69.3 us
    psum x1, waiting for transfers between devices, on_device(): lax.psum(jnp.dot(inputs_mid, both, preferred_element_type=jnp.float32), '...  64.2 us
    psum x1, blocking collectives, on_device(): mixed = lax.psum(partial_qkv, 'req').astype(jnp.bfloat16)  37.9 us
    all_gather x3, blocking collectives, full_rows(): return lax.all_gather(values, 'head', axis=1, tiled=True)  17.3 us
    all_gather x3, blocking collectives, joined(): gathered = jax.tree.map(lambda a: lax.all_gather(a, axis), part)  15.6 us
    all_gather x1, blocking collectives, on_device(): qkv = lax.all_gather(mixed, 'head', axis=1, tiled=True)  5.23 us
  transfers between devices with their start and end apart: 2, of which 2 were waited for; matrix products, arithmetic and copies ran while one was open for 2% of the time, Pallas kernels for 0%

commit v1 on v0

--- a/solution.py
+++ b/solution.py
@@ -14,25 +14,19 @@
 R_DEV = 2
 KVW = 640
 
+DIRECT = 8
 
 epsilon = 1e-06
 negative = -1e30
-
-
-def joined(part, axis, combine):
-    gathered = jax.tree.map(lambda a: lax.all_gather(a, axis), part)
-
-    def take(source):
-        return jax.tree.map(lambda a: lax.dynamic_index_in_dim(a, source, 0, False), gathered)
-
-    return lax.fori_loop(
-        1, lax.axis_size(axis), lambda source, state: combine(state, take(source)), take(0)
-    )
+both_axes = ("req", "head")
+
+
+def rms_scale(values):
+    return lax.rsqrt(jnp.mean(values * values, axis=-1, keepdims=True) + epsilon)
 
 
 def rms_rows(values, gain):
-    mean_square = jnp.mean(values * values, axis=-1, keepdims=True)
-    return values * lax.rsqrt(mean_square + epsilon) * gain
+    return values * rms_scale(values) * gain
 
 
 def rotate(vectors, positions):
@@ -65,17 +59,6 @@
     return (kept, means.astype(jnp.bfloat16), jnp.log(total))
 
 
-def merge_parts(first, second):
-    top_first, mass_first, sum_first = first
-    top_second, mass_second, sum_second = second
-    top = jnp.maximum(top_first, top_second)
-    scale_first = jnp.exp(top_first - top)
-    scale_second = jnp.exp(top_second - top)
-    mass = mass_first * scale_first + mass_second * scale_second
-    summed = sum_first * scale_first[..., None] + sum_second * scale_second[..., None]
-    return (top, mass, summed)
-
-
 def held_request(rows, source):
     half = R_DEV // 2
     position = rows % R_DEV
@@ -87,26 +70,39 @@
     return jnp.where(position < half, rows, carried)
 
 
-def full_rows(values):
-    return lax.all_gather(values, "head", axis=1, tiled=True)
-
-
-def feature_block(rows, count):
-    return lax.dynamic_slice_in_dim(rows, lax.axis_index("req") * count, count, 1)
-
-
-def normed_block(rows, gain, count):
-    whole = full_rows(rows)
-    normed = rms_rows(whole.astype(jnp.float32), gain).astype(jnp.bfloat16)
-    return feature_block(normed, count)
-
-
-def input_block(rows, count):
-    return feature_block(full_rows(rows), count)
-
-
-def project(inputs, weight):
-    return lax.psum(jnp.dot(inputs, weight, preferred_element_type=jnp.float32), "req")
+def pick_rows(order, rows):
+    chosen = order[:, None] == jnp.arange(rows.shape[0], dtype=jnp.int32)[None, :]
+    return jnp.dot(
+        chosen.astype(jnp.bfloat16), rows, preferred_element_type=jnp.float32
+    ).astype(jnp.bfloat16)
+
+
+def block_pieces(partial):
+    groups = lax.axis_size("req")
+    lanes = lax.axis_size("head")
+    per_lane = groups // lanes
+    group = lax.axis_index("req")
+    width = partial.shape[-1] // per_lane
+    if groups > DIRECT:
+        whole = lax.all_gather(lax.psum(partial, "req"), "head", axis=1, tiled=True)
+        return [lax.dynamic_slice_in_dim(whole, group * width, width, 1)]
+    pieces = []
+    for turn in range(groups):
+        pairs = []
+        for g in range(groups):
+            for h in range(lanes):
+                m = g ^ turn
+                pairs.append((g * lanes + h, (per_lane * h + m % per_lane) * lanes + m // per_lane))
+        part = (group ^ turn) % per_lane
+        block = lax.dynamic_slice_in_dim(partial, part * width, width, 1)
+        pieces.append(lax.ppermute(block, both_axes, pairs))
+    return pieces
+
+
+def whole_sum(partial):
+    if lax.axis_size("req") > DIRECT:
+        return lax.psum(partial, "req")
+    return jnp.sum(lax.all_gather(partial, "req"), axis=0)
 
 
 def on_device(
@@ -138,15 +134,24 @@
     ratio = HEADS // KVH
     scale = HD ** (-0.5)
     pages_here = old_cache.shape[0]
-    slots = jnp.arange(R_DEV, dtype=jnp.int32)
-    held = held_request(group * R_DEV + slots, source)
+    everyone = jnp.arange(requests, dtype=jnp.int32)
+    holders = held_request(everyone, source)
+    held = lax.dynamic_slice_in_dim(holders, group * R_DEV, R_DEV, 0)
     held_len = lengths[held]
     positions = held_len * PAGE
-    inputs = normed_block(hidden_in, attention_gain, D // groups)
+
+    whole = lax.all_gather(hidden_in, "head", axis=1, tiled=True)
+    normed = rms_rows(whole.astype(jnp.float32), attention_gain).astype(jnp.bfloat16)
+    features = D // groups
+    inputs = pick_rows(holders, lax.dynamic_slice_in_dim(normed, group * features, features, 1))
     partial_qkv = jnp.dot(inputs, input_weight, preferred_element_type=jnp.float32)
-    mixed = lax.psum(partial_qkv, "req").astype(jnp.bfloat16)
-    qkv = lax.all_gather(mixed, "head", axis=1, tiled=True)
-    held_qkv = qkv[held].astype(jnp.float32)
+    sent = jnp.broadcast_to(
+        partial_qkv.reshape(groups, 1, R_DEV, -1), (groups, lanes, R_DEV, partial_qkv.shape[1])
+    ).reshape(groups * lanes, R_DEV, -1)
+    got = lax.all_to_all(sent, both_axes, split_axis=0, concat_axis=0, tiled=True)
+    mixed = jnp.sum(got.reshape(groups, lanes, R_DEV, -1), axis=0).astype(jnp.bfloat16)
+    held_qkv = jnp.swapaxes(mixed, 0, 1).reshape(R_DEV, -1).astype(jnp.float32)
+
     query = rotate(
         rms_rows(held_qkv[:, : HEADS * HD].reshape(R_DEV, HEADS, HD), query_gain), positions
     ).astype(jnp.bfloat16)
@@ -188,10 +193,17 @@
     )
     mean_allowed = owner[:, None, None, :]
     mean_scores = jnp.where(mean_allowed, mean_scores, negative)
+    own_score = (
+        jnp.einsum("rngd,rnd->rng", query_groups, key_new, preferred_element_type=jnp.float32)
+        * scale
+    )
+    own_score = jnp.where(lane == 0, own_score, negative)
     top = jnp.maximum(jnp.max(scores, axis=(3, 4)), jnp.max(mean_scores, axis=3))
+    top = jnp.maximum(top, own_score)
     row_weight = jnp.where(allowed, jnp.exp(scores - top[..., None, None]), 0.0)
     mean_weight = jnp.where(mean_allowed, jnp.exp(mean_scores - top[..., None]), 0.0)
-    mass = jnp.sum(row_weight, axis=(3, 4)) + jnp.sum(mean_weight, axis=3)
+    own_weight = jnp.where(lane == 0, jnp.exp(own_score - top), 0.0)
+    mass = jnp.sum(row_weight, axis=(3, 4)) + jnp.sum(mean_weight, axis=3) + own_weight
     total = jnp.einsum(
         "rngpm,pmnd->rngd",
         row_weight,
@@ -204,35 +216,55 @@
         mean_values.astype(jnp.float32),
         precision=lax.Precision.HIGHEST,
     )
-    top, mass, total = joined((top, mass, total), "head", merge_parts)
-    own_score = (
-        jnp.einsum("rngd,rnd->rng", query_groups, key_new, preferred_element_type=jnp.float32)
-        * scale
-    )
-    final_top = jnp.maximum(top, own_score)
-    earlier = jnp.exp(top - final_top)
-    own_weight = jnp.exp(own_score - final_top)
-    mass = mass * earlier + own_weight
-    total = total * earlier[..., None] + own_weight[..., None] * value_new[:, :, None, :]
-    attention = (total / mass[..., None]).reshape(R_DEV, HEADS * HD).astype(jnp.bfloat16)
-    moved = lax.all_to_all(attention, "req", split_axis=1, concat_axis=0, tiled=True)
-    everyone = jnp.arange(requests, dtype=jnp.int32)
-    position = everyone % R_DEV
-    cont_index = everyone // R_DEV * half + position - half
-    slot_of = source[jnp.clip(cont_index, 0, source.shape[0] - 1)]
-    held_row = slot_of // half * R_DEV + half + slot_of % half
-    row_of = jnp.where(position < half, everyone, held_row)
-    attention_rows = moved[row_of]
-    projected = project(attention_rows, output_weight)
-    mid = (hidden_in.astype(jnp.float32) + projected).astype(jnp.bfloat16)
-    inputs_mid = normed_block(mid, feedforward_gain, D // groups)
-    both = jnp.concatenate([gate_weight, up_weight], axis=1)
+    total = total + own_weight[..., None] * value_new[:, :, None, :]
+
+    parts = jnp.stack(
+        [
+            jnp.broadcast_to(top[..., None], total.shape).reshape(R_DEV, HEADS * HD),
+            jnp.broadcast_to(mass[..., None], total.shape).reshape(R_DEV, HEADS * HD),
+            total.reshape(R_DEV, HEADS * HD),
+        ]
+    )
+    own = HEADS * HD // groups
+    parts = jnp.moveaxis(parts.reshape(3, R_DEV, groups, own), 2, 0)
+    parts = jnp.broadcast_to(parts[:, None], (groups, lanes, 3, R_DEV, own))
+    came = lax.all_to_all(
+        parts.reshape(groups * lanes, 3, R_DEV, own), both_axes, 0, 0, tiled=True
+    ).reshape(groups, lanes, 3, R_DEV, own)
+    tops, masses, sums = came[:, :, 0], came[:, :, 1], came[:, :, 2]
+    weights = jnp.exp(tops - jnp.max(tops, axis=1, keepdims=True))
+    attention = jnp.sum(sums * weights, axis=1) / jnp.sum(masses * weights, axis=1)
+    attention = attention.reshape(requests, own).astype(jnp.bfloat16)
+    back = jnp.sum(
+        jnp.where(holders[None, :] == everyone[:, None], everyone[None, :], 0), axis=1
+    )
+    projected = jnp.dot(
+        pick_rows(back, attention), output_weight, preferred_element_type=jnp.float32
+    )
+    projected = projected + jnp.where(group == 0, hidden_in.astype(jnp.float32), 0.0)
+
+    mid = sum(block_pieces(projected)).astype(jnp.bfloat16).astype(jnp.float32)
+    squares = jnp.sum(mid * mid, axis=1, keepdims=True)
+    mean_square = lax.all_gather(squares, "req", axis=1, tiled=True)
+    mean_square = jnp.sum(mean_square, axis=1, keepdims=True) / D
+    gain_here = lax.dynamic_slice_in_dim(feedforward_gain, group * features, features, 0)
+    inputs_mid = (mid * lax.rsqrt(mean_square + epsilon) * gain_here).astype(jnp.bfloat16)
     local_units = gate_weight.shape[1]
-    sums = lax.psum(jnp.dot(inputs_mid, both, preferred_element_type=jnp.float32), "req")
-    active = (jax.nn.silu(sums[:, :local_units]) * sums[:, local_units:]).astype(jnp.bfloat16)
-    down = project(input_block(active, FF // groups), down_weight)
-    residual = lax.optimization_barrier(mid).astype(jnp.float32)
-    result = (residual + down).astype(jnp.bfloat16)
+    piece = local_units // groups
+    gates = jnp.dot(inputs_mid, gate_weight, preferred_element_type=jnp.float32)
+    ups = jnp.dot(inputs_mid, up_weight, preferred_element_type=jnp.float32)
+    both = jnp.stack([gates.reshape(requests, groups, piece), ups.reshape(requests, groups, piece)])
+    both = lax.all_to_all(jnp.moveaxis(both, 2, 0), "req", 0, 0, tiled=True)
+    sums = jnp.sum(both, axis=0)
+    active = (jax.nn.silu(sums[0]) * sums[1]).astype(jnp.bfloat16)
+    active = lax.all_gather(active, ("head", "req"), axis=1, tiled=True)
+    units = FF // groups
+    active_here = lax.dynamic_slice_in_dim(active, group * units, units, 1)
+    down = jnp.dot(active_here, down_weight, preferred_element_type=jnp.float32)
+    share = groups // lanes
+    residual = [jnp.where(group == lane * share + k, mid, 0.0) for k in range(share)]
+    down = down + jnp.concatenate(residual, axis=1)
+    result = whole_sum(down).astype(jnp.bfloat16)
     return (compact, summaries, result)
 
 

time: 255 us -> 195 us (0.76)
  waiting for transfers between devices: 69 us -> 20.8 us
  starting transfers between devices: 3.37 us -> 28.9 us
  blocking collectives: 145 us -> 120 us
  between operations: 14.4 us -> 1.23 us
    psum x3 -> x0, blocking collectives: 107 us -> none  [the longest x2 69.3 us: project(): lax.psum(jnp.dot(inputs, weight, preferred_element_type=jnp.float32), 'req')]
    all_gather x7 -> x4, blocking collectives: 38.2 us -> 120 us  [the longest x1 64.9 us: on_device(): active = lax.all_gather(active, ('head', 'req'), axis=1, tiled=True)]
    psum x1 -> x0, waiting for transfers between devices: 64.2 us -> none  [on_device(): lax.psum(jnp.dot(inputs_mid, both, preferred_element_type=jnp.float32), '...]
    ppermute x0 -> x8, starting transfers between devices: none -> 15.2 us  [block_pieces(): pieces.append(lax.ppermute(block, both_axes, pairs))]
    all_to_all x1 -> x3, waiting for transfers between devices: 4.79 us -> 15.9 us  [the longest x1 8.6 us: on_device(): lax.all_to_all(parts.reshape(groups * lanes, 3, R_DEV, own), both_axes, 0...]
    all_to_all x1 -> x3, starting transfers between devices: 3.33 us -> 13.7 us  [the longest x1 6.33 us: on_device(): lax.all_to_all(sent, both_axes, split_axis=0, concat_axis=0, tiled=True)]
    ppermute x0 -> x8, waiting for transfers between devices: none -> 4.89 us  [block_pieces(): pieces.append(lax.ppermute(block, both_axes, pairs))]
  transfers between devices with their start and end apart: 2 -> 11, of which waited for: 2 -> 5; matrix products, arithmetic and copies ran while one was open for 2% -> 5% of each run, Pallas kernels for 0% -> 0%
where the time goes in v1:
time: 195 us; the launch traced here: 194 us
  blocking collectives  120 us (62%)
  starting transfers between devices  28.9 us (15%)
  waiting for transfers between devices  20.8 us (11%)
  local copies, waits for them, and re-layouts  10.3 us (5%)
  matrix products  6.8 us (3%)
  other arithmetic  6.18 us (3%)
    all_gather x1, blocking collectives, on_device(): active = lax.all_gather(active, ('head', 'req'), axis=1, tiled=True)  64.9 us
    all_gather x1, blocking collectives, whole_sum(): return jnp.sum(lax.all_gather(partial, 'req'), axis=0)  30.8 us
    all_gather x1, blocking collectives, on_device(): mean_square = lax.all_gather(squares, 'req', axis=1, tiled=True)  17.4 us
    ppermute x8, starting transfers between devices, block_pieces(): pieces.append(lax.ppermute(block, both_axes, pairs))  15.2 us
    all_to_all x1, waiting for transfers between devices, on_device(): lax.all_to_all(parts.reshape(groups * lanes, 3, R_DEV, own), both_axes, 0...  8.6 us
    all_gather x1, blocking collectives, on_device(): whole = lax.all_gather(hidden_in, 'head', axis=1, tiled=True)  6.56 us
    all_to_all x1, starting transfers between devices, on_device(): lax.all_to_all(sent, both_axes, split_axis=0, concat_axis=0, tiled=True)  6.33 us
    all_to_all x1, waiting for transfers between devices, on_device(): both = lax.all_to_all(jnp.moveaxis(both, 2, 0), 'req', 0, 0, tiled=True)  5.51 us
  transfers between devices with their start and end apart: 11, of which 5 were waited for; matrix products, arithmetic and copies ran while one was open for 5% of the time, Pallas kernels for 0%

profile of v1, /device:TPU:0, one launch (start us, length us, event | category | flops | bytes accessed | tf_op | source)
XLA Modules:
  0.0 194.0 jit_solution(15047181803108923321)
XLA Ops:
  0.7 6.6 %all_gather.15 = bf16[16,2048]{1,0:T(8,128)(2,1)S(1)} all-gather(bf16[16,512]{1,0:T(8,128)(2,1)} %param.17), channel_id=1, replica_groups=mesh['req'=8,'head'=4] {'head'}, dimensions={1}, use_global_device_ids=true | all-gather | bytes 81920 | tf_op jit(solution)/shard_map/all_gather | solution.py:143
  8.9 1.2 fusion.7
  10.9 6.3 %all-to-all-start = ((f32[32,2,480]{2,1,0:T(2,128)}), f32[32,2,480]{2,1,0:T(2,128)S(1)}, u32[]{:S(2)}, u32[]{:S(2)}) async-start(f32[32,2,480]{2,1,0:T(2,128)} %bitcast.9), calls=%async_computation | async-start | bytes 262144 | tf_op jit(solution)/shard_map/all_to_all | solution.py:151
  17.9 0.8 convert_reduce_fusion
  21.9 1.1 copy.113
  23.6 1.8 all-to-all-done
  26.7 1.4 fusion.67
  31.0 4.0 %all-to-all-start.1 = ((f32[32,3,2,160]{3,2,1,0:T(2,128)}), f32[32,3,2,160]{3,2,1,0:T(2,128)S(1)}, u32[]{:S(2)}, u32[]{:S(2)}) async-start(f32[32,3,2,160]{3,2,1,0:T(2,128)} %bitcast.28), calls=%async_computation.1 | async-start | bytes 393216 | tf_op jit(solution)/shard_map/all_to_all | solution.py:231
  35.3 8.6 %all-to-all-done.1 = f32[32,3,2,160]{3,2,1,0:T(2,128)S(1)} async-done(((f32[32,3,2,160]{3,2,1,0:T(2,128)}), f32[32,3,2,160]{3,2,1,0:T(2,128)S(1)}, u32[]{:S(2)}, u32[]{:S(2)}) %all-to-all-start.1) | async-done | bytes 122912 | tf_op jit(solution)/shard_map/all_to_all | solution.py:231
  44.1 1.2 convolution_add_fusion.1
  46.0 1.0 collective-permute-start.1
  47.0 2.1 %collective-permute-start.2 = (f32[16,256]{1,0:T(8,128)S(1)}, f32[16,256]{1,0:T(8,128)S(1)}, u32[]{:S(2)}, u32[]{:S(2)}) collective-permute-start(f32[16,256]{1,0:T(8,128)S(1)} %get-tuple-element.21), channel_id=1, source_target_pairs={{0,1},{1,9},{2,17},{3,25},{4,5},{5,13},{6,21},{7,29},{8,0},{9,8},{... | collective-permute-start | bytes 49160 | tf_op jit(solution)/shard_map/ppermute | solution.py:98
  49.2 1.7 collective-permute-start.3
  50.9 4.2 %collective-permute-start.4 = (f32[16,256]{1,0:T(8,128)S(1)}, f32[16,256]{1,0:T(8,128)S(1)}, u32[]{:S(2)}, u32[]{:S(2)}) collective-permute-start(f32[16,256]{1,0:T(8,128)S(1)} %get-tuple-element.19), channel_id=1, source_target_pairs={{0,2},{1,10},{2,18},{3,26},{4,6},{5,14},{6,22},{7,30},{8,3},{9,11}... | collective-permute-start | bytes 49160 | tf_op jit(solution)/shard_map/ppermute | solution.py:98
  55.1 4.7 %collective-permute-start.6 = (f32[16,256]{1,0:T(8,128)S(1)}, f32[16,256]{1,0:T(8,128)S(1)}, u32[]{:S(2)}, u32[]{:S(2)}) collective-permute-start(f32[16,256]{1,0:T(8,128)S(1)} %get-tuple-element.17), channel_id=1, source_target_pairs={{0,3},{1,11},{2,19},{3,27},{4,7},{5,15},{6,23},{7,31},{8,2},{9,10}... | collective-permute-start | bytes 49160 | tf_op jit(solution)/shard_map/ppermute | solution.py:98
  61.4 1.6 collective-permute-done.6
  63.0 3.3 %collective-permute-done.7 = f32[16,256]{1,0:T(8,128)S(1)} collective-permute-done((f32[16,256]{1,0:T(8,128)S(1)}, f32[16,256]{1,0:T(8,128)S(1)}, u32[]{:S(2)}, u32[]{:S(2)}) %collective-permute-start.7) | collective-permute-done | bytes 16416 | tf_op jit(solution)/shard_map/ppermute | solution.py:98
  66.4 17.4 %all-gather.1 = f32[8,1,16]{2,1,0:T(1,128)S(1)} all-gather(f32[1,1,16]{2,1,0:T(1,128)S(1)} %bitcast.135), channel_id=1, replica_groups=mesh['req'=8,'head'=4] {'req'}, dimensions={0}, use_global_device_ids=true | all-gather | bytes 576 | tf_op jit(solution)/shard_map/all_gather | solution.py:248
  85.4 3.4 %all-to-all-start.2 = ((f32[8,2,16,160]{3,2,1,0:T(8,128)}), f32[8,2,16,160]{3,2,1,0:T(8,128)S(1)}, u32[]{:S(2)}, u32[]{:S(2)}) async-start(f32[8,2,16,160]{3,2,1,0:T(8,128)} %maximum_bitcast_fusion), calls=%async_computation.2 | async-start | bytes 524288 | tf_op jit(solution)/shard_map/all_to_all | solution.py:257
  88.9 1.2 gather_fusion.1
  90.0 1.5 gather_fusion
  91.5 5.5 %all-to-all-done.2 = f32[8,2,16,160]{3,2,1,0:T(8,128)S(1)} async-done(((f32[8,2,16,160]{3,2,1,0:T(8,128)}), f32[8,2,16,160]{3,2,1,0:T(8,128)S(1)}, u32[]{:S(2)}, u32[]{:S(2)}) %all-to-all-start.2) | async-done | bytes 163872 | tf_op jit(solution)/shard_map/all_to_all | solution.py:257
  97.1 64.9 %all-gather.2 = bf16[32,160,16]{1,2,0:T(8,128)(2,1)S(1)} all-gather(bf16[1,160,16]{1,2,0:T(8,128)(2,1)S(1)} %fusion.42), channel_id=1, replica_groups=mesh['req'=8,'head'=4] {'head','req'}, dimensions={0}, use_global_device_ids=true | all-gather | bytes 168960 | tf_op jit(solution)/shard_map/all_gather | solution.py:260
  162.6 30.8 %all-gather = f32[128,512]{1,0:T(8,128)S(1)} all-gather(f32[16,512]{1,0:T(8,128)S(1)} %convolution_add_fusion), channel_id=2, replica_groups=mesh['req'=8,'head'=4] {'req'}, dimensions={0}, use_global_device_ids=true | all-gather | bytes 294912 | tf_op jit(solution)/shard_map/all_gather | solution.py:105
  (137 shorter events, 16.4 us)
Async XLA Ops:
  0.6 19.0 %copy-start = (bf16[8,128,640]{2,1,0:T(8,128)(2,1)S(1)}, bf16[8,128,640]{2,1,0:T(8,128)(2,1)}, u32[]{:S(2)}) copy-start(bf16[8,128,640]{2,1,0:T(8,128)(2,1)} %param.27) | copy-start | bytes 3932164
  0.6 19.0 %copy-start.6 = (s32[8,64]{1,0:T(8,128)S(1)}, s32[8,64]{1,0:T(8,128)}, u32[]{:S(2)}) copy-start(s32[8,64]{1,0:T(8,128)} %param.28) | copy-start | bytes 6148
  0.7 18.2 %copy-start.1 = (s32[16]{0:T(128)S(1)}, s32[16]{0:T(128)}, u32[]{:S(2)}) copy-start(s32[16]{0:T(128)} %param.31) | copy-start | bytes 196
  0.7 18.9 %copy-start.8 = (s32[2,16]{1,0:T(2,128)S(1)}, s32[2,16]{1,0:T(2,128)}, u32[]{:S(2)}) copy-start(s32[2,16]{1,0:T(2,128)} %param.32) | copy-start | bytes 388
  10.9 14.6 %all-to-all-start = ((f32[32,2,480]{2,1,0:T(2,128)}), f32[32,2,480]{2,1,0:T(2,128)S(1)}, u32[]{:S(2)}, u32[]{:S(2)}) async-start(f32[32,2,480]{2,1,0:T(2,128)} %bitcast.9), calls=%async_computation | async-start | bytes 262144 | tf_op jit(solution)/shard_map/all_to_all | solution.py:151
  19.7 0.7 copy-start.7
  21.2 4.7 %copy-start.9 = (f32[64]{0:T(128)S(1)}, f32[64]{0:T(128)}, u32[]{:S(2)}) copy-start(f32[64]{0:T(128)} %param.19) | copy-start | bytes 772
  21.9 4.4 %copy-start.10 = (f32[64]{0:T(128)S(1)}, f32[64]{0:T(128)}, u32[]{:S(2)}) copy-start(f32[64]{0:T(128)} %param.20) | copy-start | bytes 772
  29.5 14.6 %copy-start.5 = (bf16[16,512]{1,0:T(8,128)(2,1)S(1)}, bf16[16,512]{1,0:T(8,128)(2,1)}, u32[]{:S(2)}) copy-start(bf16[16,512]{1,0:T(8,128)(2,1)} %param.17) | copy-start | bytes 49156
  29.5 19.6 %copy-start.11 = (s32[1,8]{1,0:T(1,128)S(1)}, s32[1,8]{1,0:T(1,128)}, u32[]{:S(2)}) copy-start(s32[1,8]{1,0:T(1,128)} %param.30) | copy-start | bytes 100
  29.7 54.1 %copy-start.2 = (bf16[256,1280]{1,0:T(8,128)(2,1)S(1)}, bf16[256,1280]{1,0:T(8,128)(2,1)}, u32[]{:S(2)}) copy-start(bf16[256,1280]{1,0:T(8,128)(2,1)} %param.24) | copy-start | bytes 1966084
  31.0 12.9 %all-to-all-start.1 = ((f32[32,3,2,160]{3,2,1,0:T(2,128)}), f32[32,3,2,160]{3,2,1,0:T(2,128)S(1)}, u32[]{:S(2)}, u32[]{:S(2)}) async-start(f32[32,3,2,160]{3,2,1,0:T(2,128)} %bitcast.28), calls=%async_computation.1 | async-start | bytes 393216 | tf_op jit(solution)/shard_map/all_to_all | solution.py:231
  35.0 49.3 %copy-start.3 = (bf16[256,1280]{1,0:T(8,128)(2,1)S(1)}, bf16[256,1280]{1,0:T(8,128)(2,1)}, u32[]{:S(2)}) copy-start(bf16[256,1280]{1,0:T(8,128)(2,1)} %param.25) | copy-start | bytes 1966084
  45.3 9.8 %collective-permute-start = (f32[16,256]{1,0:T(8,128)S(1)}, f32[16,256]{1,0:T(8,128)S(1)}, u32[]{:S(2)}, u32[]{:S(2)}) collective-permute-start(f32[16,256]{1,0:T(8,128)S(1)} %get-tuple-element.22), channel_id=1, source_target_pairs={{0,0},{1,8},{2,16},{3,24},{4,4},{5,12},{6,20},{7,28},{8,1},{9,9},{... | collective-permute-start | bytes 49160 | tf_op jit(solution)/shard_map/ppermute | solution.py:98
  46.0 9.1 %collective-permute-start.1 = (f32[16,256]{1,0:T(8,128)S(1)}, f32[16,256]{1,0:T(8,128)S(1)}, u32[]{:S(2)}, u32[]{:S(2)}) collective-permute-start(f32[16,256]{1,0:T(8,128)S(1)} %get-tuple-element.15), channel_id=1, source_target_pairs={{0,4},{1,12},{2,20},{3,28},{4,0},{5,8},{6,16},{7,24},{8,5},{9,13},... | collective-permute-start | bytes 49160 | tf_op jit(solution)/shard_map/ppermute | solution.py:98
  47.0 12.9 %collective-permute-start.2 = (f32[16,256]{1,0:T(8,128)S(1)}, f32[16,256]{1,0:T(8,128)S(1)}, u32[]{:S(2)}, u32[]{:S(2)}) collective-permute-start(f32[16,256]{1,0:T(8,128)S(1)} %get-tuple-element.21), channel_id=1, source_target_pairs={{0,1},{1,9},{2,17},{3,25},{4,5},{5,13},{6,21},{7,29},{8,0},{9,8},{... | collective-permute-start | bytes 49160 | tf_op jit(solution)/shard_map/ppermute | solution.py:98
  49.2 12.2 %collective-permute-start.3 = (f32[16,256]{1,0:T(8,128)S(1)}, f32[16,256]{1,0:T(8,128)S(1)}, u32[]{:S(2)}, u32[]{:S(2)}) collective-permute-start(f32[16,256]{1,0:T(8,128)S(1)} %get-tuple-element.20), channel_id=1, source_target_pairs={{0,5},{1,13},{2,21},{3,29},{4,1},{5,9},{6,17},{7,25},{8,4},{9,12},... | collective-permute-start | bytes 49160 | tf_op jit(solution)/shard_map/ppermute | solution.py:98
  50.9 10.5 %collective-permute-start.4 = (f32[16,256]{1,0:T(8,128)S(1)}, f32[16,256]{1,0:T(8,128)S(1)}, u32[]{:S(2)}, u32[]{:S(2)}) collective-permute-start(f32[16,256]{1,0:T(8,128)S(1)} %get-tuple-element.19), channel_id=1, source_target_pairs={{0,2},{1,10},{2,18},{3,26},{4,6},{5,14},{6,22},{7,30},{8,3},{9,11}... | collective-permute-start | bytes 49160 | tf_op jit(solution)/shard_map/ppermute | solution.py:98
  55.1 6.3 %collective-permute-start.5 = (f32[16,256]{1,0:T(8,128)S(1)}, f32[16,256]{1,0:T(8,128)S(1)}, u32[]{:S(2)}, u32[]{:S(2)}) collective-permute-start(f32[16,256]{1,0:T(8,128)S(1)} %get-tuple-element.18), channel_id=1, source_target_pairs={{0,6},{1,14},{2,22},{3,30},{4,2},{5,10},{6,18},{7,26},{8,7},{9,15}... | collective-permute-start | bytes 49160 | tf_op jit(solution)/shard_map/ppermute | solution.py:98
  55.1 7.9 %collective-permute-start.6 = (f32[16,256]{1,0:T(8,128)S(1)}, f32[16,256]{1,0:T(8,128)S(1)}, u32[]{:S(2)}, u32[]{:S(2)}) collective-permute-start(f32[16,256]{1,0:T(8,128)S(1)} %get-tuple-element.17), channel_id=1, source_target_pairs={{0,3},{1,11},{2,19},{3,27},{4,7},{5,15},{6,23},{7,31},{8,2},{9,10}... | collective-permute-start | bytes 49160 | tf_op jit(solution)/shard_map/ppermute | solution.py:98
  59.8 6.4 %collective-permute-start.7 = (f32[16,256]{1,0:T(8,128)S(1)}, f32[16,256]{1,0:T(8,128)S(1)}, u32[]{:S(2)}, u32[]{:S(2)}) collective-permute-start(f32[16,256]{1,0:T(8,128)S(1)} %get-tuple-element.16), channel_id=1, source_target_pairs={{0,7},{1,15},{2,23},{3,31},{4,3},{5,11},{6,19},{7,27},{8,6},{9,14}... | collective-permute-start | bytes 49160 | tf_op jit(solution)/shard_map/ppermute | solution.py:98
  85.4 11.6 %all-to-all-start.2 = ((f32[8,2,16,160]{3,2,1,0:T(8,128)}), f32[8,2,16,160]{3,2,1,0:T(8,128)S(1)}, u32[]{:S(2)}, u32[]{:S(2)}) async-start(f32[8,2,16,160]{3,2,1,0:T(8,128)} %maximum_bitcast_fusion), calls=%async_computation.2 | async-start | bytes 524288 | tf_op jit(solution)/shard_map/all_to_all | solution.py:257
  90.0 72.3 %copy-start.4 = (bf16[640,512]{1,0:T(8,128)(2,1)S(1)}, bf16[640,512]{1,0:T(8,128)(2,1)}, u32[]{:S(2)}) copy-start(bf16[640,512]{1,0:T(8,128)(2,1)} %param.26) | copy-start | bytes 1966084

commit v2 on v1

--- a/solution.py
+++ b/solution.py
@@ -77,32 +77,27 @@
     ).astype(jnp.bfloat16)
 
 
-def block_pieces(partial):
+def exchange(parts):
+    return lax.all_to_all(parts, "req", split_axis=0, concat_axis=0, tiled=True)
+
+
+def to_block_owner(rows):
     groups = lax.axis_size("req")
     lanes = lax.axis_size("head")
     per_lane = groups // lanes
-    group = lax.axis_index("req")
-    width = partial.shape[-1] // per_lane
-    if groups > DIRECT:
-        whole = lax.all_gather(lax.psum(partial, "req"), "head", axis=1, tiled=True)
-        return [lax.dynamic_slice_in_dim(whole, group * width, width, 1)]
-    pieces = []
-    for turn in range(groups):
-        pairs = []
-        for g in range(groups):
-            for h in range(lanes):
-                m = g ^ turn
-                pairs.append((g * lanes + h, (per_lane * h + m % per_lane) * lanes + m // per_lane))
-        part = (group ^ turn) % per_lane
-        block = lax.dynamic_slice_in_dim(partial, part * width, width, 1)
-        pieces.append(lax.ppermute(block, both_axes, pairs))
-    return pieces
+    pairs = [
+        (g * lanes + h, (per_lane * h + g // lanes) * lanes + g % lanes)
+        for g in range(groups)
+        for h in range(lanes)
+    ]
+    return lax.ppermute(rows, both_axes, pairs)
 
 
 def whole_sum(partial):
     if lax.axis_size("req") > DIRECT:
         return lax.psum(partial, "req")
-    return jnp.sum(lax.all_gather(partial, "req"), axis=0)
+    groups = lax.axis_size("req")
+    return jnp.sum(exchange(jnp.broadcast_to(partial[None], (groups,) + partial.shape)), axis=0)
 
 
 def on_device(
@@ -218,22 +213,20 @@
     )
     total = total + own_weight[..., None] * value_new[:, :, None, :]
 
-    parts = jnp.stack(
-        [
-            jnp.broadcast_to(top[..., None], total.shape).reshape(R_DEV, HEADS * HD),
-            jnp.broadcast_to(mass[..., None], total.shape).reshape(R_DEV, HEADS * HD),
-            total.reshape(R_DEV, HEADS * HD),
-        ]
-    )
+    some = mass > 0.0
+    level = jnp.where(some, top + jnp.log(jnp.where(some, mass, 1.0)), negative)
+    means_out = total / jnp.where(some, mass, 1.0)[..., None]
     own = HEADS * HD // groups
-    parts = jnp.moveaxis(parts.reshape(3, R_DEV, groups, own), 2, 0)
-    parts = jnp.broadcast_to(parts[:, None], (groups, lanes, 3, R_DEV, own))
-    came = lax.all_to_all(
-        parts.reshape(groups * lanes, 3, R_DEV, own), both_axes, 0, 0, tiled=True
-    ).reshape(groups, lanes, 3, R_DEV, own)
-    tops, masses, sums = came[:, :, 0], came[:, :, 1], came[:, :, 2]
-    weights = jnp.exp(tops - jnp.max(tops, axis=1, keepdims=True))
-    attention = jnp.sum(sums * weights, axis=1) / jnp.sum(masses * weights, axis=1)
+    parts = jnp.stack([means_out, jnp.broadcast_to(level[..., None], total.shape)])
+    parts = jnp.transpose(parts.reshape(2, R_DEV, groups, own), (2, 1, 0, 3))
+    parts = jnp.broadcast_to(
+        parts.reshape(groups, 1, R_DEV, 2 * own), (groups, lanes, R_DEV, 2 * own)
+    ).reshape(groups * lanes, R_DEV, 2 * own)
+    came = lax.all_to_all(parts, both_axes, 0, 0, tiled=True)
+    came = came.reshape(groups, lanes, R_DEV, 2 * own)
+    outs, levels = came[..., :own], came[..., own:]
+    weights = jnp.exp(levels - jnp.max(levels, axis=1, keepdims=True))
+    attention = jnp.sum(outs * weights, axis=1) / jnp.sum(weights, axis=1)
     attention = attention.reshape(requests, own).astype(jnp.bfloat16)
     back = jnp.sum(
         jnp.where(holders[None, :] == everyone[:, None], everyone[None, :], 0), axis=1
@@ -243,25 +236,32 @@
     )
     projected = projected + jnp.where(group == 0, hidden_in.astype(jnp.float32), 0.0)
 
-    mid = sum(block_pieces(projected)).astype(jnp.bfloat16).astype(jnp.float32)
+    share = groups // lanes
+    blocks = jnp.moveaxis(projected.reshape(requests, share, 1, features), 0, 2)
+    blocks = jnp.broadcast_to(blocks, (share, lanes, requests, features))
+    mid = jnp.sum(exchange(blocks.reshape(groups, requests, features)), axis=0)
+    mid = to_block_owner(mid.astype(jnp.bfloat16)).astype(jnp.float32)
     squares = jnp.sum(mid * mid, axis=1, keepdims=True)
-    mean_square = lax.all_gather(squares, "req", axis=1, tiled=True)
-    mean_square = jnp.sum(mean_square, axis=1, keepdims=True) / D
     gain_here = lax.dynamic_slice_in_dim(feedforward_gain, group * features, features, 0)
-    inputs_mid = (mid * lax.rsqrt(mean_square + epsilon) * gain_here).astype(jnp.bfloat16)
+    inputs_mid = (mid * gain_here).astype(jnp.bfloat16)
     local_units = gate_weight.shape[1]
     piece = local_units // groups
     gates = jnp.dot(inputs_mid, gate_weight, preferred_element_type=jnp.float32)
     ups = jnp.dot(inputs_mid, up_weight, preferred_element_type=jnp.float32)
-    both = jnp.stack([gates.reshape(requests, groups, piece), ups.reshape(requests, groups, piece)])
-    both = lax.all_to_all(jnp.moveaxis(both, 2, 0), "req", 0, 0, tiled=True)
-    sums = jnp.sum(both, axis=0)
-    active = (jax.nn.silu(sums[0]) * sums[1]).astype(jnp.bfloat16)
-    active = lax.all_gather(active, ("head", "req"), axis=1, tiled=True)
-    units = FF // groups
-    active_here = lax.dynamic_slice_in_dim(active, group * units, units, 1)
+    both = jnp.concatenate(
+        [
+            gates.reshape(requests, groups, piece),
+            ups.reshape(requests, groups, piece),
+            jnp.broadcast_to(squares[:, :, None], (requests, groups, 1)),
+        ],
+        axis=2,
+    )
+    sums = jnp.sum(exchange(jnp.swapaxes(both, 0, 1)), axis=0)
+    factor = lax.rsqrt(sums[:, 2 * piece :] / D + epsilon)
+    gate = sums[:, :piece] * factor
+    active = (jax.nn.silu(gate) * (sums[:, piece : 2 * piece] * factor)).astype(jnp.bfloat16)
+    active_here = lax.all_gather(to_block_owner(active), "head", axis=1, tiled=True)
     down = jnp.dot(active_here, down_weight, preferred_element_type=jnp.float32)
-    share = groups // lanes
     residual = [jnp.where(group == lane * share + k, mid, 0.0) for k in range(share)]
     down = down + jnp.concatenate(residual, axis=1)
     result = whole_sum(down).astype(jnp.bfloat16)

time: 195 us -> 99.6 us (0.51)
  blocking collectives: 120 us -> 42.8 us
  starting transfers between devices: 28.9 us -> 15.7 us
  waiting for transfers between devices: 20.8 us -> 16.2 us
    all_gather x3 -> x1, blocking collectives: 113 us -> 10.5 us  [on_device(): lax.all_gather(to_block_owner(active), 'head', axis=1, tiled=True)]
    all_to_all x0 -> x2, blocking collectives: none -> 25.8 us  [exchange(): return lax.all_to_all(parts, 'req', split_axis=0, concat_axis=0, tiled=True)]
    ppermute x8 -> x2, starting transfers between devices: 15.2 us -> 1.32 us  [to_block_owner(): return lax.ppermute(rows, both_axes, pairs)]
    ppermute x8 -> x2, waiting for transfers between devices: 4.89 us -> 0.01 us  [to_block_owner(): return lax.ppermute(rows, both_axes, pairs)]
  transfers between devices with their start and end apart: 11 -> 5, of which waited for: 5 -> 3; matrix products, arithmetic and copies ran while one was open for 5% -> 10% of each run, Pallas kernels for 0% -> 0%
where the time goes in v2:
time: 99.6 us; the launch traced here: 98.9 us
  blocking collectives  42.8 us (43%)
  waiting for transfers between devices  16.2 us (16%)
  starting transfers between devices  15.7 us (16%)
  local copies, waits for them, and re-layouts  10.8 us (11%)
  matrix products  6.52 us (7%)
  other arithmetic  5.9 us (6%)
  between operations  1.08 us (1%)
    all_to_all x2, blocking collectives, exchange(): return lax.all_to_all(parts, 'req', split_axis=0, concat_axis=0, tiled=True)  25.8 us
    all_gather x1, blocking collectives, on_device(): lax.all_gather(to_block_owner(active), 'head', axis=1, tiled=True)  10.5 us
    all_to_all x1, waiting for transfers between devices, on_device(): came = lax.all_to_all(parts, both_axes, 0, 0, tiled=True)  7.69 us
    all_to_all x1, waiting for transfers between devices, exchange(): return lax.all_to_all(parts, 'req', split_axis=0, concat_axis=0, tiled=True)  6.63 us
    all_gather x1, blocking collectives, on_device(): whole = lax.all_gather(hidden_in, 'head', axis=1, tiled=True)  6.56 us
    all_to_all x1, starting transfers between devices, on_device(): lax.all_to_all(sent, both_axes, split_axis=0, concat_axis=0, tiled=True)  6.33 us
    all_to_all x1, starting transfers between devices, on_device(): came = lax.all_to_all(parts, both_axes, 0, 0, tiled=True)  4.01 us
    all_to_all x1, starting transfers between devices, exchange(): return lax.all_to_all(parts, 'req', split_axis=0, concat_axis=0, tiled=True)  4.01 us
  transfers between devices with their start and end apart: 5, of which 3 were waited for; matrix products, arithmetic and copies ran while one was open for 10% of the time, Pallas kernels for 0%

profile of v2, /device:TPU:0, one launch (start us, length us, event | category | flops | bytes accessed | tf_op | source)
XLA Modules:
  0.0 98.9 jit_solution(5705280840872586453)
XLA Ops:
  0.7 6.6 %all_gather.6 = bf16[16,2048]{1,0:T(8,128)(2,1)S(1)} all-gather(bf16[16,512]{1,0:T(8,128)(2,1)} %param.17), channel_id=1, replica_groups=mesh['req'=8,'head'=4] {'head'}, dimensions={1}, use_global_device_ids=true | all-gather | bytes 81920 | tf_op jit(solution)/shard_map/all_gather | solution.py:138
  7.4 0.7 select_reduce_fusion.1
  8.2 0.8 dynamic-slice
  8.9 1.2 %fusion.8 = f32[16,480]{1,0:T(8,128)S(1)} fusion(bf16[256,480]{0,1:T(8,128)(2,1)} %param.22, f32[16,2048]{1,0:T(8,128)S(1)} %convert_element_type.79, s32[]{:T(128)S(6)} %select_n.158, f32[256]{0:T(256)S(1)} %dynamic-slice, f32[16]{0:T(128)S(1)} %add_rsqrt_fusion.2, s32[16]{0:T(128)S(1)} %compare_select_fusion.4), kind=kOutput, calls=%fused_computation.20 | convolution fusion | flops 4079872 | bytes 294916 | tf_op jit(solution)/shard_map/dot_general | solution.py:142
  10.2 0.7 broadcast_in_dim.190
  10.9 6.3 %all-to-all-start = ((f32[32,2,480]{2,1,0:T(2,128)}), f32[32,2,480]{2,1,0:T(2,128)S(1)}, u32[]{:S(2)}, u32[]{:S(2)}) async-start(f32[32,2,480]{2,1,0:T(2,128)} %bitcast.11), calls=%async_computation | async-start | bytes 262144 | tf_op jit(solution)/shard_map/all_to_all | solution.py:146
  17.2 0.7 broadcast_compare_fusion
  17.9 0.8 convert_reduce_fusion
  20.5 0.7 fusion.67
  21.9 1.1 %copy.141 = bf16[8,64,320]{1,2,0:T(8,128)(2,1)} copy(bf16[8,64,320]{2,1,0:T(8,128)(2,1)S(1)} %get-tuple-element.12) | data formatting | bytes 655360 | tf_op jit(solution)/shard_map/slice | solution.py:173
  23.6 1.8 %all-to-all-done = f32[32,2,480]{2,1,0:T(2,128)S(1)} async-done(((f32[32,2,480]{2,1,0:T(2,128)}), f32[32,2,480]{2,1,0:T(2,128)S(1)}, u32[]{:S(2)}, u32[]{:S(2)}) %all-to-all-start) | async-done | bytes 122912 | tf_op jit(solution)/shard_map/all_to_all | solution.py:146
  26.7 1.4 %fusion.65 = (f32[2,5,4]{2,0,1:T(2,128)S(1)}, f32[2,5,4,8,64]{4,2,0,3,1:T(4,128)S(1)}) fusion(bf16[2,5,4,64]{3,2,0,1:T(4,128)(2,1)S(1)} %pad_maximum_fusion, bf16[8,64,5,64,1]{1,3,2,0,4:T(8,128)(2,1)} %bitcast.90, pred[2,8,64]{2,0,1:T(4,128)(4,1)S(1)} %broadcast_and_fusion), kind=kOutput, calls=%fused_computation.136 | convolution fusion | flops 2682840 | bytes 415904 | tf_op jit(solution)/shard_map/rngd,pmnd->rngpm/dot_general | solution.py:178
  30.8 4.0 %all-to-all-start.1 = ((f32[32,2,320]{2,1,0:T(2,128)}), f32[32,2,320]{2,1,0:T(2,128)S(1)}, u32[]{:S(2)}, u32[]{:S(2)}) async-start(f32[32,2,320]{2,1,0:T(2,128)} %bitcast.28), calls=%async_computation.1 | async-start | bytes 196608 | tf_op jit(solution)/shard_map/all_to_all | solution.py:225
  35.0 7.7 %all-to-all-done.1 = f32[32,2,320]{2,1,0:T(2,128)S(1)} async-done(((f32[32,2,320]{2,1,0:T(2,128)}), f32[32,2,320]{2,1,0:T(2,128)S(1)}, u32[]{:S(2)}, u32[]{:S(2)}) %all-to-all-start.1) | async-done | bytes 81952 | tf_op jit(solution)/shard_map/all_to_all | solution.py:225
  43.0 1.0 %convolution_add_fusion.1 = f32[16,512]{1,0:T(8,128)S(1)} fusion(bf16[160,512]{1,0:T(8,128)(2,1)S(1)} %copy-done.5, bf16[16,160]{1,0:T(8,128)(2,1)S(1)} %convert_element_type.88, bf16[16,512]{1,0:T(8,128)(2,1)} %param.17, pred[]{:T(512)S(6)} %eq.129, s32[16]{0:T(128)S(1)} %select_reduce_fusion), kind=kOutput, calls=%fused_computation.8 | convolution fusion | flops 2730752 | bytes 218177 | tf_op jit(solution)/shard_map/dot_general | solution.py:234
  44.0 9.9 %all_to_all.25 = f32[8,16,256]{2,1,0:T(8,128)S(1)} all-to-all(f32[8,16,256]{2,1,0:T(8,128)S(1)} %bitcast.92), channel_id=1, replica_groups=mesh['req'=8,'head'=4] {'req'}, dimensions={0} | all-to-all | bytes 262144 | tf_op jit(solution)/shard_map/all_to_all | solution.py:81
  54.7 0.8 dynamic_slice.15
  56.5 15.8 %all_to_all.26 = f32[8,16,321]{2,1,0:T(8,128)S(1)} all-to-all(f32[8,16,321]{2,1,0:T(8,128)S(1)} %maximum_bitcast_fusion), channel_id=1, replica_groups=mesh['req'=8,'head'=4] {'req'}, dimensions={0} | all-to-all | bytes 328704 | tf_op jit(solution)/shard_map/all_to_all | solution.py:81
  73.4 10.5 %all-gather = bf16[4,160,16]{1,2,0:T(8,128)(2,1)S(1)} all-gather(bf16[1,160,16]{1,2,0:T(8,128)(2,1)S(1)} %bitcast.100), channel_id=1, replica_groups=mesh['req'=8,'head'=4] {'head'}, dimensions={0}, use_global_device_ids=true | all-gather | bytes 25600 | tf_op jit(solution)/shard_map/all_gather | solution.py:263
  84.2 0.7 broadcast_in_dim.206
  84.9 4.0 %all-to-all-start.4 = ((f32[8,16,512]{2,1,0:T(8,128)}), f32[8,16,512]{2,1,0:T(8,128)S(1)}, u32[]{:S(2)}, u32[]{:S(2)}) async-start(f32[8,16,512]{2,1,0:T(8,128)} %broadcast_in_dim.206), calls=%async_computation.4 | async-start | bytes 524288 | tf_op jit(solution)/shard_map/all_to_all | solution.py:81
  89.1 1.2 %gather_fusion.1 = bf16[8,640]{1,0:T(8,128)(2,1)} fusion(bf16[8,640]{1,0:T(8,128)(2,1)S(1)} %fusion.16, s32[1024]{0:T(1024)S(1)} %pad_clamp_fusion.1), kind=kCustom, calls=%fused_computation.1 | custom fusion | bytes 20512 | tf_op jit(solution)/shard_map/gather | solution.py:165
  90.2 1.5 %gather_fusion = bf16[8,64,640]{2,1,0:T(8,128)(2,1)} fusion(bf16[8,64,640]{2,1,0:T(8,128)(2,1)S(1)} %convolution_convert_fusion, s32[1024]{0:T(1024)S(1)} %pad_clamp_fusion.1), kind=kCustom, calls=%fused_computation | custom fusion | bytes 1310752 | tf_op jit(solution)/shard_map/gather | solution.py:164
  91.7 6.6 %all-to-all-done.4 = f32[8,16,512]{2,1,0:T(8,128)S(1)} async-done(((f32[8,16,512]{2,1,0:T(8,128)}), f32[8,16,512]{2,1,0:T(8,128)S(1)}, u32[]{:S(2)}, u32[]{:S(2)}) %all-to-all-start.4) | async-done | bytes 262176 | tf_op jit(solution)/shard_map/all_to_all | solution.py:81
  (128 shorter events, 11.3 us)
Async XLA Ops:
  0.6 19.0 %copy-start = (bf16[8,128,640]{2,1,0:T(8,128)(2,1)S(1)}, bf16[8,128,640]{2,1,0:T(8,128)(2,1)}, u32[]{:S(2)}) copy-start(bf16[8,128,640]{2,1,0:T(8,128)(2,1)} %param.27) | copy-start | bytes 3932164
  0.6 19.0 %copy-start.6 = (s32[8,64]{1,0:T(8,128)S(1)}, s32[8,64]{1,0:T(8,128)}, u32[]{:S(2)}) copy-start(s32[8,64]{1,0:T(8,128)} %param.28) | copy-start | bytes 6148
  0.7 18.2 %copy-start.1 = (s32[16]{0:T(128)S(1)}, s32[16]{0:T(128)}, u32[]{:S(2)}) copy-start(s32[16]{0:T(128)} %param.31) | copy-start | bytes 196
  0.7 18.9 %copy-start.8 = (s32[2,16]{1,0:T(2,128)S(1)}, s32[2,16]{1,0:T(2,128)}, u32[]{:S(2)}) copy-start(s32[2,16]{1,0:T(2,128)} %param.32) | copy-start | bytes 388
  10.9 14.6 %all-to-all-start = ((f32[32,2,480]{2,1,0:T(2,128)}), f32[32,2,480]{2,1,0:T(2,128)S(1)}, u32[]{:S(2)}, u32[]{:S(2)}) async-start(f32[32,2,480]{2,1,0:T(2,128)} %bitcast.11), calls=%async_computation | async-start | bytes 262144 | tf_op jit(solution)/shard_map/all_to_all | solution.py:146
  19.7 0.7 copy-start.7
  21.2 4.9 %copy-start.10 = (f32[64]{0:T(128)S(1)}, f32[64]{0:T(128)}, u32[]{:S(2)}) copy-start(f32[64]{0:T(128)} %param.20) | copy-start | bytes 772
  21.2 4.9 %copy-start.9 = (f32[64]{0:T(128)S(1)}, f32[64]{0:T(128)}, u32[]{:S(2)}) copy-start(f32[64]{0:T(128)} %param.19) | copy-start | bytes 772
  29.5 13.5 %copy-start.5 = (bf16[160,512]{1,0:T(8,128)(2,1)S(1)}, bf16[160,512]{1,0:T(8,128)(2,1)}, u32[]{:S(2)}) copy-start(bf16[160,512]{1,0:T(8,128)(2,1)} %param.23) | copy-start | bytes 491524
  29.7 25.7 %copy-start.2 = (bf16[256,1280]{1,0:T(8,128)(2,1)S(1)}, bf16[256,1280]{1,0:T(8,128)(2,1)}, u32[]{:S(2)}) copy-start(bf16[256,1280]{1,0:T(8,128)(2,1)} %param.24) | copy-start | bytes 1966084
  30.8 11.8 %all-to-all-start.1 = ((f32[32,2,320]{2,1,0:T(2,128)}), f32[32,2,320]{2,1,0:T(2,128)S(1)}, u32[]{:S(2)}, u32[]{:S(2)}) async-start(f32[32,2,320]{2,1,0:T(2,128)} %bitcast.28), calls=%async_computation.1 | async-start | bytes 196608 | tf_op jit(solution)/shard_map/all_to_all | solution.py:225
  42.7 13.1 %copy-start.3 = (bf16[256,1280]{1,0:T(8,128)(2,1)S(1)}, bf16[256,1280]{1,0:T(8,128)(2,1)}, u32[]{:S(2)}) copy-start(bf16[256,1280]{1,0:T(8,128)(2,1)} %param.25) | copy-start | bytes 1966084
  54.0 1.4 %collective-permute-start = (bf16[16,256]{1,0:T(8,128)(2,1)S(1)}, bf16[16,256]{1,0:T(8,128)(2,1)S(1)}, u32[]{:S(2)}, u32[]{:S(2)}) collective-permute-start(bf16[16,256]{1,0:T(8,128)(2,1)S(1)} %reduce_sum.169), channel_id=1, source_target_pairs={{0,0},{1,8},{2,16},{3,24},{4,1},{5,9},{6,17},{7,25},{8,2},{9,10},{... | collective-permute-start | bytes 24584 | tf_op jit(solution)/shard_map/ppermute | solution.py:93
  56.0 28.0 %copy-start.4 = (bf16[640,512]{1,0:T(8,128)(2,1)S(1)}, bf16[640,512]{1,0:T(8,128)(2,1)}, u32[]{:S(2)}) copy-start(bf16[640,512]{1,0:T(8,128)(2,1)} %param.26) | copy-start | bytes 1966084
  56.5 32.4 %copy-start.11 = (s32[1,8]{1,0:T(1,128)S(1)}, s32[1,8]{1,0:T(1,128)}, u32[]{:S(2)}) copy-start(s32[1,8]{1,0:T(1,128)} %param.30) | copy-start | bytes 100
  72.7 0.7 collective-permute-start.1
  84.9 13.4 %all-to-all-start.4 = ((f32[8,16,512]{2,1,0:T(8,128)}), f32[8,16,512]{2,1,0:T(8,128)S(1)}, u32[]{:S(2)}, u32[]{:S(2)}) async-start(f32[8,16,512]{2,1,0:T(8,128)} %broadcast_in_dim.206), calls=%async_computation.4 | async-start | bytes 524288 | tf_op jit(solution)/shard_map/all_to_all | solution.py:81

commit v3 on v2

--- a/solution.py
+++ b/solution.py
@@ -81,16 +81,8 @@
     return lax.all_to_all(parts, "req", split_axis=0, concat_axis=0, tiled=True)
 
 
-def to_block_owner(rows):
-    groups = lax.axis_size("req")
-    lanes = lax.axis_size("head")
-    per_lane = groups // lanes
-    pairs = [
-        (g * lanes + h, (per_lane * h + g // lanes) * lanes + g % lanes)
-        for g in range(groups)
-        for h in range(lanes)
-    ]
-    return lax.ppermute(rows, both_axes, pairs)
+def over_lanes(parts):
+    return lax.all_to_all(parts, "head", split_axis=0, concat_axis=0, tiled=True)
 
 
 def whole_sum(partial):
@@ -147,6 +139,18 @@
     mixed = jnp.sum(got.reshape(groups, lanes, R_DEV, -1), axis=0).astype(jnp.bfloat16)
     held_qkv = jnp.swapaxes(mixed, 0, 1).reshape(R_DEV, -1).astype(jnp.float32)
 
+    share = groups // lanes
+    piece = gate_weight.shape[1] // groups
+    kept, means, bias = compact_pages(old_cache, keep_rows, drop_weights)
+    output_weight, gate_weight, up_weight, means, _ = lax.optimization_barrier(
+        (output_weight, gate_weight, up_weight, means, partial_qkv)
+    )
+    outputs = over_lanes(jnp.broadcast_to(output_weight[None], (lanes,) + output_weight.shape))
+    outputs = jnp.swapaxes(outputs, 0, 1).reshape(output_weight.shape[0], -1)
+    units = jnp.stack([gate_weight, up_weight]).reshape(2, features, share, lanes, piece)
+    units = over_lanes(jnp.moveaxis(units, 3, 0))
+    units = jnp.transpose(units, (2, 1, 0, 3, 4)).reshape(features, 2 * groups * piece)
+
     query = rotate(
         rms_rows(held_qkv[:, : HEADS * HD].reshape(R_DEV, HEADS, HD), query_gain), positions
     ).astype(jnp.bfloat16)
@@ -155,7 +159,6 @@
         positions,
     ).astype(jnp.bfloat16)
     value_new = held_qkv[:, (HEADS + KVH) * HD :].reshape(R_DEV, KVH, HD)
-    kept, means, bias = compact_pages(old_cache, keep_rows, drop_weights)
     destination = dest_slots[0]
     fresh_ids = jnp.arange(pages_here, dtype=jnp.int32)
     inverse = jnp.sum(
@@ -232,26 +235,22 @@
         jnp.where(holders[None, :] == everyone[:, None], everyone[None, :], 0), axis=1
     )
     projected = jnp.dot(
-        pick_rows(back, attention), output_weight, preferred_element_type=jnp.float32
-    )
-    projected = projected + jnp.where(group == 0, hidden_in.astype(jnp.float32), 0.0)
-
-    share = groups // lanes
-    blocks = jnp.moveaxis(projected.reshape(requests, share, 1, features), 0, 2)
-    blocks = jnp.broadcast_to(blocks, (share, lanes, requests, features))
-    mid = jnp.sum(exchange(blocks.reshape(groups, requests, features)), axis=0)
-    mid = to_block_owner(mid.astype(jnp.bfloat16)).astype(jnp.float32)
+        pick_rows(back, attention), outputs, preferred_element_type=jnp.float32
+    )
+
+    blocks = jnp.swapaxes(projected.reshape(requests, groups, features), 0, 1)
+    hidden_here = lax.dynamic_slice_in_dim(whole, group * features, features, 1)
+    mid = hidden_here.astype(jnp.float32) + jnp.sum(exchange(blocks), axis=0)
+    mid = mid.astype(jnp.bfloat16).astype(jnp.float32)
     squares = jnp.sum(mid * mid, axis=1, keepdims=True)
     gain_here = lax.dynamic_slice_in_dim(feedforward_gain, group * features, features, 0)
     inputs_mid = (mid * gain_here).astype(jnp.bfloat16)
-    local_units = gate_weight.shape[1]
-    piece = local_units // groups
-    gates = jnp.dot(inputs_mid, gate_weight, preferred_element_type=jnp.float32)
-    ups = jnp.dot(inputs_mid, up_weight, preferred_element_type=jnp.float32)
+    both = jnp.dot(inputs_mid, units, preferred_element_type=jnp.float32)
+    both = both.reshape(requests, 2, groups, piece)
     both = jnp.concatenate(
         [
-            gates.reshape(requests, groups, piece),
-            ups.reshape(requests, groups, piece),
+            both[:, 0],
+            both[:, 1],
             jnp.broadcast_to(squares[:, :, None], (requests, groups, 1)),
         ],
         axis=2,
@@ -260,7 +259,7 @@
     factor = lax.rsqrt(sums[:, 2 * piece :] / D + epsilon)
     gate = sums[:, :piece] * factor
     active = (jax.nn.silu(gate) * (sums[:, piece : 2 * piece] * factor)).astype(jnp.bfloat16)
-    active_here = lax.all_gather(to_block_owner(active), "head", axis=1, tiled=True)
+    active_here = lax.all_gather(active, "head", axis=1, tiled=True)
     down = jnp.dot(active_here, down_weight, preferred_element_type=jnp.float32)
     residual = [jnp.where(group == lane * share + k, mid, 0.0) for k in range(share)]
     down = down + jnp.concatenate(residual, axis=1)

time: 99.6 us -> 122 us (1.22)
  waiting for transfers between devices: 16.2 us -> 46 us
  blocking collectives: 42.8 us -> 22.2 us
  starting transfers between devices: 15.7 us -> 24.1 us
  local copies, waits for them, and re-layouts: 10.8 us -> 15.3 us
    all_to_all x0 -> x2, waiting for transfers between devices: none -> 26.3 us  [over_lanes(): lax.all_to_all(parts, 'head', split_axis=0, concat_axis=0, tiled=True)]
    all_to_all x2 -> x1, blocking collectives: 25.8 us -> 10.4 us  [exchange(): return lax.all_to_all(parts, 'req', split_axis=0, concat_axis=0, tiled=True)]
    all_to_all x0 -> x2, starting transfers between devices: none -> 7.02 us  [over_lanes(): lax.all_to_all(parts, 'head', split_axis=0, concat_axis=0, tiled=True)]
    all_gather x1, blocking collectives: 10.5 us -> 5.19 us  [on_device(): active_here = lax.all_gather(active, 'head', axis=1, tiled=True)]
    all_to_all x1 -> x2, waiting for transfers between devices: 6.63 us -> 10.2 us  [exchange(): return lax.all_to_all(parts, 'req', split_axis=0, concat_axis=0, tiled=True)]
    all_to_all x1 -> x2, starting transfers between devices: 4.01 us -> 6.78 us  [exchange(): return lax.all_to_all(parts, 'req', split_axis=0, concat_axis=0, tiled=True)]
    optimization_barrier x0 -> x2, local copies, waits for them, and re-layouts: none -> 2.65 us  [on_device(): lax.optimization_barrier((output_weight, gate_weight, up_weight, means, p...]
    ppermute x2 -> x0, starting transfers between devices: 1.32 us -> none  [to_block_owner(): return lax.ppermute(rows, both_axes, pairs)]
  transfers between devices with their start and end apart: 5 -> 6, of which waited for: 3 -> 6; matrix products, arithmetic and copies ran while one was open for 10% -> 12% of each run, Pallas kernels for 0% -> 0%
where the time goes in v3:
time: 122 us; the launch traced here: 121 us
  waiting for transfers between devices  46 us (38%)
  starting transfers between devices  24.1 us (20%)
  blocking collectives  22.2 us (18%)
  local copies, waits for them, and re-layouts  15.3 us (13%)
  matrix products  6.58 us (5%)
  other arithmetic  6.03 us (5%)
    all_to_all x2, waiting for transfers between devices, over_lanes(): lax.all_to_all(parts, 'head', split_axis=0, concat_axis=0, tiled=True)  26.3 us
    all_to_all x1, blocking collectives, exchange(): return lax.all_to_all(parts, 'req', split_axis=0, concat_axis=0, tiled=True)  10.4 us
    all_to_all x2, waiting for transfers between devices, exchange(): return lax.all_to_all(parts, 'req', split_axis=0, concat_axis=0, tiled=True)  10.2 us
    all_to_all x1, waiting for transfers between devices, on_device(): came = lax.all_to_all(parts, both_axes, 0, 0, tiled=True)  7.7 us
    all_to_all x2, starting transfers between devices, over_lanes(): lax.all_to_all(parts, 'head', split_axis=0, concat_axis=0, tiled=True)  7.02 us
    all_to_all x2, starting transfers between devices, exchange(): return lax.all_to_all(parts, 'req', split_axis=0, concat_axis=0, tiled=True)  6.78 us
    all_gather x1, blocking collectives, on_device(): whole = lax.all_gather(hidden_in, 'head', axis=1, tiled=True)  6.56 us
    all_to_all x1, starting transfers between devices, on_device(): lax.all_to_all(sent, both_axes, split_axis=0, concat_axis=0, tiled=True)  6.33 us
  transfers between devices with their start and end apart: 6, of which 6 were waited for; matrix products, arithmetic and copies ran while one was open for 12% of the time, Pallas kernels for 0%

profile of v3, /device:TPU:0, one launch (start us, length us, event | category | flops | bytes accessed | tf_op | source)
XLA Modules:
  0.0 121.3 jit_solution(12578455115748690961)
XLA Ops:
  0.7 6.6 %all_gather.6 = bf16[16,2048]{1,0:T(8,128)(2,1)S(1)} all-gather(bf16[16,512]{1,0:T(8,128)(2,1)} %param.17), channel_id=1, replica_groups=mesh['req'=8,'head'=4] {'head'}, dimensions={1}, use_global_device_ids=true | all-gather | bytes 81920 | tf_op jit(solution)/shard_map/all_gather | solution.py:130
  8.9 1.2 %fusion.8 = f32[16,480]{1,0:T(8,128)S(1)} fusion(bf16[256,480]{0,1:T(8,128)(2,1)} %param.22, f32[16,2048]{1,0:T(8,128)S(1)} %convert_element_type.79, s32[]{:T(128)S(6)} %select_n.147, f32[256]{0:T(256)S(1)} %dynamic-slice, f32[16]{0:T(128)S(1)} %add_rsqrt_fusion.2, s32[16]{0:T(128)S(1)} %compare_select_fusion.4), kind=kOutput, calls=%fused_computation.21 | convolution fusion | flops 4079872 | bytes 294916 | tf_op jit(solution)/shard_map/dot_general | solution.py:134
  10.9 6.3 %all-to-all-start = ((f32[32,2,480]{2,1,0:T(2,128)}), f32[32,2,480]{2,1,0:T(2,128)S(1)}, u32[]{:S(2)}, u32[]{:S(2)}) async-start(f32[32,2,480]{2,1,0:T(2,128)} %bitcast.11), calls=%async_computation | async-start | bytes 262144 | tf_op jit(solution)/shard_map/all_to_all | solution.py:138
  21.9 1.1 copy.172
  23.6 1.8 %all-to-all-done = f32[32,2,480]{2,1,0:T(2,128)S(1)} async-done(((f32[32,2,480]{2,1,0:T(2,128)}), f32[32,2,480]{2,1,0:T(2,128)S(1)}, u32[]{:S(2)}, u32[]{:S(2)}) %all-to-all-start) | async-done | bytes 122912 | tf_op jit(solution)/shard_map/all_to_all | solution.py:138
  26.7 1.4 %fusion.69 = (f32[2,5,4]{2,0,1:T(2,128)S(1)}, f32[2,5,4,8,64]{4,2,0,3,1:T(4,128)S(1)}) fusion(bf16[2,5,4,64]{3,2,0,1:T(4,128)(2,1)S(1)} %pad_maximum_fusion, bf16[8,64,5,64,1]{1,3,2,0,4:T(8,128)(2,1)} %bitcast.125, pred[2,8,64]{2,0,1:T(4,128)(4,1)S(1)} %broadcast_and_fusion), kind=kOutput, calls=%fused_computation.145 | convolution fusion | flops 2682840 | bytes 415904 | tf_op jit(solution)/shard_map/rngd,pmnd->rngpm/dot_general | solution.py:181
  30.8 4.0 %all-to-all-start.1 = ((f32[32,2,320]{2,1,0:T(2,128)}), f32[32,2,320]{2,1,0:T(2,128)S(1)}, u32[]{:S(2)}, u32[]{:S(2)}) async-start(f32[32,2,320]{2,1,0:T(2,128)} %bitcast.28), calls=%async_computation.1 | async-start | bytes 196608 | tf_op jit(solution)/shard_map/all_to_all | solution.py:228
  35.0 7.7 %all-to-all-done.1 = f32[32,2,320]{2,1,0:T(2,128)S(1)} async-done(((f32[32,2,320]{2,1,0:T(2,128)}), f32[32,2,320]{2,1,0:T(2,128)S(1)}, u32[]{:S(2)}, u32[]{:S(2)}) %all-to-all-start.1) | async-done | bytes 81952 | tf_op jit(solution)/shard_map/all_to_all | solution.py:228
  43.6 3.5 %all-to-all-start.2 = ((bf16[4,160,512]{2,1,0:T(8,128)(2,1)}), bf16[4,160,512]{2,1,0:T(8,128)(2,1)S(1)}, u32[]{:S(2)}, u32[]{:S(2)}) async-start(bf16[4,160,512]{2,1,0:T(8,128)(2,1)} %broadcast_in_dim.187), calls=%async_computation.2 | async-start | bytes 1310720 | tf_op jit(solution)/shard_map/all_to_all | solution.py:85
  47.3 9.9 %all-to-all-done.2 = bf16[4,160,512]{2,1,0:T(8,128)(2,1)S(1)} async-done(((bf16[4,160,512]{2,1,0:T(8,128)(2,1)}), bf16[4,160,512]{2,1,0:T(8,128)(2,1)S(1)}, u32[]{:S(2)}, u32[]{:S(2)}) %all-to-all-start.2) | async-done | bytes 655392 | tf_op jit(solution)/shard_map/all_to_all | solution.py:85
  57.4 1.0 convolution_bitcast_fusion
  58.4 3.4 %all-to-all-start.3 = ((f32[8,16,256]{2,1,0:T(8,128)}), f32[8,16,256]{2,1,0:T(8,128)S(1)}, u32[]{:S(2)}, u32[]{:S(2)}) async-start(f32[8,16,256]{2,1,0:T(8,128)} %convolution_bitcast_fusion), calls=%async_computation.3 | async-start | bytes 262144 | tf_op jit(solution)/shard_map/all_to_all | solution.py:81
  61.8 1.3 %copy.194 = bf16[256,1280]{0,1:T(8,128)(2,1)S(1)} copy(bf16[256,1280]{1,0:T(8,128)(2,1)} %param.24) | data formatting | bytes 1310720 | tf_op jit(solution)/shard_map/optimization_barrier | solution.py:145
  63.1 1.3 %copy.195 = bf16[256,1280]{0,1:T(8,128)(2,1)S(1)} copy(bf16[256,1280]{1,0:T(8,128)(2,1)} %param.25) | data formatting | bytes 1310720 | tf_op jit(solution)/shard_map/optimization_barrier | solution.py:145
  64.5 1.2 copy.196
  65.7 3.3 %all-to-all-done.3 = f32[8,16,256]{2,1,0:T(8,128)S(1)} async-done(((f32[8,16,256]{2,1,0:T(8,128)}), f32[8,16,256]{2,1,0:T(8,128)S(1)}, u32[]{:S(2)}, u32[]{:S(2)}) %all-to-all-start.3) | async-done | bytes 131104 | tf_op jit(solution)/shard_map/all_to_all | solution.py:81
  69.0 3.5 %all-to-all-start.4 = ((bf16[4,2,256,2,160]{2,4,3,1,0:T(8,128)(2,1)}), bf16[4,2,256,2,160]{2,4,3,1,0:T(8,128)(2,1)S(1)}, u32[]{:S(2)}, u32[]{:S(2)}) async-start(bf16[4,2,256,2,160]{2,4,3,1,0:T(8,128)(2,1)} %copy.196), calls=%async_computation.4 | async-start | bytes 2621440 | tf_op jit(solution)/shard_map/all_to_all | solution.py:85
  73.5 16.3 %all-to-all-done.4 = bf16[4,2,256,2,160]{2,4,3,1,0:T(8,128)(2,1)S(1)} async-done(((bf16[4,2,256,2,160]{2,4,3,1,0:T(8,128)(2,1)}), bf16[4,2,256,2,160]{2,4,3,1,0:T(8,128)(2,1)S(1)}, u32[]{:S(2)}, u32[]{:S(2)}) %all-to-all-start.4) | async-done | bytes 1310752 | tf_op jit(solution)/shard_map/all_to_all | solution.py:85
  90.6 10.4 %all_to_all.35 = f32[8,16,321]{2,1,0:T(8,128)S(1)} all-to-all(f32[8,16,321]{2,1,0:T(8,128)S(1)} %maximum_bitcast_fusion.1), channel_id=1, replica_groups=mesh['req'=8,'head'=4] {'req'}, dimensions={0} | all-to-all | bytes 328704 | tf_op jit(solution)/shard_map/all_to_all | solution.py:81
  101.4 5.2 %all-gather = bf16[4,160,16]{1,2,0:T(8,128)(2,1)S(1)} all-gather(bf16[1,160,16]{1,2,0:T(8,128)(2,1)S(1)} %fusion.48), channel_id=1, replica_groups=mesh['req'=8,'head'=4] {'head'}, dimensions={0}, use_global_device_ids=true | all-gather | bytes 25600 | tf_op jit(solution)/shard_map/all_gather | solution.py:262
  107.6 3.4 %all-to-all-start.6 = ((f32[8,16,512]{2,1,0:T(8,128)}), f32[8,16,512]{2,1,0:T(8,128)S(1)}, u32[]{:S(2)}, u32[]{:S(2)}) async-start(f32[8,16,512]{2,1,0:T(8,128)} %broadcast_in_dim.190), calls=%async_computation.6 | async-start | bytes 524288 | tf_op jit(solution)/shard_map/all_to_all | solution.py:81
  111.2 1.2 gather_fusion.1
  112.3 1.5 %gather_fusion = bf16[8,64,640]{2,1,0:T(8,128)(2,1)} fusion(bf16[8,64,640]{2,1,0:T(8,128)(2,1)S(1)} %convolution_convert_fusion, s32[1024]{0:T(1024)S(1)} %pad_clamp_fusion.1), kind=kCustom, calls=%fused_computation | custom fusion | bytes 1310752 | tf_op jit(solution)/shard_map/gather | solution.py:167
  113.8 6.8 %all-to-all-done.6 = f32[8,16,512]{2,1,0:T(8,128)S(1)} async-done(((f32[8,16,512]{2,1,0:T(8,128)}), f32[8,16,512]{2,1,0:T(8,128)S(1)}, u32[]{:S(2)}, u32[]{:S(2)}) %all-to-all-start.6) | async-done | bytes 262176 | tf_op jit(solution)/shard_map/all_to_all | solution.py:81
  (126 shorter events, 16.7 us)
Async XLA Ops:
  0.6 19.0 %copy-start = (bf16[8,128,640]{2,1,0:T(8,128)(2,1)S(1)}, bf16[8,128,640]{2,1,0:T(8,128)(2,1)}, u32[]{:S(2)}) copy-start(bf16[8,128,640]{2,1,0:T(8,128)(2,1)} %param.27) | copy-start | bytes 3932164
  0.6 19.0 %copy-start.4 = (s32[8,64]{1,0:T(8,128)S(1)}, s32[8,64]{1,0:T(8,128)}, u32[]{:S(2)}) copy-start(s32[8,64]{1,0:T(8,128)} %param.28) | copy-start | bytes 6148
  0.7 18.2 %copy-start.1 = (s32[16]{0:T(128)S(1)}, s32[16]{0:T(128)}, u32[]{:S(2)}) copy-start(s32[16]{0:T(128)} %param.31) | copy-start | bytes 196
  0.7 18.9 %copy-start.6 = (s32[2,16]{1,0:T(2,128)S(1)}, s32[2,16]{1,0:T(2,128)}, u32[]{:S(2)}) copy-start(s32[2,16]{1,0:T(2,128)} %param.32) | copy-start | bytes 388
  10.9 14.6 %all-to-all-start = ((f32[32,2,480]{2,1,0:T(2,128)}), f32[32,2,480]{2,1,0:T(2,128)S(1)}, u32[]{:S(2)}, u32[]{:S(2)}) async-start(f32[32,2,480]{2,1,0:T(2,128)} %bitcast.11), calls=%async_computation | async-start | bytes 262144 | tf_op jit(solution)/shard_map/all_to_all | solution.py:138
  19.7 0.7 copy-start.5
  21.2 4.7 %copy-start.7 = (f32[64]{0:T(128)S(1)}, f32[64]{0:T(128)}, u32[]{:S(2)}) copy-start(f32[64]{0:T(128)} %param.19) | copy-start | bytes 772
  21.9 4.4 %copy-start.8 = (f32[64]{0:T(128)S(1)}, f32[64]{0:T(128)}, u32[]{:S(2)}) copy-start(f32[64]{0:T(128)} %param.20) | copy-start | bytes 772
  28.9 13.8 %copy-start.3 = (bf16[160,512]{1,0:T(8,128)(2,1)S(1)}, bf16[160,512]{1,0:T(8,128)(2,1)}, u32[]{:S(2)}) copy-start(bf16[160,512]{1,0:T(8,128)(2,1)} %param.23) | copy-start | bytes 491524
  30.8 11.8 %all-to-all-start.1 = ((f32[32,2,320]{2,1,0:T(2,128)}), f32[32,2,320]{2,1,0:T(2,128)S(1)}, u32[]{:S(2)}, u32[]{:S(2)}) async-start(f32[32,2,320]{2,1,0:T(2,128)} %bitcast.28), calls=%async_computation.1 | async-start | bytes 196608 | tf_op jit(solution)/shard_map/all_to_all | solution.py:228
  43.6 13.7 %all-to-all-start.2 = ((bf16[4,160,512]{2,1,0:T(8,128)(2,1)}), bf16[4,160,512]{2,1,0:T(8,128)(2,1)S(1)}, u32[]{:S(2)}, u32[]{:S(2)}) async-start(bf16[4,160,512]{2,1,0:T(8,128)(2,1)} %broadcast_in_dim.187), calls=%async_computation.2 | async-start | bytes 1310720 | tf_op jit(solution)/shard_map/all_to_all | solution.py:85
  58.4 10.7 %all-to-all-start.3 = ((f32[8,16,256]{2,1,0:T(8,128)}), f32[8,16,256]{2,1,0:T(8,128)S(1)}, u32[]{:S(2)}, u32[]{:S(2)}) async-start(f32[8,16,256]{2,1,0:T(8,128)} %convolution_bitcast_fusion), calls=%async_computation.3 | async-start | bytes 262144 | tf_op jit(solution)/shard_map/all_to_all | solution.py:81
  69.0 20.8 %all-to-all-start.4 = ((bf16[4,2,256,2,160]{2,4,3,1,0:T(8,128)(2,1)}), bf16[4,2,256,2,160]{2,4,3,1,0:T(8,128)(2,1)S(1)}, u32[]{:S(2)}, u32[]{:S(2)}) async-start(bf16[4,2,256,2,160]{2,4,3,1,0:T(8,128)(2,1)} %copy.196), calls=%async_computation.4 | async-start | bytes 2621440 | tf_op jit(solution)/shard_map/all_to_all | solution.py:85
  90.4 16.3 %copy-start.2 = (bf16[640,512]{1,0:T(8,128)(2,1)S(1)}, bf16[640,512]{1,0:T(8,128)(2,1)}, u32[]{:S(2)}) copy-start(bf16[640,512]{1,0:T(8,128)(2,1)} %param.26) | copy-start | bytes 1966084
  90.6 20.4 %copy-start.9 = (s32[1,8]{1,0:T(1,128)S(1)}, s32[1,8]{1,0:T(1,128)}, u32[]{:S(2)}) copy-start(s32[1,8]{1,0:T(1,128)} %param.30) | copy-start | bytes 100
  107.6 13.0 %all-to-all-start.6 = ((f32[8,16,512]{2,1,0:T(8,128)}), f32[8,16,512]{2,1,0:T(8,128)S(1)}, u32[]{:S(2)}, u32[]{:S(2)}) async-start(f32[8,16,512]{2,1,0:T(8,128)} %broadcast_in_dim.190), calls=%async_computation.6 | async-start | bytes 524288 | tf_op jit(solution)/shard_map/all_to_all | solution.py:81

commit v4 on v2

--- a/solution.py
+++ b/solution.py
@@ -1,6 +1,8 @@
 import jax
 import jax.numpy as jnp
 from jax import lax
+from jax.experimental import pallas as pl
+from jax.experimental.pallas import tpu as pltpu
 from jax.sharding import PartitionSpec as P
 
 D = 2048
@@ -100,7 +102,7 @@
     return jnp.sum(exchange(jnp.broadcast_to(partial[None], (groups,) + partial.shape)), axis=0)
 
 
-def on_device(
+def on_device_wide(
     hidden_in,
     attention_gain,
     query_gain,
@@ -268,6 +270,481 @@
     return (compact, summaries, result)
 
 
+TILE = 128
+bfloat = jnp.bfloat16
+single = jnp.float32
+
+
+def iota(shape, axis):
+    return lax.broadcasted_iota(jnp.int32, shape, axis)
+
+
+def run(kernel, outs, scalars, arrays, scratch=(), flops=0):
+    in_specs = [pl.BlockSpec(memory_space=pltpu.SMEM) for _ in scalars]
+    in_specs += [pl.BlockSpec(memory_space=pltpu.VMEM) for _ in arrays]
+    moved = sum(a.size * a.dtype.itemsize for a in list(arrays) + list(outs))
+    return pl.pallas_call(
+        kernel,
+        out_shape=list(outs),
+        in_specs=in_specs,
+        out_specs=[pl.BlockSpec(memory_space=pltpu.VMEM) for _ in outs],
+        scratch_shapes=list(scratch),
+        compiler_params=pltpu.CompilerParams(vmem_limit_bytes=16 * 2**20),
+        cost_estimate=pl.CostEstimate(flops=flops, bytes_accessed=moved, transcendentals=0),
+    )(*scalars, *arrays)
+
+
+def shaped(shape, dtype):
+    return jax.ShapeDtypeStruct(shape, dtype)
+
+
+def first_kernel(ids, whole, gain, holders, weight, sent, wide):
+    rows = whole.shape[0]
+    groups = rows // R_DEV
+    lanes = sent.shape[0] // groups
+    features, columns = weight.shape
+    values = whole[...].astype(single)
+    factor = lax.rsqrt(jnp.mean(values * values, axis=1, keepdims=True) + epsilon)
+    here = pl.ds(pl.multiple_of(ids[0] * features, features), features)
+    normed = (whole[:, here].astype(single) * factor * gain[:, here]).astype(bfloat)
+    order = (holders[...] == iota((rows, rows), 1)).astype(single).astype(bfloat)
+    normed = jnp.dot(order, normed, preferred_element_type=single).astype(bfloat)
+    wide[...] = jnp.zeros_like(wide)
+    wide[:, :columns] = jnp.dot(normed, weight[...], preferred_element_type=single)
+    for g in range(groups):
+        tile = jnp.concatenate(
+            [
+                wide[R_DEV * g : R_DEV * (g + 1), TILE * j : TILE * (j + 1)]
+                for j in range(wide.shape[1] // TILE)
+            ],
+            axis=0,
+        )
+        for k in range(lanes):
+            sent[g * lanes + k] = tile
+
+
+def compact_kernel(
+    dest, pages, keep, weights, compact, summaries, kept, means, bias, ordered, plain
+):
+    count, rows, _ = pages.shape
+    row = iota((rows, TILE), 0)
+    column = iota((rows, TILE), 1)
+    for p in range(count):
+        picks = (keep[p : p + 1, :] == row).astype(single)
+        dropped = weights[:, p : p + 1] * (1.0 - jnp.sum(picks, axis=1, keepdims=True))
+        total = jnp.sum(dropped, axis=0, keepdims=True)
+        high = dropped.astype(bfloat).astype(single)
+        rest = dropped - high
+        middle = rest.astype(bfloat).astype(single)
+        low = rest - middle
+        left = jnp.where(column == KEEP, high, picks)
+        left = jnp.where(column == KEEP + 1, middle, left)
+        left = jnp.where(column == KEEP + 2, low, left).astype(bfloat)
+        both = lax.dot_general(
+            left, pages[p], (((0,), (0,)), ((), ())), preferred_element_type=single
+        )
+        rows_kept = both[:KEEP].astype(bfloat)
+        kept[KEEP * p : KEEP * (p + 1), :] = rows_kept
+        slot = dest[p]
+        start = pl.multiple_of((slot & 1) * KEEP, KEEP)
+        compact[slot >> 1, pl.ds(start, KEEP), :] = rows_kept
+        mean = both[KEEP : KEEP + 1] + both[KEEP + 1 : KEEP + 2] + both[KEEP + 2 : KEEP + 3]
+        mean = mean / total
+        plain[p : p + 1, :] = mean
+        ordered[pl.ds(slot, 1), :] = mean
+        bias[p : p + 1, :] = jnp.broadcast_to(jnp.log(total), (1, TILE))
+    means[...] = plain[...].astype(bfloat)
+    summaries[...] = ordered[...].astype(bfloat)
+
+
+def deal_kernel(ids, gate, up, own, one, two, three, dealt):
+    outs = (own, one, two, three)
+    lanes = len(outs)
+    piece = own.shape[1] // 4
+    block = lanes * piece
+    for k in range(lanes):
+        for b in range(2):
+            columns = slice(b * block + k * piece, b * block + (k + 1) * piece)
+            start = 2 * b * piece
+            dealt[k, :, start : start + piece] = gate[:, columns].astype(single)
+            dealt[k, :, start + piece : start + 2 * piece] = up[:, columns].astype(single)
+    for turn in range(lanes):
+        outs[turn][...] = dealt[lax.rem(ids[1] + turn, lanes)].astype(bfloat)
+
+
+def attend_kernel(
+    came, cosine, sine, gain, kept, means, bias, mask, extra_mask, sent, x, extra_k, extra_v, out
+):
+    lanes = 4
+    groups = came.shape[0] // lanes
+    width = (HEADS + 2 * KVH) * HD // lanes
+    span = -(-KVH * HD // TILE) * TILE
+    key_cols = slice(0, span)
+    value_cols = slice(KVW - span, KVW)
+    first_key = HEADS * HD // TILE * R_DEV
+    scale = HD ** (-0.5)
+    x[...] = jnp.zeros_like(x)
+    column = iota((8, TILE), 1)
+    for k in range(lanes):
+        tile = came[k]
+        for g in range(1, groups):
+            tile = tile + came[g * lanes + k]
+        tile = tile.astype(bfloat).astype(single)
+        base, shift = divmod(width * k, TILE)
+        base = base * R_DEV
+        if shift:
+            tile = pltpu.roll(tile, shift, 1)
+            x[base + 2 : base + 10, :] += jnp.where(column < shift, tile, 0.0)
+        x[base : base + 8, :] += jnp.where(column >= shift, tile, 0.0)
+    values = x[...]
+    same_head = (iota((TILE, TILE), 0) // HD == iota((TILE, TILE), 1) // HD).astype(single)
+    squares = jnp.dot(
+        values * values, same_head, precision=lax.Precision.HIGHEST, preferred_element_type=single
+    )
+    normed = values * lax.rsqrt(squares / HD + epsilon) * gain[...]
+    early = iota(values.shape, 1) % HD < HD // 2
+    swapped = jnp.where(
+        early, pltpu.roll(normed, TILE - HD // 2, 1), pltpu.roll(normed, HD // 2, 1)
+    )
+    turned = (normed * cosine[...] + swapped * sine[...]).astype(bfloat).astype(single)
+
+    rows = 24
+    row = iota((rows, TILE), 0)
+    half = iota((rows, TILE), 1) // HD
+    key_head = row >> 2
+    query = jnp.where(row < first_key, turned[:rows], 0.0)
+    other = pltpu.roll(query, HD, 1)
+    queries = []
+    for u in range(2):
+        placed = jnp.where(
+            half == (key_head & 1), jnp.where((key_head & 1) == u, query, other), 0.0
+        )
+        queries.append(
+            jnp.concatenate(
+                [jnp.where((key_head >> 1) == c, placed, 0.0) for c in range(span // TILE)], axis=1
+            )
+        )
+    queries = jnp.concatenate(queries, axis=0).astype(bfloat)
+
+    extra_k[...] = jnp.zeros_like(extra_k)
+    extra_v[...] = jnp.zeros_like(extra_v)
+    count = means.shape[0]
+    extra_k[:count, :] = means[:, key_cols].astype(single)
+    extra_v[:count, :] = means[:, value_cols].astype(single)
+    first_value = first_key + KVH * HD // TILE * R_DEV
+    for c in range(span // TILE):
+        at = slice(c * TILE, (c + 1) * TILE)
+        r = first_key + R_DEV * c
+        extra_k[count : count + R_DEV, at] = turned[r : r + R_DEV]
+        r = first_value + R_DEV * c
+        extra_v[count : count + R_DEV, at] = values[r : r + R_DEV]
+
+    def by_request(pair, size):
+        odd = iota((2 * rows, size), 0) & 1
+        return jnp.where(odd == 0, pair[0:1, :], pair[1:2, :])
+
+    def dot_rows(left, right):
+        return lax.dot_general(
+            left, right, (((1,), (1,)), ((), ())), preferred_element_type=single
+        )
+
+    entries = kept.shape[0]
+    extras = extra_k.shape[0]
+    scores = dot_rows(queries, kept[:, key_cols]) * scale + by_request(mask, entries)
+    diagonal = jnp.where(iota(bias.shape, 0) == iota(bias.shape, 1), bias[...], 0.0)
+    bias_row = jnp.sum(diagonal, axis=0, keepdims=True)[:, :extras]
+    extra = dot_rows(queries, extra_k[...].astype(bfloat)) * scale + bias_row
+    extra = extra + by_request(extra_mask, extras)
+    top = jnp.maximum(
+        jnp.max(scores, axis=1, keepdims=True), jnp.max(extra, axis=1, keepdims=True)
+    )
+    weight = jnp.where(scores > 0.5 * negative, jnp.exp(scores - top), 0.0)
+    extra_weight = jnp.where(extra > 0.5 * negative, jnp.exp(extra - top), 0.0)
+    mass = jnp.sum(weight, axis=1, keepdims=True) + jnp.sum(extra_weight, axis=1, keepdims=True)
+
+    def weighted(parts, right):
+        high = parts.astype(bfloat)
+        low = (parts - high.astype(single)).astype(bfloat)
+        return jnp.dot(high, right, preferred_element_type=single) + jnp.dot(
+            low, right, preferred_element_type=single
+        )
+
+    total = weighted(weight, kept[:, value_cols]) + weighted(
+        extra_weight, extra_v[...].astype(bfloat)
+    )
+    some = mass > 0.0
+    mass = jnp.where(some, mass, 1.0)
+    total = total / mass
+    level = jnp.where(some, top + jnp.log(mass), negative)
+
+    lead = (KVW - span) % TILE + (KVW // 2 - (KVW - span)) // HD
+    slot = key_head + lead
+    results = []
+    for u in range(2):
+        mine = total[rows * u : rows * (u + 1)]
+        picked = mine[:, :TILE]
+        for c in range(1, span // TILE):
+            picked = jnp.where((slot >> 1) == c, mine[:, c * TILE : (c + 1) * TILE], picked)
+        results.append(jnp.where((slot & 1) == u, picked, pltpu.roll(picked, HD, 1)))
+    out[:rows, :] = jnp.where(half == 0, results[0], results[1])
+    out[rows:, :] = jnp.where(half == 0, level[:rows], level[rows:])
+    own = HEADS * HD // groups
+    for g in range(groups):
+        r = own * g // TILE * R_DEV
+        tile = jnp.concatenate([out[r : r + 4, :], out[rows + r : rows + r + 4, :]], axis=0)
+        for k in range(lanes):
+            sent[g * lanes + k] = tile
+
+
+def project_kernel(ids, came, back, own, one, two, three, sent, rows):
+    weights = (own, one, two, three)
+    lanes = len(weights)
+    groups = came.shape[0] // lanes
+    features = own.shape[0]
+    requests = rows.shape[0]
+    for g in range(groups):
+        tiles = [came[g * lanes + k] for k in range(lanes)]
+        levels = [tile[4:8] for tile in tiles]
+        top = jnp.maximum(
+            jnp.maximum(levels[0], levels[1]), jnp.maximum(levels[2], levels[3])
+        )
+        shares = [jnp.exp(level - top) for level in levels]
+        mixed = sum(share * tile[0:4] for share, tile in zip(shares, tiles)) / sum(shares)
+        rows[R_DEV * g : R_DEV * (g + 1), :TILE] = mixed[:R_DEV]
+        rows[R_DEV * g : R_DEV * (g + 1), TILE:] = mixed[R_DEV:]
+    shift = lax.rem(2 * TILE - lax.rem(ids[0] * features, TILE), 2 * TILE)
+    attention = pltpu.roll(rows[...].astype(bfloat).astype(single), shift, 1)
+    order = (back[...] == iota((requests, requests), 1)).astype(single).astype(bfloat)
+    attention = jnp.dot(order, attention.astype(bfloat), preferred_element_type=single)
+    attention = attention[:, :features].astype(bfloat)
+    width = sent.shape[2]
+    for turn in range(lanes):
+        projected = jnp.dot(attention, weights[turn][...], preferred_element_type=single)
+        source = lax.rem(ids[1] + lanes - turn, lanes)
+        for b in range(2):
+            sent[2 * source + b] = projected[:, width * b : width * (b + 1)]
+
+
+def units_kernel(ids, came, whole, gain, own, one, two, three, sent, mid_out):
+    weights = (own, one, two, three)
+    lanes = len(weights)
+    groups, rows, features = came.shape
+    here = pl.ds(pl.multiple_of(ids[0] * features, features), features)
+    mid = came[0]
+    for g in range(1, groups):
+        mid = mid + came[g]
+    mid = (mid + whole[:, here].astype(single)).astype(bfloat)
+    mid_out[...] = mid
+    mid = mid.astype(single)
+    squares = jnp.sum(mid * mid, axis=1, keepdims=True)
+    inputs = (mid * gain[:, here]).astype(bfloat)
+    width = own.shape[1] // 2
+    for turn in range(lanes):
+        units = jnp.dot(inputs, weights[turn][...], preferred_element_type=single)
+        source = lax.rem(ids[1] + lanes - turn, lanes)
+        for b in range(2):
+            sent[2 * source + b, :, :width] = units[:, width * b : width * (b + 1)]
+            sent[2 * source + b, :, width:] = jnp.broadcast_to(
+                squares, (rows, sent.shape[2] - width)
+            )
+
+
+def active_kernel(came, active):
+    total = came[0]
+    for g in range(1, came.shape[0]):
+        total = total + came[g]
+    piece = active.shape[1]
+    factor = lax.rsqrt(total[:, 2 * piece : 2 * piece + 1] / D + epsilon)
+    gate = total[:, :piece] * factor
+    up = total[:, piece : 2 * piece] * factor
+    active[...] = (gate / (1.0 + jnp.exp(-gate)) * up).astype(bfloat)
+
+
+def down_kernel(ids, active, weight, mid, sent):
+    groups, rows, width = sent.shape
+    lanes, _, piece = active.shape
+    half = mid.shape[1]
+    down = jnp.dot(active[0], weight[:piece, :], preferred_element_type=single)
+    for k in range(1, lanes):
+        down = down + jnp.dot(
+            active[k], weight[piece * k : piece * (k + 1), :], preferred_element_type=single
+        )
+    added = mid[...].astype(single)
+    for b in range(width // half):
+        columns = slice(half * b, half * (b + 1))
+        mine = ids[0] == ids[1] * (width // half) + b
+        total = down[:, columns] + jnp.where(mine, added, 0.0)
+        for g in range(groups):
+            sent[g, :, columns] = total
+
+
+def result_kernel(came, result):
+    total = came[0]
+    for g in range(1, came.shape[0]):
+        total = total + came[g]
+    result[...] = total.astype(bfloat)
+
+
+def turned_lanes(value, turn):
+    lanes = lax.axis_size("head")
+    return lax.ppermute(value, "head", [(k, (k + turn) % lanes) for k in range(lanes)])
+
+
+def on_device(
+    hidden_in,
+    attention_gain,
+    query_gain,
+    key_gain,
+    feedforward_gain,
+    input_weight,
+    output_weight,
+    gate_weight,
+    up_weight,
+    down_weight,
+    old_cache,
+    keep_rows,
+    drop_weights,
+    dest_slots,
+    lengths,
+    page_table,
+    source,
+):
+    groups = lax.axis_size("req")
+    lanes = lax.axis_size("head")
+    group = lax.axis_index("req")
+    lane = lax.axis_index("head")
+    requests = hidden_in.shape[0]
+    pages_here = old_cache.shape[0]
+    everyone = jnp.arange(requests, dtype=jnp.int32)
+    ids = jnp.stack([group, lane]).astype(jnp.int32)
+    holders = held_request(everyone, source)
+    back = jnp.sum(
+        jnp.where(holders[None, :] == everyone[:, None], everyone[None, :], 0), axis=1
+    )
+    held = lax.dynamic_slice_in_dim(holders, group * R_DEV, R_DEV, 0)
+    chosen = held[:, None] == everyone[None, :]
+    held_len = jnp.sum(jnp.where(chosen, lengths[None, :], 0), axis=1)
+    devices = groups * lanes
+    features = D // groups
+    piece = gate_weight.shape[1] // groups
+
+    whole = lax.all_gather(hidden_in, "head", axis=1, tiled=True)
+    columns = input_weight.shape[1]
+    padded = -(-columns // TILE) * TILE
+    (sent,) = run(
+        first_kernel,
+        [shaped((devices, R_DEV * padded // TILE, TILE), single)],
+        [ids],
+        [whole, attention_gain[None, :], holders[:, None], input_weight],
+        [pltpu.VMEM((requests, padded), single)],
+        2 * requests * features * columns,
+    )
+    came = lax.all_to_all(sent, both_axes, 0, 0, tiled=True)
+
+    compact, summaries, kept, means, bias = run(
+        compact_kernel,
+        [
+            shaped((pages_here // 2, PAGE, KVW), bfloat),
+            shaped((pages_here, KVW), bfloat),
+            shaped((pages_here * KEEP, KVW), bfloat),
+            shaped((pages_here, KVW), bfloat),
+            shaped((pages_here, TILE), single),
+        ],
+        [dest_slots[0]],
+        [
+            old_cache,
+            jnp.pad(keep_rows, ((0, 0), (0, TILE - KEEP)), constant_values=-1),
+            drop_weights.T,
+        ],
+        [pltpu.VMEM((pages_here, KVW), single), pltpu.VMEM((pages_here, KVW), single)],
+        2 * pages_here * TILE * PAGE * KVW,
+    )
+    own_units, *other_units = run(
+        deal_kernel,
+        [shaped((features, 4 * piece), bfloat)] * lanes,
+        [ids],
+        [gate_weight, up_weight],
+        [pltpu.VMEM((lanes, features, 4 * piece), single)],
+    )
+    output_weights = [output_weight]
+    unit_weights = [own_units]
+    for turn in range(1, lanes):
+        output_weights.append(turned_lanes(output_weight, turn))
+    for turn in range(1, lanes):
+        unit_weights.append(turned_lanes(other_units[turn - 1], turn))
+
+    per_lane = NP // lanes
+    slots = jnp.arange(pages_here, dtype=jnp.int32)
+    logical = jnp.arange(NP, dtype=jnp.int32)
+    live = (logical[None, :] < held_len[:, None]) & (logical % lanes == lane)[None, :]
+    owner = jnp.any(
+        (page_table[:, :, None] == slots[None, None, :]) & live[:, :, None], axis=1
+    )
+    mask = jnp.where(owner[:, :, None] & (keep_rows >= 0)[None], 0.0, negative)
+    mask = mask.reshape(R_DEV, pages_here * KEEP)
+    own_entry = (jnp.arange(R_DEV)[:, None] == jnp.arange(8)[None, :]) & (lane == 0)
+    extra_mask = jnp.where(jnp.concatenate([owner, own_entry], axis=1), 0.0, negative)
+    half = HD // 2
+    frequency = 10000.0 ** (-jnp.arange(half, dtype=jnp.float32) / half)
+    angles = (held_len * PAGE).astype(jnp.float32)[:, None] * frequency[None, :]
+    cosine = jnp.tile(jnp.cos(angles), (16, TILE // half))
+    sine = jnp.sin(angles)
+    sine = jnp.tile(jnp.concatenate([-sine, sine], axis=1), (16, TILE // HD))
+    query_rows = HEADS * HD // TILE * R_DEV
+    gain_rows = jnp.concatenate(
+        [
+            jnp.broadcast_to(jnp.tile(query_gain, TILE // HD)[None], (query_rows, TILE)),
+            jnp.broadcast_to(jnp.tile(key_gain, TILE // HD)[None], (32 - query_rows, TILE)),
+        ]
+    )
+    span = -(-KVH * HD // TILE) * TILE
+    (parts,) = run(
+        attend_kernel,
+        [shaped((devices, 8, TILE), single)],
+        [],
+        [came, cosine, sine, gain_rows, kept, means, bias, mask, extra_mask],
+        [
+            pltpu.VMEM((32, TILE), single),
+            pltpu.VMEM((16, span), single),
+            pltpu.VMEM((16, span), single),
+            pltpu.VMEM((48, TILE), single),
+        ],
+        6 * 48 * pages_here * KEEP * span,
+    )
+    came = lax.all_to_all(parts, both_axes, 0, 0, tiled=True)
+    (sent,) = run(
+        project_kernel,
+        [shaped((groups, requests, features), single)],
+        [ids],
+        [came, back[:, None], *output_weights],
+        [pltpu.VMEM((requests, 2 * TILE), single)],
+        2 * requests * output_weight.size * lanes,
+    )
+    came = exchange(sent)
+    sent, mid = run(
+        units_kernel,
+        [shaped((groups, requests, 3 * TILE), single), shaped((requests, features), bfloat)],
+        [ids],
+        [came, whole, feedforward_gain[None, :], *unit_weights],
+        [],
+        4 * requests * gate_weight.size,
+    )
+    (active,) = run(active_kernel, [shaped((requests, piece), bfloat)], [], [exchange(sent)])
+    active = lax.all_gather(active, "head")
+    (sent,) = run(
+        down_kernel,
+        [shaped((groups, requests, down_weight.shape[1]), single)],
+        [ids],
+        [active, down_weight, mid],
+        [],
+        2 * requests * down_weight.size,
+    )
+    (result,) = run(
+        result_kernel, [shaped((requests, down_weight.shape[1]), bfloat)], [], [exchange(sent)]
+    )
+    return (compact, summaries, result)
+
+
 def solution(mesh):
     placed = (
         P(None, "head"),
@@ -289,7 +766,7 @@
         P(),
     )
     return jax.shard_map(
-        on_device,
+        on_device if mesh.shape["req"] <= DIRECT else on_device_wide,
         mesh=mesh,
         in_specs=placed,
         out_specs=(P(("req", "head"), None, None), P(("req", "head"), None), P(None, "head")),

time: 99.6 us -> 102 us (1.024)
  Pallas kernels: 0 us -> 13 us
  starting transfers between devices: 15.7 us -> 25 us
  waiting for transfers between devices: 16.2 us -> 7.35 us
  blocking collectives: 42.8 us -> 34.4 us
  matrix products: 6.52 us -> 0 us
  local copies, waits for them, and re-layouts: 10.8 us -> 15.4 us
    pallas_call x0 -> x9, Pallas kernels: none -> 13 us  [run(): pl.pallas_call(kernel, out_shape=list(outs), in_specs=in_specs, out_specs...]
    unnamed x26 -> x46, local copies, waits for them, and re-layouts: 0.22 us -> 11.4 us
    all_to_all x1, waiting for transfers between devices: 7.69 us -> 0.01 us  [on_device(): came = lax.all_to_all(parts, both_axes, 0, 0, tiled=True)]
    ppermute x2 -> x6, starting transfers between devices: 1.32 us -> 8.06 us  [turned_lanes(): lax.ppermute(value, 'head', [(k, (k + turn) % lanes) for k in range(lanes)])]
    dot_general x12 -> x0, matrix products: 6.52 us -> none  [the longest x1 1.38 us: on_device(): jnp.einsum('rngd,pmnd->rngpm', query_groups, row_keys, preferred_element_...]
    all_gather x1, blocking collectives: 10.5 us -> 5.19 us  [on_device(): active = lax.all_gather(active, 'head')]
    ppermute x2 -> x6, waiting for transfers between devices: 0.01 us -> 4.6 us  [turned_lanes(): lax.ppermute(value, 'head', [(k, (k + turn) % lanes) for k in range(lanes)])]
    all_to_all x1, waiting for transfers between devices: 6.63 us -> 2.74 us  [exchange(): return lax.all_to_all(parts, 'req', split_axis=0, concat_axis=0, tiled=True)]
  transfers between devices with their start and end apart: 5 -> 9, of which waited for: 3 -> 2; matrix products, arithmetic and copies ran while one was open for 10% -> 11% of each run, Pallas kernels for 0% -> 10%
where the time goes in v4:
time: 102 us; the launch traced here: 101 us
  blocking collectives  34.4 us (34%)
  starting transfers between devices  25 us (25%)
  local copies, waits for them, and re-layouts  15.4 us (15%)
  Pallas kernels  13 us (13%)
  waiting for transfers between devices  7.35 us (7%)
  other arithmetic  5.41 us (5%)
    all_to_all x2, blocking collectives, exchange(): return lax.all_to_all(parts, 'req', split_axis=0, concat_axis=0, tiled=True)  23.8 us
    pallas_call x9, Pallas kernels, run(): pl.pallas_call(kernel, out_shape=list(outs), in_specs=in_specs, out_specs...  13 us
    unnamed x46, local copies, waits for them, and re-layouts  11.4 us
    ppermute x6, starting transfers between devices, turned_lanes(): lax.ppermute(value, 'head', [(k, (k + turn) % lanes) for k in range(lanes)])  8.06 us
    all_to_all x1, starting transfers between devices, on_device(): came = lax.all_to_all(parts, both_axes, 0, 0, tiled=True)  5.83 us
    all_to_all x1, starting transfers between devices, exchange(): return lax.all_to_all(parts, 'req', split_axis=0, concat_axis=0, tiled=True)  5.65 us
    all_gather x1, blocking collectives, on_device(): whole = lax.all_gather(hidden_in, 'head', axis=1, tiled=True)  5.44 us
    all_to_all x1, starting transfers between devices, on_device(): came = lax.all_to_all(sent, both_axes, 0, 0, tiled=True)  5.42 us
  transfers between devices with their start and end apart: 9, of which 2 were waited for; matrix products, arithmetic and copies ran while one was open for 11% of the time, Pallas kernels for 10%

profile of v4, /device:TPU:0, one launch (start us, length us, event | category | flops | bytes accessed | tf_op | source)
XLA Modules:
  0.0 101.3 jit_solution(7560260027885868756)
XLA Ops:
  0.6 3.0 %collective-permute-start.1 = (bf16[160,512]{1,0:T(8,128)(2,1)}, bf16[160,512]{1,0:T(8,128)(2,1)}, u32[]{:S(2)}, u32[]{:S(2)}) collective-permute-start(bf16[160,512]{1,0:T(8,128)(2,1)} %own.1), channel_id=1, source_target_pairs={{0,2},{1,3},{2,0},{3,1},{4,6},{5,7},{6,4},{7,5},{8,10},{9,11},{10,... | collective-permute-start | bytes 491528 | tf_op jit(solution)/shard_map/ppermute | solution.py:590
  4.5 5.4 %all_gather.9.whole = bf16[16,2048]{1,0:T(8,128)(2,1)S(1)} all-gather(bf16[16,512]{1,0:T(8,128)(2,1)} %param.17), channel_id=1, replica_groups=mesh['req'=8,'head'=4] {'head'}, dimensions={1}, use_global_device_ids=true | all-gather | bytes 81920 | tf_op jit(solution)/shard_map/all_gather | solution.py:631
  9.9 1.1 %copy.26.weight = bf16[256,480]{1,0:T(8,128)(2,1)S(1)} copy(bf16[256,480]{0,1:T(8,128)(2,1)} %param.22) | data formatting | bytes 491520 | tf_op args[5]
  12.4 1.5 %shard_map.185 = f32[32,8,128]{2,1,0:T(8,128)} custom-call(s32[2]{0:T(128)S(1)} %pad_add_fusion.ids, bf16[16,2048]{1,0:T(8,128)(2,1)S(1)} %all_gather.9.whole, f32[1,2048]{1,0:T(1,128)S(1)} %bitcast.12, s32[16,1]{1,0:T(8,128)S(1)} %iota_select_fusion.holders, bf16[256,480]{1,0:T(8,128)(2,1)S(1)} %copy.26.weight), custom_call_target="tpu_custom_call" | custom-call | flops 3932160 | bytes 450624 | tf_op jit(solution)/shard_map/pallas_call | solution.py:286
  13.9 5.4 %all-to-all-start = ((f32[32,8,128]{2,1,0:T(8,128)}), f32[32,8,128]{2,1,0:T(8,128)S(1)}, u32[]{:S(2)}, u32[]{:S(2)}) async-start(f32[32,8,128]{2,1,0:T(8,128)} %shard_map.185), calls=%async_computation | async-start | bytes 262144 | tf_op jit(solution)/shard_map/all_to_all | solution.py:642
  19.5 0.8 fusion.6
  21.2 0.8 fusion.5
  25.6 1.3 %pad.4.keep = s32[8,128]{1,0:T(8,128)} pad(s32[8,64]{1,0:T(8,128)} %param.28, s32[]{:T(128)} %constant.86.clone.1), padding=0_0x0_64 | pad | bytes 6148 | tf_op jit(solution)/shard_map/jit(_pad)/pad | solution.py:656
  29.9 3.0 %shard_map.184 = (bf16[4,128,640]{2,1,0:T(8,128)(2,1)}, bf16[8,640]{1,0:T(8,128)(2,1)}, bf16[512,640]{1,0:T(8,128)(2,1)S(1)}, bf16[8,640]{1,0:T(8,128)(2,1)S(1)}, f32[8,128]{1,0:T(8,128)S(1)}) custom-call(s32[8]{0:T(128)S(1)} %bitcast.14, bf16[8,128,640]{2,1,0:T(8,128)(2,1)S(1)} %copy-done, s32[8,128]{1,0:T(8,128)S(1)} %copy-done.7, f32[128,8]{1,0:T(8,128)S(1)} %bitcast.10), custom_call_target="tpu_custom_call" | custom-call | flops 167772160 | bytes 2654208 | tf_op jit(solution)/shard_map/pallas_call | solution.py:286
  38.2 1.7 %shard_map.186 = f32[32,8,128]{2,1,0:T(8,128)} custom-call(f32[32,8,128]{2,1,0:T(8,128)S(1)} %all-to-all-done.came, f32[32,128]{1,0:T(8,128)S(1)} %copy-done.5, f32[32,128]{1,0:T(8,128)S(1)} %tile.15.sine, f32[32,128]{1,0:T(8,128)S(1)} %copy-done.6, bf16[512,640]{1,0:T(8,128)(2,1)S(1)} %get-tuple-element.16.kept, bf16[8,640]{1,0:T(8,128)(2,1)S(1)} %copy-done.13, ...), custom_call_target="tpu_custom_call" | custom-call | flops 56623104 | bytes 985216 | tf_op jit(solution)/shard_map/pallas_call | solution.py:286
  39.9 5.8 %all-to-all-start.1 = ((f32[32,8,128]{2,1,0:T(8,128)}), f32[32,8,128]{2,1,0:T(8,128)S(1)}, u32[]{:S(2)}, u32[]{:S(2)}) async-start(f32[32,8,128]{2,1,0:T(8,128)} %shard_map.186), calls=%async_computation.1 | async-start | bytes 262144 | tf_op jit(solution)/shard_map/all_to_all | solution.py:714
  46.1 1.5 %collective-permute-start.2 = (bf16[160,512]{1,0:T(8,128)(2,1)}, bf16[160,512]{1,0:T(8,128)(2,1)S(1)}, u32[]{:S(2)}, u32[]{:S(2)}) collective-permute-start(bf16[160,512]{1,0:T(8,128)(2,1)} %own.1), channel_id=1, source_target_pairs={{0,3},{1,0},{2,1},{3,2},{4,7},{5,4},{6,5},{7,6},{8,11},{9,8},{10,9... | collective-permute-start | bytes 491528 | tf_op jit(solution)/shard_map/ppermute | solution.py:590
  48.2 2.3 %shard_map.188 = (bf16[256,640]{1,0:T(8,128)(2,1)S(1)}, bf16[256,640]{1,0:T(8,128)(2,1)}, bf16[256,640]{1,0:T(8,128)(2,1)}, bf16[256,640]{1,0:T(8,128)(2,1)}) custom-call(s32[2]{0:T(128)S(1)} %copy-done.10, bf16[256,1280]{1,0:T(8,128)(2,1)S(1)} %copy-done.1, bf16[256,1280]{1,0:T(8,128)(2,1)S(1)} %copy-done.2), custom_call_target="tpu_custom_call" | custom-call | bytes 2621440 | tf_op jit(solution)/shard_map/pallas_call | solution.py:286
  50.7 1.7 %collective-permute-start.4 = (bf16[256,640]{1,0:T(8,128)(2,1)}, bf16[256,640]{1,0:T(8,128)(2,1)S(1)}, u32[]{:S(2)}, u32[]{:S(2)}) collective-permute-start(bf16[256,640]{1,0:T(8,128)(2,1)} %get-tuple-element.21), channel_id=1, source_target_pairs={{0,2},{1,3},{2,0},{3,1},{4,6},{5,7},{6,4},{7,5},{8,10},{9,11},{10,... | collective-permute-start | bytes 983048 | tf_op jit(solution)/shard_map/ppermute | solution.py:590
  52.4 1.4 %collective-permute-start.5 = (bf16[256,640]{1,0:T(8,128)(2,1)}, bf16[256,640]{1,0:T(8,128)(2,1)S(1)}, u32[]{:S(2)}, u32[]{:S(2)}) collective-permute-start(bf16[256,640]{1,0:T(8,128)(2,1)} %get-tuple-element.22), channel_id=1, source_target_pairs={{0,3},{1,0},{2,1},{3,2},{4,7},{5,4},{6,5},{7,6},{8,11},{9,8},{10,9... | collective-permute-start | bytes 983048 | tf_op jit(solution)/shard_map/ppermute | solution.py:590
  54.1 0.9 copy-done.4
  55.0 2.0 %shard_map.187 = f32[8,16,256]{2,1,0:T(8,128)} custom-call(s32[2]{0:T(128)S(1)} %copy-done.11, f32[32,8,128]{2,1,0:T(8,128)S(1)} %all-to-all-done.1.came, s32[16,1]{1,0:T(8,128)S(1)} %copy.27.back, bf16[160,512]{1,0:T(8,128)(2,1)S(1)} %copy-done.4, bf16[160,512]{1,0:T(8,128)(2,1)S(1)} %collective-permute-done.one, ...), custom_call_target="tpu_custom_call" | custom-call | flops 10485760 | bytes 917568 | tf_op jit(solution)/shard_map/pallas_call | solution.py:286
  57.0 5.6 %all-to-all-start.2 = ((f32[8,16,256]{2,1,0:T(8,128)}), f32[8,16,256]{2,1,0:T(8,128)S(1)}, u32[]{:S(2)}, u32[]{:S(2)}) async-start(f32[8,16,256]{2,1,0:T(8,128)} %shard_map.187), calls=%async_computation.2 | async-start | bytes 262144 | tf_op jit(solution)/shard_map/all_to_all | solution.py:83
  62.6 4.6 %collective-permute-done.5.three = bf16[256,640]{1,0:T(8,128)(2,1)S(1)} collective-permute-done((bf16[256,640]{1,0:T(8,128)(2,1)}, bf16[256,640]{1,0:T(8,128)(2,1)S(1)}, u32[]{:S(2)}, u32[]{:S(2)}) %collective-permute-start.5) | collective-permute-done | bytes 327712 | tf_op jit(solution)/shard_map/ppermute | solution.py:590
  67.2 2.7 %all-to-all-done.2.came = f32[8,16,256]{2,1,0:T(8,128)S(1)} async-done(((f32[8,16,256]{2,1,0:T(8,128)}), f32[8,16,256]{2,1,0:T(8,128)S(1)}, u32[]{:S(2)}, u32[]{:S(2)}) %all-to-all-start.2) | async-done | bytes 131104 | tf_op jit(solution)/shard_map/all_to_all | solution.py:83
  70.0 0.9 shard_map.189
  70.8 11.4 %all_to_all.25.came = f32[8,16,384]{2,1,0:T(8,128)S(1)} all-to-all(f32[8,16,384]{2,1,0:T(8,128)S(1)} %get-tuple-element.23), channel_id=1, replica_groups=mesh['req'=8,'head'=4] {'req'}, dimensions={0} | all-to-all | bytes 393216 | tf_op jit(solution)/shard_map/all_to_all | solution.py:83
  82.4 5.2 %all-gather = bf16[64,160]{1,0:T(8,128)(2,1)S(1)} all-gather(bf16[16,160]{1,0:T(8,128)(2,1)S(1)} %shard_map.190), channel_id=2, replica_groups=mesh['req'=8,'head'=4] {'head'}, dimensions={0}, use_global_device_ids=true | all-gather | bytes 25600 | tf_op jit(solution)/shard_map/all_gather | solution.py:733
  88.4 12.3 %all_to_all.26.came = f32[8,16,512]{2,1,0:T(8,128)S(1)} all-to-all(f32[8,16,512]{2,1,0:T(8,128)S(1)} %shard_map.191), channel_id=1, replica_groups=mesh['req'=8,'head'=4] {'req'}, dimensions={0} | all-to-all | bytes 524288 | tf_op jit(solution)/shard_map/all_to_all | solution.py:83
  (89 shorter events, 17.9 us)
Async XLA Ops:
  0.6 27.9 %copy-start = (bf16[8,128,640]{2,1,0:T(8,128)(2,1)S(1)}, bf16[8,128,640]{2,1,0:T(8,128)(2,1)}, u32[]{:S(2)}) copy-start(bf16[8,128,640]{2,1,0:T(8,128)(2,1)} %pages.1) | copy-start | bytes 3932164
  0.6 51.7 %collective-permute-start.1 = (bf16[160,512]{1,0:T(8,128)(2,1)}, bf16[160,512]{1,0:T(8,128)(2,1)}, u32[]{:S(2)}, u32[]{:S(2)}) collective-permute-start(bf16[160,512]{1,0:T(8,128)(2,1)} %own.1), channel_id=1, source_target_pairs={{0,2},{1,3},{2,0},{3,1},{4,6},{5,7},{6,4},{7,5},{8,10},{9,11},{10,... | collective-permute-start | bytes 491528 | tf_op jit(solution)/shard_map/ppermute | solution.py:590
  4.4 24.1 %copy-start.20 = (s32[16]{0:T(128)}, s32[16]{0:T(128)S(1)}, u32[]{:S(2)}) copy-start(s32[16]{0:T(128)S(1)} %get-tuple-element.28) | copy-start | bytes 196
  11.7 0.7 copy-start.14
  13.9 20.2 %all-to-all-start = ((f32[32,8,128]{2,1,0:T(8,128)}), f32[32,8,128]{2,1,0:T(8,128)S(1)}, u32[]{:S(2)}, u32[]{:S(2)}) async-start(f32[32,8,128]{2,1,0:T(8,128)} %shard_map.185), calls=%async_computation | async-start | bytes 262144 | tf_op jit(solution)/shard_map/all_to_all | solution.py:642
  28.5 0.7 copy-start.7
  29.9 17.7 %copy-start.1 = (bf16[256,1280]{1,0:T(8,128)(2,1)S(1)}, bf16[256,1280]{1,0:T(8,128)(2,1)}, u32[]{:S(2)}) copy-start(bf16[256,1280]{1,0:T(8,128)(2,1)} %gate.1) | copy-start | bytes 1966084
  29.9 17.7 %copy-start.2 = (bf16[256,1280]{1,0:T(8,128)(2,1)S(1)}, bf16[256,1280]{1,0:T(8,128)(2,1)}, u32[]{:S(2)}) copy-start(bf16[256,1280]{1,0:T(8,128)(2,1)} %up.1) | copy-start | bytes 1966084
  34.1 19.7 %copy-start.21 = (s32[16]{0:T(128)S(1)}, s32[16]{0:T(128)}, u32[]{:S(2)}) copy-start(s32[16]{0:T(128)} %copy-done.20) | copy-start | bytes 196
  34.1 20.0 %copy-start.11 = (s32[2]{0:T(128)S(1)}, s32[2]{0:T(128)}, u32[]{:S(2)}) copy-start(s32[2]{0:T(128)} %copy-done.9) | copy-start | bytes 28
  34.1 0.7 copy-start.5
  34.8 0.7 copy-start.6
  36.2 0.7 copy-start.13
  36.9 0.7 copy-start.17
  39.9 30.0 %copy-start.15 = (f32[2048]{0:T(1024)S(1)}, f32[2048]{0:T(1024)}, u32[]{:S(2)}) copy-start(f32[2048]{0:T(1024)} %param.21) | copy-start | bytes 24580
  39.9 14.1 %all-to-all-start.1 = ((f32[32,8,128]{2,1,0:T(8,128)}), f32[32,8,128]{2,1,0:T(8,128)S(1)}, u32[]{:S(2)}, u32[]{:S(2)}) async-start(f32[32,8,128]{2,1,0:T(8,128)} %shard_map.186), calls=%async_computation.1 | async-start | bytes 262144 | tf_op jit(solution)/shard_map/all_to_all | solution.py:714
  45.8 8.2 %collective-permute-start = (bf16[160,512]{1,0:T(8,128)(2,1)}, bf16[160,512]{1,0:T(8,128)(2,1)S(1)}, u32[]{:S(2)}, u32[]{:S(2)}) collective-permute-start(bf16[160,512]{1,0:T(8,128)(2,1)} %own.1), channel_id=1, source_target_pairs={{0,1},{1,2},{2,3},{3,0},{4,5},{5,6},{6,7},{7,4},{8,9},{9,10},{10,1... | collective-permute-start | bytes 491528 | tf_op jit(solution)/shard_map/ppermute | solution.py:590
  46.1 7.9 %collective-permute-start.2 = (bf16[160,512]{1,0:T(8,128)(2,1)}, bf16[160,512]{1,0:T(8,128)(2,1)S(1)}, u32[]{:S(2)}, u32[]{:S(2)}) collective-permute-start(bf16[160,512]{1,0:T(8,128)(2,1)} %own.1), channel_id=1, source_target_pairs={{0,3},{1,0},{2,1},{3,2},{4,7},{5,4},{6,5},{7,6},{8,11},{9,8},{10,9... | collective-permute-start | bytes 491528 | tf_op jit(solution)/shard_map/ppermute | solution.py:590
  50.6 12.1 %collective-permute-start.3 = (bf16[256,640]{1,0:T(8,128)(2,1)}, bf16[256,640]{1,0:T(8,128)(2,1)S(1)}, u32[]{:S(2)}, u32[]{:S(2)}) collective-permute-start(bf16[256,640]{1,0:T(8,128)(2,1)} %get-tuple-element.20), channel_id=1, source_target_pairs={{0,1},{1,2},{2,3},{3,0},{4,5},{5,6},{6,7},{7,4},{8,9},{9,10},{10,1... | collective-permute-start | bytes 983048 | tf_op jit(solution)/shard_map/ppermute | solution.py:590
  50.7 11.9 %collective-permute-start.4 = (bf16[256,640]{1,0:T(8,128)(2,1)}, bf16[256,640]{1,0:T(8,128)(2,1)S(1)}, u32[]{:S(2)}, u32[]{:S(2)}) collective-permute-start(bf16[256,640]{1,0:T(8,128)(2,1)} %get-tuple-element.21), channel_id=1, source_target_pairs={{0,2},{1,3},{2,0},{3,1},{4,6},{5,7},{6,4},{7,5},{8,10},{9,11},{10,... | collective-permute-start | bytes 983048 | tf_op jit(solution)/shard_map/ppermute | solution.py:590
  52.4 14.8 %collective-permute-start.5 = (bf16[256,640]{1,0:T(8,128)(2,1)}, bf16[256,640]{1,0:T(8,128)(2,1)S(1)}, u32[]{:S(2)}, u32[]{:S(2)}) collective-permute-start(bf16[256,640]{1,0:T(8,128)(2,1)} %get-tuple-element.22), channel_id=1, source_target_pairs={{0,3},{1,0},{2,1},{3,2},{4,7},{5,4},{6,5},{7,6},{8,11},{9,8},{10,9... | collective-permute-start | bytes 983048 | tf_op jit(solution)/shard_map/ppermute | solution.py:590
  54.0 0.9 copy-start.4
  57.0 30.6 %copy-start.3 = (bf16[640,512]{1,0:T(8,128)(2,1)S(1)}, bf16[640,512]{1,0:T(8,128)(2,1)}, u32[]{:S(2)}) copy-start(bf16[640,512]{1,0:T(8,128)(2,1)} %weight.2) | copy-start | bytes 1966084
  57.0 13.0 %all-to-all-start.2 = ((f32[8,16,256]{2,1,0:T(8,128)}), f32[8,16,256]{2,1,0:T(8,128)S(1)}, u32[]{:S(2)}, u32[]{:S(2)}) async-start(f32[8,16,256]{2,1,0:T(8,128)} %shard_map.187), calls=%async_computation.2 | async-start | bytes 262144 | tf_op jit(solution)/shard_map/all_to_all | solution.py:83
  (7 other events, 4.4 us)

commit v5 on v4

--- a/solution.py
+++ b/solution.py
@@ -1,5 +1,6 @@
 import jax
 import jax.numpy as jnp
+import numpy as np
 from jax import lax
 from jax.experimental import pallas as pl
 from jax.experimental.pallas import tpu as pltpu
@@ -279,10 +280,10 @@
     return lax.broadcasted_iota(jnp.int32, shape, axis)
 
 
-def run(kernel, outs, scalars, arrays, scratch=(), flops=0):
-    in_specs = [pl.BlockSpec(memory_space=pltpu.SMEM) for _ in scalars]
-    in_specs += [pl.BlockSpec(memory_space=pltpu.VMEM) for _ in arrays]
-    moved = sum(a.size * a.dtype.itemsize for a in list(arrays) + list(outs))
+def run(kernel, outs, far, near, scratch=(), flops=0):
+    in_specs = [pl.BlockSpec(memory_space=pltpu.HBM) for _ in far]
+    in_specs += [pl.BlockSpec(memory_space=pltpu.VMEM) for _ in near]
+    moved = sum(a.size * a.dtype.itemsize for a in [*far, *near, *outs])
     return pl.pallas_call(
         kernel,
         out_shape=list(outs),
@@ -291,26 +292,59 @@
         scratch_shapes=list(scratch),
         compiler_params=pltpu.CompilerParams(vmem_limit_bytes=16 * 2**20),
         cost_estimate=pl.CostEstimate(flops=flops, bytes_accessed=moved, transcendentals=0),
-    )(*scalars, *arrays)
+    )(*far, *near)
+
+
+def fetch(sources, targets, done):
+    copies = [
+        pltpu.make_async_copy(source, target, done.at[k])
+        for k, (source, target) in enumerate(zip(sources, targets))
+    ]
+    for copy in copies:
+        copy.start()
+    return copies
+
+
+def local_like(*arrays):
+    return [pltpu.VMEM(a.shape, a.dtype) for a in arrays]
+
+
+def scalar_like(*arrays):
+    return [pltpu.SMEM(a.shape, a.dtype) for a in arrays]
+
+
+def row_order(source, count, to_holder):
+    first, second = iota((count, count), 0), iota((count, count), 1)
+    if not to_holder:
+        first, second = second, first
+    order = (first == second) & (first % R_DEV == 0)
+    for c in range(source.shape[1]):
+        order = order | ((first == source[0, c] * R_DEV + 1) & (second == c * R_DEV + 1))
+    return order.astype(single).astype(bfloat)
 
 
 def shaped(shape, dtype):
     return jax.ShapeDtypeStruct(shape, dtype)
 
 
-def first_kernel(ids, whole, gain, holders, weight, sent, wide):
+def first_kernel(
+    source_far, gain_far, weight_far, whole, sent, source, gain, weight, wide, done
+):
+    copies = fetch((source_far, gain_far, weight_far), (source, gain, weight), done)
     rows = whole.shape[0]
     groups = rows // R_DEV
     lanes = sent.shape[0] // groups
-    features, columns = weight.shape
+    columns, features = weight.shape
     values = whole[...].astype(single)
     factor = lax.rsqrt(jnp.mean(values * values, axis=1, keepdims=True) + epsilon)
-    here = pl.ds(pl.multiple_of(ids[0] * features, features), features)
+    here = pl.ds(pl.multiple_of(lax.axis_index("req") * features, features), features)
+    wide[...] = jnp.zeros_like(wide)
+    for copy in copies:
+        copy.wait()
     normed = (whole[:, here].astype(single) * factor * gain[:, here]).astype(bfloat)
-    order = (holders[...] == iota((rows, rows), 1)).astype(single).astype(bfloat)
+    order = row_order(source, rows, True)
     normed = jnp.dot(order, normed, preferred_element_type=single).astype(bfloat)
-    wide[...] = jnp.zeros_like(wide)
-    wide[:, :columns] = jnp.dot(normed, weight[...], preferred_element_type=single)
+    wide[:, :columns] = dot_rows(normed, weight[...])
     for g in range(groups):
         tile = jnp.concatenate(
             [
@@ -323,45 +357,107 @@
             sent[g * lanes + k] = tile
 
 
-def compact_kernel(
-    dest, pages, keep, weights, compact, summaries, kept, means, bias, ordered, plain
-):
+def dot_rows(left, right):
+    return lax.dot_general(left, right, (((1,), (1,)), ((), ())), preferred_element_type=single)
+
+
+def prepare_kernel(*refs):
+    far, refs = refs[:12], refs[12:]
+    (compact, summaries, kept, added, tables, own, one, two, three), refs = refs[:9], refs[9:]
+    near, (ordered, plain, dealt, done) = refs[:12], refs[12:]
+    copies = fetch(far, near, done)
+    (dest, lengths, source, table, keep, weights, query_gain, key_gain, turns) = near[:9]
+    pages, gate, up = near[9:]
+    group = lax.axis_index("req")
+    lane = lax.axis_index("head")
+    lanes = lax.axis_size("head")
+    for copy in copies[:9]:
+        copy.wait()
+
+    carried = 0
+    for c in range(source.shape[1]):
+        carried = carried + jnp.where(source[0, c] == group, c, 0)
+    held_len = (lengths[0, group * R_DEV], lengths[0, carried * R_DEV + 1])
     count, rows, _ = pages.shape
-    row = iota((rows, TILE), 0)
-    column = iota((rows, TILE), 1)
+    owned = []
+    for r in range(R_DEV):
+        slots = []
+        for i in range(table.shape[1] // lanes):
+            j = i * lanes + lane
+            slots.append(jnp.where(j < held_len[r], table[r, j], -1))
+        owned.append(slots)
+
+    def owner(r, p):
+        found = owned[r][0] == p
+        for slot in owned[r][1:]:
+            found = found | (slot == p)
+        return found
+
+    row = iota((32, TILE), 0)
+    odd = (row & 1) == 1
+    half_rows = turns.shape[0] // 2
+    for part in range(2):
+        pair = [turns[pl.ds(part * half_rows + held_len[r], 1), :] for r in range(R_DEV)]
+        tables[32 * part : 32 * (part + 1), :] = jnp.where(odd, pair[1], pair[0])
+    query_rows = HEADS * HD // TILE * R_DEV
+    for c in range(TILE // HD):
+        columns = slice(HD * c, HD * (c + 1))
+        tables[64 : 64 + query_rows, columns] = jnp.broadcast_to(
+            query_gain[...], (query_rows, HD)
+        )
+        tables[64 + query_rows : 96, columns] = jnp.broadcast_to(
+            key_gain[...], (32 - query_rows, HD)
+        )
+
+    column = iota((1, TILE), 1)
+    entries = count * KEEP
+    added[...] = jnp.full_like(added, negative)
+    extra = [
+        jnp.where((column == count + r) & (lane == 0), 0.0, negative) for r in range(R_DEV)
+    ]
+    weight_columns = weights[...].T
+    rows_of = iota((rows, KEEP), 0)
+    place = iota((rows, KEEP), 1)
+    copies[9].wait()
     for p in range(count):
-        picks = (keep[p : p + 1, :] == row).astype(single)
-        dropped = weights[:, p : p + 1] * (1.0 - jnp.sum(picks, axis=1, keepdims=True))
+        picks = (keep[p : p + 1, :] == rows_of).astype(single)
+        dropped = weight_columns[:, p : p + 1] * (1.0 - jnp.sum(picks, axis=1, keepdims=True))
         total = jnp.sum(dropped, axis=0, keepdims=True)
         high = dropped.astype(bfloat).astype(single)
         rest = dropped - high
         middle = rest.astype(bfloat).astype(single)
-        low = rest - middle
-        left = jnp.where(column == KEEP, high, picks)
-        left = jnp.where(column == KEEP + 1, middle, left)
-        left = jnp.where(column == KEEP + 2, low, left).astype(bfloat)
+        terms = jnp.where(place == 0, high, jnp.where(place == 1, middle, rest - middle))
+        terms = jnp.where(place < 3, terms, 0.0)
+        left = jnp.concatenate([picks, terms], axis=1).astype(bfloat)
         both = lax.dot_general(
             left, pages[p], (((0,), (0,)), ((), ())), preferred_element_type=single
         )
         rows_kept = both[:KEEP].astype(bfloat)
         kept[KEEP * p : KEEP * (p + 1), :] = rows_kept
-        slot = dest[p]
+        slot = dest[0, p]
         start = pl.multiple_of((slot & 1) * KEEP, KEEP)
         compact[slot >> 1, pl.ds(start, KEEP), :] = rows_kept
         mean = both[KEEP : KEEP + 1] + both[KEEP + 1 : KEEP + 2] + both[KEEP + 2 : KEEP + 3]
         mean = mean / total
         plain[p : p + 1, :] = mean
         ordered[pl.ds(slot, 1), :] = mean
-        bias[p : p + 1, :] = jnp.broadcast_to(jnp.log(total), (1, TILE))
-    means[...] = plain[...].astype(bfloat)
+        live = jnp.where(keep[p : p + 1, :] >= 0, 0.0, negative)
+        for r in range(R_DEV):
+            here = owner(r, p)
+            added[r : r + 1, KEEP * p : KEEP * (p + 1)] = jnp.where(here, live, negative)
+            level = jnp.where(here, jnp.log(total), negative)
+            extra[r] = jnp.where(column == p, level, extra[r])
+    for r in range(R_DEV):
+        added[r : r + 1, entries : entries + TILE] = extra[r]
+    plain[count:, :] = jnp.zeros_like(plain[count:, :])
+    kept[entries:, :] = plain[...].astype(bfloat)
     summaries[...] = ordered[...].astype(bfloat)
 
-
-def deal_kernel(ids, gate, up, own, one, two, three, dealt):
     outs = (own, one, two, three)
-    lanes = len(outs)
     piece = own.shape[1] // 4
     block = lanes * piece
+    for copy in copies[10:]:
+        copy.wait()
     for k in range(lanes):
         for b in range(2):
             columns = slice(b * block + k * piece, b * block + (k + 1) * piece)
@@ -369,13 +465,11 @@
             dealt[k, :, start : start + piece] = gate[:, columns].astype(single)
             dealt[k, :, start + piece : start + 2 * piece] = up[:, columns].astype(single)
     for turn in range(lanes):
-        outs[turn][...] = dealt[lax.rem(ids[1] + turn, lanes)].astype(bfloat)
-
-
-def attend_kernel(
-    came, cosine, sine, gain, kept, means, bias, mask, extra_mask, sent, x, extra_k, extra_v, out
-):
-    lanes = 4
+        outs[turn][...] = dealt[lax.rem(lane + turn, lanes)].astype(bfloat)
+
+
+def attend_kernel(came, kept, added, tables, sent, x, extra_k, extra_v, out):
+    lanes = lax.axis_size("head")
     groups = came.shape[0] // lanes
     width = (HEADS + 2 * KVH) * HD // lanes
     span = -(-KVH * HD // TILE) * TILE
@@ -401,12 +495,13 @@
     squares = jnp.dot(
         values * values, same_head, precision=lax.Precision.HIGHEST, preferred_element_type=single
     )
-    normed = values * lax.rsqrt(squares / HD + epsilon) * gain[...]
+    normed = values * lax.rsqrt(squares / HD + epsilon) * tables[64:96, :]
     early = iota(values.shape, 1) % HD < HD // 2
     swapped = jnp.where(
         early, pltpu.roll(normed, TILE - HD // 2, 1), pltpu.roll(normed, HD // 2, 1)
     )
-    turned = (normed * cosine[...] + swapped * sine[...]).astype(bfloat).astype(single)
+    turned = normed * tables[0:32, :] + swapped * tables[32:64, :]
+    turned = turned.astype(bfloat).astype(single)
 
     rows = 24
     row = iota((rows, TILE), 0)
@@ -426,11 +521,11 @@
         )
     queries = jnp.concatenate(queries, axis=0).astype(bfloat)
 
-    extra_k[...] = jnp.zeros_like(extra_k)
-    extra_v[...] = jnp.zeros_like(extra_v)
-    count = means.shape[0]
-    extra_k[:count, :] = means[:, key_cols].astype(single)
-    extra_v[:count, :] = means[:, value_cols].astype(single)
+    extras = extra_k.shape[0]
+    entries = kept.shape[0] - extras
+    count = entries // KEEP
+    extra_k[...] = kept[entries:, key_cols].astype(single)
+    extra_v[...] = kept[entries:, value_cols].astype(single)
     first_value = first_key + KVH * HD // TILE * R_DEV
     for c in range(span // TILE):
         at = slice(c * TILE, (c + 1) * TILE)
@@ -439,22 +534,14 @@
         r = first_value + R_DEV * c
         extra_v[count : count + R_DEV, at] = values[r : r + R_DEV]
 
-    def by_request(pair, size):
-        odd = iota((2 * rows, size), 0) & 1
-        return jnp.where(odd == 0, pair[0:1, :], pair[1:2, :])
-
-    def dot_rows(left, right):
-        return lax.dot_general(
-            left, right, (((1,), (1,)), ((), ())), preferred_element_type=single
-        )
-
-    entries = kept.shape[0]
-    extras = extra_k.shape[0]
-    scores = dot_rows(queries, kept[:, key_cols]) * scale + by_request(mask, entries)
-    diagonal = jnp.where(iota(bias.shape, 0) == iota(bias.shape, 1), bias[...], 0.0)
-    bias_row = jnp.sum(diagonal, axis=0, keepdims=True)[:, :extras]
-    extra = dot_rows(queries, extra_k[...].astype(bfloat)) * scale + bias_row
-    extra = extra + by_request(extra_mask, extras)
+    def by_request(columns, size):
+        odd = (iota((2 * rows, size), 0) & 1) == 1
+        return jnp.where(odd, added[1:2, columns], added[0:1, columns])
+
+    scores = dot_rows(queries, kept[:entries, key_cols]) * scale
+    scores = scores + by_request(slice(0, entries), entries)
+    extra = dot_rows(queries, extra_k[...].astype(bfloat)) * scale
+    extra = extra + by_request(slice(entries, entries + extras), extras)
     top = jnp.maximum(
         jnp.max(scores, axis=1, keepdims=True), jnp.max(extra, axis=1, keepdims=True)
     )
@@ -469,7 +556,7 @@
             low, right, preferred_element_type=single
         )
 
-    total = weighted(weight, kept[:, value_cols]) + weighted(
+    total = weighted(weight, kept[:entries, value_cols]) + weighted(
         extra_weight, extra_v[...].astype(bfloat)
     )
     some = mass > 0.0
@@ -477,8 +564,7 @@
     total = total / mass
     level = jnp.where(some, top + jnp.log(mass), negative)
 
-    lead = (KVW - span) % TILE + (KVW // 2 - (KVW - span)) // HD
-    slot = key_head + lead
+    slot = key_head + (KVW // 2 - (KVW - span)) // HD
     results = []
     for u in range(2):
         mine = total[rows * u : rows * (u + 1)]
@@ -496,11 +582,11 @@
             sent[g * lanes + k] = tile
 
 
-def project_kernel(ids, came, back, own, one, two, three, sent, rows):
-    weights = (own, one, two, three)
-    lanes = len(weights)
+def project_kernel(source_far, weight_far, came, sent, source, weight, rows, done):
+    copies = fetch((source_far, weight_far), (source, weight), done)
+    lanes = lax.axis_size("head")
     groups = came.shape[0] // lanes
-    features = own.shape[0]
+    features = weight.shape[0]
     requests = rows.shape[0]
     for g in range(groups):
         tiles = [came[g * lanes + k] for k in range(lanes)]
@@ -512,77 +598,108 @@
         mixed = sum(share * tile[0:4] for share, tile in zip(shares, tiles)) / sum(shares)
         rows[R_DEV * g : R_DEV * (g + 1), :TILE] = mixed[:R_DEV]
         rows[R_DEV * g : R_DEV * (g + 1), TILE:] = mixed[R_DEV:]
-    shift = lax.rem(2 * TILE - lax.rem(ids[0] * features, TILE), 2 * TILE)
+    shift = lax.rem(2 * TILE - lax.rem(lax.axis_index("req") * features, TILE), 2 * TILE)
     attention = pltpu.roll(rows[...].astype(bfloat).astype(single), shift, 1)
-    order = (back[...] == iota((requests, requests), 1)).astype(single).astype(bfloat)
+    for copy in copies:
+        copy.wait()
+    order = row_order(source, requests, False)
     attention = jnp.dot(order, attention.astype(bfloat), preferred_element_type=single)
     attention = attention[:, :features].astype(bfloat)
+    projected = jnp.dot(attention, weight[...], preferred_element_type=single).astype(bfloat)
     width = sent.shape[2]
-    for turn in range(lanes):
-        projected = jnp.dot(attention, weights[turn][...], preferred_element_type=single)
-        source = lax.rem(ids[1] + lanes - turn, lanes)
-        for b in range(2):
-            sent[2 * source + b] = projected[:, width * b : width * (b + 1)]
-
-
-def units_kernel(ids, came, whole, gain, own, one, two, three, sent, mid_out):
+    share = groups // lanes
+    for g in range(groups):
+        b = g % share
+        for k in range(lanes):
+            sent[g * lanes + k] = projected[:, width * b : width * (b + 1)]
+
+
+def units_kernel(gain_far, came, whole, own, one, two, three, sent, mid_out, gain, done):
+    (copy,) = fetch((gain_far,), (gain,), done)
     weights = (own, one, two, three)
     lanes = len(weights)
-    groups, rows, features = came.shape
-    here = pl.ds(pl.multiple_of(ids[0] * features, features), features)
-    mid = came[0]
-    for g in range(1, groups):
-        mid = mid + came[g]
-    mid = (mid + whole[:, here].astype(single)).astype(bfloat)
+    devices, rows, features = came.shape
+    groups = devices // lanes
+    share = groups // lanes
+    group = lax.axis_index("req")
+    lane = lax.axis_index("head")
+    here = pl.ds(pl.multiple_of(group * features, features), features)
+    mid = whole[:, here].astype(single)
+    for g in range(groups):
+        mid = mid + came[g * lanes + group // share].astype(single)
+    mid = mid.astype(bfloat)
     mid_out[...] = mid
     mid = mid.astype(single)
     squares = jnp.sum(mid * mid, axis=1, keepdims=True)
+    width = own.shape[1] // 2
+    place = iota((rows, sent.shape[2] - width), 1)
+    high = squares.astype(bfloat).astype(single)
+    rest = squares - high
+    middle = rest.astype(bfloat).astype(single)
+    terms = jnp.where(place == 0, high, jnp.where(place == 1, middle, rest - middle))
+    terms = jnp.where(place < 3, terms, 0.0).astype(bfloat)
+    copy.wait()
     inputs = (mid * gain[:, here]).astype(bfloat)
-    width = own.shape[1] // 2
     for turn in range(lanes):
         units = jnp.dot(inputs, weights[turn][...], preferred_element_type=single)
-        source = lax.rem(ids[1] + lanes - turn, lanes)
-        for b in range(2):
-            sent[2 * source + b, :, :width] = units[:, width * b : width * (b + 1)]
-            sent[2 * source + b, :, width:] = jnp.broadcast_to(
-                squares, (rows, sent.shape[2] - width)
-            )
+        target = lax.rem(lane + lanes - turn, lanes) * share
+        for b in range(share):
+            sent[target + b, :, :width] = units[:, width * b : width * (b + 1)].astype(bfloat)
+            sent[target + b, :, width:] = terms
+
+
+def summed(came):
+    total = came[0].astype(single)
+    for g in range(1, came.shape[0]):
+        total = total + came[g].astype(single)
+    return total
 
 
 def active_kernel(came, active):
-    total = came[0]
-    for g in range(1, came.shape[0]):
-        total = total + came[g]
+    total = summed(came)
     piece = active.shape[1]
-    factor = lax.rsqrt(total[:, 2 * piece : 2 * piece + 1] / D + epsilon)
+    squares = total[:, 2 * piece : 2 * piece + 1] + total[:, 2 * piece + 1 : 2 * piece + 2]
+    squares = squares + total[:, 2 * piece + 2 : 2 * piece + 3]
+    factor = lax.rsqrt(squares / D + epsilon)
     gate = total[:, :piece] * factor
     up = total[:, piece : 2 * piece] * factor
     active[...] = (gate / (1.0 + jnp.exp(-gate)) * up).astype(bfloat)
 
 
-def down_kernel(ids, active, weight, mid, sent):
+def down_kernel(active, weight, mid, sent):
     groups, rows, width = sent.shape
     lanes, _, piece = active.shape
     half = mid.shape[1]
+    share = width // half
     down = jnp.dot(active[0], weight[:piece, :], preferred_element_type=single)
     for k in range(1, lanes):
         down = down + jnp.dot(
             active[k], weight[piece * k : piece * (k + 1), :], preferred_element_type=single
         )
-    added = mid[...].astype(single)
-    for b in range(width // half):
+    residual = mid[...].astype(single)
+    group = lax.axis_index("req")
+    lane = lax.axis_index("head")
+    for b in range(share):
         columns = slice(half * b, half * (b + 1))
-        mine = ids[0] == ids[1] * (width // half) + b
-        total = down[:, columns] + jnp.where(mine, added, 0.0)
+        mine = group == lane * share + b
+        total = (down[:, columns] + jnp.where(mine, residual, 0.0)).astype(bfloat)
         for g in range(groups):
             sent[g, :, columns] = total
 
 
 def result_kernel(came, result):
-    total = came[0]
-    for g in range(1, came.shape[0]):
-        total = total + came[g]
-    result[...] = total.astype(bfloat)
+    result[...] = summed(came).astype(bfloat)
+
+
+def rotation_table():
+    half = HD // 2
+    size = -(-(NP + 1) // 8) * 8
+    frequency = 10000.0 ** (-np.arange(half) / half)
+    angles = PAGE * np.arange(size)[:, None] * frequency[None, :]
+    cosine, sine = np.cos(angles), np.sin(angles)
+    wide = [np.tile(np.concatenate(pair, axis=1), (1, TILE // HD)) for pair in
+            ((cosine, cosine), (-sine, sine))]
+    return jnp.asarray(np.concatenate(wide), dtype=single)
 
 
 def turned_lanes(value, turn):
@@ -611,130 +728,117 @@
 ):
     groups = lax.axis_size("req")
     lanes = lax.axis_size("head")
-    group = lax.axis_index("req")
-    lane = lax.axis_index("head")
     requests = hidden_in.shape[0]
     pages_here = old_cache.shape[0]
-    everyone = jnp.arange(requests, dtype=jnp.int32)
-    ids = jnp.stack([group, lane]).astype(jnp.int32)
-    holders = held_request(everyone, source)
-    back = jnp.sum(
-        jnp.where(holders[None, :] == everyone[:, None], everyone[None, :], 0), axis=1
-    )
-    held = lax.dynamic_slice_in_dim(holders, group * R_DEV, R_DEV, 0)
-    chosen = held[:, None] == everyone[None, :]
-    held_len = jnp.sum(jnp.where(chosen, lengths[None, :], 0), axis=1)
     devices = groups * lanes
     features = D // groups
     piece = gate_weight.shape[1] // groups
+    copies = pltpu.SemaphoreType.DMA
 
     whole = lax.all_gather(hidden_in, "head", axis=1, tiled=True)
     columns = input_weight.shape[1]
     padded = -(-columns // TILE) * TILE
+    holds = source[None, :]
+    gain = attention_gain[None, :]
+    weight = input_weight.T
     (sent,) = run(
         first_kernel,
         [shaped((devices, R_DEV * padded // TILE, TILE), single)],
-        [ids],
-        [whole, attention_gain[None, :], holders[:, None], input_weight],
-        [pltpu.VMEM((requests, padded), single)],
+        [holds, gain, weight],
+        [whole],
+        [
+            *scalar_like(holds),
+            *local_like(gain, weight),
+            pltpu.VMEM((requests, padded), single),
+            copies((3,)),
+        ],
         2 * requests * features * columns,
     )
     came = lax.all_to_all(sent, both_axes, 0, 0, tiled=True)
 
-    compact, summaries, kept, means, bias = run(
-        compact_kernel,
+    scalars = [dest_slots, lengths[None, :], holds, page_table]
+    arrays = [
+        keep_rows,
+        drop_weights,
+        query_gain[None, :],
+        key_gain[None, :],
+        rotation_table(),
+        old_cache,
+        gate_weight,
+        up_weight,
+    ]
+    entries = pages_here * KEEP
+    extras = 16
+    compact, summaries, kept, added, tables, own_units, *other_units = run(
+        prepare_kernel,
         [
             shaped((pages_here // 2, PAGE, KVW), bfloat),
             shaped((pages_here, KVW), bfloat),
-            shaped((pages_here * KEEP, KVW), bfloat),
-            shaped((pages_here, KVW), bfloat),
-            shaped((pages_here, TILE), single),
+            shaped((entries + extras, KVW), bfloat),
+            shaped((8, entries + TILE), single),
+            shaped((96, TILE), single),
+        ]
+        + [shaped((features, 4 * piece), bfloat)] * lanes,
+        scalars + arrays,
+        [],
+        [
+            *scalar_like(*scalars),
+            *local_like(*arrays),
+            pltpu.VMEM((pages_here, KVW), single),
+            pltpu.VMEM((extras, KVW), single),
+            pltpu.VMEM((lanes, features, 4 * piece), single),
+            copies((len(scalars + arrays),)),
         ],
-        [dest_slots[0]],
-        [
-            old_cache,
-            jnp.pad(keep_rows, ((0, 0), (0, TILE - KEEP)), constant_values=-1),
-            drop_weights.T,
-        ],
-        [pltpu.VMEM((pages_here, KVW), single), pltpu.VMEM((pages_here, KVW), single)],
         2 * pages_here * TILE * PAGE * KVW,
-    )
-    own_units, *other_units = run(
-        deal_kernel,
-        [shaped((features, 4 * piece), bfloat)] * lanes,
-        [ids],
-        [gate_weight, up_weight],
-        [pltpu.VMEM((lanes, features, 4 * piece), single)],
-    )
-    output_weights = [output_weight]
-    unit_weights = [own_units]
-    for turn in range(1, lanes):
-        output_weights.append(turned_lanes(output_weight, turn))
-    for turn in range(1, lanes):
-        unit_weights.append(turned_lanes(other_units[turn - 1], turn))
-
-    per_lane = NP // lanes
-    slots = jnp.arange(pages_here, dtype=jnp.int32)
-    logical = jnp.arange(NP, dtype=jnp.int32)
-    live = (logical[None, :] < held_len[:, None]) & (logical % lanes == lane)[None, :]
-    owner = jnp.any(
-        (page_table[:, :, None] == slots[None, None, :]) & live[:, :, None], axis=1
-    )
-    mask = jnp.where(owner[:, :, None] & (keep_rows >= 0)[None], 0.0, negative)
-    mask = mask.reshape(R_DEV, pages_here * KEEP)
-    own_entry = (jnp.arange(R_DEV)[:, None] == jnp.arange(8)[None, :]) & (lane == 0)
-    extra_mask = jnp.where(jnp.concatenate([owner, own_entry], axis=1), 0.0, negative)
-    half = HD // 2
-    frequency = 10000.0 ** (-jnp.arange(half, dtype=jnp.float32) / half)
-    angles = (held_len * PAGE).astype(jnp.float32)[:, None] * frequency[None, :]
-    cosine = jnp.tile(jnp.cos(angles), (16, TILE // half))
-    sine = jnp.sin(angles)
-    sine = jnp.tile(jnp.concatenate([-sine, sine], axis=1), (16, TILE // HD))
-    query_rows = HEADS * HD // TILE * R_DEV
-    gain_rows = jnp.concatenate(
-        [
-            jnp.broadcast_to(jnp.tile(query_gain, TILE // HD)[None], (query_rows, TILE)),
-            jnp.broadcast_to(jnp.tile(key_gain, TILE // HD)[None], (32 - query_rows, TILE)),
-        ]
     )
     span = -(-KVH * HD // TILE) * TILE
     (parts,) = run(
         attend_kernel,
         [shaped((devices, 8, TILE), single)],
         [],
-        [came, cosine, sine, gain_rows, kept, means, bias, mask, extra_mask],
+        [came, kept, added, tables],
         [
             pltpu.VMEM((32, TILE), single),
-            pltpu.VMEM((16, span), single),
-            pltpu.VMEM((16, span), single),
+            pltpu.VMEM((extras, span), single),
+            pltpu.VMEM((extras, span), single),
             pltpu.VMEM((48, TILE), single),
         ],
-        6 * 48 * pages_here * KEEP * span,
-    )
+        6 * 48 * entries * span,
+    )
+    *other_units, _ = lax.optimization_barrier((*other_units, parts))
+    units = [own_units]
+    for turn in range(1, lanes):
+        units.append(turned_lanes(other_units[turn - 1], turn))
     came = lax.all_to_all(parts, both_axes, 0, 0, tiled=True)
     (sent,) = run(
         project_kernel,
-        [shaped((groups, requests, features), single)],
-        [ids],
-        [came, back[:, None], *output_weights],
-        [pltpu.VMEM((requests, 2 * TILE), single)],
-        2 * requests * output_weight.size * lanes,
-    )
-    came = exchange(sent)
+        [shaped((devices, requests, features), bfloat)],
+        [holds, output_weight],
+        [came],
+        [
+            *scalar_like(holds),
+            *local_like(output_weight),
+            pltpu.VMEM((requests, 2 * TILE), single),
+            copies((2,)),
+        ],
+        2 * requests * output_weight.size,
+    )
+    came = lax.all_to_all(sent, both_axes, 0, 0, tiled=True)
+    gain = feedforward_gain[None, :]
     sent, mid = run(
         units_kernel,
-        [shaped((groups, requests, 3 * TILE), single), shaped((requests, features), bfloat)],
-        [ids],
-        [came, whole, feedforward_gain[None, :], *unit_weights],
-        [],
+        [shaped((groups, requests, 3 * TILE), bfloat), shaped((requests, features), bfloat)],
+        [gain],
+        [came, whole, *units],
+        [*local_like(gain), copies((1,))],
         4 * requests * gate_weight.size,
     )
     (active,) = run(active_kernel, [shaped((requests, piece), bfloat)], [], [exchange(sent)])
     active = lax.all_gather(active, "head")
     (sent,) = run(
         down_kernel,
-        [shaped((groups, requests, down_weight.shape[1]), single)],
-        [ids],
+        [shaped((groups, requests, down_weight.shape[1]), bfloat)],
+        [],
         [active, down_weight, mid],
         [],
         2 * requests * down_weight.size,

time: 102 us -> 97.9 us (0.960)
  blocking collectives: 34.4 us -> 48 us
  starting transfers between devices: 25 us -> 12.2 us
  waiting for transfers between devices: 7.35 us -> 14.9 us
  other arithmetic: 5.41 us -> 0 us
  Pallas kernels: 13 us -> 9.36 us
  local copies, waits for them, and re-layouts: 15.4 us -> 11.9 us
    all_to_all x0 -> x1, blocking collectives: none -> 13.9 us  [on_device(): came = lax.all_to_all(parts, both_axes, 0, 0, tiled=True)]
    all_to_all x2 -> x0, starting transfers between devices: 11.5 us -> none  [the longest x1 5.83 us: on_device(): came = lax.all_to_all(parts, both_axes, 0, 0, tiled=True)]
    ppermute x6 -> x3, waiting for transfers between devices: 4.6 us -> 14.9 us  [turned_lanes(): lax.ppermute(value, 'head', [(k, (k + turn) % lanes) for k in range(lanes)])]
    ppermute x6 -> x3, starting transfers between devices: 8.06 us -> 3.15 us  [turned_lanes(): lax.ppermute(value, 'head', [(k, (k + turn) % lanes) for k in range(lanes)])]
    all_to_all x1 -> x2, starting transfers between devices: 5.42 us -> 9.06 us  [on_device(): came = lax.all_to_all(sent, both_axes, 0, 0, tiled=True)]
    pallas_call x9 -> x8, Pallas kernels: 13 us -> 9.36 us  [run(): pl.pallas_call(kernel, out_shape=list(outs), in_specs=in_specs, out_specs...]
    all_to_all x2 -> x0, waiting for transfers between devices: 2.74 us -> none  [the longest x1 2.74 us: exchange(): return lax.all_to_all(parts, 'req', split_axis=0, concat_axis=0, tiled=True)]
    another operation x6 -> x0, local copies, waits for them, and re-layouts: 2.12 us -> none  [the longest x2 0.71 us: on_device(): cosine = jnp.tile(jnp.cos(angles), (16, TILE // half))]
  transfers between devices with their start and end apart: 9 -> 5, of which waited for: 2 -> 3; matrix products, arithmetic and copies ran while one was open for 11% -> 0% of each run, Pallas kernels for 10% -> 4%
where the time goes in v5:
time: 97.9 us; the launch traced here: 97.2 us
  blocking collectives  48 us (49%)
  waiting for transfers between devices  14.9 us (15%)
  starting transfers between devices  12.2 us (12%)
  local copies, waits for them, and re-layouts  11.9 us (12%)
  Pallas kernels  9.36 us (10%)
    all_to_all x2, blocking collectives, exchange(): return lax.all_to_all(parts, 'req', split_axis=0, concat_axis=0, tiled=True)  22.5 us
    ppermute x3, waiting for transfers between devices, turned_lanes(): lax.ppermute(value, 'head', [(k, (k + turn) % lanes) for k in range(lanes)])  14.9 us
    all_to_all x1, blocking collectives, on_device(): came = lax.all_to_all(parts, both_axes, 0, 0, tiled=True)  13.9 us
    unnamed x38, local copies, waits for them, and re-layouts  11.9 us
    pallas_call x8, Pallas kernels, run(): pl.pallas_call(kernel, out_shape=list(outs), in_specs=in_specs, out_specs...  9.36 us
    all_to_all x2, starting transfers between devices, on_device(): came = lax.all_to_all(sent, both_axes, 0, 0, tiled=True)  9.06 us
    all_gather x1, blocking collectives, on_device(): whole = lax.all_gather(hidden_in, 'head', axis=1, tiled=True)  6.43 us
    all_gather x1, blocking collectives, on_device(): active = lax.all_gather(active, 'head')  5.22 us
  transfers between devices with their start and end apart: 5, of which 3 were waited for; matrix products, arithmetic and copies ran while one was open for 0% of the time, Pallas kernels for 4%

profile of v5, /device:TPU:0, one launch (start us, length us, event | category | flops | bytes accessed | tf_op | source)
XLA Modules:
  0.0 97.2 jit_solution(13021668855367372022)
XLA Ops:
  0.6 6.4 %all_gather.9.whole = bf16[16,2048]{1,0:T(8,128)(2,1)S(1)} all-gather(bf16[16,512]{1,0:T(8,128)(2,1)} %param.18), channel_id=1, replica_groups=mesh['req'=8,'head'=4] {'head'}, dimensions={1}, use_global_device_ids=true | all-gather | bytes 81920 | tf_op jit(solution)/shard_map/all_gather | solution.py:738
  7.1 0.9 copy-done.4
  8.0 0.7 copy-done.7
  9.4 1.5 %shard_map.194 = f32[32,8,128]{2,1,0:T(8,128)} custom-call(s32[1,8]{1,0:T(1,128)S(1)} %bitcast.12, f32[1,2048]{1,0:T(1,128)S(1)} %bitcast.10, bf16[480,256]{1,0:T(8,128)(2,1)S(1)} %bitcast.8, bf16[16,2048]{1,0:T(8,128)(2,1)S(1)} %all_gather.9.whole), custom_call_target="tpu_custom_call" | custom-call | flops 3932160 | bytes 450592 | tf_op jit(solution)/shard_map/pallas_call | solution.py:287
  10.9 6.3 %all-to-all-start = ((f32[32,8,128]{2,1,0:T(8,128)}), f32[32,8,128]{2,1,0:T(8,128)S(1)}, u32[]{:S(2)}, u32[]{:S(2)}) async-start(f32[32,8,128]{2,1,0:T(8,128)} %shard_map.194), calls=%async_computation | async-start | bytes 262144 | tf_op jit(solution)/shard_map/all_to_all | solution.py:757
  17.2 1.3 %copy-done = bf16[8,128,640]{2,1,0:T(8,128)(2,1)S(1)} copy-done((bf16[8,128,640]{2,1,0:T(8,128)(2,1)S(1)}, bf16[8,128,640]{2,1,0:T(8,128)(2,1)}, u32[]{:S(2)}) %copy-start) | copy-done | bytes 1310744
  18.5 1.1 %copy-done.2 = bf16[256,1280]{1,0:T(8,128)(2,1)S(1)} copy-done((bf16[256,1280]{1,0:T(8,128)(2,1)S(1)}, bf16[256,1280]{1,0:T(8,128)(2,1)}, u32[]{:S(2)}) %copy-start.2) | copy-done | bytes 655384
  19.6 1.1 %copy-done.3 = bf16[256,1280]{1,0:T(8,128)(2,1)S(1)} copy-done((bf16[256,1280]{1,0:T(8,128)(2,1)S(1)}, bf16[256,1280]{1,0:T(8,128)(2,1)}, u32[]{:S(2)}) %copy-start.3) | copy-done | bytes 655384
  20.7 0.7 copy-done.6
  22.1 0.7 copy-done.12
  22.8 0.7 copy-done.13
  26.8 3.7 %shard_map.193 = (bf16[4,128,640]{2,1,0:T(8,128)(2,1)}, bf16[8,640]{1,0:T(8,128)(2,1)}, bf16[528,640]{1,0:T(8,128)(2,1)S(1)}, f32[8,640]{1,0:T(8,128)S(1)}, f32[...) custom-call(s32[1,8]{1,0:T(1,128)S(1)} %copy-done.15, ...), custom_call_target="tpu_custom_call" | custom-call | flops 167772160 | bytes 5374720 | tf_op jit(solution)/shard_map/pallas_call | solution.py:287
  30.5 1.1 %shard_map.195 = f32[32,8,128]{2,1,0:T(8,128)S(1)} custom-call(f32[32,8,128]{2,1,0:T(8,128)S(1)} %all-to-all-done.came, bf16[528,640]{1,0:T(8,128)(2,1)S(1)} %get-tuple-element.19.kept, f32[8,640]{1,0:T(8,128)S(1)} %get-tuple-element.20.added, f32[96,128]{1,0:T(8,128)S(1)} %get-tuple-element.21.tables), custom_call_target="tpu_custom_call" | custom-call | flops 56623104 | bytes 1007616 | tf_op jit(solution)/shard_map/pallas_call | solution.py:287
  31.6 13.9 %all_to_all.25.came = f32[32,8,128]{2,1,0:T(8,128)S(1)} all-to-all(f32[32,8,128]{2,1,0:T(8,128)S(1)} %shard_map.195), channel_id=1, replica_groups=mesh['req'=8,'head'=4] {'req','head'}, dimensions={0} | all-to-all | bytes 262144 | tf_op jit(solution)/shard_map/all_to_all | solution.py:812
  45.5 1.5 %shard_map.196 = bf16[32,16,256]{2,1,0:T(8,128)(2,1)} custom-call(s32[1,8]{1,0:T(1,128)S(1)} %bitcast.14, bf16[160,512]{1,0:T(8,128)(2,1)S(1)} %copy-done.5, f32[32,8,128]{2,1,0:T(8,128)S(1)} %all_to_all.25.came), custom_call_target="tpu_custom_call" | custom-call | flops 2621440 | bytes 557088 | tf_op jit(solution)/shard_map/pallas_call | solution.py:287
  47.0 2.7 %all-to-all-start.2 = ((bf16[32,16,256]{2,1,0:T(8,128)(2,1)}), bf16[32,16,256]{2,1,0:T(8,128)(2,1)S(1)}, u32[]{:S(2)}, u32[]{:S(2)}) async-start(bf16[32,16,256]{2,1,0:T(8,128)(2,1)} %shard_map.196), calls=%async_computation.2 | async-start | bytes 524288 | tf_op jit(solution)/shard_map/all_to_all | solution.py:826
  49.9 1.7 %collective-permute-start.1 = (bf16[256,640]{1,0:T(8,128)(2,1)S(1)}, bf16[256,640]{1,0:T(8,128)(2,1)S(1)}, u32[]{:S(2)}, u32[]{:S(2)}) collective-permute-start(bf16[256,640]{1,0:T(8,128)(2,1)S(1)} %get-tuple-element.27), channel_id=1, source_target_pairs={{0,2},{1,3},{2,0},{3,1},{4,6},{5,7},{6,4},{7,5},{8,10},{9,11},{10,... | collective-permute-start | bytes 983048 | tf_op jit(solution)/shard_map/ppermute | solution.py:707
  51.6 1.3 %collective-permute-start.2 = (bf16[256,640]{1,0:T(8,128)(2,1)S(1)}, bf16[256,640]{1,0:T(8,128)(2,1)S(1)}, u32[]{:S(2)}, u32[]{:S(2)}) collective-permute-start(bf16[256,640]{1,0:T(8,128)(2,1)S(1)} %get-tuple-element.28), channel_id=1, source_target_pairs={{0,3},{1,0},{2,1},{3,2},{4,7},{5,4},{6,5},{7,6},{8,11},{9,8},{10,9... | collective-permute-start | bytes 983048 | tf_op jit(solution)/shard_map/ppermute | solution.py:707
  52.9 8.9 %collective-permute-done.one = bf16[256,640]{1,0:T(8,128)(2,1)S(1)} collective-permute-done((bf16[256,640]{1,0:T(8,128)(2,1)S(1)}, bf16[256,640]{1,0:T(8,128)(2,1)S(1)}, u32[]{:S(2)}, u32[]{:S(2)}) %collective-permute-start) | collective-permute-done | bytes 327712 | tf_op jit(solution)/shard_map/ppermute | solution.py:707
  61.9 1.0 collective-permute-done.1.two
  62.8 5.0 %collective-permute-done.2.three = bf16[256,640]{1,0:T(8,128)(2,1)S(1)} collective-permute-done((bf16[256,640]{1,0:T(8,128)(2,1)S(1)}, bf16[256,640]{1,0:T(8,128)(2,1)S(1)}, u32[]{:S(2)}, u32[]{:S(2)}) %collective-permute-start.2) | collective-permute-done | bytes 327712 | tf_op jit(solution)/shard_map/ppermute | solution.py:707
  68.4 12.4 %all_to_all.26.came = bf16[8,16,384]{2,1,0:T(8,128)(2,1)S(1)} all-to-all(bf16[8,16,384]{2,1,0:T(8,128)(2,1)S(1)} %get-tuple-element.29), channel_id=1, replica_groups=mesh['req'=8,'head'=4] {'req'}, dimensions={0} | all-to-all | bytes 196608 | tf_op jit(solution)/shard_map/all_to_all | solution.py:84
  80.9 5.2 %all-gather = bf16[64,160]{1,0:T(8,128)(2,1)S(1)} all-gather(bf16[16,160]{1,0:T(8,128)(2,1)S(1)} %shard_map.198), channel_id=2, replica_groups=mesh['req'=8,'head'=4] {'head'}, dimensions={0}, use_global_device_ids=true | all-gather | bytes 25600 | tf_op jit(solution)/shard_map/all_gather | solution.py:837
  86.4 10.2 %all_to_all.27.came = bf16[8,16,512]{2,1,0:T(8,128)(2,1)S(1)} all-to-all(bf16[8,16,512]{2,1,0:T(8,128)(2,1)S(1)} %shard_map.199), channel_id=1, replica_groups=mesh['req'=8,'head'=4] {'req'}, dimensions={0} | all-to-all | bytes 262144 | tf_op jit(solution)/shard_map/all_to_all | solution.py:84
  (37 shorter events, 6.3 us)
Async XLA Ops:
  7.1 0.9 copy-start.4
  8.0 0.7 copy-start.7
  8.7 0.7 copy-start.9
  10.9 19.7 %all-to-all-start = ((f32[32,8,128]{2,1,0:T(8,128)}), f32[32,8,128]{2,1,0:T(8,128)S(1)}, u32[]{:S(2)}, u32[]{:S(2)}) async-start(f32[32,8,128]{2,1,0:T(8,128)} %shard_map.194), calls=%async_computation | async-start | bytes 262144 | tf_op jit(solution)/shard_map/all_to_all | solution.py:757
  17.2 1.3 %copy-start = (bf16[8,128,640]{2,1,0:T(8,128)(2,1)S(1)}, bf16[8,128,640]{2,1,0:T(8,128)(2,1)}, u32[]{:S(2)}) copy-start(bf16[8,128,640]{2,1,0:T(8,128)(2,1)} %refs_9_.1) | copy-start | bytes 3932164
  18.5 1.1 %copy-start.2 = (bf16[256,1280]{1,0:T(8,128)(2,1)S(1)}, bf16[256,1280]{1,0:T(8,128)(2,1)}, u32[]{:S(2)}) copy-start(bf16[256,1280]{1,0:T(8,128)(2,1)} %refs_10_.1) | copy-start | bytes 1966084
  19.6 1.1 %copy-start.3 = (bf16[256,1280]{1,0:T(8,128)(2,1)S(1)}, bf16[256,1280]{1,0:T(8,128)(2,1)}, u32[]{:S(2)}) copy-start(bf16[256,1280]{1,0:T(8,128)(2,1)} %refs_11_.1) | copy-start | bytes 1966084
  20.7 0.7 copy-start.6
  21.4 0.7 copy-start.10
  22.1 0.7 copy-start.12
  22.8 0.7 copy-start.13
  23.5 0.7 copy-start.14
  24.1 0.7 copy-start.15
  24.8 0.7 copy-start.16
  25.4 0.7 copy-start.17
  26.1 0.7 copy-start.18
  26.8 18.7 %copy-start.5 = (bf16[160,512]{1,0:T(8,128)(2,1)S(1)}, bf16[160,512]{1,0:T(8,128)(2,1)}, u32[]{:S(2)}) copy-start(bf16[160,512]{1,0:T(8,128)(2,1)} %weight_far.1) | copy-start | bytes 491524
  26.8 18.7 %copy-start.11 = (s32[8]{0:T(128)S(1)}, s32[8]{0:T(128)}, u32[]{:S(2)}) copy-start(s32[8]{0:T(128)} %param.34) | copy-start | bytes 100
  30.5 37.4 %copy-start.8 = (f32[2048]{0:T(1024)S(1)}, f32[2048]{0:T(1024)}, u32[]{:S(2)}) copy-start(f32[2048]{0:T(1024)} %param.22) | copy-start | bytes 24580
  47.0 39.1 %copy-start.1 = (bf16[640,512]{1,0:T(8,128)(2,1)S(1)}, bf16[640,512]{1,0:T(8,128)(2,1)}, u32[]{:S(2)}) copy-start(bf16[640,512]{1,0:T(8,128)(2,1)} %weight.1) | copy-start | bytes 1966084
  47.0 20.8 %all-to-all-start.2 = ((bf16[32,16,256]{2,1,0:T(8,128)(2,1)}), bf16[32,16,256]{2,1,0:T(8,128)(2,1)S(1)}, u32[]{:S(2)}, u32[]{:S(2)}) async-start(bf16[32,16,256]{2,1,0:T(8,128)(2,1)} %shard_map.196), calls=%async_computation.2 | async-start | bytes 524288 | tf_op jit(solution)/shard_map/all_to_all | solution.py:826
  49.8 12.1 %collective-permute-start = (bf16[256,640]{1,0:T(8,128)(2,1)S(1)}, bf16[256,640]{1,0:T(8,128)(2,1)S(1)}, u32[]{:S(2)}, u32[]{:S(2)}) collective-permute-start(bf16[256,640]{1,0:T(8,128)(2,1)S(1)} %get-tuple-element.26), channel_id=1, source_target_pairs={{0,1},{1,2},{2,3},{3,0},{4,5},{5,6},{6,7},{7,4},{8,9},{9,10},{10,1... | collective-permute-start | bytes 983048 | tf_op jit(solution)/shard_map/ppermute | solution.py:707
  49.9 12.9 %collective-permute-start.1 = (bf16[256,640]{1,0:T(8,128)(2,1)S(1)}, bf16[256,640]{1,0:T(8,128)(2,1)S(1)}, u32[]{:S(2)}, u32[]{:S(2)}) collective-permute-start(bf16[256,640]{1,0:T(8,128)(2,1)S(1)} %get-tuple-element.27), channel_id=1, source_target_pairs={{0,2},{1,3},{2,0},{3,1},{4,6},{5,7},{6,4},{7,5},{8,10},{9,11},{10,... | collective-permute-start | bytes 983048 | tf_op jit(solution)/shard_map/ppermute | solution.py:707
  51.6 16.2 %collective-permute-start.2 = (bf16[256,640]{1,0:T(8,128)(2,1)S(1)}, bf16[256,640]{1,0:T(8,128)(2,1)S(1)}, u32[]{:S(2)}, u32[]{:S(2)}) collective-permute-start(bf16[256,640]{1,0:T(8,128)(2,1)S(1)} %get-tuple-element.28), channel_id=1, source_target_pairs={{0,3},{1,0},{2,1},{3,2},{4,7},{5,4},{6,5},{7,6},{8,11},{9,8},{10,9... | collective-permute-start | bytes 983048 | tf_op jit(solution)/shard_map/ppermute | solution.py:707

commit v6 on v5

--- a/solution.py
+++ b/solution.py
@@ -292,7 +292,7 @@
         scratch_shapes=list(scratch),
         compiler_params=pltpu.CompilerParams(vmem_limit_bytes=16 * 2**20),
         cost_estimate=pl.CostEstimate(flops=flops, bytes_accessed=moved, transcendentals=0),
-    )(*far, *near)
+    )(*[pltpu.with_memory_space_constraint(a, pltpu.HBM) for a in far], *near)
 
 
 def fetch(sources, targets, done):
@@ -465,7 +465,7 @@
             dealt[k, :, start : start + piece] = gate[:, columns].astype(single)
             dealt[k, :, start + piece : start + 2 * piece] = up[:, columns].astype(single)
     for turn in range(lanes):
-        outs[turn][...] = dealt[lax.rem(lane + turn, lanes)].astype(bfloat)
+        outs[turn][...] = dealt[lane ^ turn].astype(bfloat)
 
 
 def attend_kernel(came, kept, added, tables, sent, x, extra_k, extra_v, out):
@@ -642,7 +642,7 @@
     inputs = (mid * gain[:, here]).astype(bfloat)
     for turn in range(lanes):
         units = jnp.dot(inputs, weights[turn][...], preferred_element_type=single)
-        target = lax.rem(lane + lanes - turn, lanes) * share
+        target = (lane ^ turn) * share
         for b in range(share):
             sent[target + b, :, :width] = units[:, width * b : width * (b + 1)].astype(bfloat)
             sent[target + b, :, width:] = terms
@@ -702,9 +702,9 @@
     return jnp.asarray(np.concatenate(wide), dtype=single)
 
 
-def turned_lanes(value, turn):
+def swapped_lanes(value, turn):
     lanes = lax.axis_size("head")
-    return lax.ppermute(value, "head", [(k, (k + turn) % lanes) for k in range(lanes)])
+    return lax.ppermute(value, "head", [(k, k ^ turn) for k in range(lanes)])
 
 
 def on_device(
@@ -806,10 +806,10 @@
         6 * 48 * entries * span,
     )
     *other_units, _ = lax.optimization_barrier((*other_units, parts))
-    units = [own_units]
-    for turn in range(1, lanes):
-        units.append(turned_lanes(other_units[turn - 1], turn))
+    units = [swapped_lanes(other_units[turn - 1], turn) for turn in range(1, lanes)]
     came = lax.all_to_all(parts, both_axes, 0, 0, tiled=True)
+    came, *units[:2] = lax.optimization_barrier((came, *units[:2]))
+    units = [own_units, *units]
     (sent,) = run(
         project_kernel,
         [shaped((devices, requests, features), bfloat)],

time: 97.9 us -> 83.7 us (0.85)
  local copies, waits for them, and re-layouts: 11.9 us -> 0.01 us
  Pallas kernels: 9.36 us -> 12.1 us
  blocking collectives: 48 us -> 45.5 us
  waiting for transfers between devices: 14.9 us -> 13.7 us
  starting transfers between devices: 12.2 us -> 11.2 us
    unnamed x38 -> x2, local copies, waits for them, and re-layouts: 11.9 us -> 0.01 us
    ppermute x3, waiting for transfers between devices: 14.9 us -> 10.6 us  [swapped_lanes(): return lax.ppermute(value, 'head', [(k, k ^ turn) for k in range(lanes)])]
    all_to_all x2, waiting for transfers between devices: 0.01 us -> 3.1 us  [on_device(): came = lax.all_to_all(sent, both_axes, 0, 0, tiled=True)]
    all_to_all x1, blocking collectives: 13.9 us -> 11 us  [on_device(): came = lax.all_to_all(parts, both_axes, 0, 0, tiled=True)]
    pallas_call x8, Pallas kernels: 9.36 us -> 12.1 us  [run(): pl.pallas_call(kernel, out_shape=list(outs), in_specs=in_specs, out_specs...]
    ppermute x3, starting transfers between devices: 3.15 us -> 2.11 us  [swapped_lanes(): return lax.ppermute(value, 'head', [(k, k ^ turn) for k in range(lanes)])]
  transfers between devices with their start and end apart: 5 -> 5, of which waited for: 3 -> 2; matrix products, arithmetic and copies ran while one was open for 0% -> 0% of each run, Pallas kernels for 4% -> 6%
where the time goes in v6:
time: 83.7 us; the launch traced here: 83.3 us
  blocking collectives  45.5 us (54%)
  waiting for transfers between devices  13.7 us (16%)
  Pallas kernels  12.1 us (14%)
  starting transfers between devices  11.2 us (13%)
    all_to_all x2, blocking collectives, exchange(): return lax.all_to_all(parts, 'req', split_axis=0, concat_axis=0, tiled=True)  22.9 us
    pallas_call x8, Pallas kernels, run(): pl.pallas_call(kernel, out_shape=list(outs), in_specs=in_specs, out_specs...  12.1 us
    all_to_all x1, blocking collectives, on_device(): came = lax.all_to_all(parts, both_axes, 0, 0, tiled=True)  11 us
    ppermute x3, waiting for transfers between devices, swapped_lanes(): return lax.ppermute(value, 'head', [(k, k ^ turn) for k in range(lanes)])  10.6 us
    all_to_all x2, starting transfers between devices, on_device(): came = lax.all_to_all(sent, both_axes, 0, 0, tiled=True)  9.06 us
    all_gather x1, blocking collectives, on_device(): whole = lax.all_gather(hidden_in, 'head', axis=1, tiled=True)  6.43 us
    all_gather x1, blocking collectives, on_device(): active = lax.all_gather(active, 'head')  5.18 us
    all_to_all x2, waiting for transfers between devices, on_device(): came = lax.all_to_all(sent, both_axes, 0, 0, tiled=True)  3.1 us
  transfers between devices with their start and end apart: 5, of which 2 were waited for; matrix products, arithmetic and copies ran while one was open for 0% of the time, Pallas kernels for 6%

profile of v6, /device:TPU:0, one launch (start us, length us, event | category | flops | bytes accessed | tf_op | source)
XLA Modules:
  0.0 83.3 jit_solution(7927199166598490312)
XLA Ops:
  0.6 6.4 %all_gather.9.whole = bf16[16,2048]{1,0:T(8,128)(2,1)S(1)} all-gather(bf16[16,512]{1,0:T(8,128)(2,1)} %param.18), channel_id=1, replica_groups=mesh['req'=8,'head'=4] {'head'}, dimensions={1}, use_global_device_ids=true | all-gather | bytes 81920 | tf_op jit(solution)/shard_map/all_gather | solution.py:738
  7.1 1.9 %shard_map.194 = f32[32,8,128]{2,1,0:T(8,128)} custom-call(s32[1,8]{1,0:T(1,128)} %bitcast.12, f32[1,2048]{1,0:T(1,128)} %bitcast.10, bf16[480,256]{1,0:T(8,128)(2,1)} %bitcast.9, bf16[16,2048]{1,0:T(8,128)(2,1)S(1)} %all_gather.9.whole), custom_call_target="tpu_custom_call" | custom-call | flops 3932160 | bytes 450592 | tf_op jit(solution)/shard_map/pallas_call | solution.py:287
  9.0 6.3 %all-to-all-start = ((f32[32,8,128]{2,1,0:T(8,128)}), f32[32,8,128]{2,1,0:T(8,128)S(1)}, u32[]{:S(2)}, u32[]{:S(2)}) async-start(f32[32,8,128]{2,1,0:T(8,128)} %shard_map.194), calls=%async_computation | async-start | bytes 262144 | tf_op jit(solution)/shard_map/all_to_all | solution.py:757
  15.3 5.1 %shard_map.193 = (bf16[4,128,640]{2,1,0:T(8,128)(2,1)}, bf16[8,640]{1,0:T(8,128)(2,1)}, bf16[528,640]{1,0:T(8,128)(2,1)S(1)}, f32[8,640]{1,0:T(8,128)S(1)}, f32[...) custom-call(s32[1,8]{1,0:T(1,128)} %refs_0_.1, ...), custom_call_target="tpu_custom_call" | custom-call | flops 167772160 | bytes 5374720 | tf_op jit(solution)/shard_map/pallas_call | solution.py:287
  20.4 3.1 %all-to-all-done.came = f32[32,8,128]{2,1,0:T(8,128)S(1)} async-done(((f32[32,8,128]{2,1,0:T(8,128)}), f32[32,8,128]{2,1,0:T(8,128)S(1)}, u32[]{:S(2)}, u32[]{:S(2)}) %all-to-all-start) | async-done | bytes 131104 | tf_op jit(solution)/shard_map/all_to_all | solution.py:757
  23.5 1.1 %shard_map.195 = f32[32,8,128]{2,1,0:T(8,128)S(1)} custom-call(f32[32,8,128]{2,1,0:T(8,128)S(1)} %all-to-all-done.came, bf16[528,640]{1,0:T(8,128)(2,1)S(1)} %get-tuple-element.22.kept, f32[8,640]{1,0:T(8,128)S(1)} %get-tuple-element.23.added, f32[96,128]{1,0:T(8,128)S(1)} %get-tuple-element.24.tables), custom_call_target="tpu_custom_call" | custom-call | flops 56623104 | bytes 1007616 | tf_op jit(solution)/shard_map/pallas_call | solution.py:287
  24.6 0.3 collective-permute-start
  24.9 0.4 collective-permute-start.1
  25.3 11.0 %all_to_all.25.came = f32[32,8,128]{2,1,0:T(8,128)S(1)} all-to-all(f32[32,8,128]{2,1,0:T(8,128)S(1)} %shard_map.195), channel_id=1, replica_groups=mesh['req'=8,'head'=4] {'req','head'}, dimensions={0} | all-to-all | bytes 262144 | tf_op jit(solution)/shard_map/all_to_all | solution.py:810
  36.3 0.0 collective-permute-done.one
  36.3 0.0 collective-permute-done.1.two
  36.3 1.9 %shard_map.196 = bf16[32,16,256]{2,1,0:T(8,128)(2,1)} custom-call(s32[1,8]{1,0:T(1,128)} %bitcast.14, bf16[160,512]{1,0:T(8,128)(2,1)} %weight_far.1, f32[32,8,128]{2,1,0:T(8,128)S(1)} %all_to_all.25.came), custom_call_target="tpu_custom_call" | custom-call | flops 2621440 | bytes 557088 | tf_op jit(solution)/shard_map/pallas_call | solution.py:287
  38.2 0.0 copy-start
  38.2 2.7 %all-to-all-start.2 = ((bf16[32,16,256]{2,1,0:T(8,128)(2,1)}), bf16[32,16,256]{2,1,0:T(8,128)(2,1)S(1)}, u32[]{:S(2)}, u32[]{:S(2)}) async-start(bf16[32,16,256]{2,1,0:T(8,128)(2,1)} %shard_map.196), calls=%async_computation.2 | async-start | bytes 524288 | tf_op jit(solution)/shard_map/all_to_all | solution.py:826
  41.0 1.5 %collective-permute-start.2 = (bf16[256,640]{1,0:T(8,128)(2,1)S(1)}, bf16[256,640]{1,0:T(8,128)(2,1)S(1)}, u32[]{:S(2)}, u32[]{:S(2)}) collective-permute-start(bf16[256,640]{1,0:T(8,128)(2,1)S(1)} %get-tuple-element.34), channel_id=1, source_target_pairs={{0,3},{1,2},{2,1},{3,0},{4,7},{5,6},{6,5},{7,4},{8,11},{9,10},{10,... | collective-permute-start | bytes 983048 | tf_op jit(solution)/shard_map/ppermute | solution.py:707
  42.4 10.6 %collective-permute-done.2.three = bf16[256,640]{1,0:T(8,128)(2,1)S(1)} collective-permute-done((bf16[256,640]{1,0:T(8,128)(2,1)S(1)}, bf16[256,640]{1,0:T(8,128)(2,1)S(1)}, u32[]{:S(2)}, u32[]{:S(2)}) %collective-permute-start.2) | collective-permute-done | bytes 327712 | tf_op jit(solution)/shard_map/ppermute | solution.py:707
  53.0 0.0 all-to-all-done.2.came
  53.0 1.1 %shard_map.197 = (bf16[8,16,384]{2,1,0:T(8,128)(2,1)S(1)}, bf16[16,256]{1,0:T(8,128)(2,1)S(1)}) custom-call(f32[1,2048]{1,0:T(1,128)} %bitcast.11, bf16[32,16,256]{2,1,0:T(8,128)(2,1)S(1)} %all-to-all-done.2.came, bf16[16,2048]{1,0:T(8,128)(2,1)S(1)} %all_gather.9.whole, bf16[256,640]{1,0:T(8,128)(2,1)S(1)} %get-tuple-element.31.own, ...), custom_call_target="tpu_custom_call" | custom-call | flops 20971520 | bytes 1753088 | tf_op jit(solution)/shard_map/pallas_call | solution.py:287
  54.1 12.8 %all_to_all.26.came = bf16[8,16,384]{2,1,0:T(8,128)(2,1)S(1)} all-to-all(bf16[8,16,384]{2,1,0:T(8,128)(2,1)S(1)} %get-tuple-element.35), channel_id=1, replica_groups=mesh['req'=8,'head'=4] {'req'}, dimensions={0} | all-to-all | bytes 196608 | tf_op jit(solution)/shard_map/all_to_all | solution.py:84
  66.9 0.2 shard_map.198
  67.1 5.2 %all-gather = bf16[64,160]{1,0:T(8,128)(2,1)S(1)} all-gather(bf16[16,160]{1,0:T(8,128)(2,1)S(1)} %shard_map.198), channel_id=2, replica_groups=mesh['req'=8,'head'=4] {'head'}, dimensions={0}, use_global_device_ids=true | all-gather | bytes 25600 | tf_op jit(solution)/shard_map/all_gather | solution.py:837
  72.3 0.2 shard_map.199
  72.5 10.1 %all_to_all.27.came = bf16[8,16,512]{2,1,0:T(8,128)(2,1)S(1)} all-to-all(bf16[8,16,512]{2,1,0:T(8,128)(2,1)S(1)} %shard_map.199), channel_id=1, replica_groups=mesh['req'=8,'head'=4] {'req'}, dimensions={0} | all-to-all | bytes 262144 | tf_op jit(solution)/shard_map/all_to_all | solution.py:84
  82.7 0.6 shard_map.200
  (1 shorter events, 0.0 us)
Async XLA Ops:
  9.0 14.6 %all-to-all-start = ((f32[32,8,128]{2,1,0:T(8,128)}), f32[32,8,128]{2,1,0:T(8,128)S(1)}, u32[]{:S(2)}, u32[]{:S(2)}) async-start(f32[32,8,128]{2,1,0:T(8,128)} %shard_map.194), calls=%async_computation | async-start | bytes 262144 | tf_op jit(solution)/shard_map/all_to_all | solution.py:757
  24.6 11.7 %collective-permute-start = (bf16[256,640]{1,0:T(8,128)(2,1)S(1)}, bf16[256,640]{1,0:T(8,128)(2,1)S(1)}, u32[]{:S(2)}, u32[]{:S(2)}) collective-permute-start(bf16[256,640]{1,0:T(8,128)(2,1)S(1)} %get-tuple-element.28), channel_id=1, source_target_pairs={{0,1},{1,0},{2,3},{3,2},{4,5},{5,4},{6,7},{7,6},{8,9},{9,8},{10,11... | collective-permute-start | bytes 983048 | tf_op jit(solution)/shard_map/ppermute | solution.py:707
  24.9 11.4 %collective-permute-start.1 = (bf16[256,640]{1,0:T(8,128)(2,1)S(1)}, bf16[256,640]{1,0:T(8,128)(2,1)S(1)}, u32[]{:S(2)}, u32[]{:S(2)}) collective-permute-start(bf16[256,640]{1,0:T(8,128)(2,1)S(1)} %get-tuple-element.29), channel_id=1, source_target_pairs={{0,2},{1,3},{2,0},{3,1},{4,6},{5,7},{6,4},{7,5},{8,10},{9,11},{10,... | collective-permute-start | bytes 983048 | tf_op jit(solution)/shard_map/ppermute | solution.py:707
  38.2 34.1 %copy-start = (bf16[640,512]{1,0:T(8,128)(2,1)S(1)}, bf16[640,512]{1,0:T(8,128)(2,1)}, u32[]{:S(2)}) copy-start(bf16[640,512]{1,0:T(8,128)(2,1)} %weight.1) | copy-start | bytes 1966084
  38.2 14.8 %all-to-all-start.2 = ((bf16[32,16,256]{2,1,0:T(8,128)(2,1)}), bf16[32,16,256]{2,1,0:T(8,128)(2,1)S(1)}, u32[]{:S(2)}, u32[]{:S(2)}) async-start(bf16[32,16,256]{2,1,0:T(8,128)(2,1)} %shard_map.196), calls=%async_computation.2 | async-start | bytes 524288 | tf_op jit(solution)/shard_map/all_to_all | solution.py:826
  41.0 12.1 %collective-permute-start.2 = (bf16[256,640]{1,0:T(8,128)(2,1)S(1)}, bf16[256,640]{1,0:T(8,128)(2,1)S(1)}, u32[]{:S(2)}, u32[]{:S(2)}) collective-permute-start(bf16[256,640]{1,0:T(8,128)(2,1)S(1)} %get-tuple-element.34), channel_id=1, source_target_pairs={{0,3},{1,2},{2,1},{3,0},{4,7},{5,6},{6,5},{7,4},{8,11},{9,10},{10,... | collective-permute-start | bytes 983048 | tf_op jit(solution)/shard_map/ppermute | solution.py:707

commit v7 on v6

--- a/solution.py
+++ b/solution.py
@@ -362,12 +362,12 @@
 
 
 def prepare_kernel(*refs):
-    far, refs = refs[:12], refs[12:]
-    (compact, summaries, kept, added, tables, own, one, two, three), refs = refs[:9], refs[9:]
-    near, (ordered, plain, dealt, done) = refs[:12], refs[12:]
+    far, refs = refs[:10], refs[10:]
+    (compact, summaries, kept, added, tables), refs = refs[:5], refs[5:]
+    near, (ordered, plain, done) = refs[:10], refs[10:]
     copies = fetch(far, near, done)
     (dest, lengths, source, table, keep, weights, query_gain, key_gain, turns) = near[:9]
-    pages, gate, up = near[9:]
+    pages = near[9]
     group = lax.axis_index("req")
     lane = lax.axis_index("head")
     lanes = lax.axis_size("head")
@@ -452,20 +452,6 @@
     plain[count:, :] = jnp.zeros_like(plain[count:, :])
     kept[entries:, :] = plain[...].astype(bfloat)
     summaries[...] = ordered[...].astype(bfloat)
-
-    outs = (own, one, two, three)
-    piece = own.shape[1] // 4
-    block = lanes * piece
-    for copy in copies[10:]:
-        copy.wait()
-    for k in range(lanes):
-        for b in range(2):
-            columns = slice(b * block + k * piece, b * block + (k + 1) * piece)
-            start = 2 * b * piece
-            dealt[k, :, start : start + piece] = gate[:, columns].astype(single)
-            dealt[k, :, start + piece : start + 2 * piece] = up[:, columns].astype(single)
-    for turn in range(lanes):
-        outs[turn][...] = dealt[lane ^ turn].astype(bfloat)
 
 
 def attend_kernel(came, kept, added, tables, sent, x, extra_k, extra_v, out):
@@ -614,15 +600,13 @@
             sent[g * lanes + k] = projected[:, width * b : width * (b + 1)]
 
 
-def units_kernel(gain_far, came, whole, own, one, two, three, sent, mid_out, gain, done):
+def units_kernel(gain_far, came, whole, gate, up, sent, mid_out, gain, done):
     (copy,) = fetch((gain_far,), (gain,), done)
-    weights = (own, one, two, three)
-    lanes = len(weights)
+    lanes = lax.axis_size("head")
     devices, rows, features = came.shape
     groups = devices // lanes
     share = groups // lanes
     group = lax.axis_index("req")
-    lane = lax.axis_index("head")
     here = pl.ds(pl.multiple_of(group * features, features), features)
     mid = whole[:, here].astype(single)
     for g in range(groups):
@@ -631,8 +615,8 @@
     mid_out[...] = mid
     mid = mid.astype(single)
     squares = jnp.sum(mid * mid, axis=1, keepdims=True)
-    width = own.shape[1] // 2
-    place = iota((rows, sent.shape[2] - width), 1)
+    piece = gate.shape[1] // groups
+    place = iota((rows, sent.shape[2] - 2 * piece), 1)
     high = squares.astype(bfloat).astype(single)
     rest = squares - high
     middle = rest.astype(bfloat).astype(single)
@@ -640,23 +624,24 @@
     terms = jnp.where(place < 3, terms, 0.0).astype(bfloat)
     copy.wait()
     inputs = (mid * gain[:, here]).astype(bfloat)
-    for turn in range(lanes):
-        units = jnp.dot(inputs, weights[turn][...], preferred_element_type=single)
-        target = (lane ^ turn) * share
-        for b in range(share):
-            sent[target + b, :, :width] = units[:, width * b : width * (b + 1)].astype(bfloat)
-            sent[target + b, :, width:] = terms
-
-
-def summed(came):
-    total = came[0].astype(single)
-    for g in range(1, came.shape[0]):
-        total = total + came[g].astype(single)
-    return total
+    gates = jnp.dot(inputs, gate[...], preferred_element_type=single).astype(bfloat)
+    ups = jnp.dot(inputs, up[...], preferred_element_type=single).astype(bfloat)
+    for b in range(share):
+        for k in range(lanes):
+            columns = slice((b * lanes + k) * piece, (b * lanes + k + 1) * piece)
+            for g in range(b, groups, share):
+                sent[g * lanes + k, :, :piece] = gates[:, columns]
+                sent[g * lanes + k, :, piece : 2 * piece] = ups[:, columns]
+                sent[g * lanes + k, :, 2 * piece :] = terms
 
 
 def active_kernel(came, active):
-    total = summed(came)
+    lanes = lax.axis_size("head")
+    groups = came.shape[0] // lanes
+    source = lax.axis_index("req") // (groups // lanes)
+    total = came[source].astype(single)
+    for g in range(1, groups):
+        total = total + came[g * lanes + source].astype(single)
     piece = active.shape[1]
     squares = total[:, 2 * piece : 2 * piece + 1] + total[:, 2 * piece + 1 : 2 * piece + 2]
     squares = squares + total[:, 2 * piece + 2 : 2 * piece + 3]
@@ -688,7 +673,10 @@
 
 
 def result_kernel(came, result):
-    result[...] = summed(came).astype(bfloat)
+    total = came[0].astype(single)
+    for g in range(1, came.shape[0]):
+        total = total + came[g].astype(single)
+    result[...] = total.astype(bfloat)
 
 
 def rotation_table():
@@ -700,11 +688,6 @@
     wide = [np.tile(np.concatenate(pair, axis=1), (1, TILE // HD)) for pair in
             ((cosine, cosine), (-sine, sine))]
     return jnp.asarray(np.concatenate(wide), dtype=single)
-
-
-def swapped_lanes(value, turn):
-    lanes = lax.axis_size("head")
-    return lax.ppermute(value, "head", [(k, k ^ turn) for k in range(lanes)])
 
 
 def on_device(
@@ -764,12 +747,10 @@
         key_gain[None, :],
         rotation_table(),
         old_cache,
-        gate_weight,
-        up_weight,
     ]
     entries = pages_here * KEEP
     extras = 16
-    compact, summaries, kept, added, tables, own_units, *other_units = run(
+    compact, summaries, kept, added, tables = run(
         prepare_kernel,
         [
             shaped((pages_here // 2, PAGE, KVW), bfloat),
@@ -777,8 +758,7 @@
             shaped((entries + extras, KVW), bfloat),
             shaped((8, entries + TILE), single),
             shaped((96, TILE), single),
-        ]
-        + [shaped((features, 4 * piece), bfloat)] * lanes,
+        ],
         scalars + arrays,
         [],
         [
@@ -786,7 +766,6 @@
             *local_like(*arrays),
             pltpu.VMEM((pages_here, KVW), single),
             pltpu.VMEM((extras, KVW), single),
-            pltpu.VMEM((lanes, features, 4 * piece), single),
             copies((len(scalars + arrays),)),
         ],
         2 * pages_here * TILE * PAGE * KVW,
@@ -805,11 +784,7 @@
         ],
         6 * 48 * entries * span,
     )
-    *other_units, _ = lax.optimization_barrier((*other_units, parts))
-    units = [swapped_lanes(other_units[turn - 1], turn) for turn in range(1, lanes)]
     came = lax.all_to_all(parts, both_axes, 0, 0, tiled=True)
-    came, *units[:2] = lax.optimization_barrier((came, *units[:2]))
-    units = [own_units, *units]
     (sent,) = run(
         project_kernel,
         [shaped((devices, requests, features), bfloat)],
@@ -827,13 +802,14 @@
     gain = feedforward_gain[None, :]
     sent, mid = run(
         units_kernel,
-        [shaped((groups, requests, 3 * TILE), bfloat), shaped((requests, features), bfloat)],
+        [shaped((devices, requests, 3 * TILE), bfloat), shaped((requests, features), bfloat)],
         [gain],
-        [came, whole, *units],
+        [came, whole, gate_weight, up_weight],
         [*local_like(gain), copies((1,))],
         4 * requests * gate_weight.size,
     )
-    (active,) = run(active_kernel, [shaped((requests, piece), bfloat)], [], [exchange(sent)])
+    came = lax.all_to_all(sent, both_axes, 0, 0, tiled=True)
+    (active,) = run(active_kernel, [shaped((requests, piece), bfloat)], [], [came])
     active = lax.all_gather(active, "head")
     (sent,) = run(
         down_kernel,

time: 83.7 us -> 81.6 us (0.975)
  blocking collectives: 45.5 us -> 59.6 us
  waiting for transfers between devices: 13.7 us -> 3.79 us
  starting transfers between devices: 11.2 us -> 6.33 us
  Pallas kernels: 12.1 us -> 10.8 us
    all_to_all x0 -> x2, blocking collectives: none -> 27.8 us  [on_device(): came = lax.all_to_all(sent, both_axes, 0, 0, tiled=True)]
    all_to_all x2 -> x1, blocking collectives: 22.9 us -> 10.1 us  [exchange(): return lax.all_to_all(parts, 'req', split_axis=0, concat_axis=0, tiled=True)]
    ppermute x3 -> x0, waiting for transfers between devices: 10.6 us -> none  [swapped_lanes(): return lax.ppermute(value, 'head', [(k, k ^ turn) for k in range(lanes)])]
    all_to_all x2 -> x1, starting transfers between devices: 9.06 us -> 6.33 us  [on_device(): came = lax.all_to_all(sent, both_axes, 0, 0, tiled=True)]
    ppermute x3 -> x0, starting transfers between devices: 2.11 us -> none  [swapped_lanes(): return lax.ppermute(value, 'head', [(k, k ^ turn) for k in range(lanes)])]
    pallas_call x8, Pallas kernels: 12.1 us -> 10.8 us  [run(): pl.pallas_call(kernel, out_shape=list(outs), in_specs=in_specs, out_specs...]
    all_to_all x1, blocking collectives: 11 us -> 10.1 us  [on_device(): came = lax.all_to_all(parts, both_axes, 0, 0, tiled=True)]
    all_to_all x2 -> x1, waiting for transfers between devices: 3.1 us -> 3.79 us  [on_device(): came = lax.all_to_all(sent, both_axes, 0, 0, tiled=True)]
  transfers between devices with their start and end apart: 5 -> 1, of which waited for: 2 -> 1; matrix products, arithmetic and copies ran while one was open for 0% -> 0% of each run, Pallas kernels for 6% -> 5%
where the time goes in v7:
time: 81.6 us; the launch traced here: 81.3 us
  blocking collectives  59.6 us (73%)
  Pallas kernels  10.8 us (13%)
  starting transfers between devices  6.33 us (8%)
  waiting for transfers between devices  3.79 us (5%)
    all_to_all x2, blocking collectives, on_device(): came = lax.all_to_all(sent, both_axes, 0, 0, tiled=True)  27.8 us
    pallas_call x8, Pallas kernels, run(): pl.pallas_call(kernel, out_shape=list(outs), in_specs=in_specs, out_specs...  10.8 us
    all_to_all x1, blocking collectives, exchange(): return lax.all_to_all(parts, 'req', split_axis=0, concat_axis=0, tiled=True)  10.1 us
    all_to_all x1, blocking collectives, on_device(): came = lax.all_to_all(parts, both_axes, 0, 0, tiled=True)  10.1 us
    all_gather x1, blocking collectives, on_device(): whole = lax.all_gather(hidden_in, 'head', axis=1, tiled=True)  6.43 us
    all_to_all x1, starting transfers between devices, on_device(): came = lax.all_to_all(sent, both_axes, 0, 0, tiled=True)  6.33 us
    all_gather x1, blocking collectives, on_device(): active = lax.all_gather(active, 'head')  5.18 us
    all_to_all x1, waiting for transfers between devices, on_device(): came = lax.all_to_all(sent, both_axes, 0, 0, tiled=True)  3.79 us
  transfers between devices with their start and end apart: 1, of which 1 were waited for; matrix products, arithmetic and copies ran while one was open for 0% of the time, Pallas kernels for 5%

profile of v7, /device:TPU:0, one launch (start us, length us, event | category | flops | bytes accessed | tf_op | source)
XLA Modules:
  0.0 81.3 jit_solution(8454996545632367989)
XLA Ops:
  0.6 6.4 %all_gather.9.whole = bf16[16,2048]{1,0:T(8,128)(2,1)S(1)} all-gather(bf16[16,512]{1,0:T(8,128)(2,1)} %param.18), channel_id=1, replica_groups=mesh['req'=8,'head'=4] {'head'}, dimensions={1}, use_global_device_ids=true | all-gather | bytes 81920 | tf_op jit(solution)/shard_map/all_gather | solution.py:721
  7.1 1.9 %shard_map.194 = f32[32,8,128]{2,1,0:T(8,128)} custom-call(s32[1,8]{1,0:T(1,128)} %bitcast.12, f32[1,2048]{1,0:T(1,128)} %bitcast.10, bf16[480,256]{1,0:T(8,128)(2,1)} %bitcast.9, bf16[16,2048]{1,0:T(8,128)(2,1)S(1)} %all_gather.9.whole), custom_call_target="tpu_custom_call" | custom-call | flops 3932160 | bytes 450592 | tf_op jit(solution)/shard_map/pallas_call | solution.py:287
  9.0 6.3 %all-to-all-start = ((f32[32,8,128]{2,1,0:T(8,128)}), f32[32,8,128]{2,1,0:T(8,128)S(1)}, u32[]{:S(2)}, u32[]{:S(2)}) async-start(f32[32,8,128]{2,1,0:T(8,128)} %shard_map.194), calls=%async_computation | async-start | bytes 262144 | tf_op jit(solution)/shard_map/all_to_all | solution.py:740
  15.3 4.4 %shard_map.193 = (bf16[4,128,640]{2,1,0:T(8,128)(2,1)}, bf16[8,640]{1,0:T(8,128)(2,1)}, bf16[528,640]{1,0:T(8,128)(2,1)S(1)}, f32[8,640]{1,0:T(8,128)S(1)}, f32[96,128]{1,0:T(8,128)S(1)}) custom-call(s32[1,8]{1,0:T(1,128)} %refs_0_.1, s32[1,16]{1,0:T(1,128)} %bitcast.15, s32[1,8]{1,0:T(1,128)} %bitcast.13, s32[2,16]{1,0:T(2,128)} %refs_3_.1, ...), custom_call_target="tpu_custom_call" | custom-call | flops 167772160 | bytes 2753280 | tf_op jit(solution)/shard_map/pallas_call | solution.py:287
  19.7 0.0 copy-start
  19.7 0.0 copy-start.1
  19.7 3.8 %all-to-all-done.came = f32[32,8,128]{2,1,0:T(8,128)S(1)} async-done(((f32[32,8,128]{2,1,0:T(8,128)}), f32[32,8,128]{2,1,0:T(8,128)S(1)}, u32[]{:S(2)}, u32[]{:S(2)}) %all-to-all-start) | async-done | bytes 131104 | tf_op jit(solution)/shard_map/all_to_all | solution.py:740
  23.5 1.1 %shard_map.195 = f32[32,8,128]{2,1,0:T(8,128)S(1)} custom-call(f32[32,8,128]{2,1,0:T(8,128)S(1)} %all-to-all-done.came, bf16[528,640]{1,0:T(8,128)(2,1)S(1)} %get-tuple-element.12.kept, f32[8,640]{1,0:T(8,128)S(1)} %get-tuple-element.13.added, f32[96,128]{1,0:T(8,128)S(1)} %get-tuple-element.14.tables), custom_call_target="tpu_custom_call" | custom-call | flops 56623104 | bytes 1007616 | tf_op jit(solution)/shard_map/pallas_call | solution.py:287
  24.6 10.1 %all_to_all.25.came = f32[32,8,128]{2,1,0:T(8,128)S(1)} all-to-all(f32[32,8,128]{2,1,0:T(8,128)S(1)} %shard_map.195), channel_id=1, replica_groups=mesh['req'=8,'head'=4] {'req','head'}, dimensions={0} | all-to-all | bytes 262144 | tf_op jit(solution)/shard_map/all_to_all | solution.py:787
  34.7 1.2 %shard_map.196 = bf16[32,16,256]{2,1,0:T(8,128)(2,1)S(1)} custom-call(s32[1,8]{1,0:T(1,128)} %bitcast.14, bf16[160,512]{1,0:T(8,128)(2,1)} %weight_far.1, f32[32,8,128]{2,1,0:T(8,128)S(1)} %all_to_all.25.came), custom_call_target="tpu_custom_call" | custom-call | flops 2621440 | bytes 557088 | tf_op jit(solution)/shard_map/pallas_call | solution.py:287
  35.9 12.4 %all_to_all.26.came = bf16[32,16,256]{2,1,0:T(8,128)(2,1)S(1)} all-to-all(bf16[32,16,256]{2,1,0:T(8,128)(2,1)S(1)} %shard_map.196), channel_id=1, replica_groups=mesh['req'=8,'head'=4] {'req','head'}, dimensions={0} | all-to-all | bytes 524288 | tf_op jit(solution)/shard_map/all_to_all | solution.py:801
  48.3 0.0 copy-done
  48.3 0.0 copy-done.1
  48.3 0.0 copy-start.2
  48.3 1.2 %shard_map.197 = (bf16[32,16,384]{2,1,0:T(8,128)(2,1)S(1)}, bf16[16,256]{1,0:T(8,128)(2,1)S(1)}) custom-call(f32[1,2048]{1,0:T(1,128)} %bitcast.11, bf16[32,16,256]{2,1,0:T(8,128)(2,1)S(1)} %all_to_all.26.came, bf16[16,2048]{1,0:T(8,128)(2,1)S(1)} %all_gather.9.whole, bf16[256,1280]{1,0:T(8,128)(2,1)S(1)} %copy-done, bf16[256,1280]{1,0:T(8,128)(2,1)S(1)} %copy-done.1), custom_call_target="tpu_custom_call" | custom-call | flops 20971520 | bytes 2048000 | tf_op jit(solution)/shard_map/pallas_call | solution.py:287
  49.5 15.4 %all_to_all.27.came = bf16[32,16,384]{2,1,0:T(8,128)(2,1)S(1)} all-to-all(bf16[32,16,384]{2,1,0:T(8,128)(2,1)S(1)} %get-tuple-element.15), channel_id=1, replica_groups=mesh['req'=8,'head'=4] {'req','head'}, dimensions={0} | all-to-all | bytes 786432 | tf_op jit(solution)/shard_map/all_to_all | solution.py:811
  64.9 0.2 shard_map.198
  65.1 5.2 %all-gather = bf16[64,160]{1,0:T(8,128)(2,1)S(1)} all-gather(bf16[16,160]{1,0:T(8,128)(2,1)S(1)} %shard_map.198), channel_id=2, replica_groups=mesh['req'=8,'head'=4] {'head'}, dimensions={0}, use_global_device_ids=true | all-gather | bytes 25600 | tf_op jit(solution)/shard_map/all_gather | solution.py:813
  70.3 0.0 copy-done.2
  70.3 0.2 shard_map.199
  70.5 10.1 %all_to_all.28.came = bf16[8,16,512]{2,1,0:T(8,128)(2,1)S(1)} all-to-all(bf16[8,16,512]{2,1,0:T(8,128)(2,1)S(1)} %shard_map.199), channel_id=1, replica_groups=mesh['req'=8,'head'=4] {'req'}, dimensions={0} | all-to-all | bytes 262144 | tf_op jit(solution)/shard_map/all_to_all | solution.py:84
  80.6 0.6 shard_map.200
Async XLA Ops:
  9.0 14.6 %all-to-all-start = ((f32[32,8,128]{2,1,0:T(8,128)}), f32[32,8,128]{2,1,0:T(8,128)S(1)}, u32[]{:S(2)}, u32[]{:S(2)}) async-start(f32[32,8,128]{2,1,0:T(8,128)} %shard_map.194), calls=%async_computation | async-start | bytes 262144 | tf_op jit(solution)/shard_map/all_to_all | solution.py:740
  19.7 28.6 %copy-start = (bf16[256,1280]{1,0:T(8,128)(2,1)S(1)}, bf16[256,1280]{1,0:T(8,128)(2,1)}, u32[]{:S(2)}) copy-start(bf16[256,1280]{1,0:T(8,128)(2,1)} %gate.1) | copy-start | bytes 1966084
  19.7 28.6 %copy-start.1 = (bf16[256,1280]{1,0:T(8,128)(2,1)S(1)}, bf16[256,1280]{1,0:T(8,128)(2,1)}, u32[]{:S(2)}) copy-start(bf16[256,1280]{1,0:T(8,128)(2,1)} %up.1) | copy-start | bytes 1966084
  48.3 22.0 %copy-start.2 = (bf16[640,512]{1,0:T(8,128)(2,1)S(1)}, bf16[640,512]{1,0:T(8,128)(2,1)}, u32[]{:S(2)}) copy-start(bf16[640,512]{1,0:T(8,128)(2,1)} %weight.1) | copy-start | bytes 1966084

commit v8 on v6

--- a/solution.py
+++ b/solution.py
@@ -276,6 +276,17 @@
 single = jnp.float32
 
 
+TERMS = 4
+
+
+def three_terms(value, place):
+    high = value.astype(bfloat).astype(single)
+    rest = value - high
+    middle = rest.astype(bfloat).astype(single)
+    low = jnp.where(place == 2, rest - middle, 0.0)
+    return jnp.where(place == 0, high, jnp.where(place == 1, middle, low))
+
+
 def iota(shape, axis):
     return lax.broadcasted_iota(jnp.int32, shape, axis)
 
@@ -363,7 +374,7 @@
 
 def prepare_kernel(*refs):
     far, refs = refs[:12], refs[12:]
-    (compact, summaries, kept, added, tables, own, one, two, three), refs = refs[:9], refs[9:]
+    (compact, summaries, kept, added, tables, mine, theirs), refs = refs[:7], refs[7:]
     near, (ordered, plain, dealt, done) = refs[:12], refs[12:]
     copies = fetch(far, near, done)
     (dest, lengths, source, table, keep, weights, query_gain, key_gain, turns) = near[:9]
@@ -423,12 +434,7 @@
         picks = (keep[p : p + 1, :] == rows_of).astype(single)
         dropped = weight_columns[:, p : p + 1] * (1.0 - jnp.sum(picks, axis=1, keepdims=True))
         total = jnp.sum(dropped, axis=0, keepdims=True)
-        high = dropped.astype(bfloat).astype(single)
-        rest = dropped - high
-        middle = rest.astype(bfloat).astype(single)
-        terms = jnp.where(place == 0, high, jnp.where(place == 1, middle, rest - middle))
-        terms = jnp.where(place < 3, terms, 0.0)
-        left = jnp.concatenate([picks, terms], axis=1).astype(bfloat)
+        left = jnp.concatenate([picks, three_terms(dropped, place)], axis=1).astype(bfloat)
         both = lax.dot_general(
             left, pages[p], (((0,), (0,)), ((), ())), preferred_element_type=single
         )
@@ -453,19 +459,18 @@
     kept[entries:, :] = plain[...].astype(bfloat)
     summaries[...] = ordered[...].astype(bfloat)
 
-    outs = (own, one, two, three)
-    piece = own.shape[1] // 4
-    block = lanes * piece
     for copy in copies[10:]:
         copy.wait()
-    for k in range(lanes):
+    block = gate.shape[1] // 2
+    piece = block // 2
+    for k in range(2):
         for b in range(2):
             columns = slice(b * block + k * piece, b * block + (k + 1) * piece)
-            start = 2 * b * piece
+            start = b * block
             dealt[k, :, start : start + piece] = gate[:, columns].astype(single)
-            dealt[k, :, start + piece : start + 2 * piece] = up[:, columns].astype(single)
-    for turn in range(lanes):
-        outs[turn][...] = dealt[lane ^ turn].astype(bfloat)
+            dealt[k, :, start + piece : start + block] = up[:, columns].astype(single)
+    mine[...] = dealt[lane & 1].astype(bfloat)
+    theirs[...] = dealt[1 - (lane & 1)].astype(bfloat)
 
 
 def attend_kernel(came, kept, added, tables, sent, x, extra_k, extra_v, out):
@@ -573,29 +578,34 @@
             picked = jnp.where((slot >> 1) == c, mine[:, c * TILE : (c + 1) * TILE], picked)
         results.append(jnp.where((slot & 1) == u, picked, pltpu.roll(picked, HD, 1)))
     out[:rows, :] = jnp.where(half == 0, results[0], results[1])
-    out[rows:, :] = jnp.where(half == 0, level[:rows], level[rows:])
+    level = jnp.where(half == 0, level[:rows], level[rows:])
+    out[rows:, :] = three_terms(level, iota(level.shape, 1) % TERMS)
     own = HEADS * HD // groups
     for g in range(groups):
         r = own * g // TILE * R_DEV
         tile = jnp.concatenate([out[r : r + 4, :], out[rows + r : rows + r + 4, :]], axis=0)
         for k in range(lanes):
-            sent[g * lanes + k] = tile
-
-
-def project_kernel(source_far, weight_far, came, sent, source, weight, rows, done):
-    copies = fetch((source_far, weight_far), (source, weight), done)
+            sent[g * lanes + k] = tile.astype(bfloat)
+
+
+def project_kernel(
+    source_far, own_far, came, one, two, three, sent, source, own, rows, done
+):
+    copies = fetch((source_far, own_far), (source, own), done)
     lanes = lax.axis_size("head")
     groups = came.shape[0] // lanes
-    features = weight.shape[0]
+    features = own.shape[0]
     requests = rows.shape[0]
+    near = (iota((TILE, TILE), 0) // TERMS == iota((TILE, TILE), 1) // TERMS).astype(single)
+    tiles = came[...].reshape(groups * lanes * 8, TILE)
+    levels = jnp.dot(tiles, near.astype(bfloat), preferred_element_type=single)
+    tiles = tiles.astype(single).reshape(groups, lanes, 8, TILE)
+    levels = levels.reshape(groups, lanes, 8, TILE)
     for g in range(groups):
-        tiles = [came[g * lanes + k] for k in range(lanes)]
-        levels = [tile[4:8] for tile in tiles]
-        top = jnp.maximum(
-            jnp.maximum(levels[0], levels[1]), jnp.maximum(levels[2], levels[3])
-        )
-        shares = [jnp.exp(level - top) for level in levels]
-        mixed = sum(share * tile[0:4] for share, tile in zip(shares, tiles)) / sum(shares)
+        mine = [levels[g, k, 4:8] for k in range(lanes)]
+        top = jnp.maximum(jnp.maximum(mine[0], mine[1]), jnp.maximum(mine[2], mine[3]))
+        shares = [jnp.exp(level - top) for level in mine]
+        mixed = sum(share * tiles[g, k, 0:4] for k, share in enumerate(shares)) / sum(shares)
         rows[R_DEV * g : R_DEV * (g + 1), :TILE] = mixed[:R_DEV]
         rows[R_DEV * g : R_DEV * (g + 1), TILE:] = mixed[R_DEV:]
     shift = lax.rem(2 * TILE - lax.rem(lax.axis_index("req") * features, TILE), 2 * TILE)
@@ -605,61 +615,47 @@
     order = row_order(source, requests, False)
     attention = jnp.dot(order, attention.astype(bfloat), preferred_element_type=single)
     attention = attention[:, :features].astype(bfloat)
-    projected = jnp.dot(attention, weight[...], preferred_element_type=single).astype(bfloat)
     width = sent.shape[2]
     share = groups // lanes
-    for g in range(groups):
-        b = g % share
-        for k in range(lanes):
-            sent[g * lanes + k] = projected[:, width * b : width * (b + 1)]
-
-
-def units_kernel(gain_far, came, whole, own, one, two, three, sent, mid_out, gain, done):
+    for turn, weight in enumerate((own, one, two, three)):
+        projected = jnp.dot(attention, weight[...], preferred_element_type=single)
+        target = (lax.axis_index("head") ^ turn) * share
+        for b in range(share):
+            sent[target + b] = projected[:, width * b : width * (b + 1)].astype(bfloat)
+
+
+def units_kernel(gain_far, came, whole, mine, theirs, sent, mid_out, gain, done):
     (copy,) = fetch((gain_far,), (gain,), done)
-    weights = (own, one, two, three)
-    lanes = len(weights)
-    devices, rows, features = came.shape
-    groups = devices // lanes
-    share = groups // lanes
+    groups, rows, features = came.shape
+    share = groups // lax.axis_size("head")
     group = lax.axis_index("req")
     lane = lax.axis_index("head")
     here = pl.ds(pl.multiple_of(group * features, features), features)
     mid = whole[:, here].astype(single)
     for g in range(groups):
-        mid = mid + came[g * lanes + group // share].astype(single)
+        mid = mid + came[g].astype(single)
     mid = mid.astype(bfloat)
     mid_out[...] = mid
     mid = mid.astype(single)
     squares = jnp.sum(mid * mid, axis=1, keepdims=True)
-    width = own.shape[1] // 2
-    place = iota((rows, sent.shape[2] - width), 1)
-    high = squares.astype(bfloat).astype(single)
-    rest = squares - high
-    middle = rest.astype(bfloat).astype(single)
-    terms = jnp.where(place == 0, high, jnp.where(place == 1, middle, rest - middle))
-    terms = jnp.where(place < 3, terms, 0.0).astype(bfloat)
+    block = mine.shape[1] // share
+    terms = three_terms(squares, iota((rows, sent.shape[2] - block), 1)).astype(bfloat)
     copy.wait()
     inputs = (mid * gain[:, here]).astype(bfloat)
-    for turn in range(lanes):
-        units = jnp.dot(inputs, weights[turn][...], preferred_element_type=single)
+    for turn, weight in enumerate((mine, theirs)):
+        units = jnp.dot(inputs, weight[...], preferred_element_type=single).astype(bfloat)
         target = (lane ^ turn) * share
         for b in range(share):
-            sent[target + b, :, :width] = units[:, width * b : width * (b + 1)].astype(bfloat)
-            sent[target + b, :, width:] = terms
-
-
-def summed(came):
+            sent[target + b, :, :block] = units[:, block * b : block * (b + 1)]
+            sent[target + b, :, block:] = terms
+
+
+def active_kernel(came, active):
     total = came[0].astype(single)
     for g in range(1, came.shape[0]):
         total = total + came[g].astype(single)
-    return total
-
-
-def active_kernel(came, active):
-    total = summed(came)
     piece = active.shape[1]
-    squares = total[:, 2 * piece : 2 * piece + 1] + total[:, 2 * piece + 1 : 2 * piece + 2]
-    squares = squares + total[:, 2 * piece + 2 : 2 * piece + 3]
+    squares = jnp.sum(total[:, 2 * piece : 2 * piece + 3], axis=1, keepdims=True)
     factor = lax.rsqrt(squares / D + epsilon)
     gate = total[:, :piece] * factor
     up = total[:, piece : 2 * piece] * factor
@@ -671,14 +667,12 @@
     lanes, _, piece = active.shape
     half = mid.shape[1]
     share = width // half
-    down = jnp.dot(active[0], weight[:piece, :], preferred_element_type=single)
-    for k in range(1, lanes):
-        down = down + jnp.dot(
-            active[k], weight[piece * k : piece * (k + 1), :], preferred_element_type=single
-        )
-    residual = mid[...].astype(single)
     group = lax.axis_index("req")
     lane = lax.axis_index("head")
+    first = group // (2 * share) * 2
+    down = jnp.dot(active[first], weight[:piece, :], preferred_element_type=single)
+    down = down + jnp.dot(active[first + 1], weight[piece:, :], preferred_element_type=single)
+    residual = mid[...].astype(single)
     for b in range(share):
         columns = slice(half * b, half * (b + 1))
         mine = group == lane * share + b
@@ -688,7 +682,10 @@
 
 
 def result_kernel(came, result):
-    result[...] = summed(came).astype(bfloat)
+    total = came[0].astype(single)
+    for g in range(1, came.shape[0]):
+        total = total + came[g].astype(single)
+    result[...] = total.astype(bfloat)
 
 
 def rotation_table():
@@ -732,7 +729,6 @@
     pages_here = old_cache.shape[0]
     devices = groups * lanes
     features = D // groups
-    piece = gate_weight.shape[1] // groups
     copies = pltpu.SemaphoreType.DMA
 
     whole = lax.all_gather(hidden_in, "head", axis=1, tiled=True)
@@ -769,7 +765,7 @@
     ]
     entries = pages_here * KEEP
     extras = 16
-    compact, summaries, kept, added, tables, own_units, *other_units = run(
+    compact, summaries, kept, added, tables, mine, theirs = run(
         prepare_kernel,
         [
             shaped((pages_here // 2, PAGE, KVW), bfloat),
@@ -777,8 +773,9 @@
             shaped((entries + extras, KVW), bfloat),
             shaped((8, entries + TILE), single),
             shaped((96, TILE), single),
-        ]
-        + [shaped((features, 4 * piece), bfloat)] * lanes,
+            shaped(gate_weight.shape, bfloat),
+            shaped(gate_weight.shape, bfloat),
+        ],
         scalars + arrays,
         [],
         [
@@ -786,7 +783,7 @@
             *local_like(*arrays),
             pltpu.VMEM((pages_here, KVW), single),
             pltpu.VMEM((extras, KVW), single),
-            pltpu.VMEM((lanes, features, 4 * piece), single),
+            pltpu.VMEM((2,) + gate_weight.shape, single),
             copies((len(scalars + arrays),)),
         ],
         2 * pages_here * TILE * PAGE * KVW,
@@ -794,7 +791,7 @@
     span = -(-KVH * HD // TILE) * TILE
     (parts,) = run(
         attend_kernel,
-        [shaped((devices, 8, TILE), single)],
+        [shaped((devices, 8, TILE), bfloat)],
         [],
         [came, kept, added, tables],
         [
@@ -805,35 +802,40 @@
         ],
         6 * 48 * entries * span,
     )
-    *other_units, _ = lax.optimization_barrier((*other_units, parts))
-    units = [swapped_lanes(other_units[turn - 1], turn) for turn in range(1, lanes)]
+    output_weights, theirs, _ = lax.optimization_barrier((output_weight, theirs, parts))
+    others = [swapped_lanes(output_weights, turn) for turn in range(1, lanes)]
+    theirs = swapped_lanes(theirs, 1)
     came = lax.all_to_all(parts, both_axes, 0, 0, tiled=True)
-    came, *units[:2] = lax.optimization_barrier((came, *units[:2]))
-    units = [own_units, *units]
+    came, theirs, *others = lax.optimization_barrier((came, theirs, *others))
     (sent,) = run(
         project_kernel,
-        [shaped((devices, requests, features), bfloat)],
+        [shaped((groups, requests, features), bfloat)],
         [holds, output_weight],
-        [came],
+        [came, *others],
         [
             *scalar_like(holds),
             *local_like(output_weight),
             pltpu.VMEM((requests, 2 * TILE), single),
             copies((2,)),
         ],
-        2 * requests * output_weight.size,
-    )
-    came = lax.all_to_all(sent, both_axes, 0, 0, tiled=True)
+        2 * requests * output_weight.size * lanes,
+    )
     gain = feedforward_gain[None, :]
+    block = gate_weight.shape[1] // 2
     sent, mid = run(
         units_kernel,
-        [shaped((groups, requests, 3 * TILE), bfloat), shaped((requests, features), bfloat)],
+        [
+            shaped((groups, requests, block + TILE), bfloat),
+            shaped((requests, features), bfloat),
+        ],
         [gain],
-        [came, whole, *units],
+        [exchange(sent), whole, mine, theirs],
         [*local_like(gain), copies((1,))],
         4 * requests * gate_weight.size,
     )
-    (active,) = run(active_kernel, [shaped((requests, piece), bfloat)], [], [exchange(sent)])
+    (active,) = run(
+        active_kernel, [shaped((requests, block // 2), bfloat)], [], [exchange(sent)]
+    )
     active = lax.all_gather(active, "head")
     (sent,) = run(
         down_kernel,

time: 83.7 us -> 75.3 us (0.90)
  waiting for transfers between devices: 13.7 us -> 3.71 us
  blocking collectives: 45.5 us -> 51.1 us
  starting transfers between devices: 11.2 us -> 8.47 us
  Pallas kernels: 12.1 us -> 10.8 us
    ppermute x3 -> x4, waiting for transfers between devices: 10.6 us -> 0.01 us  [swapped_lanes(): return lax.ppermute(value, 'head', [(k, k ^ turn) for k in range(lanes)])]
    all_to_all x2 -> x3, blocking collectives: 22.9 us -> 29.9 us  [exchange(): return lax.all_to_all(parts, 'req', split_axis=0, concat_axis=0, tiled=True)]
    all_to_all x2 -> x1, starting transfers between devices: 9.06 us -> 6.33 us  [on_device(): came = lax.all_to_all(sent, both_axes, 0, 0, tiled=True)]
    all_to_all x1, blocking collectives: 11 us -> 9.53 us  [on_device(): came = lax.all_to_all(parts, both_axes, 0, 0, tiled=True)]
    pallas_call x8, Pallas kernels: 12.1 us -> 10.8 us  [run(): pl.pallas_call(kernel, out_shape=list(outs), in_specs=in_specs, out_specs...]
    all_to_all x2 -> x1, waiting for transfers between devices: 3.1 us -> 3.7 us  [on_device(): came = lax.all_to_all(sent, both_axes, 0, 0, tiled=True)]
    ppermute x3 -> x4, starting transfers between devices: 2.11 us -> 2.14 us  [swapped_lanes(): return lax.ppermute(value, 'head', [(k, k ^ turn) for k in range(lanes)])]
  transfers between devices with their start and end apart: 5 -> 5, of which waited for: 2 -> 1; matrix products, arithmetic and copies ran while one was open for 0% -> 0% of each run, Pallas kernels for 6% -> 6%
where the time goes in v8:
time: 75.3 us; the launch traced here: 74.8 us
  blocking collectives  51.1 us (68%)
  Pallas kernels  10.8 us (14%)
  starting transfers between devices  8.47 us (11%)
  waiting for transfers between devices  3.71 us (5%)
    all_to_all x3, blocking collectives, exchange(): return lax.all_to_all(parts, 'req', split_axis=0, concat_axis=0, tiled=True)  29.9 us
    pallas_call x8, Pallas kernels, run(): pl.pallas_call(kernel, out_shape=list(outs), in_specs=in_specs, out_specs...  10.8 us
    all_to_all x1, blocking collectives, on_device(): came = lax.all_to_all(parts, both_axes, 0, 0, tiled=True)  9.53 us
    all_gather x1, blocking collectives, on_device(): whole = lax.all_gather(hidden_in, 'head', axis=1, tiled=True)  6.43 us
    all_to_all x1, starting transfers between devices, on_device(): came = lax.all_to_all(sent, both_axes, 0, 0, tiled=True)  6.33 us
    all_gather x1, blocking collectives, on_device(): active = lax.all_gather(active, 'head')  5.23 us
    all_to_all x1, waiting for transfers between devices, on_device(): came = lax.all_to_all(sent, both_axes, 0, 0, tiled=True)  3.7 us
    ppermute x4, starting transfers between devices, swapped_lanes(): return lax.ppermute(value, 'head', [(k, k ^ turn) for k in range(lanes)])  2.14 us
  transfers between devices with their start and end apart: 5, of which 1 were waited for; matrix products, arithmetic and copies ran while one was open for 0% of the time, Pallas kernels for 6%

profile of v8, /device:TPU:0, one launch (start us, length us, event | category | flops | bytes accessed | tf_op | source)
XLA Modules:
  0.0 74.8 jit_solution(4340368798337734434)
XLA Ops:
  0.6 6.4 %all_gather.9.whole = bf16[16,2048]{1,0:T(8,128)(2,1)S(1)} all-gather(bf16[16,512]{1,0:T(8,128)(2,1)} %param.18), channel_id=1, replica_groups=mesh['req'=8,'head'=4] {'head'}, dimensions={1}, use_global_device_ids=true | all-gather | bytes 81920 | tf_op jit(solution)/shard_map/all_gather | solution.py:734
  7.1 1.9 %shard_map.194 = f32[32,8,128]{2,1,0:T(8,128)} custom-call(s32[1,8]{1,0:T(1,128)} %bitcast.12, f32[1,2048]{1,0:T(1,128)} %bitcast.10, bf16[480,256]{1,0:T(8,128)(2,1)} %bitcast.9, bf16[16,2048]{1,0:T(8,128)(2,1)S(1)} %all_gather.9.whole), custom_call_target="tpu_custom_call" | custom-call | flops 3932160 | bytes 450592 | tf_op jit(solution)/shard_map/pallas_call | solution.py:298
  9.0 6.3 %all-to-all-start = ((f32[32,8,128]{2,1,0:T(8,128)}), f32[32,8,128]{2,1,0:T(8,128)S(1)}, u32[]{:S(2)}, u32[]{:S(2)}) async-start(f32[32,8,128]{2,1,0:T(8,128)} %shard_map.194), calls=%async_computation | async-start | bytes 262144 | tf_op jit(solution)/shard_map/all_to_all | solution.py:753
  15.3 0.0 copy-start.1
  15.3 4.5 %shard_map.193 = (bf16[4,128,640]{2,1,0:T(8,128)(2,1)}, bf16[8,640]{1,0:T(8,128)(2,1)}, bf16[528,640]{1,0:T(8,128)(2,1)S(1)}, f32[8,640]{1,0:T(8,128)S(1)}, f32[...) custom-call(s32[1,8]{1,0:T(1,128)} %refs_0_.1, s32[1,16]{1,0:T(1,128)} %bitcast.15, ...), custom_call_target="tpu_custom_call" | custom-call | flops 167772160 | bytes 5374720 | tf_op jit(solution)/shard_map/pallas_call | solution.py:298
  19.8 3.7 %all-to-all-done.came = f32[32,8,128]{2,1,0:T(8,128)S(1)} async-done(((f32[32,8,128]{2,1,0:T(8,128)}), f32[32,8,128]{2,1,0:T(8,128)S(1)}, u32[]{:S(2)}, u32[]{:S(2)}) %all-to-all-start) | async-done | bytes 131104 | tf_op jit(solution)/shard_map/all_to_all | solution.py:753
  23.5 1.1 %shard_map.195 = bf16[32,8,128]{2,1,0:T(8,128)(2,1)S(1)} custom-call(f32[32,8,128]{2,1,0:T(8,128)S(1)} %all-to-all-done.came, bf16[528,640]{1,0:T(8,128)(2,1)S(1)} %get-tuple-element.21.kept, f32[8,640]{1,0:T(8,128)S(1)} %get-tuple-element.22.added, f32[96,128]{1,0:T(8,128)S(1)} %get-tuple-element.23.tables), custom_call_target="tpu_custom_call" | custom-call | flops 56623104 | bytes 942080 | tf_op jit(solution)/shard_map/pallas_call | solution.py:298
  24.6 0.3 collective-permute-start
  24.9 0.3 collective-permute-start.1
  25.2 0.4 collective-permute-start.2
  25.7 1.1 %collective-permute-start.3 = (bf16[160,512]{1,0:T(8,128)(2,1)S(1)}, bf16[160,512]{1,0:T(8,128)(2,1)S(1)}, u32[]{:S(2)}, u32[]{:S(2)}) collective-permute-start(bf16[160,512]{1,0:T(8,128)(2,1)S(1)} %copy-done.1), channel_id=1, source_target_pairs={{0,3},{1,2},{2,1},{3,0},{4,7},{5,6},{6,5},{7,4},{8,11},{9,10},{10,... | collective-permute-start | bytes 491528 | tf_op jit(solution)/shard_map/ppermute | solution.py:704
  26.8 9.5 %all_to_all.25.came = bf16[32,8,128]{2,1,0:T(8,128)(2,1)S(1)} all-to-all(bf16[32,8,128]{2,1,0:T(8,128)(2,1)S(1)} %shard_map.195), channel_id=1, replica_groups=mesh['req'=8,'head'=4] {'req','head'}, dimensions={0} | all-to-all | bytes 131072 | tf_op jit(solution)/shard_map/all_to_all | solution.py:808
  36.3 0.0 collective-permute-done.3.three
  36.3 0.0 collective-permute-done.theirs
  36.3 1.3 %shard_map.196 = bf16[8,16,256]{2,1,0:T(8,128)(2,1)S(1)} custom-call(s32[1,8]{1,0:T(1,128)} %bitcast.14, bf16[160,512]{1,0:T(8,128)(2,1)} %own_far.1, bf16[32,8,128]{2,1,0:T(8,128)(2,1)S(1)} %all_to_all.25.came, bf16[160,512]{1,0:T(8,128)(2,1)S(1)} %collective-permute-done.1.one, bf16[160,512]{1,0:T(8,128)(2,1)S(1)} %collective-permute-done.2.two, ...), custom_call_target="tpu_custom_call" | custom-call | flops 10485760 | bytes 786464 | tf_op jit(solution)/shard_map/pallas_call | solution.py:298
  37.6 0.0 copy-start
  37.6 9.6 %all_to_all.26.came = bf16[8,16,256]{2,1,0:T(8,128)(2,1)S(1)} all-to-all(bf16[8,16,256]{2,1,0:T(8,128)(2,1)S(1)} %shard_map.196), channel_id=1, replica_groups=mesh['req'=8,'head'=4] {'req'}, dimensions={0} | all-to-all | bytes 131072 | tf_op jit(solution)/shard_map/all_to_all | solution.py:84
  47.2 1.0 %shard_map.197 = (bf16[8,16,768]{2,1,0:T(8,128)(2,1)S(1)}, bf16[16,256]{1,0:T(8,128)(2,1)S(1)}) custom-call(f32[1,2048]{1,0:T(1,128)} %bitcast.11, bf16[8,16,256]{2,1,0:T(8,128)(2,1)S(1)} %all_to_all.26.came, bf16[16,2048]{1,0:T(8,128)(2,1)S(1)} %all_gather.9.whole, bf16[256,1280]{1,0:T(8,128)(2,1)S(1)} %get-tuple-element.31.mine, ...), custom_call_target="tpu_custom_call" | custom-call | flops 20971520 | bytes 1654784 | tf_op jit(solution)/shard_map/pallas_call | solution.py:298
  48.3 10.2 %all_to_all.27.came = bf16[8,16,768]{2,1,0:T(8,128)(2,1)S(1)} all-to-all(bf16[8,16,768]{2,1,0:T(8,128)(2,1)S(1)} %get-tuple-element.33), channel_id=1, replica_groups=mesh['req'=8,'head'=4] {'req'}, dimensions={0} | all-to-all | bytes 393216 | tf_op jit(solution)/shard_map/all_to_all | solution.py:84
  58.4 0.2 shard_map.198
  58.6 5.2 %all-gather = bf16[64,320]{1,0:T(8,128)(2,1)S(1)} all-gather(bf16[16,320]{1,0:T(8,128)(2,1)S(1)} %shard_map.198), channel_id=2, replica_groups=mesh['req'=8,'head'=4] {'head'}, dimensions={0}, use_global_device_ids=true | all-gather | bytes 51200 | tf_op jit(solution)/shard_map/all_gather | solution.py:839
  63.8 0.2 shard_map.199
  64.1 10.2 %all_to_all.28.came = bf16[8,16,512]{2,1,0:T(8,128)(2,1)S(1)} all-to-all(bf16[8,16,512]{2,1,0:T(8,128)(2,1)S(1)} %shard_map.199), channel_id=1, replica_groups=mesh['req'=8,'head'=4] {'req'}, dimensions={0} | all-to-all | bytes 262144 | tf_op jit(solution)/shard_map/all_to_all | solution.py:84
  74.2 0.6 shard_map.200
  (4 shorter events, 0.0 us)
Async XLA Ops:
  9.0 14.6 %all-to-all-start = ((f32[32,8,128]{2,1,0:T(8,128)}), f32[32,8,128]{2,1,0:T(8,128)S(1)}, u32[]{:S(2)}, u32[]{:S(2)}) async-start(f32[32,8,128]{2,1,0:T(8,128)} %shard_map.194), calls=%async_computation | async-start | bytes 262144 | tf_op jit(solution)/shard_map/all_to_all | solution.py:753
  15.3 9.6 %copy-start.1 = (bf16[160,512]{1,0:T(8,128)(2,1)S(1)}, bf16[160,512]{1,0:T(8,128)(2,1)}, u32[]{:S(2)}) copy-start(bf16[160,512]{1,0:T(8,128)(2,1)} %own_far.1) | copy-start | bytes 491524
  24.6 11.7 %collective-permute-start = (bf16[256,1280]{1,0:T(8,128)(2,1)S(1)}, bf16[256,1280]{1,0:T(8,128)(2,1)S(1)}, u32[]{:S(2)}, u32[]{:S(2)}) collective-permute-start(bf16[256,1280]{1,0:T(8,128)(2,1)S(1)} %get-tuple-element.25), channel_id=1, source_target_pairs={{0,1},{1,0},{2,3},{3,2},{4,5},{5,4},{6,7},{7,6},{8,9},{9,8},{10,11... | collective-permute-start | bytes 1966088 | tf_op jit(solution)/shard_map/ppermute | solution.py:704
  24.9 11.4 %collective-permute-start.1 = (bf16[160,512]{1,0:T(8,128)(2,1)S(1)}, bf16[160,512]{1,0:T(8,128)(2,1)S(1)}, u32[]{:S(2)}, u32[]{:S(2)}) collective-permute-start(bf16[160,512]{1,0:T(8,128)(2,1)S(1)} %copy-done.1), channel_id=1, source_target_pairs={{0,1},{1,0},{2,3},{3,2},{4,5},{5,4},{6,7},{7,6},{8,9},{9,8},{10,11... | collective-permute-start | bytes 491528 | tf_op jit(solution)/shard_map/ppermute | solution.py:704
  25.2 11.1 %collective-permute-start.2 = (bf16[160,512]{1,0:T(8,128)(2,1)S(1)}, bf16[160,512]{1,0:T(8,128)(2,1)S(1)}, u32[]{:S(2)}, u32[]{:S(2)}) collective-permute-start(bf16[160,512]{1,0:T(8,128)(2,1)S(1)} %copy-done.1), channel_id=1, source_target_pairs={{0,2},{1,3},{2,0},{3,1},{4,6},{5,7},{6,4},{7,5},{8,10},{9,11},{10,... | collective-permute-start | bytes 491528 | tf_op jit(solution)/shard_map/ppermute | solution.py:704
  25.7 10.7 %collective-permute-start.3 = (bf16[160,512]{1,0:T(8,128)(2,1)S(1)}, bf16[160,512]{1,0:T(8,128)(2,1)S(1)}, u32[]{:S(2)}, u32[]{:S(2)}) collective-permute-start(bf16[160,512]{1,0:T(8,128)(2,1)S(1)} %copy-done.1), channel_id=1, source_target_pairs={{0,3},{1,2},{2,1},{3,0},{4,7},{5,6},{6,5},{7,4},{8,11},{9,10},{10,... | collective-permute-start | bytes 491528 | tf_op jit(solution)/shard_map/ppermute | solution.py:704
  37.6 26.2 %copy-start = (bf16[640,512]{1,0:T(8,128)(2,1)S(1)}, bf16[640,512]{1,0:T(8,128)(2,1)}, u32[]{:S(2)}) copy-start(bf16[640,512]{1,0:T(8,128)(2,1)} %weight.1) | copy-start | bytes 1966084

commit v9 on v8

--- a/solution.py
+++ b/solution.py
@@ -373,12 +373,12 @@
 
 
 def prepare_kernel(*refs):
-    far, refs = refs[:12], refs[12:]
-    (compact, summaries, kept, added, tables, mine, theirs), refs = refs[:7], refs[7:]
-    near, (ordered, plain, dealt, done) = refs[:12], refs[12:]
+    far, refs = refs[:13], refs[13:]
+    (compact, summaries, kept, added, tables, mine, theirs, *handed), refs = refs[:9], refs[9:]
+    near, (ordered, plain, dealt, done) = refs[:13], refs[13:]
     copies = fetch(far, near, done)
     (dest, lengths, source, table, keep, weights, query_gain, key_gain, turns) = near[:9]
-    pages, gate, up = near[9:]
+    pages, gate, up, output = near[9:]
     group = lax.axis_index("req")
     lane = lax.axis_index("head")
     lanes = lax.axis_size("head")
@@ -471,9 +471,13 @@
             dealt[k, :, start + piece : start + block] = up[:, columns].astype(single)
     mine[...] = dealt[lane & 1].astype(bfloat)
     theirs[...] = dealt[1 - (lane & 1)].astype(bfloat)
-
-
-def attend_kernel(came, kept, added, tables, sent, x, extra_k, extra_v, out):
+    width = handed[0].shape[1]
+    for turn, block in enumerate(handed):
+        start = pl.multiple_of(((group & 1) ^ turn) * width, width)
+        block[...] = output[:, pl.ds(start, width)]
+
+
+def attend_kernel(came, kept, added, tables, sent, x, extra_k, extra_v, out, logs):
     lanes = lax.axis_size("head")
     groups = came.shape[0] // lanes
     width = (HEADS + 2 * KVH) * HD // lanes
@@ -485,9 +489,9 @@
     x[...] = jnp.zeros_like(x)
     column = iota((8, TILE), 1)
     for k in range(lanes):
-        tile = came[k]
+        tile = came[k].astype(single)
         for g in range(1, groups):
-            tile = tile + came[g * lanes + k]
+            tile = tile + came[g * lanes + k].astype(single)
         tile = tile.astype(bfloat).astype(single)
         base, shift = divmod(width * k, TILE)
         base = base * R_DEV
@@ -577,64 +581,79 @@
         for c in range(1, span // TILE):
             picked = jnp.where((slot >> 1) == c, mine[:, c * TILE : (c + 1) * TILE], picked)
         results.append(jnp.where((slot & 1) == u, picked, pltpu.roll(picked, HD, 1)))
-    out[:rows, :] = jnp.where(half == 0, results[0], results[1])
-    level = jnp.where(half == 0, level[:rows], level[rows:])
-    out[rows:, :] = three_terms(level, iota(level.shape, 1) % TERMS)
-    own = HEADS * HD // groups
-    for g in range(groups):
-        r = own * g // TILE * R_DEV
-        tile = jnp.concatenate([out[r : r + 4, :], out[rows + r : rows + r + 4, :]], axis=0)
-        for k in range(lanes):
-            sent[g * lanes + k] = tile.astype(bfloat)
-
-
-def project_kernel(
-    source_far, own_far, came, one, two, three, sent, source, own, rows, done
-):
-    copies = fetch((source_far, own_far), (source, own), done)
+    out[...] = jnp.where(half == 0, results[0], results[1])
+    logs[...] = jnp.broadcast_to(level, logs.shape)
+    own = HEADS * HD // lanes
+    size = 6
+    column = iota((size, TILE), 1)
+    here = column // TERMS == iota((size, TILE), 0)
+    for k in range(lanes):
+        r = own * k // TILE * R_DEV
+        tile = [out[r : r + size, :]]
+        for u in range(2):
+            coded = three_terms(logs[rows * u + r : rows * u + r + size, :], column % TERMS)
+            tile.append(jnp.sum(jnp.where(here, coded, 0.0), axis=0, keepdims=True))
+        tile = jnp.concatenate(tile, axis=0).astype(bfloat)
+        for g in range(groups):
+            sent[g * lanes + k] = tile
+
+
+def project_kernel(source_far, came, first, second, sent, source, logs, rows, pieces, done):
+    (copy,) = fetch((source_far,), (source,), done)
     lanes = lax.axis_size("head")
     groups = came.shape[0] // lanes
-    features = own.shape[0]
+    group = lax.axis_index("req")
+    features = first.shape[0]
     requests = rows.shape[0]
-    near = (iota((TILE, TILE), 0) // TERMS == iota((TILE, TILE), 1) // TERMS).astype(single)
-    tiles = came[...].reshape(groups * lanes * 8, TILE)
-    levels = jnp.dot(tiles, near.astype(bfloat), preferred_element_type=single)
-    tiles = tiles.astype(single).reshape(groups, lanes, 8, TILE)
-    levels = levels.reshape(groups, lanes, 8, TILE)
+    size = 6
+    tiles = [came[d].astype(single) for d in range(groups * lanes)]
     for g in range(groups):
-        mine = [levels[g, k, 4:8] for k in range(lanes)]
-        top = jnp.maximum(jnp.maximum(mine[0], mine[1]), jnp.maximum(mine[2], mine[3]))
-        shares = [jnp.exp(level - top) for level in mine]
-        mixed = sum(share * tiles[g, k, 0:4] for k, share in enumerate(shares)) / sum(shares)
-        rows[R_DEV * g : R_DEV * (g + 1), :TILE] = mixed[:R_DEV]
-        rows[R_DEV * g : R_DEV * (g + 1), TILE:] = mixed[R_DEV:]
-    shift = lax.rem(2 * TILE - lax.rem(lax.axis_index("req") * features, TILE), 2 * TILE)
-    attention = pltpu.roll(rows[...].astype(bfloat).astype(single), shift, 1)
-    for copy in copies:
-        copy.wait()
+        for k in range(lanes):
+            logs[k, 2 * g : 2 * g + 2, :] = tiles[g * lanes + k][size:]
+    spread = (iota((8, TILE), 1) // TERMS == iota((8, TILE), 0)).astype(single).astype(bfloat)
+    levels = [dot_rows(spread, logs[k].astype(bfloat)) for k in range(lanes)]
+    top = jnp.maximum(jnp.maximum(levels[0], levels[1]), jnp.maximum(levels[2], levels[3]))
+    shares = [jnp.exp(level - top) for level in levels]
+    mass = sum(shares)
+    shares = [share / mass for share in shares]
+    lower = iota((8, TILE), 1) < HD
+    for g in range(groups):
+        mixed = 0.0
+        for k in range(lanes):
+            share = shares[k]
+            share = jnp.where(lower, share[:, 2 * g : 2 * g + 1], share[:, 2 * g + 1 : 2 * g + 2])
+            mixed = mixed + share * tiles[g * lanes + k]
+        for j in range(size // R_DEV):
+            rows[R_DEV * g : R_DEV * (g + 1), TILE * j : TILE * (j + 1)] = mixed[
+                R_DEV * j : R_DEV * (j + 1)
+            ]
+    width = rows.shape[1]
+    shift = lax.rem(lax.axis_index("head") * (2 * features), TILE)
+    attention = rows[...].astype(bfloat).astype(single)
+    attention = pltpu.roll(attention, lax.rem(width - shift, width), 1)
+    copy.wait()
     order = row_order(source, requests, False)
     attention = jnp.dot(order, attention.astype(bfloat), preferred_element_type=single)
-    attention = attention[:, :features].astype(bfloat)
-    width = sent.shape[2]
-    share = groups // lanes
-    for turn, weight in enumerate((own, one, two, three)):
-        projected = jnp.dot(attention, weight[...], preferred_element_type=single)
-        target = (lax.axis_index("head") ^ turn) * share
-        for b in range(share):
-            sent[target + b] = projected[:, width * b : width * (b + 1)].astype(bfloat)
+    for b in range(2):
+        pieces[b] = attention[:, features * b : features * (b + 1)]
+    total = 0.0
+    for turn, weight in enumerate((first, second)):
+        piece = pieces[(group & 1) ^ turn].astype(bfloat)
+        total = total + jnp.dot(piece, weight[...], preferred_element_type=single)
+    sent[...] = total
 
 
 def units_kernel(gain_far, came, whole, mine, theirs, sent, mid_out, gain, done):
     (copy,) = fetch((gain_far,), (gain,), done)
-    groups, rows, features = came.shape
-    share = groups // lax.axis_size("head")
+    lanes, rows, features = came.shape
+    share = sent.shape[0] // lanes
     group = lax.axis_index("req")
     lane = lax.axis_index("head")
     here = pl.ds(pl.multiple_of(group * features, features), features)
-    mid = whole[:, here].astype(single)
-    for g in range(groups):
-        mid = mid + came[g].astype(single)
-    mid = mid.astype(bfloat)
+    mid = came[0]
+    for k in range(1, lanes):
+        mid = mid + came[k]
+    mid = (whole[:, here].astype(single) + mid).astype(bfloat)
     mid_out[...] = mid
     mid = mid.astype(single)
     squares = jnp.sum(mid * mid, axis=1, keepdims=True)
@@ -702,6 +721,18 @@
 def swapped_lanes(value, turn):
     lanes = lax.axis_size("head")
     return lax.ppermute(value, "head", [(k, k ^ turn) for k in range(lanes)])
+
+
+def handed_over(value, turn):
+    groups = lax.axis_size("req")
+    lanes = lax.axis_size("head")
+    share = groups // lanes
+    pairs = [
+        (g * lanes + h, (share * h + ((g & 1) ^ turn)) * lanes + g // share)
+        for g in range(groups)
+        for h in range(lanes)
+    ]
+    return lax.ppermute(value, both_axes, pairs)
 
 
 def on_device(
@@ -762,10 +793,11 @@
         old_cache,
         gate_weight,
         up_weight,
+        output_weight,
     ]
     entries = pages_here * KEEP
     extras = 16
-    compact, summaries, kept, added, tables, mine, theirs = run(
+    compact, summaries, kept, added, tables, mine, theirs, *handed = run(
         prepare_kernel,
         [
             shaped((pages_here // 2, PAGE, KVW), bfloat),
@@ -775,6 +807,8 @@
             shaped((96, TILE), single),
             shaped(gate_weight.shape, bfloat),
             shaped(gate_weight.shape, bfloat),
+            shaped((output_weight.shape[0], features), bfloat),
+            shaped((output_weight.shape[0], features), bfloat),
         ],
         scalars + arrays,
         [],
@@ -798,27 +832,29 @@
             pltpu.VMEM((32, TILE), single),
             pltpu.VMEM((extras, span), single),
             pltpu.VMEM((extras, span), single),
+            pltpu.VMEM((24, TILE), single),
             pltpu.VMEM((48, TILE), single),
         ],
         6 * 48 * entries * span,
     )
-    output_weights, theirs, _ = lax.optimization_barrier((output_weight, theirs, parts))
-    others = [swapped_lanes(output_weights, turn) for turn in range(1, lanes)]
+    theirs, *handed, _ = lax.optimization_barrier((theirs, *handed, parts))
     theirs = swapped_lanes(theirs, 1)
+    handed = [handed_over(value, turn) for turn, value in enumerate(handed)]
     came = lax.all_to_all(parts, both_axes, 0, 0, tiled=True)
-    came, theirs, *others = lax.optimization_barrier((came, theirs, *others))
+    came, theirs, *handed = lax.optimization_barrier((came, theirs, *handed))
     (sent,) = run(
         project_kernel,
-        [shaped((groups, requests, features), bfloat)],
-        [holds, output_weight],
-        [came, *others],
+        [shaped((requests, features), single)],
+        [holds],
+        [came, *handed],
         [
             *scalar_like(holds),
-            *local_like(output_weight),
-            pltpu.VMEM((requests, 2 * TILE), single),
-            copies((2,)),
+            pltpu.VMEM((lanes, 2 * groups, TILE), single),
+            pltpu.VMEM((requests, 3 * TILE), single),
+            pltpu.VMEM((2, requests, output_weight.shape[0]), single),
+            copies((1,)),
         ],
-        2 * requests * output_weight.size * lanes,
+        2 * requests * output_weight.size,
     )
     gain = feedforward_gain[None, :]
     block = gate_weight.shape[1] // 2
@@ -829,7 +865,7 @@
             shaped((requests, features), bfloat),
         ],
         [gain],
-        [exchange(sent), whole, mine, theirs],
+        [lax.all_gather(sent, "head"), whole, mine, theirs],
         [*local_like(gain), copies((1,))],
         4 * requests * gate_weight.size,
     )

time: 75.3 us -> 77.8 us (1.033)
  blocking collectives: 51.1 us -> 45.4 us
  waiting for transfers between devices: 3.71 us -> 8.75 us
  starting transfers between devices: 8.47 us -> 11.5 us
    all_gather x0 -> x1, blocking collectives: none -> 12.2 us  [on_device(): lax.all_gather(sent, 'head')]
    all_to_all x1 -> x0, blocking collectives: 9.53 us -> none  [on_device(): came = lax.all_to_all(parts, both_axes, 0, 0, tiled=True)]
    all_to_all x3 -> x2, blocking collectives: 29.9 us -> 21.6 us  [exchange(): return lax.all_to_all(parts, 'req', split_axis=0, concat_axis=0, tiled=True)]
    ppermute x0 -> x2, waiting for transfers between devices: none -> 2.99 us  [handed_over(): return lax.ppermute(value, both_axes, pairs)]
    all_to_all x0 -> x1, starting transfers between devices: none -> 2.54 us  [on_device(): came = lax.all_to_all(parts, both_axes, 0, 0, tiled=True)]
    ppermute x0 -> x2, starting transfers between devices: none -> 2.38 us  [handed_over(): return lax.ppermute(value, both_axes, pairs)]
    all_to_all x0 -> x1, waiting for transfers between devices: none -> 2.03 us  [on_device(): came = lax.all_to_all(parts, both_axes, 0, 0, tiled=True)]
    ppermute x4 -> x1, starting transfers between devices: 2.14 us -> 0.22 us  [swapped_lanes(): return lax.ppermute(value, 'head', [(k, k ^ turn) for k in range(lanes)])]
  transfers between devices with their start and end apart: 5 -> 5, of which waited for: 1 -> 3; matrix products, arithmetic and copies ran while one was open for 0% -> 0% of each run, Pallas kernels for 6% -> 6%
where the time goes in v9:
time: 77.8 us; the launch traced here: 77.4 us
  blocking collectives  45.4 us (58%)
  starting transfers between devices  11.5 us (15%)
  Pallas kernels  11.1 us (14%)
  waiting for transfers between devices  8.75 us (11%)
    all_to_all x2, blocking collectives, exchange(): return lax.all_to_all(parts, 'req', split_axis=0, concat_axis=0, tiled=True)  21.6 us
    all_gather x1, blocking collectives, on_device(): lax.all_gather(sent, 'head')  12.2 us
    pallas_call x8, Pallas kernels, run(): pl.pallas_call(kernel, out_shape=list(outs), in_specs=in_specs, out_specs...  11.1 us
    all_gather x1, blocking collectives, on_device(): whole = lax.all_gather(hidden_in, 'head', axis=1, tiled=True)  6.43 us
    all_to_all x1, starting transfers between devices, on_device(): came = lax.all_to_all(sent, both_axes, 0, 0, tiled=True)  6.33 us
    all_gather x1, blocking collectives, on_device(): active = lax.all_gather(active, 'head')  5.24 us
    all_to_all x1, waiting for transfers between devices, on_device(): came = lax.all_to_all(sent, both_axes, 0, 0, tiled=True)  3.73 us
    ppermute x2, waiting for transfers between devices, handed_over(): return lax.ppermute(value, both_axes, pairs)  2.99 us
  transfers between devices with their start and end apart: 5, of which 3 were waited for; matrix products, arithmetic and copies ran while one was open for 0% of the time, Pallas kernels for 6%

profile of v9, /device:TPU:0, one launch (start us, length us, event | category | flops | bytes accessed | tf_op | source)
XLA Modules:
  0.0 77.4 jit_solution(7916811121435735010)
XLA Ops:
  0.6 6.4 %all_gather.15.whole = bf16[16,2048]{1,0:T(8,128)(2,1)S(1)} all-gather(bf16[16,512]{1,0:T(8,128)(2,1)} %param.18), channel_id=1, replica_groups=mesh['req'=8,'head'=4] {'head'}, dimensions={1}, use_global_device_ids=true | all-gather | bytes 81920 | tf_op jit(solution)/shard_map/all_gather | solution.py:765
  7.1 1.9 %shard_map.194 = f32[32,8,128]{2,1,0:T(8,128)} custom-call(s32[1,8]{1,0:T(1,128)} %bitcast.14, f32[1,2048]{1,0:T(1,128)} %bitcast.12, bf16[480,256]{1,0:T(8,128)(2,1)} %bitcast.11, bf16[16,2048]{1,0:T(8,128)(2,1)S(1)} %all_gather.15.whole), custom_call_target="tpu_custom_call" | custom-call | flops 3932160 | bytes 450592 | tf_op jit(solution)/shard_map/pallas_call | solution.py:298
  9.0 6.3 %all-to-all-start = ((f32[32,8,128]{2,1,0:T(8,128)}), f32[32,8,128]{2,1,0:T(8,128)S(1)}, u32[]{:S(2)}, u32[]{:S(2)}) async-start(f32[32,8,128]{2,1,0:T(8,128)} %shard_map.194), calls=%async_computation | async-start | bytes 262144 | tf_op jit(solution)/shard_map/all_to_all | solution.py:784
  15.3 4.5 %shard_map.193 = (bf16[4,128,640]{2,1,0:T(8,128)(2,1)}, bf16[8,640]{1,0:T(8,128)(2,1)}, bf16[528,640]{1,0:T(8,128)(2,1)S(1)}, f32[8,640]{1,0:T(8,128)S(1)}, f32[...) custom-call(s32[1,8]{1,0:T(1,128)} %refs_0_.1, ...), custom_call_target="tpu_custom_call" | custom-call | flops 167772160 | bytes 5702400 | tf_op jit(solution)/shard_map/pallas_call | solution.py:298
  19.8 3.7 %all-to-all-done.came = f32[32,8,128]{2,1,0:T(8,128)S(1)} async-done(((f32[32,8,128]{2,1,0:T(8,128)}), f32[32,8,128]{2,1,0:T(8,128)S(1)}, u32[]{:S(2)}, u32[]{:S(2)}) %all-to-all-start) | async-done | bytes 131104 | tf_op jit(solution)/shard_map/all_to_all | solution.py:784
  23.5 1.7 %shard_map.195 = bf16[32,8,128]{2,1,0:T(8,128)(2,1)} custom-call(f32[32,8,128]{2,1,0:T(8,128)S(1)} %all-to-all-done.came, bf16[528,640]{1,0:T(8,128)(2,1)S(1)} %get-tuple-element.23.kept, f32[8,640]{1,0:T(8,128)S(1)} %get-tuple-element.24.added, f32[96,128]{1,0:T(8,128)S(1)} %get-tuple-element.25.tables), custom_call_target="tpu_custom_call" | custom-call | flops 56623104 | bytes 942080 | tf_op jit(solution)/shard_map/pallas_call | solution.py:298
  25.3 0.2 collective-permute-start
  25.5 2.5 %all-to-all-start.1 = ((bf16[32,8,128]{2,1,0:T(8,128)(2,1)}), bf16[32,8,128]{2,1,0:T(8,128)(2,1)S(1)}, u32[]{:S(2)}, u32[]{:S(2)}) async-start(bf16[32,8,128]{2,1,0:T(8,128)(2,1)} %shard_map.195), calls=%async_computation.1 | async-start | bytes 131072 | tf_op jit(solution)/shard_map/all_to_all | solution.py:843
  28.0 0.7 collective-permute-start.1
  28.7 1.7 %collective-permute-start.2 = (bf16[160,256]{1,0:T(8,128)(2,1)S(1)}, bf16[160,256]{1,0:T(8,128)(2,1)S(1)}, u32[]{:S(2)}, u32[]{:S(2)}) collective-permute-start(bf16[160,256]{1,0:T(8,128)(2,1)S(1)} %get-tuple-element.31), channel_id=1, source_target_pairs={{0,4},{1,12},{2,20},{3,28},{4,0},{5,8},{6,16},{7,24},{8,5},{9,13},... | collective-permute-start | bytes 245768 | tf_op jit(solution)/shard_map/ppermute | solution.py:735
  30.4 0.0 collective-permute-done.1.first
  30.4 3.0 %collective-permute-done.2.second = bf16[160,256]{1,0:T(8,128)(2,1)S(1)} collective-permute-done((bf16[160,256]{1,0:T(8,128)(2,1)S(1)}, bf16[160,256]{1,0:T(8,128)(2,1)S(1)}, u32[]{:S(2)}, u32[]{:S(2)}) %collective-permute-start.2) | collective-permute-done | bytes 81952 | tf_op jit(solution)/shard_map/ppermute | solution.py:735
  33.4 2.0 %all-to-all-done.1.came = bf16[32,8,128]{2,1,0:T(8,128)(2,1)S(1)} async-done(((bf16[32,8,128]{2,1,0:T(8,128)(2,1)}), bf16[32,8,128]{2,1,0:T(8,128)(2,1)S(1)}, u32[]{:S(2)}, u32[]{:S(2)}) %all-to-all-start.1) | async-done | bytes 65568 | tf_op jit(solution)/shard_map/all_to_all | solution.py:843
  35.4 0.0 collective-permute-done.theirs
  35.4 1.0 %shard_map.196 = f32[16,256]{1,0:T(8,128)S(1)} custom-call(s32[1,8]{1,0:T(1,128)} %bitcast.16, bf16[32,8,128]{2,1,0:T(8,128)(2,1)S(1)} %all-to-all-done.1.came, bf16[160,256]{1,0:T(8,128)(2,1)S(1)} %collective-permute-done.1.first, bf16[160,256]{1,0:T(8,128)(2,1)S(1)} %collective-permute-done.2.second), custom_call_target="tpu_custom_call" | custom-call | flops 2621440 | bytes 245792 | tf_op jit(solution)/shard_map/pallas_call | solution.py:298
  36.4 12.2 %all-gather = f32[64,256]{1,0:T(8,128)S(1)} all-gather(f32[16,256]{1,0:T(8,128)S(1)} %shard_map.196), channel_id=2, replica_groups=mesh['req'=8,'head'=4] {'head'}, dimensions={0}, use_global_device_ids=true | all-gather | bytes 81920 | tf_op jit(solution)/shard_map/all_gather | solution.py:868
  48.6 1.0 %shard_map.197 = (bf16[8,16,768]{2,1,0:T(8,128)(2,1)S(1)}, bf16[16,256]{1,0:T(8,128)(2,1)S(1)}) custom-call(f32[1,2048]{1,0:T(1,128)} %bitcast.13, f32[4,16,256]{2,1,0:T(8,128)S(1)} %bitcast.9, bf16[16,2048]{1,0:T(8,128)(2,1)S(1)} %all_gather.15.whole, bf16[256,1280]{1,0:T(8,128)(2,1)S(1)} %get-tuple-element.35.mine, ...), custom_call_target="tpu_custom_call" | custom-call | flops 20971520 | bytes 1654784 | tf_op jit(solution)/shard_map/pallas_call | solution.py:298
  49.6 11.2 %all_to_all.20.came = bf16[8,16,768]{2,1,0:T(8,128)(2,1)S(1)} all-to-all(bf16[8,16,768]{2,1,0:T(8,128)(2,1)S(1)} %get-tuple-element.37), channel_id=1, replica_groups=mesh['req'=8,'head'=4] {'req'}, dimensions={0} | all-to-all | bytes 393216 | tf_op jit(solution)/shard_map/all_to_all | solution.py:84
  60.8 0.2 shard_map.198
  60.9 5.2 %all-gather.1 = bf16[64,320]{1,0:T(8,128)(2,1)S(1)} all-gather(bf16[16,320]{1,0:T(8,128)(2,1)S(1)} %shard_map.198), channel_id=3, replica_groups=mesh['req'=8,'head'=4] {'head'}, dimensions={0}, use_global_device_ids=true | all-gather | bytes 51200 | tf_op jit(solution)/shard_map/all_gather | solution.py:875
  66.2 0.0 copy-done
  66.2 0.2 shard_map.199
  66.4 10.4 %all_to_all.21.came = bf16[8,16,512]{2,1,0:T(8,128)(2,1)S(1)} all-to-all(bf16[8,16,512]{2,1,0:T(8,128)(2,1)S(1)} %shard_map.199), channel_id=1, replica_groups=mesh['req'=8,'head'=4] {'req'}, dimensions={0} | all-to-all | bytes 262144 | tf_op jit(solution)/shard_map/all_to_all | solution.py:84
  76.8 0.6 shard_map.200
  (1 shorter events, 0.0 us)
Async XLA Ops:
  9.0 14.6 %all-to-all-start = ((f32[32,8,128]{2,1,0:T(8,128)}), f32[32,8,128]{2,1,0:T(8,128)S(1)}, u32[]{:S(2)}, u32[]{:S(2)}) async-start(f32[32,8,128]{2,1,0:T(8,128)} %shard_map.194), calls=%async_computation | async-start | bytes 262144 | tf_op jit(solution)/shard_map/all_to_all | solution.py:784
  25.3 40.9 %copy-start = (bf16[640,512]{1,0:T(8,128)(2,1)S(1)}, bf16[640,512]{1,0:T(8,128)(2,1)}, u32[]{:S(2)}) copy-start(bf16[640,512]{1,0:T(8,128)(2,1)} %weight.1) | copy-start | bytes 1966084
  25.3 10.2 %collective-permute-start = (bf16[256,1280]{1,0:T(8,128)(2,1)S(1)}, bf16[256,1280]{1,0:T(8,128)(2,1)S(1)}, u32[]{:S(2)}, u32[]{:S(2)}) collective-permute-start(bf16[256,1280]{1,0:T(8,128)(2,1)S(1)} %get-tuple-element.29), channel_id=1, source_target_pairs={{0,1},{1,0},{2,3},{3,2},{4,5},{5,4},{6,7},{7,6},{8,9},{9,8},{10,11... | collective-permute-start | bytes 1966088 | tf_op jit(solution)/shard_map/ppermute | solution.py:723
  25.5 10.0 %all-to-all-start.1 = ((bf16[32,8,128]{2,1,0:T(8,128)(2,1)}), bf16[32,8,128]{2,1,0:T(8,128)(2,1)S(1)}, u32[]{:S(2)}, u32[]{:S(2)}) async-start(bf16[32,8,128]{2,1,0:T(8,128)(2,1)} %shard_map.195), calls=%async_computation.1 | async-start | bytes 131072 | tf_op jit(solution)/shard_map/all_to_all | solution.py:843
  28.0 2.4 %collective-permute-start.1 = (bf16[160,256]{1,0:T(8,128)(2,1)S(1)}, bf16[160,256]{1,0:T(8,128)(2,1)S(1)}, u32[]{:S(2)}, u32[]{:S(2)}) collective-permute-start(bf16[160,256]{1,0:T(8,128)(2,1)S(1)} %get-tuple-element.30), channel_id=1, source_target_pairs={{0,0},{1,8},{2,16},{3,24},{4,4},{5,12},{6,20},{7,28},{8,1},{9,9},{... | collective-permute-start | bytes 245768 | tf_op jit(solution)/shard_map/ppermute | solution.py:735
  28.7 4.7 %collective-permute-start.2 = (bf16[160,256]{1,0:T(8,128)(2,1)S(1)}, bf16[160,256]{1,0:T(8,128)(2,1)S(1)}, u32[]{:S(2)}, u32[]{:S(2)}) collective-permute-start(bf16[160,256]{1,0:T(8,128)(2,1)S(1)} %get-tuple-element.31), channel_id=1, source_target_pairs={{0,4},{1,12},{2,20},{3,28},{4,0},{5,8},{6,16},{7,24},{8,5},{9,13},... | collective-permute-start | bytes 245768 | tf_op jit(solution)/shard_map/ppermute | solution.py:735

commit v10 on v9

--- a/solution.py
+++ b/solution.py
@@ -339,20 +339,36 @@
 
 
 def first_kernel(
-    source_far, gain_far, weight_far, whole, sent, source, gain, weight, wide, done
+    source_far, gain_far, weight_far, hidden_far, one, two, three, sent, block, source, gain,
+    weight, hidden, lanes_of, wide, done
 ):
-    copies = fetch((source_far, gain_far, weight_far), (source, gain, weight), done)
-    rows = whole.shape[0]
+    copies = fetch(
+        (source_far, gain_far, weight_far, hidden_far), (source, gain, weight, hidden), done
+    )
+    rows = hidden.shape[0]
     groups = rows // R_DEV
     lanes = sent.shape[0] // groups
     columns, features = weight.shape
-    values = whole[...].astype(single)
-    factor = lax.rsqrt(jnp.mean(values * values, axis=1, keepdims=True) + epsilon)
-    here = pl.ds(pl.multiple_of(lax.axis_index("req") * features, features), features)
+    group = lax.axis_index("req")
+    share = groups // lanes
+    squares = 0.0
+    for turn, values in enumerate((one, two, three)):
+        values = values[...].astype(single)
+        lanes_of[turn + 1] = values
+        squares = squares + jnp.sum(values * values, axis=1, keepdims=True)
+    copies[3].wait()
+    values = hidden[...].astype(single)
+    lanes_of[0] = values
+    squares = squares + jnp.sum(values * values, axis=1, keepdims=True)
+    factor = lax.rsqrt(squares / D + epsilon)
+    here = pl.ds(pl.multiple_of(group * features, features), features)
+    within = pl.ds(pl.multiple_of(group % share * features, features), features)
+    mine = lanes_of[group // share ^ lax.axis_index("head"), :, within]
+    block[...] = mine.astype(bfloat)
     wide[...] = jnp.zeros_like(wide)
-    for copy in copies:
+    for copy in copies[:3]:
         copy.wait()
-    normed = (whole[:, here].astype(single) * factor * gain[:, here]).astype(bfloat)
+    normed = (mine * factor * gain[:, here]).astype(bfloat)
     order = row_order(source, rows, True)
     normed = jnp.dot(order, normed, preferred_element_type=single).astype(bfloat)
     wide[:, :columns] = dot_rows(normed, weight[...])
@@ -373,12 +389,12 @@
 
 
 def prepare_kernel(*refs):
-    far, refs = refs[:13], refs[13:]
-    (compact, summaries, kept, added, tables, mine, theirs, *handed), refs = refs[:9], refs[9:]
-    near, (ordered, plain, dealt, done) = refs[:13], refs[13:]
+    far, refs = refs[:12], refs[12:]
+    (compact, summaries, kept, added, tables, mine, theirs), refs = refs[:7], refs[7:]
+    near, (ordered, plain, dealt, done) = refs[:12], refs[12:]
     copies = fetch(far, near, done)
     (dest, lengths, source, table, keep, weights, query_gain, key_gain, turns) = near[:9]
-    pages, gate, up, output = near[9:]
+    pages, gate, up = near[9:]
     group = lax.axis_index("req")
     lane = lax.axis_index("head")
     lanes = lax.axis_size("head")
@@ -471,10 +487,6 @@
             dealt[k, :, start + piece : start + block] = up[:, columns].astype(single)
     mine[...] = dealt[lane & 1].astype(bfloat)
     theirs[...] = dealt[1 - (lane & 1)].astype(bfloat)
-    width = handed[0].shape[1]
-    for turn, block in enumerate(handed):
-        start = pl.multiple_of(((group & 1) ^ turn) * width, width)
-        block[...] = output[:, pl.ds(start, width)]
 
 
 def attend_kernel(came, kept, added, tables, sent, x, extra_k, extra_v, out, logs):
@@ -637,23 +649,25 @@
     for b in range(2):
         pieces[b] = attention[:, features * b : features * (b + 1)]
     total = 0.0
+    width = sent.shape[1]
+    columns = pl.ds(pl.multiple_of((group & 1) * width, width), width)
     for turn, weight in enumerate((first, second)):
         piece = pieces[(group & 1) ^ turn].astype(bfloat)
-        total = total + jnp.dot(piece, weight[...], preferred_element_type=single)
+        total = total + jnp.dot(piece, weight[:, columns], preferred_element_type=single)
     sent[...] = total
 
 
-def units_kernel(gain_far, came, whole, mine, theirs, sent, mid_out, gain, done):
+def units_kernel(
+    gain_far, own, one, two, three, hidden, mine, theirs, sent, mid_out, gain, done
+):
     (copy,) = fetch((gain_far,), (gain,), done)
-    lanes, rows, features = came.shape
-    share = sent.shape[0] // lanes
+    rows, features = own.shape
+    share = sent.shape[0] // lax.axis_size("head")
     group = lax.axis_index("req")
     lane = lax.axis_index("head")
     here = pl.ds(pl.multiple_of(group * features, features), features)
-    mid = came[0]
-    for k in range(1, lanes):
-        mid = mid + came[k]
-    mid = (whole[:, here].astype(single) + mid).astype(bfloat)
+    mid = (own[...] + one[...]) + (two[...] + three[...])
+    mid = (hidden[...].astype(single) + mid).astype(bfloat)
     mid_out[...] = mid
     mid = mid.astype(single)
     squares = jnp.sum(mid * mid, axis=1, keepdims=True)
@@ -681,16 +695,18 @@
     active[...] = (gate / (1.0 + jnp.exp(-gate)) * up).astype(bfloat)
 
 
-def down_kernel(active, weight, mid, sent):
+def down_kernel(own, one, two, three, weight, mid, sent, active):
     groups, rows, width = sent.shape
-    lanes, _, piece = active.shape
+    piece = own.shape[1]
     half = mid.shape[1]
+    for turn, values in enumerate((own, one, two, three)):
+        active[turn] = values[...]
     share = width // half
     group = lax.axis_index("req")
     lane = lax.axis_index("head")
-    first = group // (2 * share) * 2
+    first = group // (2 * share) * 2 ^ lane
     down = jnp.dot(active[first], weight[:piece, :], preferred_element_type=single)
-    down = down + jnp.dot(active[first + 1], weight[piece:, :], preferred_element_type=single)
+    down = down + jnp.dot(active[first ^ 1], weight[piece:, :], preferred_element_type=single)
     residual = mid[...].astype(single)
     for b in range(share):
         columns = slice(half * b, half * (b + 1))
@@ -721,6 +737,10 @@
 def swapped_lanes(value, turn):
     lanes = lax.axis_size("head")
     return lax.ppermute(value, "head", [(k, k ^ turn) for k in range(lanes)])
+
+
+def from_lanes(value):
+    return [value] + [swapped_lanes(value, turn) for turn in range(1, lax.axis_size("head"))]
 
 
 def handed_over(value, turn):
@@ -762,26 +782,32 @@
     features = D // groups
     copies = pltpu.SemaphoreType.DMA
 
-    whole = lax.all_gather(hidden_in, "head", axis=1, tiled=True)
     columns = input_weight.shape[1]
     padded = -(-columns // TILE) * TILE
     holds = source[None, :]
     gain = attention_gain[None, :]
     weight = input_weight.T
-    (sent,) = run(
+    far = [holds, gain, weight, hidden_in]
+    sent, hidden_block = run(
         first_kernel,
-        [shaped((devices, R_DEV * padded // TILE, TILE), single)],
-        [holds, gain, weight],
-        [whole],
+        [
+            shaped((devices, R_DEV * padded // TILE, TILE), single),
+            shaped((requests, features), bfloat),
+        ],
+        far,
+        from_lanes(hidden_in)[1:],
         [
             *scalar_like(holds),
-            *local_like(gain, weight),
+            *local_like(*far[1:]),
+            pltpu.VMEM((lanes,) + hidden_in.shape, single),
             pltpu.VMEM((requests, padded), single),
-            copies((3,)),
+            copies((len(far),)),
         ],
         2 * requests * features * columns,
     )
     came = lax.all_to_all(sent, both_axes, 0, 0, tiled=True)
+    output_weights, _ = lax.optimization_barrier((output_weight, sent))
+    handed = [handed_over(output_weights, turn) for turn in range(2)]
 
     scalars = [dest_slots, lengths[None, :], holds, page_table]
     arrays = [
@@ -793,11 +819,10 @@
         old_cache,
         gate_weight,
         up_weight,
-        output_weight,
     ]
     entries = pages_here * KEEP
     extras = 16
-    compact, summaries, kept, added, tables, mine, theirs, *handed = run(
+    compact, summaries, kept, added, tables, mine, theirs = run(
         prepare_kernel,
         [
             shaped((pages_here // 2, PAGE, KVW), bfloat),
@@ -807,8 +832,6 @@
             shaped((96, TILE), single),
             shaped(gate_weight.shape, bfloat),
             shaped(gate_weight.shape, bfloat),
-            shaped((output_weight.shape[0], features), bfloat),
-            shaped((output_weight.shape[0], features), bfloat),
         ],
         scalars + arrays,
         [],
@@ -822,6 +845,7 @@
         ],
         2 * pages_here * TILE * PAGE * KVW,
     )
+    came, *handed = lax.optimization_barrier((came, *handed))
     span = -(-KVH * HD // TILE) * TILE
     (parts,) = run(
         attend_kernel,
@@ -837,11 +861,10 @@
         ],
         6 * 48 * entries * span,
     )
-    theirs, *handed, _ = lax.optimization_barrier((theirs, *handed, parts))
+    theirs, _ = lax.optimization_barrier((theirs, parts))
     theirs = swapped_lanes(theirs, 1)
-    handed = [handed_over(value, turn) for turn, value in enumerate(handed)]
     came = lax.all_to_all(parts, both_axes, 0, 0, tiled=True)
-    came, theirs, *handed = lax.optimization_barrier((came, theirs, *handed))
+    came, theirs = lax.optimization_barrier((came, theirs))
     (sent,) = run(
         project_kernel,
         [shaped((requests, features), single)],
@@ -865,20 +888,19 @@
             shaped((requests, features), bfloat),
         ],
         [gain],
-        [lax.all_gather(sent, "head"), whole, mine, theirs],
+        [*from_lanes(sent), hidden_block, mine, theirs],
         [*local_like(gain), copies((1,))],
         4 * requests * gate_weight.size,
     )
     (active,) = run(
         active_kernel, [shaped((requests, block // 2), bfloat)], [], [exchange(sent)]
     )
-    active = lax.all_gather(active, "head")
     (sent,) = run(
         down_kernel,
         [shaped((groups, requests, down_weight.shape[1]), bfloat)],
         [],
-        [active, down_weight, mid],
-        [],
+        [*from_lanes(active), down_weight, mid],
+        [pltpu.VMEM((lanes,) + active.shape, bfloat)],
         2 * requests * down_weight.size,
     )
     (result,) = run(

time: 77.8 us -> 78.4 us (level)
  starting transfers between devices: 11.5 us -> 18.5 us
  blocking collectives: 45.4 us -> 40.5 us
  waiting for transfers between devices: 8.75 us -> 7.75 us
    all_gather x3 -> x0, blocking collectives: 23.8 us -> none  [the longest x1 12.2 us: on_device(): lax.all_gather(sent, 'head')]
    all_to_all x0 -> x1, blocking collectives: none -> 19.7 us  [on_device(): came = lax.all_to_all(parts, both_axes, 0, 0, tiled=True)]
    ppermute x1 -> x10, starting transfers between devices: 0.22 us -> 10.1 us  [swapped_lanes(): return lax.ppermute(value, 'head', [(k, k ^ turn) for k in range(lanes)])]
    ppermute x1 -> x10, waiting for transfers between devices: 0.01 us -> 7.08 us  [swapped_lanes(): return lax.ppermute(value, 'head', [(k, k ^ turn) for k in range(lanes)])]
    all_to_all x1, waiting for transfers between devices: 3.73 us -> 0.01 us  [on_device(): came = lax.all_to_all(sent, both_axes, 0, 0, tiled=True)]
    all_to_all x1 -> x0, starting transfers between devices: 2.54 us -> none  [on_device(): came = lax.all_to_all(parts, both_axes, 0, 0, tiled=True)]
    ppermute x2, waiting for transfers between devices: 2.99 us -> 0.66 us  [handed_over(): return lax.ppermute(value, both_axes, pairs)]
    all_to_all x1 -> x0, waiting for transfers between devices: 2.03 us -> none  [on_device(): came = lax.all_to_all(parts, both_axes, 0, 0, tiled=True)]
  transfers between devices with their start and end apart: 5 -> 13, of which waited for: 3 -> 7; matrix products, arithmetic and copies ran while one was open for 0% -> 0% of each run, Pallas kernels for 6% -> 6%
where the time goes in v10:
time: 78.4 us; the launch traced here: 78 us
  blocking collectives  40.5 us (52%)
  starting transfers between devices  18.5 us (24%)
  Pallas kernels  10.5 us (13%)
  waiting for transfers between devices  7.75 us (10%)
    all_to_all x2, blocking collectives, exchange(): return lax.all_to_all(parts, 'req', split_axis=0, concat_axis=0, tiled=True)  20.9 us
    all_to_all x1, blocking collectives, on_device(): came = lax.all_to_all(parts, both_axes, 0, 0, tiled=True)  19.7 us
    pallas_call x8, Pallas kernels, run(): pl.pallas_call(kernel, out_shape=list(outs), in_specs=in_specs, out_specs...  10.5 us
    ppermute x10, starting transfers between devices, swapped_lanes(): return lax.ppermute(value, 'head', [(k, k ^ turn) for k in range(lanes)])  10.1 us
    ppermute x10, waiting for transfers between devices, swapped_lanes(): return lax.ppermute(value, 'head', [(k, k ^ turn) for k in range(lanes)])  7.08 us
    all_to_all x1, starting transfers between devices, on_device(): came = lax.all_to_all(sent, both_axes, 0, 0, tiled=True)  5.08 us
    ppermute x2, starting transfers between devices, handed_over(): return lax.ppermute(value, both_axes, pairs)  3.4 us
  transfers between devices with their start and end apart: 13, of which 7 were waited for; matrix products, arithmetic and copies ran while one was open for 0% of the time, Pallas kernels for 6%

profile of v10, /device:TPU:0, one launch (start us, length us, event | category | flops | bytes accessed | tf_op | source)
XLA Modules:
  0.0 78.0 jit_solution(3996618364555010501)
XLA Ops:
  0.6 3.0 %collective-permute-start.1 = (bf16[16,512]{1,0:T(8,128)(2,1)}, bf16[16,512]{1,0:T(8,128)(2,1)S(1)}, u32[]{:S(2)}, u32[]{:S(2)}) collective-permute-start(bf16[16,512]{1,0:T(8,128)(2,1)} %hidden_far.1), channel_id=1, source_target_pairs={{0,2},{1,3},{2,0},{3,1},{4,6},{5,7},{6,4},{7,5},{8,10},{9,11},{10,... | collective-permute-start | bytes 49160 | tf_op jit(solution)/shard_map/ppermute | solution.py:739
  3.8 1.7 %collective-permute-done.1.two = bf16[16,512]{1,0:T(8,128)(2,1)S(1)} collective-permute-done((bf16[16,512]{1,0:T(8,128)(2,1)}, bf16[16,512]{1,0:T(8,128)(2,1)S(1)}, u32[]{:S(2)}, u32[]{:S(2)}) %collective-permute-start.1) | collective-permute-done | bytes 16416 | tf_op jit(solution)/shard_map/ppermute | solution.py:739
  5.6 1.4 %collective-permute-done.2.three = bf16[16,512]{1,0:T(8,128)(2,1)S(1)} collective-permute-done((bf16[16,512]{1,0:T(8,128)(2,1)}, bf16[16,512]{1,0:T(8,128)(2,1)S(1)}, u32[]{:S(2)}, u32[]{:S(2)}) %collective-permute-start.2) | collective-permute-done | bytes 16416 | tf_op jit(solution)/shard_map/ppermute | solution.py:739
  7.0 1.9 %shard_map.194 = (f32[32,8,128]{2,1,0:T(8,128)}, bf16[16,256]{1,0:T(8,128)(2,1)S(1)}) custom-call(s32[1,8]{1,0:T(1,128)} %bitcast.10, f32[1,2048]{1,0:T(1,128)} %bitcast.9, bf16[480,256]{1,0:T(8,128)(2,1)} %bitcast.7, bf16[16,512]{1,0:T(8,128)(2,1)} %hidden_far.1, bf16[16,512]{1,0:T(8,128)(2,1)S(1)} %collective-permute-done.one, ...), custom_call_target="tpu_custom_call" | custom-call | flops 3932160 | bytes 458784 | tf_op jit(solution)/shard_map/pallas_call | solution.py:298
  8.9 5.1 %all-to-all-start = ((f32[32,8,128]{2,1,0:T(8,128)}), f32[32,8,128]{2,1,0:T(8,128)S(1)}, u32[]{:S(2)}, u32[]{:S(2)}) async-start(f32[32,8,128]{2,1,0:T(8,128)} %get-tuple-element.23), calls=%async_computation | async-start | bytes 262144 | tf_op jit(solution)/shard_map/all_to_all | solution.py:808
  14.0 1.8 %collective-permute-start.4 = (bf16[160,512]{1,0:T(8,128)(2,1)}, bf16[160,512]{1,0:T(8,128)(2,1)S(1)}, u32[]{:S(2)}, u32[]{:S(2)}) collective-permute-start(bf16[160,512]{1,0:T(8,128)(2,1)} %param.24), channel_id=1, source_target_pairs={{0,4},{1,12},{2,20},{3,28},{4,0},{5,8},{6,16},{7,24},{8,5},{9,13},... | collective-permute-start | bytes 491528 | tf_op jit(solution)/shard_map/ppermute | solution.py:755
  15.9 1.6 %collective-permute-start.3 = (bf16[160,512]{1,0:T(8,128)(2,1)}, bf16[160,512]{1,0:T(8,128)(2,1)S(1)}, u32[]{:S(2)}, u32[]{:S(2)}) collective-permute-start(bf16[160,512]{1,0:T(8,128)(2,1)} %param.24), channel_id=1, source_target_pairs={{0,0},{1,8},{2,16},{3,24},{4,4},{5,12},{6,20},{7,28},{8,1},{9,9},{... | collective-permute-start | bytes 491528 | tf_op jit(solution)/shard_map/ppermute | solution.py:755
  17.4 4.4 %shard_map.193 = (bf16[4,128,640]{2,1,0:T(8,128)(2,1)}, bf16[8,640]{1,0:T(8,128)(2,1)}, bf16[528,640]{1,0:T(8,128)(2,1)S(1)}, f32[8,640]{1,0:T(8,128)S(1)}, f32[...) custom-call(s32[1,8]{1,0:T(1,128)} %refs_0_.1, s32[1,16]{1,0:T(1,128)} %bitcast.13, ...), custom_call_target="tpu_custom_call" | custom-call | flops 167772160 | bytes 5374720 | tf_op jit(solution)/shard_map/pallas_call | solution.py:298
  21.9 0.7 collective-permute-done.4.second
  22.5 1.1 %shard_map.195 = bf16[32,8,128]{2,1,0:T(8,128)(2,1)S(1)} custom-call(f32[32,8,128]{2,1,0:T(8,128)S(1)} %all-to-all-done.came, bf16[528,640]{1,0:T(8,128)(2,1)S(1)} %get-tuple-element.26.kept, f32[8,640]{1,0:T(8,128)S(1)} %get-tuple-element.27.added, f32[96,128]{1,0:T(8,128)S(1)} %get-tuple-element.28.tables), custom_call_target="tpu_custom_call" | custom-call | flops 56623104 | bytes 942080 | tf_op jit(solution)/shard_map/pallas_call | solution.py:298
  23.7 3.0 %collective-permute-start.5 = (bf16[256,1280]{1,0:T(8,128)(2,1)S(1)}, bf16[256,1280]{1,0:T(8,128)(2,1)S(1)}, u32[]{:S(2)}, u32[]{:S(2)}) collective-permute-start(bf16[256,1280]{1,0:T(8,128)(2,1)S(1)} %get-tuple-element.30), channel_id=1, source_target_pairs={{0,1},{1,0},{2,3},{3,2},{4,5},{5,4},{6,7},{7,6},{8,9},{9,8},{10,11... | collective-permute-start | bytes 1966088 | tf_op jit(solution)/shard_map/ppermute | solution.py:739
  26.6 19.7 %all_to_all.20.came = bf16[32,8,128]{2,1,0:T(8,128)(2,1)S(1)} all-to-all(bf16[32,8,128]{2,1,0:T(8,128)(2,1)S(1)} %shard_map.195), channel_id=1, replica_groups=mesh['req'=8,'head'=4] {'req','head'}, dimensions={0} | all-to-all | bytes 131072 | tf_op jit(solution)/shard_map/all_to_all | solution.py:866
  46.3 1.0 %shard_map.196.own = f32[16,256]{1,0:T(8,128)S(1)} custom-call(s32[1,8]{1,0:T(1,128)} %bitcast.12, bf16[32,8,128]{2,1,0:T(8,128)(2,1)S(1)} %all_to_all.20.came, bf16[160,512]{1,0:T(8,128)(2,1)S(1)} %collective-permute-done.3.first, bf16[160,512]{1,0:T(8,128)(2,1)S(1)} %collective-permute-done.4.second), custom_call_target="tpu_custom_call" | custom-call | flops 2621440 | bytes 409632 | tf_op jit(solution)/shard_map/pallas_call | solution.py:298
  47.5 1.6 %collective-permute-start.7 = (f32[16,256]{1,0:T(8,128)S(1)}, f32[16,256]{1,0:T(8,128)S(1)}, u32[]{:S(2)}, u32[]{:S(2)}) collective-permute-start(f32[16,256]{1,0:T(8,128)S(1)} %shard_map.196.own), channel_id=1, source_target_pairs={{0,2},{1,3},{2,0},{3,1},{4,6},{5,7},{6,4},{7,5},{8,10},{9,11},{10,... | collective-permute-start | bytes 49160 | tf_op jit(solution)/shard_map/ppermute | solution.py:739
  49.3 1.3 %collective-permute-done.8.three = f32[16,256]{1,0:T(8,128)S(1)} collective-permute-done((f32[16,256]{1,0:T(8,128)S(1)}, f32[16,256]{1,0:T(8,128)S(1)}, u32[]{:S(2)}, u32[]{:S(2)}) %collective-permute-start.8) | collective-permute-done | bytes 16416 | tf_op jit(solution)/shard_map/ppermute | solution.py:739
  50.5 0.7 collective-permute-done.7.two
  51.3 1.0 %shard_map.197 = (bf16[8,16,768]{2,1,0:T(8,128)(2,1)S(1)}, bf16[16,256]{1,0:T(8,128)(2,1)S(1)}) custom-call(f32[1,2048]{1,0:T(1,128)} %bitcast.8, f32[16,256]{1,0:T(8,128)S(1)} %shard_map.196.own, f32[16,256]{1,0:T(8,128)S(1)} %collective-permute-done.6.one, f32[16,256]{1,0:T(8,128)S(1)} %collective-permute-done.7.two, ...), custom_call_target="tpu_custom_call" | custom-call | flops 20971520 | bytes 1597440 | tf_op jit(solution)/shard_map/pallas_call | solution.py:298
  52.3 10.3 %all_to_all.21.came = bf16[8,16,768]{2,1,0:T(8,128)(2,1)S(1)} all-to-all(bf16[8,16,768]{2,1,0:T(8,128)(2,1)S(1)} %get-tuple-element.37), channel_id=1, replica_groups=mesh['req'=8,'head'=4] {'req'}, dimensions={0} | all-to-all | bytes 393216 | tf_op jit(solution)/shard_map/all_to_all | solution.py:84
  62.8 1.6 %collective-permute-start.10 = (bf16[16,320]{1,0:T(8,128)(2,1)S(1)}, bf16[16,320]{1,0:T(8,128)(2,1)S(1)}, u32[]{:S(2)}, u32[]{:S(2)}) collective-permute-start(bf16[16,320]{1,0:T(8,128)(2,1)S(1)} %shard_map.198.own), channel_id=1, source_target_pairs={{0,2},{1,3},{2,0},{3,1},{4,6},{5,7},{6,4},{7,5},{8,10},{9,11},{10,... | collective-permute-start | bytes 30728 | tf_op jit(solution)/shard_map/ppermute | solution.py:739
  64.4 0.3 collective-permute-start.9
  64.6 1.3 %collective-permute-done.11.three = bf16[16,320]{1,0:T(8,128)(2,1)S(1)} collective-permute-done((bf16[16,320]{1,0:T(8,128)(2,1)S(1)}, bf16[16,320]{1,0:T(8,128)(2,1)S(1)}, u32[]{:S(2)}, u32[]{:S(2)}) %collective-permute-start.11) | collective-permute-done | bytes 10272 | tf_op jit(solution)/shard_map/ppermute | solution.py:739
  65.9 0.6 collective-permute-done.10.two
  66.8 10.6 %all_to_all.22.came = bf16[8,16,512]{2,1,0:T(8,128)(2,1)S(1)} all-to-all(bf16[8,16,512]{2,1,0:T(8,128)(2,1)S(1)} %shard_map.199), channel_id=1, replica_groups=mesh['req'=8,'head'=4] {'req'}, dimensions={0} | all-to-all | bytes 262144 | tf_op jit(solution)/shard_map/all_to_all | solution.py:84
  77.4 0.6 shard_map.200
  (15 shorter events, 1.0 us)
Async XLA Ops:
  0.6 4.9 %collective-permute-start.1 = (bf16[16,512]{1,0:T(8,128)(2,1)}, bf16[16,512]{1,0:T(8,128)(2,1)S(1)}, u32[]{:S(2)}, u32[]{:S(2)}) collective-permute-start(bf16[16,512]{1,0:T(8,128)(2,1)} %hidden_far.1), channel_id=1, source_target_pairs={{0,2},{1,3},{2,0},{3,1},{4,6},{5,7},{6,4},{7,5},{8,10},{9,11},{10,... | collective-permute-start | bytes 49160 | tf_op jit(solution)/shard_map/ppermute | solution.py:739
  3.6 1.9 %collective-permute-start = (bf16[16,512]{1,0:T(8,128)(2,1)}, bf16[16,512]{1,0:T(8,128)(2,1)S(1)}, u32[]{:S(2)}, u32[]{:S(2)}) collective-permute-start(bf16[16,512]{1,0:T(8,128)(2,1)} %hidden_far.1), channel_id=1, source_target_pairs={{0,1},{1,0},{2,3},{3,2},{4,5},{5,4},{6,7},{7,6},{8,9},{9,8},{10,11... | collective-permute-start | bytes 49160 | tf_op jit(solution)/shard_map/ppermute | solution.py:739
  3.6 3.4 %collective-permute-start.2 = (bf16[16,512]{1,0:T(8,128)(2,1)}, bf16[16,512]{1,0:T(8,128)(2,1)S(1)}, u32[]{:S(2)}, u32[]{:S(2)}) collective-permute-start(bf16[16,512]{1,0:T(8,128)(2,1)} %hidden_far.1), channel_id=1, source_target_pairs={{0,3},{1,2},{2,1},{3,0},{4,7},{5,6},{6,5},{7,4},{8,11},{9,10},{10,... | collective-permute-start | bytes 49160 | tf_op jit(solution)/shard_map/ppermute | solution.py:739
  8.9 13.6 %all-to-all-start = ((f32[32,8,128]{2,1,0:T(8,128)}), f32[32,8,128]{2,1,0:T(8,128)S(1)}, u32[]{:S(2)}, u32[]{:S(2)}) async-start(f32[32,8,128]{2,1,0:T(8,128)} %get-tuple-element.23), calls=%async_computation | async-start | bytes 262144 | tf_op jit(solution)/shard_map/all_to_all | solution.py:808
  14.0 8.5 %collective-permute-start.4 = (bf16[160,512]{1,0:T(8,128)(2,1)}, bf16[160,512]{1,0:T(8,128)(2,1)S(1)}, u32[]{:S(2)}, u32[]{:S(2)}) collective-permute-start(bf16[160,512]{1,0:T(8,128)(2,1)} %param.24), channel_id=1, source_target_pairs={{0,4},{1,12},{2,20},{3,28},{4,0},{5,8},{6,16},{7,24},{8,5},{9,13},... | collective-permute-start | bytes 491528 | tf_op jit(solution)/shard_map/ppermute | solution.py:755
  15.9 6.7 %collective-permute-start.3 = (bf16[160,512]{1,0:T(8,128)(2,1)}, bf16[160,512]{1,0:T(8,128)(2,1)S(1)}, u32[]{:S(2)}, u32[]{:S(2)}) collective-permute-start(bf16[160,512]{1,0:T(8,128)(2,1)} %param.24), channel_id=1, source_target_pairs={{0,0},{1,8},{2,16},{3,24},{4,4},{5,12},{6,20},{7,28},{8,1},{9,9},{... | collective-permute-start | bytes 491528 | tf_op jit(solution)/shard_map/ppermute | solution.py:755
  23.6 42.9 %copy-start = (bf16[640,512]{1,0:T(8,128)(2,1)S(1)}, bf16[640,512]{1,0:T(8,128)(2,1)}, u32[]{:S(2)}) copy-start(bf16[640,512]{1,0:T(8,128)(2,1)} %weight.1) | copy-start | bytes 1966084
  23.7 22.6 %collective-permute-start.5 = (bf16[256,1280]{1,0:T(8,128)(2,1)S(1)}, bf16[256,1280]{1,0:T(8,128)(2,1)S(1)}, u32[]{:S(2)}, u32[]{:S(2)}) collective-permute-start(bf16[256,1280]{1,0:T(8,128)(2,1)S(1)} %get-tuple-element.30), channel_id=1, source_target_pairs={{0,1},{1,0},{2,3},{3,2},{4,5},{5,4},{6,7},{7,6},{8,9},{9,8},{10,11... | collective-permute-start | bytes 1966088 | tf_op jit(solution)/shard_map/ppermute | solution.py:739
  47.3 3.2 %collective-permute-start.8 = (f32[16,256]{1,0:T(8,128)S(1)}, f32[16,256]{1,0:T(8,128)S(1)}, u32[]{:S(2)}, u32[]{:S(2)}) collective-permute-start(f32[16,256]{1,0:T(8,128)S(1)} %shard_map.196.own), channel_id=1, source_target_pairs={{0,3},{1,2},{2,1},{3,0},{4,7},{5,6},{6,5},{7,4},{8,11},{9,10},{10,... | collective-permute-start | bytes 49160 | tf_op jit(solution)/shard_map/ppermute | solution.py:739
  47.5 3.7 %collective-permute-start.7 = (f32[16,256]{1,0:T(8,128)S(1)}, f32[16,256]{1,0:T(8,128)S(1)}, u32[]{:S(2)}, u32[]{:S(2)}) collective-permute-start(f32[16,256]{1,0:T(8,128)S(1)} %shard_map.196.own), channel_id=1, source_target_pairs={{0,2},{1,3},{2,0},{3,1},{4,6},{5,7},{6,4},{7,5},{8,10},{9,11},{10,... | collective-permute-start | bytes 49160 | tf_op jit(solution)/shard_map/ppermute | solution.py:739
  49.1 2.1 %collective-permute-start.6 = (f32[16,256]{1,0:T(8,128)S(1)}, f32[16,256]{1,0:T(8,128)S(1)}, u32[]{:S(2)}, u32[]{:S(2)}) collective-permute-start(f32[16,256]{1,0:T(8,128)S(1)} %shard_map.196.own), channel_id=1, source_target_pairs={{0,1},{1,0},{2,3},{3,2},{4,5},{5,4},{6,7},{7,6},{8,9},{9,8},{10,11... | collective-permute-start | bytes 49160 | tf_op jit(solution)/shard_map/ppermute | solution.py:739
  62.7 3.2 %collective-permute-start.11 = (bf16[16,320]{1,0:T(8,128)(2,1)S(1)}, bf16[16,320]{1,0:T(8,128)(2,1)S(1)}, u32[]{:S(2)}, u32[]{:S(2)}) collective-permute-start(bf16[16,320]{1,0:T(8,128)(2,1)S(1)} %shard_map.198.own), channel_id=1, source_target_pairs={{0,3},{1,2},{2,1},{3,0},{4,7},{5,6},{6,5},{7,4},{8,11},{9,10},{10,... | collective-permute-start | bytes 30728 | tf_op jit(solution)/shard_map/ppermute | solution.py:739
  62.8 3.8 %collective-permute-start.10 = (bf16[16,320]{1,0:T(8,128)(2,1)S(1)}, bf16[16,320]{1,0:T(8,128)(2,1)S(1)}, u32[]{:S(2)}, u32[]{:S(2)}) collective-permute-start(bf16[16,320]{1,0:T(8,128)(2,1)S(1)} %shard_map.198.own), channel_id=1, source_target_pairs={{0,2},{1,3},{2,0},{3,1},{4,6},{5,7},{6,4},{7,5},{8,10},{9,11},{10,... | collective-permute-start | bytes 30728 | tf_op jit(solution)/shard_map/ppermute | solution.py:739
  64.4 2.2 %collective-permute-start.9 = (bf16[16,320]{1,0:T(8,128)(2,1)S(1)}, bf16[16,320]{1,0:T(8,128)(2,1)S(1)}, u32[]{:S(2)}, u32[]{:S(2)}) collective-permute-start(bf16[16,320]{1,0:T(8,128)(2,1)S(1)} %shard_map.198.own), channel_id=1, source_target_pairs={{0,1},{1,0},{2,3},{3,2},{4,5},{5,4},{6,7},{7,6},{8,9},{9,8},{10,11... | collective-permute-start | bytes 30728 | tf_op jit(solution)/shard_map/ppermute | solution.py:739

commit v11 on v8

--- a/solution.py
+++ b/solution.py
@@ -339,20 +339,36 @@
 
 
 def first_kernel(
-    source_far, gain_far, weight_far, whole, sent, source, gain, weight, wide, done
+    source_far, gain_far, weight_far, hidden_far, one, two, three, sent, block, source, gain,
+    weight, hidden, lanes_of, wide, done
 ):
-    copies = fetch((source_far, gain_far, weight_far), (source, gain, weight), done)
-    rows = whole.shape[0]
+    copies = fetch(
+        (source_far, gain_far, weight_far, hidden_far), (source, gain, weight, hidden), done
+    )
+    rows = hidden.shape[0]
     groups = rows // R_DEV
     lanes = sent.shape[0] // groups
     columns, features = weight.shape
-    values = whole[...].astype(single)
-    factor = lax.rsqrt(jnp.mean(values * values, axis=1, keepdims=True) + epsilon)
-    here = pl.ds(pl.multiple_of(lax.axis_index("req") * features, features), features)
+    group = lax.axis_index("req")
+    share = groups // lanes
+    squares = 0.0
+    for turn, values in enumerate((one, two, three)):
+        values = values[...].astype(single)
+        lanes_of[turn + 1] = values
+        squares = squares + jnp.sum(values * values, axis=1, keepdims=True)
+    copies[3].wait()
+    values = hidden[...].astype(single)
+    lanes_of[0] = values
+    squares = squares + jnp.sum(values * values, axis=1, keepdims=True)
+    factor = lax.rsqrt(squares / D + epsilon)
+    here = pl.ds(pl.multiple_of(group * features, features), features)
+    within = pl.ds(pl.multiple_of(group % share * features, features), features)
+    mine = lanes_of[group // share ^ lax.axis_index("head"), :, within]
+    block[...] = mine.astype(bfloat)
     wide[...] = jnp.zeros_like(wide)
-    for copy in copies:
+    for copy in copies[:3]:
         copy.wait()
-    normed = (whole[:, here].astype(single) * factor * gain[:, here]).astype(bfloat)
+    normed = (mine * factor * gain[:, here]).astype(bfloat)
     order = row_order(source, rows, True)
     normed = jnp.dot(order, normed, preferred_element_type=single).astype(bfloat)
     wide[:, :columns] = dot_rows(normed, weight[...])
@@ -589,7 +605,7 @@
 
 
 def project_kernel(
-    source_far, own_far, came, one, two, three, sent, source, own, rows, done
+    source_far, own_far, came, one, two, three, kept, given, source, own, rows, blocks, done
 ):
     copies = fetch((source_far, own_far), (source, own), done)
     lanes = lax.axis_size("head")
@@ -615,45 +631,61 @@
     order = row_order(source, requests, False)
     attention = jnp.dot(order, attention.astype(bfloat), preferred_element_type=single)
     attention = attention[:, :features].astype(bfloat)
-    width = sent.shape[2]
-    share = groups // lanes
+    width = kept.shape[2]
+    group = lax.axis_index("req")
     for turn, weight in enumerate((own, one, two, three)):
         projected = jnp.dot(attention, weight[...], preferred_element_type=single)
-        target = (lax.axis_index("head") ^ turn) * share
-        for b in range(share):
-            sent[target + b] = projected[:, width * b : width * (b + 1)].astype(bfloat)
-
-
-def units_kernel(gain_far, came, whole, mine, theirs, sent, mid_out, gain, done):
+        for b in range(2):
+            blocks[b, lax.axis_index("head") ^ turn] = projected[:, width * b : width * (b + 1)]
+    kept[...] = blocks[group & 1]
+    given[...] = blocks[1 - (group & 1)].astype(bfloat)
+
+
+def spread_kernel(kept, came, own, one, two, three, total):
+    total[...] = kept[...] + came[...].astype(single)
+    place = lax.axis_index("req") >> 1
+    own[...] = total[place]
+    for turn, block in enumerate((one, two, three)):
+        block[...] = total[place ^ (turn + 1)].astype(bfloat)
+
+
+def units_kernel(
+    gain_far, own, one, two, three, hidden, mine, theirs, kept, given, mid_out, gain, chunks, done
+):
     (copy,) = fetch((gain_far,), (gain,), done)
-    groups, rows, features = came.shape
-    share = groups // lax.axis_size("head")
+    rows, features = own.shape
     group = lax.axis_index("req")
-    lane = lax.axis_index("head")
     here = pl.ds(pl.multiple_of(group * features, features), features)
-    mid = whole[:, here].astype(single)
-    for g in range(groups):
-        mid = mid + came[g].astype(single)
+    mid = own[...] + one[...].astype(single) + two[...].astype(single)
+    mid = mid + three[...].astype(single) + hidden[...].astype(single)
     mid = mid.astype(bfloat)
     mid_out[...] = mid
     mid = mid.astype(single)
     squares = jnp.sum(mid * mid, axis=1, keepdims=True)
-    block = mine.shape[1] // share
-    terms = three_terms(squares, iota((rows, sent.shape[2] - block), 1)).astype(bfloat)
+    block = mine.shape[1] // 2
+    terms = three_terms(squares, iota((rows, chunks.shape[3] - block), 1))
     copy.wait()
     inputs = (mid * gain[:, here]).astype(bfloat)
     for turn, weight in enumerate((mine, theirs)):
-        units = jnp.dot(inputs, weight[...], preferred_element_type=single).astype(bfloat)
-        target = (lane ^ turn) * share
-        for b in range(share):
-            sent[target + b, :, :block] = units[:, block * b : block * (b + 1)]
-            sent[target + b, :, block:] = terms
-
-
-def active_kernel(came, active):
-    total = came[0].astype(single)
-    for g in range(1, came.shape[0]):
-        total = total + came[g].astype(single)
+        units = jnp.dot(inputs, weight[...], preferred_element_type=single)
+        for b in range(2):
+            chunks[b, turn, :, :block] = units[:, block * b : block * (b + 1)]
+            chunks[b, turn, :, block:] = terms
+    kept[...] = chunks[group & 1]
+    given[...] = chunks[1 - (group & 1)].astype(bfloat)
+
+
+def halves_kernel(kept, came, own, one, two, three, total):
+    total[...] = kept[...] + came[...].astype(single)
+    place = lax.axis_index("req") >> 1 ^ lax.axis_index("head")
+    own[...] = total[place & 1]
+    for turn, block in enumerate((one, two, three)):
+        block[...] = total[(place ^ (turn + 1)) & 1].astype(bfloat)
+
+
+def active_kernel(own, one, two, three, active):
+    total = own[...] + one[...].astype(single)
+    total = total + two[...].astype(single) + three[...].astype(single)
     piece = active.shape[1]
     squares = jnp.sum(total[:, 2 * piece : 2 * piece + 3], axis=1, keepdims=True)
     factor = lax.rsqrt(squares / D + epsilon)
@@ -662,30 +694,35 @@
     active[...] = (gate / (1.0 + jnp.exp(-gate)) * up).astype(bfloat)
 
 
-def down_kernel(active, weight, mid, sent):
-    groups, rows, width = sent.shape
-    lanes, _, piece = active.shape
+def down_kernel(own, one, two, three, weight, mid, sent, active):
+    width = sent.shape[1]
+    piece = own.shape[1]
     half = mid.shape[1]
+    for turn, values in enumerate((own, one, two, three)):
+        active[turn] = values[...]
     share = width // half
     group = lax.axis_index("req")
     lane = lax.axis_index("head")
-    first = group // (2 * share) * 2
+    first = group // (2 * share) * 2 ^ lane
     down = jnp.dot(active[first], weight[:piece, :], preferred_element_type=single)
-    down = down + jnp.dot(active[first + 1], weight[piece:, :], preferred_element_type=single)
+    down = down + jnp.dot(active[first ^ 1], weight[piece:, :], preferred_element_type=single)
     residual = mid[...].astype(single)
     for b in range(share):
         columns = slice(half * b, half * (b + 1))
         mine = group == lane * share + b
-        total = (down[:, columns] + jnp.where(mine, residual, 0.0)).astype(bfloat)
-        for g in range(groups):
-            sent[g, :, columns] = total
-
-
-def result_kernel(came, result):
-    total = came[0].astype(single)
-    for g in range(1, came.shape[0]):
-        total = total + came[g].astype(single)
-    result[...] = total.astype(bfloat)
+        total = down[:, columns] + jnp.where(mine, residual, 0.0)
+        sent[:, columns] = total.astype(bfloat)
+
+
+def pair_kernel(own, came, total):
+    total[...] = (own[...].astype(single) + came[...].astype(single)).astype(bfloat)
+
+
+def result_kernel(own, one, two, three, result, terms):
+    place = lax.axis_index("req") >> 1
+    for turn, values in enumerate((own, one, two, three)):
+        terms[place ^ turn] = values[...].astype(single)
+    result[...] = ((terms[0] + terms[1]) + (terms[2] + terms[3])).astype(bfloat)
 
 
 def rotation_table():
@@ -702,6 +739,22 @@
 def swapped_lanes(value, turn):
     lanes = lax.axis_size("head")
     return lax.ppermute(value, "head", [(k, k ^ turn) for k in range(lanes)])
+
+
+def from_lanes(value):
+    return [value] + [swapped_lanes(value, turn) for turn in range(1, lax.axis_size("head"))]
+
+
+def swapped_y(value):
+    return lax.ppermute(value, "req", [(g, g ^ 1) for g in range(lax.axis_size("req"))])
+
+
+def swapped_z(values):
+    groups = lax.axis_size("req")
+    return [
+        lax.ppermute(value, "req", [(g, g ^ 2 * (k + 1)) for g in range(groups)])
+        for k, value in enumerate(values)
+    ]
 
 
 def on_device(
@@ -731,22 +784,26 @@
     features = D // groups
     copies = pltpu.SemaphoreType.DMA
 
-    whole = lax.all_gather(hidden_in, "head", axis=1, tiled=True)
     columns = input_weight.shape[1]
     padded = -(-columns // TILE) * TILE
     holds = source[None, :]
     gain = attention_gain[None, :]
     weight = input_weight.T
-    (sent,) = run(
+    far = [holds, gain, weight, hidden_in]
+    sent, hidden_block = run(
         first_kernel,
-        [shaped((devices, R_DEV * padded // TILE, TILE), single)],
-        [holds, gain, weight],
-        [whole],
+        [
+            shaped((devices, R_DEV * padded // TILE, TILE), single),
+            shaped((requests, features), bfloat),
+        ],
+        far,
+        from_lanes(hidden_in)[1:],
         [
             *scalar_like(holds),
-            *local_like(gain, weight),
+            *local_like(*far[1:]),
+            pltpu.VMEM((lanes,) + hidden_in.shape, single),
             pltpu.VMEM((requests, padded), single),
-            copies((3,)),
+            copies((len(far),)),
         ],
         2 * requests * features * columns,
     )
@@ -807,46 +864,74 @@
     theirs = swapped_lanes(theirs, 1)
     came = lax.all_to_all(parts, both_axes, 0, 0, tiled=True)
     came, theirs, *others = lax.optimization_barrier((came, theirs, *others))
-    (sent,) = run(
+    places = groups // 2
+    block = shaped((requests, features), single)
+    kept, given = run(
         project_kernel,
-        [shaped((groups, requests, features), bfloat)],
+        [
+            shaped((places, requests, features), single),
+            shaped((places, requests, features), bfloat),
+        ],
         [holds, output_weight],
         [came, *others],
         [
             *scalar_like(holds),
             *local_like(output_weight),
             pltpu.VMEM((requests, 2 * TILE), single),
+            pltpu.VMEM((2, places, requests, features), single),
             copies((2,)),
         ],
         2 * requests * output_weight.size * lanes,
     )
+    own, *sends = run(
+        spread_kernel,
+        [block] + [shaped((requests, features), bfloat)] * 3,
+        [],
+        [kept, swapped_y(given)],
+        local_like(kept),
+    )
     gain = feedforward_gain[None, :]
-    block = gate_weight.shape[1] // 2
-    sent, mid = run(
+    width = gate_weight.shape[1] // 2 + TILE
+    kept, given, mid = run(
         units_kernel,
         [
-            shaped((groups, requests, block + TILE), bfloat),
+            shaped((2, requests, width), single),
+            shaped((2, requests, width), bfloat),
             shaped((requests, features), bfloat),
         ],
         [gain],
-        [exchange(sent), whole, mine, theirs],
-        [*local_like(gain), copies((1,))],
+        [own, *swapped_z(sends), hidden_block, mine, theirs],
+        [*local_like(gain), pltpu.VMEM((2, 2, requests, width), single), copies((1,))],
         4 * requests * gate_weight.size,
     )
+    own, *sends = run(
+        halves_kernel,
+        [shaped((requests, width), single)] + [shaped((requests, width), bfloat)] * 3,
+        [],
+        [kept, swapped_y(given)],
+        local_like(kept),
+    )
     (active,) = run(
-        active_kernel, [shaped((requests, block // 2), bfloat)], [], [exchange(sent)]
-    )
-    active = lax.all_gather(active, "head")
+        active_kernel,
+        [shaped((requests, gate_weight.shape[1] // 4), bfloat)],
+        [],
+        [own, *swapped_z(sends)],
+    )
     (sent,) = run(
         down_kernel,
-        [shaped((groups, requests, down_weight.shape[1]), bfloat)],
+        [shaped((requests, down_weight.shape[1]), bfloat)],
         [],
-        [active, down_weight, mid],
+        [*from_lanes(active), down_weight, mid],
+        [pltpu.VMEM((lanes,) + active.shape, bfloat)],
+        2 * requests * down_weight.size,
+    )
+    (own,) = run(pair_kernel, [shaped(sent.shape, bfloat)], [], [sent, swapped_y(sent)])
+    (result,) = run(
+        result_kernel,
+        [shaped(sent.shape, bfloat)],
         [],
-        2 * requests * down_weight.size,
-    )
-    (result,) = run(
-        result_kernel, [shaped((requests, down_weight.shape[1]), bfloat)], [], [exchange(sent)]
+        [own, *swapped_z([own] * 3)],
+        [pltpu.VMEM((places,) + sent.shape, single)],
     )
     return (compact, summaries, result)
 

time: 75.3 us -> 77.9 us (1.035)
  blocking collectives: 51.1 us -> 9.53 us
  waiting for transfers between devices: 3.71 us -> 27.8 us
  starting transfers between devices: 8.47 us -> 28.6 us
    all_to_all x3 -> x0, blocking collectives: 29.9 us -> none  [exchange(): return lax.all_to_all(parts, 'req', split_axis=0, concat_axis=0, tiled=True)]
    ppermute x0 -> x12, waiting for transfers between devices: none -> 18.9 us  [the longest x9 10 us: swapped_z(): lax.ppermute(value, 'req', [(g, g ^ 2 * (k + 1)) for g in range(groups)])]
    ppermute x0 -> x12, starting transfers between devices: none -> 16.3 us  [the longest x9 13.3 us: swapped_z(): lax.ppermute(value, 'req', [(g, g ^ 2 * (k + 1)) for g in range(groups)])]
    all_gather x2 -> x0, blocking collectives: 11.7 us -> none  [the longest x1 6.43 us: on_device(): whole = lax.all_gather(hidden_in, 'head', axis=1, tiled=True)]
    ppermute x4 -> x10, waiting for transfers between devices: 0.01 us -> 5.21 us  [swapped_lanes(): return lax.ppermute(value, 'head', [(k, k ^ turn) for k in range(lanes)])]
    ppermute x4 -> x10, starting transfers between devices: 2.14 us -> 7.23 us  [swapped_lanes(): return lax.ppermute(value, 'head', [(k, k ^ turn) for k in range(lanes)])]
    all_to_all x1, starting transfers between devices: 6.33 us -> 5.08 us  [on_device(): came = lax.all_to_all(sent, both_axes, 0, 0, tiled=True)]
    pallas_call x8 -> x11, Pallas kernels: 10.8 us -> 10.8 us  [run(): pl.pallas_call(kernel, out_shape=list(outs), in_specs=in_specs, out_specs...]
  transfers between devices with their start and end apart: 5 -> 23, of which waited for: 1 -> 13; matrix products, arithmetic and copies ran while one was open for 0% -> 0% of each run, Pallas kernels for 6% -> 6%
where the time goes in v11:
time: 77.9 us; the launch traced here: 77.6 us
  starting transfers between devices  28.6 us (37%)
  waiting for transfers between devices  27.8 us (36%)
  Pallas kernels  10.8 us (14%)
  blocking collectives  9.53 us (12%)
    ppermute x9, starting transfers between devices, swapped_z(): lax.ppermute(value, 'req', [(g, g ^ 2 * (k + 1)) for g in range(groups)])  13.3 us
    pallas_call x11, Pallas kernels, run(): pl.pallas_call(kernel, out_shape=list(outs), in_specs=in_specs, out_specs...  10.8 us
    ppermute x9, waiting for transfers between devices, swapped_z(): lax.ppermute(value, 'req', [(g, g ^ 2 * (k + 1)) for g in range(groups)])  10 us
    all_to_all x1, blocking collectives, on_device(): came = lax.all_to_all(parts, both_axes, 0, 0, tiled=True)  9.53 us
    ppermute x3, waiting for transfers between devices, swapped_y(): lax.ppermute(value, 'req', [(g, g ^ 1) for g in range(lax.axis_size('req'...  8.89 us
    ppermute x10, starting transfers between devices, swapped_lanes(): return lax.ppermute(value, 'head', [(k, k ^ turn) for k in range(lanes)])  7.23 us
    ppermute x10, waiting for transfers between devices, swapped_lanes(): return lax.ppermute(value, 'head', [(k, k ^ turn) for k in range(lanes)])  5.21 us
    all_to_all x1, starting transfers between devices, on_device(): came = lax.all_to_all(sent, both_axes, 0, 0, tiled=True)  5.08 us
  transfers between devices with their start and end apart: 23, of which 13 were waited for; matrix products, arithmetic and copies ran while one was open for 0% of the time, Pallas kernels for 6%

profile of v11, /device:TPU:0, one launch (start us, length us, event | category | flops | bytes accessed | tf_op | source)
XLA Modules:
  0.0 77.6 jit_solution(11135713676490297557)
XLA Ops:
  1.1 2.6 %collective-permute-start.1 = (bf16[16,512]{1,0:T(8,128)(2,1)}, bf16[16,512]{1,0:T(8,128)(2,1)S(1)}, u32[]{:S(2)}, u32[]{:S(2)}) collective-permute-start(bf16[16,512]{1,0:T(8,128)(2,1)} %hidden_far.1), channel_id=1, source_target_pairs={{0,2},{1,3},{2,0},{3,1},{4,6},{5,7},{6,4},{7,5},{8,10},{9,11},{10,... | collective-permute-start | bytes 49160 | tf_op jit(solution)/shard_map/ppermute | solution.py:741
  3.8 1.9 %collective-permute-done.1.two = bf16[16,512]{1,0:T(8,128)(2,1)S(1)} collective-permute-done((bf16[16,512]{1,0:T(8,128)(2,1)}, bf16[16,512]{1,0:T(8,128)(2,1)S(1)}, u32[]{:S(2)}, u32[]{:S(2)}) %collective-permute-start.1) | collective-permute-done | bytes 16416 | tf_op jit(solution)/shard_map/ppermute | solution.py:741
  5.6 1.4 %collective-permute-done.2.three = bf16[16,512]{1,0:T(8,128)(2,1)S(1)} collective-permute-done((bf16[16,512]{1,0:T(8,128)(2,1)}, bf16[16,512]{1,0:T(8,128)(2,1)S(1)}, u32[]{:S(2)}, u32[]{:S(2)}) %collective-permute-start.2) | collective-permute-done | bytes 16416 | tf_op jit(solution)/shard_map/ppermute | solution.py:741
  7.1 1.9 %shard_map.194 = (f32[32,8,128]{2,1,0:T(8,128)}, bf16[16,256]{1,0:T(8,128)(2,1)S(1)}) custom-call(s32[1,8]{1,0:T(1,128)} %bitcast.10, f32[1,2048]{1,0:T(1,128)} %bitcast.9, bf16[480,256]{1,0:T(8,128)(2,1)} %bitcast.7, bf16[16,512]{1,0:T(8,128)(2,1)} %hidden_far.1, bf16[16,512]{1,0:T(8,128)(2,1)S(1)} %collective-permute-done.one, ...), custom_call_target="tpu_custom_call" | custom-call | flops 3932160 | bytes 458784 | tf_op jit(solution)/shard_map/pallas_call | solution.py:298
  9.0 5.1 %all-to-all-start = ((f32[32,8,128]{2,1,0:T(8,128)}), f32[32,8,128]{2,1,0:T(8,128)S(1)}, u32[]{:S(2)}, u32[]{:S(2)}) async-start(f32[32,8,128]{2,1,0:T(8,128)} %get-tuple-element.34), calls=%async_computation | async-start | bytes 262144 | tf_op jit(solution)/shard_map/all_to_all | solution.py:810
  14.1 4.5 %shard_map.193 = (bf16[4,128,640]{2,1,0:T(8,128)(2,1)}, bf16[8,640]{1,0:T(8,128)(2,1)}, bf16[528,640]{1,0:T(8,128)(2,1)S(1)}, f32[8,640]{1,0:T(8,128)S(1)}, f32[...) custom-call(s32[1,8]{1,0:T(1,128)} %refs_0_.1, s32[1,16]{1,0:T(1,128)} %bitcast.13, ...), custom_call_target="tpu_custom_call" | custom-call | flops 167772160 | bytes 5374720 | tf_op jit(solution)/shard_map/pallas_call | solution.py:298
  18.6 3.7 %all-to-all-done.came = f32[32,8,128]{2,1,0:T(8,128)S(1)} async-done(((f32[32,8,128]{2,1,0:T(8,128)}), f32[32,8,128]{2,1,0:T(8,128)S(1)}, u32[]{:S(2)}, u32[]{:S(2)}) %all-to-all-start) | async-done | bytes 131104 | tf_op jit(solution)/shard_map/all_to_all | solution.py:810
  22.3 1.1 %shard_map.195 = bf16[32,8,128]{2,1,0:T(8,128)(2,1)S(1)} custom-call(f32[32,8,128]{2,1,0:T(8,128)S(1)} %all-to-all-done.came, bf16[528,640]{1,0:T(8,128)(2,1)S(1)} %get-tuple-element.35.kept, f32[8,640]{1,0:T(8,128)S(1)} %get-tuple-element.36.added, f32[96,128]{1,0:T(8,128)S(1)} %get-tuple-element.37.tables), custom_call_target="tpu_custom_call" | custom-call | flops 56623104 | bytes 942080 | tf_op jit(solution)/shard_map/pallas_call | solution.py:298
  24.5 1.1 %collective-permute-start.6 = (bf16[160,512]{1,0:T(8,128)(2,1)S(1)}, bf16[160,512]{1,0:T(8,128)(2,1)S(1)}, u32[]{:S(2)}, u32[]{:S(2)}) collective-permute-start(bf16[160,512]{1,0:T(8,128)(2,1)S(1)} %copy-done.1), channel_id=1, source_target_pairs={{0,3},{1,2},{2,1},{3,0},{4,7},{5,6},{6,5},{7,4},{8,11},{9,10},{10,... | collective-permute-start | bytes 491528 | tf_op jit(solution)/shard_map/ppermute | solution.py:741
  25.6 9.5 %all_to_all.10.came = bf16[32,8,128]{2,1,0:T(8,128)(2,1)S(1)} all-to-all(bf16[32,8,128]{2,1,0:T(8,128)(2,1)S(1)} %shard_map.195), channel_id=1, replica_groups=mesh['req'=8,'head'=4] {'req','head'}, dimensions={0} | all-to-all | bytes 131072 | tf_op jit(solution)/shard_map/all_to_all | solution.py:865
  35.1 1.3 %shard_map.196 = (f32[4,16,256]{2,1,0:T(8,128)S(1)}, bf16[4,16,256]{2,1,0:T(8,128)(2,1)S(1)}) custom-call(s32[1,8]{1,0:T(1,128)} %bitcast.12, bf16[160,512]{1,0:T(8,128)(2,1)} %own_far.1, bf16[32,8,128]{2,1,0:T(8,128)(2,1)S(1)} %all_to_all.10.came, bf16[160,512]{1,0:T(8,128)(2,1)S(1)} %collective-permute-done.4.one, ...), custom_call_target="tpu_custom_call" | custom-call | flops 10485760 | bytes 819232 | tf_op jit(solution)/shard_map/pallas_call | solution.py:298
  37.4 3.1 %collective-permute-done.7.came = bf16[4,16,256]{2,1,0:T(8,128)(2,1)S(1)} collective-permute-done((bf16[4,16,256]{2,1,0:T(8,128)(2,1)S(1)}, bf16[4,16,256]{2,1,0:T(8,128)(2,1)S(1)}, u32[]{:S(2)}, u32[]{:S(2)}) %collective-permute-start.7) | collective-permute-done | bytes 32800 | tf_op jit(solution)/shard_map/ppermute | solution.py:749
  42.0 2.9 %collective-permute-start.10 = (bf16[16,256]{1,0:T(8,128)(2,1)S(1)}, bf16[16,256]{1,0:T(8,128)(2,1)S(1)}, u32[]{:S(2)}, u32[]{:S(2)}) collective-permute-start(bf16[16,256]{1,0:T(8,128)(2,1)S(1)} %get-tuple-element.50), channel_id=1, source_target_pairs={{0,24},{4,28},{8,16},{12,20},{16,8},{20,12},{24,0},{28,4},{1,25},{... | collective-permute-start | bytes 24584 | tf_op jit(solution)/shard_map/ppermute | solution.py:755
  45.7 1.8 %collective-permute-done.10.three = bf16[16,256]{1,0:T(8,128)(2,1)S(1)} collective-permute-done((bf16[16,256]{1,0:T(8,128)(2,1)S(1)}, bf16[16,256]{1,0:T(8,128)(2,1)S(1)}, u32[]{:S(2)}, u32[]{:S(2)}) %collective-permute-start.10) | collective-permute-done | bytes 8224 | tf_op jit(solution)/shard_map/ppermute | solution.py:755
  48.4 1.2 %collective-permute-start.11 = (bf16[2,16,768]{2,1,0:T(8,128)(2,1)S(1)}, bf16[2,16,768]{2,1,0:T(8,128)(2,1)S(1)}, u32[]{:S(2)}, u32[]{:S(2)}) collective-permute-start(bf16[2,16,768]{2,1,0:T(8,128)(2,1)S(1)} %get-tuple-element.55), channel_id=1, source_target_pairs={{0,4},{4,0},{8,12},{12,8},{16,20},{20,16},{24,28},{28,24},{1,5},{5... | collective-permute-start | bytes 147464 | tf_op jit(solution)/shard_map/ppermute | solution.py:749
  49.6 2.9 %collective-permute-done.11.came = bf16[2,16,768]{2,1,0:T(8,128)(2,1)S(1)} collective-permute-done((bf16[2,16,768]{2,1,0:T(8,128)(2,1)S(1)}, bf16[2,16,768]{2,1,0:T(8,128)(2,1)S(1)}, u32[]{:S(2)}, u32[]{:S(2)}) %collective-permute-start.11) | collective-permute-done | bytes 49184 | tf_op jit(solution)/shard_map/ppermute | solution.py:749
  52.7 3.5 %collective-permute-start.13 = (bf16[16,768]{1,0:T(8,128)(2,1)S(1)}, bf16[16,768]{1,0:T(8,128)(2,1)S(1)}, u32[]{:S(2)}, u32[]{:S(2)}) collective-permute-start(bf16[16,768]{1,0:T(8,128)(2,1)S(1)} %get-tuple-element.58), channel_id=1, source_target_pairs={{0,16},{4,20},{8,24},{12,28},{16,0},{20,4},{24,8},{28,12},{1,17},{... | collective-permute-start | bytes 73736 | tf_op jit(solution)/shard_map/ppermute | solution.py:755
  58.0 3.8 %collective-permute-done.14.three = bf16[16,768]{1,0:T(8,128)(2,1)S(1)} collective-permute-done((bf16[16,768]{1,0:T(8,128)(2,1)S(1)}, bf16[16,768]{1,0:T(8,128)(2,1)S(1)}, u32[]{:S(2)}, u32[]{:S(2)}) %collective-permute-start.14) | collective-permute-done | bytes 24608 | tf_op jit(solution)/shard_map/ppermute | solution.py:755
  62.5 1.4 %collective-permute-start.17 = (bf16[16,320]{1,0:T(8,128)(2,1)S(1)}, bf16[16,320]{1,0:T(8,128)(2,1)S(1)}, u32[]{:S(2)}, u32[]{:S(2)}) collective-permute-start(bf16[16,320]{1,0:T(8,128)(2,1)S(1)} %shard_map.200.own), channel_id=1, source_target_pairs={{0,3},{1,2},{2,1},{3,0},{4,7},{5,6},{6,5},{7,4},{8,11},{9,10},{10,... | collective-permute-start | bytes 30728 | tf_op jit(solution)/shard_map/ppermute | solution.py:741
  63.9 1.9 %collective-permute-done.16.two = bf16[16,320]{1,0:T(8,128)(2,1)S(1)} collective-permute-done((bf16[16,320]{1,0:T(8,128)(2,1)S(1)}, bf16[16,320]{1,0:T(8,128)(2,1)S(1)}, u32[]{:S(2)}, u32[]{:S(2)}) %collective-permute-start.16) | collective-permute-done | bytes 10272 | tf_op jit(solution)/shard_map/ppermute | solution.py:741
  66.9 2.9 %collective-permute-done.18.came = bf16[16,512]{1,0:T(8,128)(2,1)S(1)} collective-permute-done((bf16[16,512]{1,0:T(8,128)(2,1)S(1)}, bf16[16,512]{1,0:T(8,128)(2,1)S(1)}, u32[]{:S(2)}, u32[]{:S(2)}) %collective-permute-start.18) | collective-permute-done | bytes 16416 | tf_op jit(solution)/shard_map/ppermute | solution.py:749
  69.8 1.6 %collective-permute-start.20 = (bf16[16,512]{1,0:T(8,128)(2,1)S(1)}, bf16[16,512]{1,0:T(8,128)(2,1)S(1)}, u32[]{:S(2)}, u32[]{:S(2)}) collective-permute-start(bf16[16,512]{1,0:T(8,128)(2,1)S(1)} %shard_map.202.own), channel_id=1, source_target_pairs={{0,16},{4,20},{8,24},{12,28},{16,0},{20,4},{24,8},{28,12},{1,17},{... | collective-permute-start | bytes 49160 | tf_op jit(solution)/shard_map/ppermute | solution.py:755
  71.4 2.8 %collective-permute-start.21 = (bf16[16,512]{1,0:T(8,128)(2,1)S(1)}, bf16[16,512]{1,0:T(8,128)(2,1)S(1)}, u32[]{:S(2)}, u32[]{:S(2)}) collective-permute-start(bf16[16,512]{1,0:T(8,128)(2,1)S(1)} %shard_map.202.own), channel_id=1, source_target_pairs={{0,24},{4,28},{8,16},{12,20},{16,8},{20,12},{24,0},{28,4},{1,25},{... | collective-permute-start | bytes 49160 | tf_op jit(solution)/shard_map/ppermute | solution.py:755
  74.6 2.3 %collective-permute-done.21.three = bf16[16,512]{1,0:T(8,128)(2,1)S(1)} collective-permute-done((bf16[16,512]{1,0:T(8,128)(2,1)S(1)}, bf16[16,512]{1,0:T(8,128)(2,1)S(1)}, u32[]{:S(2)}, u32[]{:S(2)}) %collective-permute-start.21) | collective-permute-done | bytes 16416 | tf_op jit(solution)/shard_map/ppermute | solution.py:755
  (38 shorter events, 10.7 us)
Async XLA Ops:
  0.6 3.2 %collective-permute-start = (bf16[16,512]{1,0:T(8,128)(2,1)}, bf16[16,512]{1,0:T(8,128)(2,1)S(1)}, u32[]{:S(2)}, u32[]{:S(2)}) collective-permute-start(bf16[16,512]{1,0:T(8,128)(2,1)} %hidden_far.1), channel_id=1, source_target_pairs={{0,1},{1,0},{2,3},{3,2},{4,5},{5,4},{6,7},{7,6},{8,9},{9,8},{10,11... | collective-permute-start | bytes 49160 | tf_op jit(solution)/shard_map/ppermute | solution.py:741
  1.1 4.5 %collective-permute-start.1 = (bf16[16,512]{1,0:T(8,128)(2,1)}, bf16[16,512]{1,0:T(8,128)(2,1)S(1)}, u32[]{:S(2)}, u32[]{:S(2)}) collective-permute-start(bf16[16,512]{1,0:T(8,128)(2,1)} %hidden_far.1), channel_id=1, source_target_pairs={{0,2},{1,3},{2,0},{3,1},{4,6},{5,7},{6,4},{7,5},{8,10},{9,11},{10,... | collective-permute-start | bytes 49160 | tf_op jit(solution)/shard_map/ppermute | solution.py:741
  3.7 3.4 %collective-permute-start.2 = (bf16[16,512]{1,0:T(8,128)(2,1)}, bf16[16,512]{1,0:T(8,128)(2,1)S(1)}, u32[]{:S(2)}, u32[]{:S(2)}) collective-permute-start(bf16[16,512]{1,0:T(8,128)(2,1)} %hidden_far.1), channel_id=1, source_target_pairs={{0,3},{1,2},{2,1},{3,0},{4,7},{5,6},{6,5},{7,4},{8,11},{9,10},{10,... | collective-permute-start | bytes 49160 | tf_op jit(solution)/shard_map/ppermute | solution.py:741
  9.0 13.3 %all-to-all-start = ((f32[32,8,128]{2,1,0:T(8,128)}), f32[32,8,128]{2,1,0:T(8,128)S(1)}, u32[]{:S(2)}, u32[]{:S(2)}) async-start(f32[32,8,128]{2,1,0:T(8,128)} %get-tuple-element.34), calls=%async_computation | async-start | bytes 262144 | tf_op jit(solution)/shard_map/all_to_all | solution.py:810
  23.4 42.4 %copy-start = (bf16[640,512]{1,0:T(8,128)(2,1)S(1)}, bf16[640,512]{1,0:T(8,128)(2,1)}, u32[]{:S(2)}) copy-start(bf16[640,512]{1,0:T(8,128)(2,1)} %weight.1) | copy-start | bytes 1966084
  23.4 11.7 %collective-permute-start.3 = (bf16[256,1280]{1,0:T(8,128)(2,1)S(1)}, bf16[256,1280]{1,0:T(8,128)(2,1)S(1)}, u32[]{:S(2)}, u32[]{:S(2)}) collective-permute-start(bf16[256,1280]{1,0:T(8,128)(2,1)S(1)} %get-tuple-element.39), channel_id=1, source_target_pairs={{0,1},{1,0},{2,3},{3,2},{4,5},{5,4},{6,7},{7,6},{8,9},{9,8},{10,11... | collective-permute-start | bytes 1966088 | tf_op jit(solution)/shard_map/ppermute | solution.py:741
  23.7 11.4 %collective-permute-start.4 = (bf16[160,512]{1,0:T(8,128)(2,1)S(1)}, bf16[160,512]{1,0:T(8,128)(2,1)S(1)}, u32[]{:S(2)}, u32[]{:S(2)}) collective-permute-start(bf16[160,512]{1,0:T(8,128)(2,1)S(1)} %copy-done.1), channel_id=1, source_target_pairs={{0,1},{1,0},{2,3},{3,2},{4,5},{5,4},{6,7},{7,6},{8,9},{9,8},{10,11... | collective-permute-start | bytes 491528 | tf_op jit(solution)/shard_map/ppermute | solution.py:741
  24.0 11.1 %collective-permute-start.5 = (bf16[160,512]{1,0:T(8,128)(2,1)S(1)}, bf16[160,512]{1,0:T(8,128)(2,1)S(1)}, u32[]{:S(2)}, u32[]{:S(2)}) collective-permute-start(bf16[160,512]{1,0:T(8,128)(2,1)S(1)} %copy-done.1), channel_id=1, source_target_pairs={{0,2},{1,3},{2,0},{3,1},{4,6},{5,7},{6,4},{7,5},{8,10},{9,11},{10,... | collective-permute-start | bytes 491528 | tf_op jit(solution)/shard_map/ppermute | solution.py:741
  24.5 10.7 %collective-permute-start.6 = (bf16[160,512]{1,0:T(8,128)(2,1)S(1)}, bf16[160,512]{1,0:T(8,128)(2,1)S(1)}, u32[]{:S(2)}, u32[]{:S(2)}) collective-permute-start(bf16[160,512]{1,0:T(8,128)(2,1)S(1)} %copy-done.1), channel_id=1, source_target_pairs={{0,3},{1,2},{2,1},{3,0},{4,7},{5,6},{6,5},{7,4},{8,11},{9,10},{10,... | collective-permute-start | bytes 491528 | tf_op jit(solution)/shard_map/ppermute | solution.py:741
  36.4 4.0 %collective-permute-start.7 = (bf16[4,16,256]{2,1,0:T(8,128)(2,1)S(1)}, bf16[4,16,256]{2,1,0:T(8,128)(2,1)S(1)}, u32[]{:S(2)}, u32[]{:S(2)}) collective-permute-start(bf16[4,16,256]{2,1,0:T(8,128)(2,1)S(1)} %get-tuple-element.46), channel_id=1, source_target_pairs={{0,4},{4,0},{8,12},{12,8},{16,20},{20,16},{24,28},{28,24},{1,5},{5... | collective-permute-start | bytes 98312 | tf_op jit(solution)/shard_map/ppermute | solution.py:749
  40.4 4.5 %collective-permute-start.8 = (bf16[16,256]{1,0:T(8,128)(2,1)S(1)}, bf16[16,256]{1,0:T(8,128)(2,1)S(1)}, u32[]{:S(2)}, u32[]{:S(2)}) collective-permute-start(bf16[16,256]{1,0:T(8,128)(2,1)S(1)} %get-tuple-element.48), channel_id=1, source_target_pairs={{0,8},{4,12},{8,0},{12,4},{16,24},{20,28},{24,16},{28,20},{1,9},{5... | collective-permute-start | bytes 24584 | tf_op jit(solution)/shard_map/ppermute | solution.py:755
  41.1 4.5 %collective-permute-start.9 = (bf16[16,256]{1,0:T(8,128)(2,1)S(1)}, bf16[16,256]{1,0:T(8,128)(2,1)S(1)}, u32[]{:S(2)}, u32[]{:S(2)}) collective-permute-start(bf16[16,256]{1,0:T(8,128)(2,1)S(1)} %get-tuple-element.49), channel_id=1, source_target_pairs={{0,16},{4,20},{8,24},{12,28},{16,0},{20,4},{24,8},{28,12},{1,17},{... | collective-permute-start | bytes 24584 | tf_op jit(solution)/shard_map/ppermute | solution.py:755
  42.0 5.4 %collective-permute-start.10 = (bf16[16,256]{1,0:T(8,128)(2,1)S(1)}, bf16[16,256]{1,0:T(8,128)(2,1)S(1)}, u32[]{:S(2)}, u32[]{:S(2)}) collective-permute-start(bf16[16,256]{1,0:T(8,128)(2,1)S(1)} %get-tuple-element.50), channel_id=1, source_target_pairs={{0,24},{4,28},{8,16},{12,20},{16,8},{20,12},{24,0},{28,4},{1,25},{... | collective-permute-start | bytes 24584 | tf_op jit(solution)/shard_map/ppermute | solution.py:755
  48.4 4.2 %collective-permute-start.11 = (bf16[2,16,768]{2,1,0:T(8,128)(2,1)S(1)}, bf16[2,16,768]{2,1,0:T(8,128)(2,1)S(1)}, u32[]{:S(2)}, u32[]{:S(2)}) collective-permute-start(bf16[2,16,768]{2,1,0:T(8,128)(2,1)S(1)} %get-tuple-element.55), channel_id=1, source_target_pairs={{0,4},{4,0},{8,12},{12,8},{16,20},{20,16},{24,28},{28,24},{1,5},{5... | collective-permute-start | bytes 147464 | tf_op jit(solution)/shard_map/ppermute | solution.py:749
  52.6 4.5 %collective-permute-start.12 = (bf16[16,768]{1,0:T(8,128)(2,1)S(1)}, bf16[16,768]{1,0:T(8,128)(2,1)S(1)}, u32[]{:S(2)}, u32[]{:S(2)}) collective-permute-start(bf16[16,768]{1,0:T(8,128)(2,1)S(1)} %get-tuple-element.57), channel_id=1, source_target_pairs={{0,8},{4,12},{8,0},{12,4},{16,24},{20,28},{24,16},{28,20},{1,9},{5... | collective-permute-start | bytes 73736 | tf_op jit(solution)/shard_map/ppermute | solution.py:755
  52.7 5.3 %collective-permute-start.13 = (bf16[16,768]{1,0:T(8,128)(2,1)S(1)}, bf16[16,768]{1,0:T(8,128)(2,1)S(1)}, u32[]{:S(2)}, u32[]{:S(2)}) collective-permute-start(bf16[16,768]{1,0:T(8,128)(2,1)S(1)} %get-tuple-element.58), channel_id=1, source_target_pairs={{0,16},{4,20},{8,24},{12,28},{16,0},{20,4},{24,8},{28,12},{1,17},{... | collective-permute-start | bytes 73736 | tf_op jit(solution)/shard_map/ppermute | solution.py:755
  56.2 5.6 %collective-permute-start.14 = (bf16[16,768]{1,0:T(8,128)(2,1)S(1)}, bf16[16,768]{1,0:T(8,128)(2,1)S(1)}, u32[]{:S(2)}, u32[]{:S(2)}) collective-permute-start(bf16[16,768]{1,0:T(8,128)(2,1)S(1)} %get-tuple-element.59), channel_id=1, source_target_pairs={{0,24},{4,28},{8,16},{12,20},{16,8},{20,12},{24,0},{28,4},{1,25},{... | collective-permute-start | bytes 73736 | tf_op jit(solution)/shard_map/ppermute | solution.py:755
  62.0 1.9 %collective-permute-start.15 = (bf16[16,320]{1,0:T(8,128)(2,1)S(1)}, bf16[16,320]{1,0:T(8,128)(2,1)S(1)}, u32[]{:S(2)}, u32[]{:S(2)}) collective-permute-start(bf16[16,320]{1,0:T(8,128)(2,1)S(1)} %shard_map.200.own), channel_id=1, source_target_pairs={{0,1},{1,0},{2,3},{3,2},{4,5},{5,4},{6,7},{7,6},{8,9},{9,8},{10,11... | collective-permute-start | bytes 30728 | tf_op jit(solution)/shard_map/ppermute | solution.py:741
  62.0 3.8 %collective-permute-start.16 = (bf16[16,320]{1,0:T(8,128)(2,1)S(1)}, bf16[16,320]{1,0:T(8,128)(2,1)S(1)}, u32[]{:S(2)}, u32[]{:S(2)}) collective-permute-start(bf16[16,320]{1,0:T(8,128)(2,1)S(1)} %shard_map.200.own), channel_id=1, source_target_pairs={{0,2},{1,3},{2,0},{3,1},{4,6},{5,7},{6,4},{7,5},{8,10},{9,11},{10,... | collective-permute-start | bytes 30728 | tf_op jit(solution)/shard_map/ppermute | solution.py:741
  62.5 3.3 %collective-permute-start.17 = (bf16[16,320]{1,0:T(8,128)(2,1)S(1)}, bf16[16,320]{1,0:T(8,128)(2,1)S(1)}, u32[]{:S(2)}, u32[]{:S(2)}) collective-permute-start(bf16[16,320]{1,0:T(8,128)(2,1)S(1)} %shard_map.200.own), channel_id=1, source_target_pairs={{0,3},{1,2},{2,1},{3,0},{4,7},{5,6},{6,5},{7,4},{8,11},{9,10},{10,... | collective-permute-start | bytes 30728 | tf_op jit(solution)/shard_map/ppermute | solution.py:741
  66.0 3.8 %collective-permute-start.18 = (bf16[16,512]{1,0:T(8,128)(2,1)S(1)}, bf16[16,512]{1,0:T(8,128)(2,1)S(1)}, u32[]{:S(2)}, u32[]{:S(2)}) collective-permute-start(bf16[16,512]{1,0:T(8,128)(2,1)S(1)} %shard_map.201.own), channel_id=1, source_target_pairs={{0,4},{4,0},{8,12},{12,8},{16,20},{20,16},{24,28},{28,24},{1,5},{5... | collective-permute-start | bytes 49160 | tf_op jit(solution)/shard_map/ppermute | solution.py:749
  69.8 4.4 %collective-permute-start.19 = (bf16[16,512]{1,0:T(8,128)(2,1)S(1)}, bf16[16,512]{1,0:T(8,128)(2,1)S(1)}, u32[]{:S(2)}, u32[]{:S(2)}) collective-permute-start(bf16[16,512]{1,0:T(8,128)(2,1)S(1)} %shard_map.202.own), channel_id=1, source_target_pairs={{0,8},{4,12},{8,0},{12,4},{16,24},{20,28},{24,16},{28,20},{1,9},{5... | collective-permute-start | bytes 49160 | tf_op jit(solution)/shard_map/ppermute | solution.py:755
  69.8 4.8 %collective-permute-start.20 = (bf16[16,512]{1,0:T(8,128)(2,1)S(1)}, bf16[16,512]{1,0:T(8,128)(2,1)S(1)}, u32[]{:S(2)}, u32[]{:S(2)}) collective-permute-start(bf16[16,512]{1,0:T(8,128)(2,1)S(1)} %shard_map.202.own), channel_id=1, source_target_pairs={{0,16},{4,20},{8,24},{12,28},{16,0},{20,4},{24,8},{28,12},{1,17},{... | collective-permute-start | bytes 49160 | tf_op jit(solution)/shard_map/ppermute | solution.py:755
  71.4 5.5 %collective-permute-start.21 = (bf16[16,512]{1,0:T(8,128)(2,1)S(1)}, bf16[16,512]{1,0:T(8,128)(2,1)S(1)}, u32[]{:S(2)}, u32[]{:S(2)}) collective-permute-start(bf16[16,512]{1,0:T(8,128)(2,1)S(1)} %shard_map.202.own), channel_id=1, source_target_pairs={{0,24},{4,28},{8,16},{12,20},{16,8},{20,12},{24,0},{28,4},{1,25},{... | collective-permute-start | bytes 49160 | tf_op jit(solution)/shard_map/ppermute | solution.py:755
  (1 other events, 9.6 us)

commit v12 on v10

--- a/solution.py
+++ b/solution.py
@@ -608,6 +608,15 @@
         tile = jnp.concatenate(tile, axis=0).astype(bfloat)
         for g in range(groups):
             sent[g * lanes + k] = tile
+
+
+def blocks_kernel(weight_far, same, other, done):
+    width = same.shape[1]
+    group = lax.axis_index("req")
+    starts = [pl.multiple_of(((group & 1) ^ turn) * width, width) for turn in range(2)]
+    parts = [weight_far.at[:, pl.ds(start, width)] for start in starts]
+    for copy in fetch(parts, (same, other), done):
+        copy.wait()
 
 
 def project_kernel(source_far, came, first, second, sent, source, logs, rows, pieces, done):
@@ -649,11 +658,9 @@
     for b in range(2):
         pieces[b] = attention[:, features * b : features * (b + 1)]
     total = 0.0
-    width = sent.shape[1]
-    columns = pl.ds(pl.multiple_of((group & 1) * width, width), width)
     for turn, weight in enumerate((first, second)):
         piece = pieces[(group & 1) ^ turn].astype(bfloat)
-        total = total + jnp.dot(piece, weight[:, columns], preferred_element_type=single)
+        total = total + jnp.dot(piece, weight[...], preferred_element_type=single)
     sent[...] = total
 
 
@@ -806,8 +813,14 @@
         2 * requests * features * columns,
     )
     came = lax.all_to_all(sent, both_axes, 0, 0, tiled=True)
-    output_weights, _ = lax.optimization_barrier((output_weight, sent))
-    handed = [handed_over(output_weights, turn) for turn in range(2)]
+    blocks = run(
+        blocks_kernel,
+        [shaped((output_weight.shape[0], features), bfloat)] * 2,
+        [output_weight],
+        [],
+        [copies((2,))],
+    )
+    handed = [handed_over(block, turn) for turn, block in enumerate(blocks)]
 
     scalars = [dest_slots, lengths[None, :], holds, page_table]
     arrays = [

time: 78.4 us -> 73.4 us (0.936)
  blocking collectives: 40.5 us -> 36.3 us
  starting transfers between devices: 18.5 us -> 17 us
  Pallas kernels: 10.5 us -> 11.4 us
    all_to_all x1, blocking collectives: 19.7 us -> 15.5 us  [on_device(): came = lax.all_to_all(parts, both_axes, 0, 0, tiled=True)]
    pallas_call x8 -> x9, Pallas kernels: 10.5 us -> 11.4 us  [run(): pl.pallas_call(kernel, out_shape=list(outs), in_specs=in_specs, out_specs...]
    ppermute x2, starting transfers between devices: 3.4 us -> 2.5 us  [handed_over(): return lax.ppermute(value, both_axes, pairs)]
  transfers between devices with their start and end apart: 13 -> 13, of which waited for: 7 -> 7; matrix products, arithmetic and copies ran while one was open for 0% -> 0% of each run, Pallas kernels for 6% -> 7%
where the time goes in v12:
time: 73.4 us; the launch traced here: 72.9 us
  blocking collectives  36.3 us (49%)
  starting transfers between devices  17 us (23%)
  Pallas kernels  11.4 us (16%)
  waiting for transfers between devices  7.37 us (10%)
  between operations  0.74 us (1%)
    all_to_all x2, blocking collectives, exchange(): return lax.all_to_all(parts, 'req', split_axis=0, concat_axis=0, tiled=True)  20.9 us
    all_to_all x1, blocking collectives, on_device(): came = lax.all_to_all(parts, both_axes, 0, 0, tiled=True)  15.5 us
    pallas_call x9, Pallas kernels, run(): pl.pallas_call(kernel, out_shape=list(outs), in_specs=in_specs, out_specs...  11.4 us
    ppermute x10, starting transfers between devices, swapped_lanes(): return lax.ppermute(value, 'head', [(k, k ^ turn) for k in range(lanes)])  9.45 us
    ppermute x10, waiting for transfers between devices, swapped_lanes(): return lax.ppermute(value, 'head', [(k, k ^ turn) for k in range(lanes)])  7.08 us
    all_to_all x1, starting transfers between devices, on_device(): came = lax.all_to_all(sent, both_axes, 0, 0, tiled=True)  5.08 us
    ppermute x2, starting transfers between devices, handed_over(): return lax.ppermute(value, both_axes, pairs)  2.5 us
  transfers between devices with their start and end apart: 13, of which 7 were waited for; matrix products, arithmetic and copies ran while one was open for 0% of the time, Pallas kernels for 7%

profile of v12, /device:TPU:0, one launch (start us, length us, event | category | flops | bytes accessed | tf_op | source)
XLA Modules:
  0.0 72.9 jit_solution(12795129280821510435)
XLA Ops:
  0.6 3.0 %collective-permute-start.1 = (bf16[16,512]{1,0:T(8,128)(2,1)}, bf16[16,512]{1,0:T(8,128)(2,1)S(1)}, u32[]{:S(2)}, u32[]{:S(2)}) collective-permute-start(bf16[16,512]{1,0:T(8,128)(2,1)} %hidden_far.1), channel_id=1, source_target_pairs={{0,2},{1,3},{2,0},{3,1},{4,6},{5,7},{6,4},{7,5},{8,10},{9,11},{10,... | collective-permute-start | bytes 49160 | tf_op jit(solution)/shard_map/ppermute | solution.py:746
  3.8 1.7 %collective-permute-done.1.two = bf16[16,512]{1,0:T(8,128)(2,1)S(1)} collective-permute-done((bf16[16,512]{1,0:T(8,128)(2,1)}, bf16[16,512]{1,0:T(8,128)(2,1)S(1)}, u32[]{:S(2)}, u32[]{:S(2)}) %collective-permute-start.1) | collective-permute-done | bytes 16416 | tf_op jit(solution)/shard_map/ppermute | solution.py:746
  5.6 1.4 %collective-permute-done.2.three = bf16[16,512]{1,0:T(8,128)(2,1)S(1)} collective-permute-done((bf16[16,512]{1,0:T(8,128)(2,1)}, bf16[16,512]{1,0:T(8,128)(2,1)S(1)}, u32[]{:S(2)}, u32[]{:S(2)}) %collective-permute-start.2) | collective-permute-done | bytes 16416 | tf_op jit(solution)/shard_map/ppermute | solution.py:746
  7.0 1.9 %shard_map.194 = (f32[32,8,128]{2,1,0:T(8,128)}, bf16[16,256]{1,0:T(8,128)(2,1)S(1)}) custom-call(s32[1,8]{1,0:T(1,128)} %bitcast.10, f32[1,2048]{1,0:T(1,128)} %bitcast.9, bf16[480,256]{1,0:T(8,128)(2,1)} %bitcast.7, bf16[16,512]{1,0:T(8,128)(2,1)} %hidden_far.1, bf16[16,512]{1,0:T(8,128)(2,1)S(1)} %collective-permute-done.one, ...), custom_call_target="tpu_custom_call" | custom-call | flops 3932160 | bytes 458784 | tf_op jit(solution)/shard_map/pallas_call | solution.py:298
  9.0 5.1 %all-to-all-start = ((f32[32,8,128]{2,1,0:T(8,128)}), f32[32,8,128]{2,1,0:T(8,128)S(1)}, u32[]{:S(2)}, u32[]{:S(2)}) async-start(f32[32,8,128]{2,1,0:T(8,128)} %get-tuple-element.24), calls=%async_computation | async-start | bytes 262144 | tf_op jit(solution)/shard_map/all_to_all | solution.py:815
  14.1 1.0 %shard_map.195 = (bf16[160,256]{1,0:T(8,128)(2,1)S(1)}, bf16[160,256]{1,0:T(8,128)(2,1)S(1)}) custom-call(bf16[160,512]{1,0:T(8,128)(2,1)} %weight_far.1), custom_call_target="tpu_custom_call" | custom-call | bytes 327680 | tf_op jit(solution)/shard_map/pallas_call | solution.py:298
  15.0 0.7 collective-permute-start.3
  15.7 1.8 %collective-permute-start.4 = (bf16[160,256]{1,0:T(8,128)(2,1)S(1)}, bf16[160,256]{1,0:T(8,128)(2,1)S(1)}, u32[]{:S(2)}, u32[]{:S(2)}) collective-permute-start(bf16[160,256]{1,0:T(8,128)(2,1)S(1)} %get-tuple-element.26), channel_id=1, source_target_pairs={{0,4},{1,12},{2,20},{3,28},{4,0},{5,8},{6,16},{7,24},{8,5},{9,13},... | collective-permute-start | bytes 245768 | tf_op jit(solution)/shard_map/ppermute | solution.py:762
  17.5 4.4 %shard_map.193 = (bf16[4,128,640]{2,1,0:T(8,128)(2,1)}, bf16[8,640]{1,0:T(8,128)(2,1)}, bf16[528,640]{1,0:T(8,128)(2,1)S(1)}, f32[8,640]{1,0:T(8,128)S(1)}, f32[...) custom-call(s32[1,8]{1,0:T(1,128)} %refs_0_.1, s32[1,16]{1,0:T(1,128)} %bitcast.13, ...), custom_call_target="tpu_custom_call" | custom-call | flops 167772160 | bytes 5374720 | tf_op jit(solution)/shard_map/pallas_call | solution.py:298
  22.0 0.3 all-to-all-done.came
  22.3 1.1 %shard_map.196 = bf16[32,8,128]{2,1,0:T(8,128)(2,1)S(1)} custom-call(f32[32,8,128]{2,1,0:T(8,128)S(1)} %all-to-all-done.came, bf16[528,640]{1,0:T(8,128)(2,1)S(1)} %get-tuple-element.28.kept, f32[8,640]{1,0:T(8,128)S(1)} %get-tuple-element.29.added, f32[96,128]{1,0:T(8,128)S(1)} %get-tuple-element.30.tables), custom_call_target="tpu_custom_call" | custom-call | flops 56623104 | bytes 942080 | tf_op jit(solution)/shard_map/pallas_call | solution.py:298
  23.4 2.4 %collective-permute-start.5 = (bf16[256,1280]{1,0:T(8,128)(2,1)S(1)}, bf16[256,1280]{1,0:T(8,128)(2,1)S(1)}, u32[]{:S(2)}, u32[]{:S(2)}) collective-permute-start(bf16[256,1280]{1,0:T(8,128)(2,1)S(1)} %get-tuple-element.32), channel_id=1, source_target_pairs={{0,1},{1,0},{2,3},{3,2},{4,5},{5,4},{6,7},{7,6},{8,9},{9,8},{10,11... | collective-permute-start | bytes 1966088 | tf_op jit(solution)/shard_map/ppermute | solution.py:746
  25.8 15.5 %all_to_all.20.came = bf16[32,8,128]{2,1,0:T(8,128)(2,1)S(1)} all-to-all(bf16[32,8,128]{2,1,0:T(8,128)(2,1)S(1)} %shard_map.196), channel_id=1, replica_groups=mesh['req'=8,'head'=4] {'req','head'}, dimensions={0} | all-to-all | bytes 131072 | tf_op jit(solution)/shard_map/all_to_all | solution.py:879
  41.2 1.0 %shard_map.197.own = f32[16,256]{1,0:T(8,128)S(1)} custom-call(s32[1,8]{1,0:T(1,128)} %bitcast.12, bf16[32,8,128]{2,1,0:T(8,128)(2,1)S(1)} %all_to_all.20.came, bf16[160,256]{1,0:T(8,128)(2,1)S(1)} %collective-permute-done.3.first, bf16[160,256]{1,0:T(8,128)(2,1)S(1)} %collective-permute-done.4.second), custom_call_target="tpu_custom_call" | custom-call | flops 2621440 | bytes 245792 | tf_op jit(solution)/shard_map/pallas_call | solution.py:298
  42.4 1.6 %collective-permute-start.7 = (f32[16,256]{1,0:T(8,128)S(1)}, f32[16,256]{1,0:T(8,128)S(1)}, u32[]{:S(2)}, u32[]{:S(2)}) collective-permute-start(f32[16,256]{1,0:T(8,128)S(1)} %shard_map.197.own), channel_id=1, source_target_pairs={{0,2},{1,3},{2,0},{3,1},{4,6},{5,7},{6,4},{7,5},{8,10},{9,11},{10,... | collective-permute-start | bytes 49160 | tf_op jit(solution)/shard_map/ppermute | solution.py:746
  44.2 1.3 %collective-permute-done.8.three = f32[16,256]{1,0:T(8,128)S(1)} collective-permute-done((f32[16,256]{1,0:T(8,128)S(1)}, f32[16,256]{1,0:T(8,128)S(1)}, u32[]{:S(2)}, u32[]{:S(2)}) %collective-permute-start.8) | collective-permute-done | bytes 16416 | tf_op jit(solution)/shard_map/ppermute | solution.py:746
  45.4 0.7 collective-permute-done.7.two
  46.2 1.0 %shard_map.198 = (bf16[8,16,768]{2,1,0:T(8,128)(2,1)S(1)}, bf16[16,256]{1,0:T(8,128)(2,1)S(1)}) custom-call(f32[1,2048]{1,0:T(1,128)} %bitcast.8, f32[16,256]{1,0:T(8,128)S(1)} %shard_map.197.own, f32[16,256]{1,0:T(8,128)S(1)} %collective-permute-done.6.one, f32[16,256]{1,0:T(8,128)S(1)} %collective-permute-done.7.two, ...), custom_call_target="tpu_custom_call" | custom-call | flops 20971520 | bytes 1597440 | tf_op jit(solution)/shard_map/pallas_call | solution.py:298
  47.2 10.3 %all_to_all.21.came = bf16[8,16,768]{2,1,0:T(8,128)(2,1)S(1)} all-to-all(bf16[8,16,768]{2,1,0:T(8,128)(2,1)S(1)} %get-tuple-element.39), channel_id=1, replica_groups=mesh['req'=8,'head'=4] {'req'}, dimensions={0} | all-to-all | bytes 393216 | tf_op jit(solution)/shard_map/all_to_all | solution.py:84
  57.7 1.6 %collective-permute-start.10 = (bf16[16,320]{1,0:T(8,128)(2,1)S(1)}, bf16[16,320]{1,0:T(8,128)(2,1)S(1)}, u32[]{:S(2)}, u32[]{:S(2)}) collective-permute-start(bf16[16,320]{1,0:T(8,128)(2,1)S(1)} %shard_map.199.own), channel_id=1, source_target_pairs={{0,2},{1,3},{2,0},{3,1},{4,6},{5,7},{6,4},{7,5},{8,10},{9,11},{10,... | collective-permute-start | bytes 30728 | tf_op jit(solution)/shard_map/ppermute | solution.py:746
  59.5 1.3 %collective-permute-done.11.three = bf16[16,320]{1,0:T(8,128)(2,1)S(1)} collective-permute-done((bf16[16,320]{1,0:T(8,128)(2,1)S(1)}, bf16[16,320]{1,0:T(8,128)(2,1)S(1)}, u32[]{:S(2)}, u32[]{:S(2)}) %collective-permute-start.11) | collective-permute-done | bytes 10272 | tf_op jit(solution)/shard_map/ppermute | solution.py:746
  60.8 0.6 collective-permute-done.10.two
  61.7 10.6 %all_to_all.22.came = bf16[8,16,512]{2,1,0:T(8,128)(2,1)S(1)} all-to-all(bf16[8,16,512]{2,1,0:T(8,128)(2,1)S(1)} %shard_map.200), channel_id=1, replica_groups=mesh['req'=8,'head'=4] {'req'}, dimensions={0} | all-to-all | bytes 262144 | tf_op jit(solution)/shard_map/all_to_all | solution.py:84
  72.3 0.6 shard_map.201
  (16 shorter events, 1.3 us)
Async XLA Ops:
  0.6 4.9 %collective-permute-start.1 = (bf16[16,512]{1,0:T(8,128)(2,1)}, bf16[16,512]{1,0:T(8,128)(2,1)S(1)}, u32[]{:S(2)}, u32[]{:S(2)}) collective-permute-start(bf16[16,512]{1,0:T(8,128)(2,1)} %hidden_far.1), channel_id=1, source_target_pairs={{0,2},{1,3},{2,0},{3,1},{4,6},{5,7},{6,4},{7,5},{8,10},{9,11},{10,... | collective-permute-start | bytes 49160 | tf_op jit(solution)/shard_map/ppermute | solution.py:746
  3.6 1.9 %collective-permute-start = (bf16[16,512]{1,0:T(8,128)(2,1)}, bf16[16,512]{1,0:T(8,128)(2,1)S(1)}, u32[]{:S(2)}, u32[]{:S(2)}) collective-permute-start(bf16[16,512]{1,0:T(8,128)(2,1)} %hidden_far.1), channel_id=1, source_target_pairs={{0,1},{1,0},{2,3},{3,2},{4,5},{5,4},{6,7},{7,6},{8,9},{9,8},{10,11... | collective-permute-start | bytes 49160 | tf_op jit(solution)/shard_map/ppermute | solution.py:746
  3.6 3.4 %collective-permute-start.2 = (bf16[16,512]{1,0:T(8,128)(2,1)}, bf16[16,512]{1,0:T(8,128)(2,1)S(1)}, u32[]{:S(2)}, u32[]{:S(2)}) collective-permute-start(bf16[16,512]{1,0:T(8,128)(2,1)} %hidden_far.1), channel_id=1, source_target_pairs={{0,3},{1,2},{2,1},{3,0},{4,7},{5,6},{6,5},{7,4},{8,11},{9,10},{10,... | collective-permute-start | bytes 49160 | tf_op jit(solution)/shard_map/ppermute | solution.py:746
  9.0 13.3 %all-to-all-start = ((f32[32,8,128]{2,1,0:T(8,128)}), f32[32,8,128]{2,1,0:T(8,128)S(1)}, u32[]{:S(2)}, u32[]{:S(2)}) async-start(f32[32,8,128]{2,1,0:T(8,128)} %get-tuple-element.24), calls=%async_computation | async-start | bytes 262144 | tf_op jit(solution)/shard_map/all_to_all | solution.py:815
  15.0 7.0 %collective-permute-start.3 = (bf16[160,256]{1,0:T(8,128)(2,1)S(1)}, bf16[160,256]{1,0:T(8,128)(2,1)S(1)}, u32[]{:S(2)}, u32[]{:S(2)}) collective-permute-start(bf16[160,256]{1,0:T(8,128)(2,1)S(1)} %get-tuple-element.25), channel_id=1, source_target_pairs={{0,0},{1,8},{2,16},{3,24},{4,4},{5,12},{6,20},{7,28},{8,1},{9,9},{... | collective-permute-start | bytes 245768 | tf_op jit(solution)/shard_map/ppermute | solution.py:762
  15.7 6.3 %collective-permute-start.4 = (bf16[160,256]{1,0:T(8,128)(2,1)S(1)}, bf16[160,256]{1,0:T(8,128)(2,1)S(1)}, u32[]{:S(2)}, u32[]{:S(2)}) collective-permute-start(bf16[160,256]{1,0:T(8,128)(2,1)S(1)} %get-tuple-element.26), channel_id=1, source_target_pairs={{0,4},{1,12},{2,20},{3,28},{4,0},{5,8},{6,16},{7,24},{8,5},{9,13},... | collective-permute-start | bytes 245768 | tf_op jit(solution)/shard_map/ppermute | solution.py:762
  23.4 38.1 %copy-start = (bf16[640,512]{1,0:T(8,128)(2,1)S(1)}, bf16[640,512]{1,0:T(8,128)(2,1)}, u32[]{:S(2)}) copy-start(bf16[640,512]{1,0:T(8,128)(2,1)} %weight.1) | copy-start | bytes 1966084
  23.4 17.8 %collective-permute-start.5 = (bf16[256,1280]{1,0:T(8,128)(2,1)S(1)}, bf16[256,1280]{1,0:T(8,128)(2,1)S(1)}, u32[]{:S(2)}, u32[]{:S(2)}) collective-permute-start(bf16[256,1280]{1,0:T(8,128)(2,1)S(1)} %get-tuple-element.32), channel_id=1, source_target_pairs={{0,1},{1,0},{2,3},{3,2},{4,5},{5,4},{6,7},{7,6},{8,9},{9,8},{10,11... | collective-permute-start | bytes 1966088 | tf_op jit(solution)/shard_map/ppermute | solution.py:746
  42.2 3.2 %collective-permute-start.8 = (f32[16,256]{1,0:T(8,128)S(1)}, f32[16,256]{1,0:T(8,128)S(1)}, u32[]{:S(2)}, u32[]{:S(2)}) collective-permute-start(f32[16,256]{1,0:T(8,128)S(1)} %shard_map.197.own), channel_id=1, source_target_pairs={{0,3},{1,2},{2,1},{3,0},{4,7},{5,6},{6,5},{7,4},{8,11},{9,10},{10,... | collective-permute-start | bytes 49160 | tf_op jit(solution)/shard_map/ppermute | solution.py:746
  42.4 3.7 %collective-permute-start.7 = (f32[16,256]{1,0:T(8,128)S(1)}, f32[16,256]{1,0:T(8,128)S(1)}, u32[]{:S(2)}, u32[]{:S(2)}) collective-permute-start(f32[16,256]{1,0:T(8,128)S(1)} %shard_map.197.own), channel_id=1, source_target_pairs={{0,2},{1,3},{2,0},{3,1},{4,6},{5,7},{6,4},{7,5},{8,10},{9,11},{10,... | collective-permute-start | bytes 49160 | tf_op jit(solution)/shard_map/ppermute | solution.py:746
  44.0 2.1 %collective-permute-start.6 = (f32[16,256]{1,0:T(8,128)S(1)}, f32[16,256]{1,0:T(8,128)S(1)}, u32[]{:S(2)}, u32[]{:S(2)}) collective-permute-start(f32[16,256]{1,0:T(8,128)S(1)} %shard_map.197.own), channel_id=1, source_target_pairs={{0,1},{1,0},{2,3},{3,2},{4,5},{5,4},{6,7},{7,6},{8,9},{9,8},{10,11... | collective-permute-start | bytes 49160 | tf_op jit(solution)/shard_map/ppermute | solution.py:746
  57.6 3.2 %collective-permute-start.11 = (bf16[16,320]{1,0:T(8,128)(2,1)S(1)}, bf16[16,320]{1,0:T(8,128)(2,1)S(1)}, u32[]{:S(2)}, u32[]{:S(2)}) collective-permute-start(bf16[16,320]{1,0:T(8,128)(2,1)S(1)} %shard_map.199.own), channel_id=1, source_target_pairs={{0,3},{1,2},{2,1},{3,0},{4,7},{5,6},{6,5},{7,4},{8,11},{9,10},{10,... | collective-permute-start | bytes 30728 | tf_op jit(solution)/shard_map/ppermute | solution.py:746
  57.7 3.8 %collective-permute-start.10 = (bf16[16,320]{1,0:T(8,128)(2,1)S(1)}, bf16[16,320]{1,0:T(8,128)(2,1)S(1)}, u32[]{:S(2)}, u32[]{:S(2)}) collective-permute-start(bf16[16,320]{1,0:T(8,128)(2,1)S(1)} %shard_map.199.own), channel_id=1, source_target_pairs={{0,2},{1,3},{2,0},{3,1},{4,6},{5,7},{6,4},{7,5},{8,10},{9,11},{10,... | collective-permute-start | bytes 30728 | tf_op jit(solution)/shard_map/ppermute | solution.py:746
  59.3 2.2 %collective-permute-start.9 = (bf16[16,320]{1,0:T(8,128)(2,1)S(1)}, bf16[16,320]{1,0:T(8,128)(2,1)S(1)}, u32[]{:S(2)}, u32[]{:S(2)}) collective-permute-start(bf16[16,320]{1,0:T(8,128)(2,1)S(1)} %shard_map.199.own), channel_id=1, source_target_pairs={{0,1},{1,0},{2,3},{3,2},{4,5},{5,4},{6,7},{7,6},{8,9},{9,8},{10,11... | collective-permute-start | bytes 30728 | tf_op jit(solution)/shard_map/ppermute | solution.py:746

commit v13 on v12

--- a/solution.py
+++ b/solution.py
@@ -444,7 +444,7 @@
     ]
     weight_columns = weights[...].T
     rows_of = iota((rows, KEEP), 0)
-    place = iota((rows, KEEP), 1)
+    place = iota((rows, 16), 1)
     copies[9].wait()
     for p in range(count):
         picks = (keep[p : p + 1, :] == rows_of).astype(single)
@@ -789,30 +789,7 @@
     features = D // groups
     copies = pltpu.SemaphoreType.DMA
 
-    columns = input_weight.shape[1]
-    padded = -(-columns // TILE) * TILE
-    holds = source[None, :]
-    gain = attention_gain[None, :]
-    weight = input_weight.T
-    far = [holds, gain, weight, hidden_in]
-    sent, hidden_block = run(
-        first_kernel,
-        [
-            shaped((devices, R_DEV * padded // TILE, TILE), single),
-            shaped((requests, features), bfloat),
-        ],
-        far,
-        from_lanes(hidden_in)[1:],
-        [
-            *scalar_like(holds),
-            *local_like(*far[1:]),
-            pltpu.VMEM((lanes,) + hidden_in.shape, single),
-            pltpu.VMEM((requests, padded), single),
-            copies((len(far),)),
-        ],
-        2 * requests * features * columns,
-    )
-    came = lax.all_to_all(sent, both_axes, 0, 0, tiled=True)
+    others = from_lanes(hidden_in)[1:]
     blocks = run(
         blocks_kernel,
         [shaped((output_weight.shape[0], features), bfloat)] * 2,
@@ -821,8 +798,7 @@
         [copies((2,))],
     )
     handed = [handed_over(block, turn) for turn, block in enumerate(blocks)]
-
-    scalars = [dest_slots, lengths[None, :], holds, page_table]
+    scalars = [dest_slots, lengths[None, :], source[None, :], page_table]
     arrays = [
         keep_rows,
         drop_weights,
@@ -858,7 +834,36 @@
         ],
         2 * pages_here * TILE * PAGE * KVW,
     )
-    came, *handed = lax.optimization_barrier((came, *handed))
+    tables, *moved = lax.optimization_barrier((tables, *others, *handed))
+    others, handed = moved[: lanes - 1], moved[lanes - 1 :]
+
+    holds = source[None, :]
+    columns = input_weight.shape[1]
+    padded = -(-columns // TILE) * TILE
+    gain = attention_gain[None, :]
+    weight = input_weight.T
+    far = [holds, gain, weight, hidden_in]
+    sent, hidden_block = run(
+        first_kernel,
+        [
+            shaped((devices, R_DEV * padded // TILE, TILE), single),
+            shaped((requests, features), bfloat),
+        ],
+        far,
+        others,
+        [
+            *scalar_like(holds),
+            *local_like(*far[1:]),
+            pltpu.VMEM((lanes,) + hidden_in.shape, single),
+            pltpu.VMEM((requests, padded), single),
+            copies((len(far),)),
+        ],
+        2 * requests * features * columns,
+    )
+    came = lax.all_to_all(sent, both_axes, 0, 0, tiled=True)
+    theirs, _ = lax.optimization_barrier((theirs, sent))
+    theirs = swapped_lanes(theirs, 1)
+    came, theirs = lax.optimization_barrier((came, theirs))
     span = -(-KVH * HD // TILE) * TILE
     (parts,) = run(
         attend_kernel,
@@ -874,10 +879,7 @@
         ],
         6 * 48 * entries * span,
     )
-    theirs, _ = lax.optimization_barrier((theirs, parts))
-    theirs = swapped_lanes(theirs, 1)
     came = lax.all_to_all(parts, both_axes, 0, 0, tiled=True)
-    came, theirs = lax.optimization_barrier((came, theirs))
     (sent,) = run(
         project_kernel,
         [shaped((requests, features), single)],

time: 73.4 us -> 72.9 us (level)
  blocking collectives: 36.3 us -> 42.9 us
  waiting for transfers between devices: 7.37 us -> 3.93 us
  starting transfers between devices: 17 us -> 14.2 us
  Pallas kernels: 11.4 us -> 10.6 us
    all_to_all x0 -> x1, blocking collectives: none -> 12.8 us  [on_device(): came = lax.all_to_all(sent, both_axes, 0, 0, tiled=True)]
    all_to_all x1, blocking collectives: 15.5 us -> 9.24 us  [on_device(): came = lax.all_to_all(parts, both_axes, 0, 0, tiled=True)]
    all_to_all x1 -> x0, starting transfers between devices: 5.08 us -> none  [on_device(): came = lax.all_to_all(sent, both_axes, 0, 0, tiled=True)]
    ppermute x10, waiting for transfers between devices: 7.08 us -> 3.92 us  [swapped_lanes(): return lax.ppermute(value, 'head', [(k, k ^ turn) for k in range(lanes)])]
    ppermute x2, starting transfers between devices: 2.5 us -> 3.7 us  [handed_over(): return lax.ppermute(value, both_axes, pairs)]
    ppermute x10, starting transfers between devices: 9.45 us -> 10.5 us  [swapped_lanes(): return lax.ppermute(value, 'head', [(k, k ^ turn) for k in range(lanes)])]
    pallas_call x9, Pallas kernels: 11.4 us -> 10.6 us  [run(): pl.pallas_call(kernel, out_shape=list(outs), in_specs=in_specs, out_specs...]
  transfers between devices with their start and end apart: 13 -> 12, of which waited for: 7 -> 4; matrix products, arithmetic and copies ran while one was open for 0% -> 0% of each run, Pallas kernels for 7% -> 6%
where the time goes in v13:
time: 72.9 us; the launch traced here: 72.5 us
  blocking collectives  42.9 us (59%)
  starting transfers between devices  14.2 us (19%)
  Pallas kernels  10.6 us (15%)
  waiting for transfers between devices  3.93 us (5%)
  between operations  0.76 us (1%)
    all_to_all x2, blocking collectives, exchange(): return lax.all_to_all(parts, 'req', split_axis=0, concat_axis=0, tiled=True)  20.9 us
    all_to_all x1, blocking collectives, on_device(): came = lax.all_to_all(sent, both_axes, 0, 0, tiled=True)  12.8 us
    pallas_call x9, Pallas kernels, run(): pl.pallas_call(kernel, out_shape=list(outs), in_specs=in_specs, out_specs...  10.6 us
    ppermute x10, starting transfers between devices, swapped_lanes(): return lax.ppermute(value, 'head', [(k, k ^ turn) for k in range(lanes)])  10.5 us
    all_to_all x1, blocking collectives, on_device(): came = lax.all_to_all(parts, both_axes, 0, 0, tiled=True)  9.24 us
    ppermute x10, waiting for transfers between devices, swapped_lanes(): return lax.ppermute(value, 'head', [(k, k ^ turn) for k in range(lanes)])  3.92 us
    ppermute x2, starting transfers between devices, handed_over(): return lax.ppermute(value, both_axes, pairs)  3.7 us
  transfers between devices with their start and end apart: 12, of which 4 were waited for; matrix products, arithmetic and copies ran while one was open for 0% of the time, Pallas kernels for 6%

profile of v13, /device:TPU:0, one launch (start us, length us, event | category | flops | bytes accessed | tf_op | source)
XLA Modules:
  0.0 72.5 jit_solution(5659773911852603904)
XLA Ops:
  0.6 1.0 %shard_map.194 = (bf16[160,256]{1,0:T(8,128)(2,1)S(1)}, bf16[160,256]{1,0:T(8,128)(2,1)S(1)}) custom-call(bf16[160,512]{1,0:T(8,128)(2,1)} %weight_far.1), custom_call_target="tpu_custom_call" | custom-call | bytes 327680 | tf_op jit(solution)/shard_map/pallas_call | solution.py:298
  1.6 0.7 collective-permute-start.3
  2.3 3.0 %collective-permute-start.4 = (bf16[160,256]{1,0:T(8,128)(2,1)S(1)}, bf16[160,256]{1,0:T(8,128)(2,1)S(1)}, u32[]{:S(2)}, u32[]{:S(2)}) collective-permute-start(bf16[160,256]{1,0:T(8,128)(2,1)S(1)} %get-tuple-element.29), channel_id=1, source_target_pairs={{0,4},{1,12},{2,20},{3,28},{4,0},{5,8},{6,16},{7,24},{8,5},{9,13},... | collective-permute-start | bytes 245768 | tf_op jit(solution)/shard_map/ppermute | solution.py:762
  5.3 6.0 %collective-permute-start.1 = (bf16[16,512]{1,0:T(8,128)(2,1)}, bf16[16,512]{1,0:T(8,128)(2,1)S(1)}, u32[]{:S(2)}, u32[]{:S(2)}) collective-permute-start(bf16[16,512]{1,0:T(8,128)(2,1)} %hidden_far.1), channel_id=1, source_target_pairs={{0,2},{1,3},{2,0},{3,1},{4,6},{5,7},{6,4},{7,5},{8,10},{9,11},{10,... | collective-permute-start | bytes 49160 | tf_op jit(solution)/shard_map/ppermute | solution.py:746
  11.5 4.3 %shard_map.193 = (bf16[4,128,640]{2,1,0:T(8,128)(2,1)}, bf16[8,640]{1,0:T(8,128)(2,1)}, bf16[528,640]{1,0:T(8,128)(2,1)S(1)}, f32[8,640]{1,0:T(8,128)S(1)}, f32[...) custom-call(s32[1,8]{1,0:T(1,128)} %refs_0_.1, s32[1,16]{1,0:T(1,128)} %bitcast.13, ...), custom_call_target="tpu_custom_call" | custom-call | flops 167772160 | bytes 5374720 | tf_op jit(solution)/shard_map/pallas_call | solution.py:298
  15.9 1.3 %shard_map.195 = (f32[32,8,128]{2,1,0:T(8,128)S(1)}, bf16[16,256]{1,0:T(8,128)(2,1)S(1)}) custom-call(s32[1,8]{1,0:T(1,128)} %bitcast.11, f32[1,2048]{1,0:T(1,128)} %bitcast.9, bf16[480,256]{1,0:T(8,128)(2,1)} %bitcast.7, bf16[16,512]{1,0:T(8,128)(2,1)} %hidden_far.1, bf16[16,512]{1,0:T(8,128)(2,1)S(1)} %collective-permute-done.one, ...), custom_call_target="tpu_custom_call" | custom-call | flops 3932160 | bytes 458784 | tf_op jit(solution)/shard_map/pallas_call | solution.py:298
  17.1 0.5 collective-permute-start.5
  17.6 12.8 %all_to_all.20.came = f32[32,8,128]{2,1,0:T(8,128)S(1)} all-to-all(f32[32,8,128]{2,1,0:T(8,128)S(1)} %get-tuple-element.33), channel_id=1, replica_groups=mesh['req'=8,'head'=4] {'req','head'}, dimensions={0} | all-to-all | bytes 262144 | tf_op jit(solution)/shard_map/all_to_all | solution.py:863
  30.4 1.1 %shard_map.196 = bf16[32,8,128]{2,1,0:T(8,128)(2,1)S(1)} custom-call(f32[32,8,128]{2,1,0:T(8,128)S(1)} %all_to_all.20.came, bf16[528,640]{1,0:T(8,128)(2,1)S(1)} %get-tuple-element.37.kept, f32[8,640]{1,0:T(8,128)S(1)} %get-tuple-element.38.added, f32[96,128]{1,0:T(8,128)S(1)} %get-tuple-element.39.tables), custom_call_target="tpu_custom_call" | custom-call | flops 56623104 | bytes 942080 | tf_op jit(solution)/shard_map/pallas_call | solution.py:298
  31.5 9.2 %all_to_all.21.came = bf16[32,8,128]{2,1,0:T(8,128)(2,1)S(1)} all-to-all(bf16[32,8,128]{2,1,0:T(8,128)(2,1)S(1)} %shard_map.196), channel_id=1, replica_groups=mesh['req'=8,'head'=4] {'req','head'}, dimensions={0} | all-to-all | bytes 131072 | tf_op jit(solution)/shard_map/all_to_all | solution.py:882
  40.8 1.0 %shard_map.197.own = f32[16,256]{1,0:T(8,128)S(1)} custom-call(s32[1,8]{1,0:T(1,128)} %bitcast.12, bf16[32,8,128]{2,1,0:T(8,128)(2,1)S(1)} %all_to_all.21.came, bf16[160,256]{1,0:T(8,128)(2,1)S(1)} %collective-permute-done.3.first, bf16[160,256]{1,0:T(8,128)(2,1)S(1)} %collective-permute-done.4.second), custom_call_target="tpu_custom_call" | custom-call | flops 2621440 | bytes 245792 | tf_op jit(solution)/shard_map/pallas_call | solution.py:298
  41.8 0.2 collective-permute-start.8
  42.0 1.6 %collective-permute-start.7 = (f32[16,256]{1,0:T(8,128)S(1)}, f32[16,256]{1,0:T(8,128)S(1)}, u32[]{:S(2)}, u32[]{:S(2)}) collective-permute-start(f32[16,256]{1,0:T(8,128)S(1)} %shard_map.197.own), channel_id=1, source_target_pairs={{0,2},{1,3},{2,0},{3,1},{4,6},{5,7},{6,4},{7,5},{8,10},{9,11},{10,... | collective-permute-start | bytes 49160 | tf_op jit(solution)/shard_map/ppermute | solution.py:746
  43.7 1.3 %collective-permute-done.8.three = f32[16,256]{1,0:T(8,128)S(1)} collective-permute-done((f32[16,256]{1,0:T(8,128)S(1)}, f32[16,256]{1,0:T(8,128)S(1)}, u32[]{:S(2)}, u32[]{:S(2)}) %collective-permute-start.8) | collective-permute-done | bytes 16416 | tf_op jit(solution)/shard_map/ppermute | solution.py:746
  45.0 0.7 %collective-permute-done.7.two = f32[16,256]{1,0:T(8,128)S(1)} collective-permute-done((f32[16,256]{1,0:T(8,128)S(1)}, f32[16,256]{1,0:T(8,128)S(1)}, u32[]{:S(2)}, u32[]{:S(2)}) %collective-permute-start.7) | collective-permute-done | bytes 16416 | tf_op jit(solution)/shard_map/ppermute | solution.py:746
  45.7 1.0 %shard_map.198 = (bf16[8,16,768]{2,1,0:T(8,128)(2,1)S(1)}, bf16[16,256]{1,0:T(8,128)(2,1)S(1)}) custom-call(f32[1,2048]{1,0:T(1,128)} %bitcast.8, f32[16,256]{1,0:T(8,128)S(1)} %shard_map.197.own, f32[16,256]{1,0:T(8,128)S(1)} %collective-permute-done.6.one, f32[16,256]{1,0:T(8,128)S(1)} %collective-permute-done.7.two, ...), custom_call_target="tpu_custom_call" | custom-call | flops 20971520 | bytes 1597440 | tf_op jit(solution)/shard_map/pallas_call | solution.py:298
  46.7 10.3 %all_to_all.22.came = bf16[8,16,768]{2,1,0:T(8,128)(2,1)S(1)} all-to-all(bf16[8,16,768]{2,1,0:T(8,128)(2,1)S(1)} %get-tuple-element.45), channel_id=1, replica_groups=mesh['req'=8,'head'=4] {'req'}, dimensions={0} | all-to-all | bytes 393216 | tf_op jit(solution)/shard_map/all_to_all | solution.py:84
  57.2 1.6 %collective-permute-start.10 = (bf16[16,320]{1,0:T(8,128)(2,1)S(1)}, bf16[16,320]{1,0:T(8,128)(2,1)S(1)}, u32[]{:S(2)}, u32[]{:S(2)}) collective-permute-start(bf16[16,320]{1,0:T(8,128)(2,1)S(1)} %shard_map.199.own), channel_id=1, source_target_pairs={{0,2},{1,3},{2,0},{3,1},{4,6},{5,7},{6,4},{7,5},{8,10},{9,11},{10,... | collective-permute-start | bytes 30728 | tf_op jit(solution)/shard_map/ppermute | solution.py:746
  58.8 0.3 collective-permute-start.9
  59.1 1.3 %collective-permute-done.11.three = bf16[16,320]{1,0:T(8,128)(2,1)S(1)} collective-permute-done((bf16[16,320]{1,0:T(8,128)(2,1)S(1)}, bf16[16,320]{1,0:T(8,128)(2,1)S(1)}, u32[]{:S(2)}, u32[]{:S(2)}) %collective-permute-start.11) | collective-permute-done | bytes 10272 | tf_op jit(solution)/shard_map/ppermute | solution.py:746
  60.4 0.6 collective-permute-done.10.two
  61.0 0.2 shard_map.200
  61.2 10.6 %all_to_all.23.came = bf16[8,16,512]{2,1,0:T(8,128)(2,1)S(1)} all-to-all(bf16[8,16,512]{2,1,0:T(8,128)(2,1)S(1)} %shard_map.200), channel_id=1, replica_groups=mesh['req'=8,'head'=4] {'req'}, dimensions={0} | all-to-all | bytes 262144 | tf_op jit(solution)/shard_map/all_to_all | solution.py:84
  71.8 0.6 shard_map.201
  (15 shorter events, 0.6 us)
Async XLA Ops:
  1.6 14.2 %collective-permute-start.3 = (bf16[160,256]{1,0:T(8,128)(2,1)S(1)}, bf16[160,256]{1,0:T(8,128)(2,1)S(1)}, u32[]{:S(2)}, u32[]{:S(2)}) collective-permute-start(bf16[160,256]{1,0:T(8,128)(2,1)S(1)} %get-tuple-element.28), channel_id=1, source_target_pairs={{0,0},{1,8},{2,16},{3,24},{4,4},{5,12},{6,20},{7,28},{8,1},{9,9},{... | collective-permute-start | bytes 245768 | tf_op jit(solution)/shard_map/ppermute | solution.py:762
  2.3 13.6 %collective-permute-start.4 = (bf16[160,256]{1,0:T(8,128)(2,1)S(1)}, bf16[160,256]{1,0:T(8,128)(2,1)S(1)}, u32[]{:S(2)}, u32[]{:S(2)}) collective-permute-start(bf16[160,256]{1,0:T(8,128)(2,1)S(1)} %get-tuple-element.29), channel_id=1, source_target_pairs={{0,4},{1,12},{2,20},{3,28},{4,0},{5,8},{6,16},{7,24},{8,5},{9,13},... | collective-permute-start | bytes 245768 | tf_op jit(solution)/shard_map/ppermute | solution.py:762
  5.3 10.5 %collective-permute-start.1 = (bf16[16,512]{1,0:T(8,128)(2,1)}, bf16[16,512]{1,0:T(8,128)(2,1)S(1)}, u32[]{:S(2)}, u32[]{:S(2)}) collective-permute-start(bf16[16,512]{1,0:T(8,128)(2,1)} %hidden_far.1), channel_id=1, source_target_pairs={{0,2},{1,3},{2,0},{3,1},{4,6},{5,7},{6,4},{7,5},{8,10},{9,11},{10,... | collective-permute-start | bytes 49160 | tf_op jit(solution)/shard_map/ppermute | solution.py:746
  11.3 4.5 %collective-permute-start = (bf16[16,512]{1,0:T(8,128)(2,1)}, bf16[16,512]{1,0:T(8,128)(2,1)S(1)}, u32[]{:S(2)}, u32[]{:S(2)}) collective-permute-start(bf16[16,512]{1,0:T(8,128)(2,1)} %hidden_far.1), channel_id=1, source_target_pairs={{0,1},{1,0},{2,3},{3,2},{4,5},{5,4},{6,7},{7,6},{8,9},{9,8},{10,11... | collective-permute-start | bytes 49160 | tf_op jit(solution)/shard_map/ppermute | solution.py:746
  11.5 4.4 %collective-permute-start.2 = (bf16[16,512]{1,0:T(8,128)(2,1)}, bf16[16,512]{1,0:T(8,128)(2,1)S(1)}, u32[]{:S(2)}, u32[]{:S(2)}) collective-permute-start(bf16[16,512]{1,0:T(8,128)(2,1)} %hidden_far.1), channel_id=1, source_target_pairs={{0,3},{1,2},{2,1},{3,0},{4,7},{5,6},{6,5},{7,4},{8,11},{9,10},{10,... | collective-permute-start | bytes 49160 | tf_op jit(solution)/shard_map/ppermute | solution.py:746
  17.1 13.3 %collective-permute-start.5 = (bf16[256,1280]{1,0:T(8,128)(2,1)S(1)}, bf16[256,1280]{1,0:T(8,128)(2,1)S(1)}, u32[]{:S(2)}, u32[]{:S(2)}) collective-permute-start(bf16[256,1280]{1,0:T(8,128)(2,1)S(1)} %get-tuple-element.35), channel_id=1, source_target_pairs={{0,1},{1,0},{2,3},{3,2},{4,5},{5,4},{6,7},{7,6},{8,9},{9,8},{10,11... | collective-permute-start | bytes 1966088 | tf_op jit(solution)/shard_map/ppermute | solution.py:746
  31.5 29.5 %copy-start = (bf16[640,512]{1,0:T(8,128)(2,1)S(1)}, bf16[640,512]{1,0:T(8,128)(2,1)}, u32[]{:S(2)}) copy-start(bf16[640,512]{1,0:T(8,128)(2,1)} %weight.1) | copy-start | bytes 1966084
  41.8 3.2 %collective-permute-start.8 = (f32[16,256]{1,0:T(8,128)S(1)}, f32[16,256]{1,0:T(8,128)S(1)}, u32[]{:S(2)}, u32[]{:S(2)}) collective-permute-start(f32[16,256]{1,0:T(8,128)S(1)} %shard_map.197.own), channel_id=1, source_target_pairs={{0,3},{1,2},{2,1},{3,0},{4,7},{5,6},{6,5},{7,4},{8,11},{9,10},{10,... | collective-permute-start | bytes 49160 | tf_op jit(solution)/shard_map/ppermute | solution.py:746
  42.0 3.7 %collective-permute-start.7 = (f32[16,256]{1,0:T(8,128)S(1)}, f32[16,256]{1,0:T(8,128)S(1)}, u32[]{:S(2)}, u32[]{:S(2)}) collective-permute-start(f32[16,256]{1,0:T(8,128)S(1)} %shard_map.197.own), channel_id=1, source_target_pairs={{0,2},{1,3},{2,0},{3,1},{4,6},{5,7},{6,4},{7,5},{8,10},{9,11},{10,... | collective-permute-start | bytes 49160 | tf_op jit(solution)/shard_map/ppermute | solution.py:746
  43.6 2.1 %collective-permute-start.6 = (f32[16,256]{1,0:T(8,128)S(1)}, f32[16,256]{1,0:T(8,128)S(1)}, u32[]{:S(2)}, u32[]{:S(2)}) collective-permute-start(f32[16,256]{1,0:T(8,128)S(1)} %shard_map.197.own), channel_id=1, source_target_pairs={{0,1},{1,0},{2,3},{3,2},{4,5},{5,4},{6,7},{7,6},{8,9},{9,8},{10,11... | collective-permute-start | bytes 49160 | tf_op jit(solution)/shard_map/ppermute | solution.py:746
  57.1 3.2 %collective-permute-start.11 = (bf16[16,320]{1,0:T(8,128)(2,1)S(1)}, bf16[16,320]{1,0:T(8,128)(2,1)S(1)}, u32[]{:S(2)}, u32[]{:S(2)}) collective-permute-start(bf16[16,320]{1,0:T(8,128)(2,1)S(1)} %shard_map.199.own), channel_id=1, source_target_pairs={{0,3},{1,2},{2,1},{3,0},{4,7},{5,6},{6,5},{7,4},{8,11},{9,10},{10,... | collective-permute-start | bytes 30728 | tf_op jit(solution)/shard_map/ppermute | solution.py:746
  57.2 3.8 %collective-permute-start.10 = (bf16[16,320]{1,0:T(8,128)(2,1)S(1)}, bf16[16,320]{1,0:T(8,128)(2,1)S(1)}, u32[]{:S(2)}, u32[]{:S(2)}) collective-permute-start(bf16[16,320]{1,0:T(8,128)(2,1)S(1)} %shard_map.199.own), channel_id=1, source_target_pairs={{0,2},{1,3},{2,0},{3,1},{4,6},{5,7},{6,4},{7,5},{8,10},{9,11},{10,... | collective-permute-start | bytes 30728 | tf_op jit(solution)/shard_map/ppermute | solution.py:746
  58.8 2.2 %collective-permute-start.9 = (bf16[16,320]{1,0:T(8,128)(2,1)S(1)}, bf16[16,320]{1,0:T(8,128)(2,1)S(1)}, u32[]{:S(2)}, u32[]{:S(2)}) collective-permute-start(bf16[16,320]{1,0:T(8,128)(2,1)S(1)} %shard_map.199.own), channel_id=1, source_target_pairs={{0,1},{1,0},{2,3},{3,2},{4,5},{5,4},{6,7},{7,6},{8,9},{9,8},{10,11... | collective-permute-start | bytes 30728 | tf_op jit(solution)/shard_map/ppermute | solution.py:746

commit v14 on v10

--- a/solution.py
+++ b/solution.py
@@ -389,8 +389,8 @@
 
 
 def prepare_kernel(*refs):
-    far, refs = refs[:12], refs[12:]
-    (compact, summaries, kept, added, tables, mine, theirs), refs = refs[:7], refs[7:]
+    far, (handed, *refs) = refs[:12], refs[12:]
+    (compact, summaries, kept, added, tables, mine, theirs, given), refs = refs[:8], refs[8:]
     near, (ordered, plain, dealt, done) = refs[:12], refs[12:]
     copies = fetch(far, near, done)
     (dest, lengths, source, table, keep, weights, query_gain, key_gain, turns) = near[:9]
@@ -444,7 +444,7 @@
     ]
     weight_columns = weights[...].T
     rows_of = iota((rows, KEEP), 0)
-    place = iota((rows, KEEP), 1)
+    place = iota((rows, 16), 1)
     copies[9].wait()
     for p in range(count):
         picks = (keep[p : p + 1, :] == rows_of).astype(single)
@@ -487,6 +487,9 @@
             dealt[k, :, start + piece : start + block] = up[:, columns].astype(single)
     mine[...] = dealt[lane & 1].astype(bfloat)
     theirs[...] = dealt[1 - (lane & 1)].astype(bfloat)
+    width = given.shape[1]
+    other = pl.multiple_of((1 - (group & 1)) * width, width)
+    given[...] = handed[:, pl.ds(other, width)]
 
 
 def attend_kernel(came, kept, added, tables, sent, x, extra_k, extra_v, out, logs):
@@ -650,10 +653,10 @@
         pieces[b] = attention[:, features * b : features * (b + 1)]
     total = 0.0
     width = sent.shape[1]
-    columns = pl.ds(pl.multiple_of((group & 1) * width, width), width)
-    for turn, weight in enumerate((first, second)):
+    here = pl.multiple_of((group & 1) * width, width)
+    for turn, weight in enumerate((first[:, pl.ds(here, width)], second[...])):
         piece = pieces[(group & 1) ^ turn].astype(bfloat)
-        total = total + jnp.dot(piece, weight[:, columns], preferred_element_type=single)
+        total = total + jnp.dot(piece, weight, preferred_element_type=single)
     sent[...] = total
 
 
@@ -743,16 +746,19 @@
     return [value] + [swapped_lanes(value, turn) for turn in range(1, lax.axis_size("head"))]
 
 
-def handed_over(value, turn):
+def transposed(value):
     groups = lax.axis_size("req")
     lanes = lax.axis_size("head")
-    share = groups // lanes
     pairs = [
-        (g * lanes + h, (share * h + ((g & 1) ^ turn)) * lanes + g // share)
+        (g * lanes + h, (2 * h + (g & 1)) * lanes + g // 2)
         for g in range(groups)
         for h in range(lanes)
     ]
     return lax.ppermute(value, both_axes, pairs)
+
+
+def swapped_y(value):
+    return lax.ppermute(value, "req", [(g, g ^ 1) for g in range(lax.axis_size("req"))])
 
 
 def on_device(
@@ -782,6 +788,7 @@
     features = D // groups
     copies = pltpu.SemaphoreType.DMA
 
+    handed = transposed(output_weight)
     columns = input_weight.shape[1]
     padded = -(-columns // TILE) * TILE
     holds = source[None, :]
@@ -806,9 +813,7 @@
         2 * requests * features * columns,
     )
     came = lax.all_to_all(sent, both_axes, 0, 0, tiled=True)
-    output_weights, _ = lax.optimization_barrier((output_weight, sent))
-    handed = [handed_over(output_weights, turn) for turn in range(2)]
-
+    handed, _ = lax.optimization_barrier((handed, sent))
     scalars = [dest_slots, lengths[None, :], holds, page_table]
     arrays = [
         keep_rows,
@@ -822,7 +827,7 @@
     ]
     entries = pages_here * KEEP
     extras = 16
-    compact, summaries, kept, added, tables, mine, theirs = run(
+    compact, summaries, kept, added, tables, mine, theirs, given = run(
         prepare_kernel,
         [
             shaped((pages_here // 2, PAGE, KVW), bfloat),
@@ -832,9 +837,10 @@
             shaped((96, TILE), single),
             shaped(gate_weight.shape, bfloat),
             shaped(gate_weight.shape, bfloat),
+            shaped((output_weight.shape[0], features), bfloat),
         ],
         scalars + arrays,
-        [],
+        [handed],
         [
             *scalar_like(*scalars),
             *local_like(*arrays),
@@ -845,7 +851,8 @@
         ],
         2 * pages_here * TILE * PAGE * KVW,
     )
-    came, *handed = lax.optimization_barrier((came, *handed))
+    theirs = swapped_lanes(theirs, 1)
+    came, theirs = lax.optimization_barrier((came, theirs))
     span = -(-KVH * HD // TILE) * TILE
     (parts,) = run(
         attend_kernel,
@@ -861,15 +868,14 @@
         ],
         6 * 48 * entries * span,
     )
-    theirs, _ = lax.optimization_barrier((theirs, parts))
-    theirs = swapped_lanes(theirs, 1)
+    given, _ = lax.optimization_barrier((given, parts))
+    given = swapped_y(given)
     came = lax.all_to_all(parts, both_axes, 0, 0, tiled=True)
-    came, theirs = lax.optimization_barrier((came, theirs))
     (sent,) = run(
         project_kernel,
         [shaped((requests, features), single)],
         [holds],
-        [came, *handed],
+        [came, handed, given],
         [
             *scalar_like(holds),
             pltpu.VMEM((lanes, 2 * groups, TILE), single),

time: 78.4 us -> 76.9 us (0.981)
  waiting for transfers between devices: 7.75 us -> 12.9 us
  blocking collectives: 40.5 us -> 35.6 us
  starting transfers between devices: 18.5 us -> 16.8 us
    all_to_all x1, blocking collectives: 19.7 us -> 14 us  [on_device(): came = lax.all_to_all(sent, both_axes, 0, 0, tiled=True)]
    all_to_all x1, waiting for transfers between devices: 0.01 us -> 2.55 us  [on_device(): came = lax.all_to_all(parts, both_axes, 0, 0, tiled=True)]
    ppermute x2, waiting for transfers between devices: 0.66 us -> 3.14 us  [the longest x1 3.14 us: swapped_y(): lax.ppermute(value, 'req', [(g, g ^ 1) for g in range(lax.axis_size('req'...]
    all_to_all x1, starting transfers between devices: 5.08 us -> 2.7 us  [on_device(): came = lax.all_to_all(parts, both_axes, 0, 0, tiled=True)]
    ppermute x10, starting transfers between devices: 10.1 us -> 10.9 us  [swapped_lanes(): return lax.ppermute(value, 'head', [(k, k ^ turn) for k in range(lanes)])]
  transfers between devices with their start and end apart: 13 -> 13, of which waited for: 7 -> 8; matrix products, arithmetic and copies ran while one was open for 0% -> 0% of each run, Pallas kernels for 6% -> 2%
where the time goes in v14:
time: 76.9 us; the launch traced here: 76.4 us
  blocking collectives  35.6 us (46%)
  starting transfers between devices  16.8 us (22%)
  waiting for transfers between devices  12.9 us (17%)
  Pallas kernels  10.3 us (13%)
    all_to_all x2, blocking collectives, exchange(): return lax.all_to_all(parts, 'req', split_axis=0, concat_axis=0, tiled=True)  21.6 us
    all_to_all x1, blocking collectives, on_device(): came = lax.all_to_all(sent, both_axes, 0, 0, tiled=True)  14 us
    ppermute x10, starting transfers between devices, swapped_lanes(): return lax.ppermute(value, 'head', [(k, k ^ turn) for k in range(lanes)])  10.9 us
    pallas_call x8, Pallas kernels, run(): pl.pallas_call(kernel, out_shape=list(outs), in_specs=in_specs, out_specs...  10.3 us
    ppermute x10, waiting for transfers between devices, swapped_lanes(): return lax.ppermute(value, 'head', [(k, k ^ turn) for k in range(lanes)])  7.25 us
    ppermute x1, waiting for transfers between devices, swapped_y(): lax.ppermute(value, 'req', [(g, g ^ 1) for g in range(lax.axis_size('req'...  3.14 us
    all_to_all x1, starting transfers between devices, on_device(): came = lax.all_to_all(parts, both_axes, 0, 0, tiled=True)  2.7 us
    all_to_all x1, waiting for transfers between devices, on_device(): came = lax.all_to_all(parts, both_axes, 0, 0, tiled=True)  2.55 us
  transfers between devices with their start and end apart: 13, of which 8 were waited for; matrix products, arithmetic and copies ran while one was open for 0% of the time, Pallas kernels for 2%

profile of v14, /device:TPU:0, one launch (start us, length us, event | category | flops | bytes accessed | tf_op | source)
XLA Modules:
  0.0 76.4 jit_solution(7407009080525444079)
XLA Ops:
  0.6 1.6 %collective-permute-start = (bf16[160,512]{1,0:T(8,128)(2,1)}, bf16[160,512]{1,0:T(8,128)(2,1)S(1)}, u32[]{:S(2)}, u32[]{:S(2)}) collective-permute-start(bf16[160,512]{1,0:T(8,128)(2,1)} %param.24), channel_id=1, source_target_pairs={{0,0},{1,8},{2,16},{3,24},{4,4},{5,12},{6,20},{7,28},{8,1},{9,9},{... | collective-permute-start | bytes 491528 | tf_op jit(solution)/shard_map/ppermute | solution.py:757
  2.2 5.9 %collective-permute-start.2 = (bf16[16,512]{1,0:T(8,128)(2,1)}, bf16[16,512]{1,0:T(8,128)(2,1)S(1)}, u32[]{:S(2)}, u32[]{:S(2)}) collective-permute-start(bf16[16,512]{1,0:T(8,128)(2,1)} %hidden_far.1), channel_id=1, source_target_pairs={{0,2},{1,3},{2,0},{3,1},{4,6},{5,7},{6,4},{7,5},{8,10},{9,11},{10,... | collective-permute-start | bytes 49160 | tf_op jit(solution)/shard_map/ppermute | solution.py:742
  8.1 0.8 %collective-permute-start.1 = (bf16[16,512]{1,0:T(8,128)(2,1)}, bf16[16,512]{1,0:T(8,128)(2,1)S(1)}, u32[]{:S(2)}, u32[]{:S(2)}) collective-permute-start(bf16[16,512]{1,0:T(8,128)(2,1)} %hidden_far.1), channel_id=1, source_target_pairs={{0,1},{1,0},{2,3},{3,2},{4,5},{5,4},{6,7},{7,6},{8,9},{9,8},{10,11... | collective-permute-start | bytes 49160 | tf_op jit(solution)/shard_map/ppermute | solution.py:742
  9.0 1.0 %collective-permute-done.2.two = bf16[16,512]{1,0:T(8,128)(2,1)S(1)} collective-permute-done((bf16[16,512]{1,0:T(8,128)(2,1)}, bf16[16,512]{1,0:T(8,128)(2,1)S(1)}, u32[]{:S(2)}, u32[]{:S(2)}) %collective-permute-start.2) | collective-permute-done | bytes 16416 | tf_op jit(solution)/shard_map/ppermute | solution.py:742
  10.0 2.3 %collective-permute-done.3.three = bf16[16,512]{1,0:T(8,128)(2,1)S(1)} collective-permute-done((bf16[16,512]{1,0:T(8,128)(2,1)}, bf16[16,512]{1,0:T(8,128)(2,1)S(1)}, u32[]{:S(2)}, u32[]{:S(2)}) %collective-permute-start.3) | collective-permute-done | bytes 16416 | tf_op jit(solution)/shard_map/ppermute | solution.py:742
  12.3 1.3 %shard_map.193 = (f32[32,8,128]{2,1,0:T(8,128)S(1)}, bf16[16,256]{1,0:T(8,128)(2,1)S(1)}) custom-call(s32[1,8]{1,0:T(1,128)} %bitcast.10, f32[1,2048]{1,0:T(1,128)} %bitcast.9, bf16[480,256]{1,0:T(8,128)(2,1)} %bitcast.7, bf16[16,512]{1,0:T(8,128)(2,1)} %hidden_far.1, bf16[16,512]{1,0:T(8,128)(2,1)S(1)} %collective-permute-done.1.one, ...), custom_call_target="tpu_custom_call" | custom-call | flops 3932160 | bytes 458784 | tf_op jit(solution)/shard_map/pallas_call | solution.py:298
  13.6 4.4 %shard_map.194 = (bf16[4,128,640]{2,1,0:T(8,128)(2,1)}, bf16[8,640]{1,0:T(8,128)(2,1)}, bf16[528,640]{1,0:T(8,128)(2,1)S(1)}, f32[8,640]{1,0:T(8,128)S(1)}, f32[...) custom-call(s32[1,8]{1,0:T(1,128)} %refs_0_.1, ...), custom_call_target="tpu_custom_call" | custom-call | flops 167772160 | bytes 5620480 | tf_op jit(solution)/shard_map/pallas_call | solution.py:298
  18.2 14.0 %all_to_all.20.came = f32[32,8,128]{2,1,0:T(8,128)S(1)} all-to-all(f32[32,8,128]{2,1,0:T(8,128)S(1)} %get-tuple-element.19), channel_id=1, replica_groups=mesh['req'=8,'head'=4] {'req','head'}, dimensions={0} | all-to-all | bytes 262144 | tf_op jit(solution)/shard_map/all_to_all | solution.py:815
  32.2 1.7 %shard_map.195 = bf16[32,8,128]{2,1,0:T(8,128)(2,1)} custom-call(f32[32,8,128]{2,1,0:T(8,128)S(1)} %all_to_all.20.came, bf16[528,640]{1,0:T(8,128)(2,1)S(1)} %get-tuple-element.25.kept, f32[8,640]{1,0:T(8,128)S(1)} %get-tuple-element.26.added, f32[96,128]{1,0:T(8,128)S(1)} %get-tuple-element.27.tables), custom_call_target="tpu_custom_call" | custom-call | flops 56623104 | bytes 942080 | tf_op jit(solution)/shard_map/pallas_call | solution.py:298
  33.9 2.7 %all-to-all-start.1 = ((bf16[32,8,128]{2,1,0:T(8,128)(2,1)}), bf16[32,8,128]{2,1,0:T(8,128)(2,1)S(1)}, u32[]{:S(2)}, u32[]{:S(2)}) async-start(bf16[32,8,128]{2,1,0:T(8,128)(2,1)} %shard_map.195), calls=%async_computation.1 | async-start | bytes 131072 | tf_op jit(solution)/shard_map/all_to_all | solution.py:873
  36.6 1.7 %collective-permute-start.5 = (bf16[160,256]{1,0:T(8,128)(2,1)S(1)}, bf16[160,256]{1,0:T(8,128)(2,1)S(1)}, u32[]{:S(2)}, u32[]{:S(2)}) collective-permute-start(bf16[160,256]{1,0:T(8,128)(2,1)S(1)} %get-tuple-element.29), channel_id=1, source_target_pairs={{0,4},{4,0},{8,12},{12,8},{16,20},{20,16},{24,28},{28,24},{1,5},{5... | collective-permute-start | bytes 245768 | tf_op jit(solution)/shard_map/ppermute | solution.py:761
  38.3 3.1 %collective-permute-done.5.second = bf16[160,256]{1,0:T(8,128)(2,1)S(1)} collective-permute-done((bf16[160,256]{1,0:T(8,128)(2,1)S(1)}, bf16[160,256]{1,0:T(8,128)(2,1)S(1)}, u32[]{:S(2)}, u32[]{:S(2)}) %collective-permute-start.5) | collective-permute-done | bytes 81952 | tf_op jit(solution)/shard_map/ppermute | solution.py:761
  41.5 2.6 %all-to-all-done.1.came = bf16[32,8,128]{2,1,0:T(8,128)(2,1)S(1)} async-done(((bf16[32,8,128]{2,1,0:T(8,128)(2,1)}), bf16[32,8,128]{2,1,0:T(8,128)(2,1)S(1)}, u32[]{:S(2)}, u32[]{:S(2)}) %all-to-all-start.1) | async-done | bytes 65568 | tf_op jit(solution)/shard_map/all_to_all | solution.py:873
  44.0 1.0 %shard_map.196.own = f32[16,256]{1,0:T(8,128)S(1)} custom-call(s32[1,8]{1,0:T(1,128)} %bitcast.12, bf16[32,8,128]{2,1,0:T(8,128)(2,1)S(1)} %all-to-all-done.1.came, bf16[160,512]{1,0:T(8,128)(2,1)S(1)} %collective-permute-done.refs_12_.first, bf16[160,256]{1,0:T(8,128)(2,1)S(1)} %collective-permute-done.5.second), custom_call_target="tpu_custom_call" | custom-call | flops 2621440 | bytes 327712 | tf_op jit(solution)/shard_map/pallas_call | solution.py:298
  45.2 1.6 %collective-permute-start.7 = (f32[16,256]{1,0:T(8,128)S(1)}, f32[16,256]{1,0:T(8,128)S(1)}, u32[]{:S(2)}, u32[]{:S(2)}) collective-permute-start(f32[16,256]{1,0:T(8,128)S(1)} %shard_map.196.own), channel_id=1, source_target_pairs={{0,2},{1,3},{2,0},{3,1},{4,6},{5,7},{6,4},{7,5},{8,10},{9,11},{10,... | collective-permute-start | bytes 49160 | tf_op jit(solution)/shard_map/ppermute | solution.py:742
  47.0 1.3 %collective-permute-done.8.three = f32[16,256]{1,0:T(8,128)S(1)} collective-permute-done((f32[16,256]{1,0:T(8,128)S(1)}, f32[16,256]{1,0:T(8,128)S(1)}, u32[]{:S(2)}, u32[]{:S(2)}) %collective-permute-start.8) | collective-permute-done | bytes 16416 | tf_op jit(solution)/shard_map/ppermute | solution.py:742
  48.2 0.7 collective-permute-done.7.two
  49.0 1.0 %shard_map.197 = (bf16[8,16,768]{2,1,0:T(8,128)(2,1)S(1)}, bf16[16,256]{1,0:T(8,128)(2,1)S(1)}) custom-call(f32[1,2048]{1,0:T(1,128)} %bitcast.8, f32[16,256]{1,0:T(8,128)S(1)} %shard_map.196.own, f32[16,256]{1,0:T(8,128)S(1)} %collective-permute-done.6.one, f32[16,256]{1,0:T(8,128)S(1)} %collective-permute-done.7.two, ...), custom_call_target="tpu_custom_call" | custom-call | flops 20971520 | bytes 1597440 | tf_op jit(solution)/shard_map/pallas_call | solution.py:298
  50.0 11.3 %all_to_all.21.came = bf16[8,16,768]{2,1,0:T(8,128)(2,1)S(1)} all-to-all(bf16[8,16,768]{2,1,0:T(8,128)(2,1)S(1)} %get-tuple-element.33), channel_id=1, replica_groups=mesh['req'=8,'head'=4] {'req'}, dimensions={0} | all-to-all | bytes 393216 | tf_op jit(solution)/shard_map/all_to_all | solution.py:84
  61.5 0.8 collective-permute-start.10
  62.3 1.1 %collective-permute-start.9 = (bf16[16,320]{1,0:T(8,128)(2,1)S(1)}, bf16[16,320]{1,0:T(8,128)(2,1)S(1)}, u32[]{:S(2)}, u32[]{:S(2)}) collective-permute-start(bf16[16,320]{1,0:T(8,128)(2,1)S(1)} %shard_map.198.own), channel_id=1, source_target_pairs={{0,1},{1,0},{2,3},{3,2},{4,5},{5,4},{6,7},{7,6},{8,9},{9,8},{10,11... | collective-permute-start | bytes 30728 | tf_op jit(solution)/shard_map/ppermute | solution.py:742
  63.4 1.3 %collective-permute-done.11.three = bf16[16,320]{1,0:T(8,128)(2,1)S(1)} collective-permute-done((bf16[16,320]{1,0:T(8,128)(2,1)S(1)}, bf16[16,320]{1,0:T(8,128)(2,1)S(1)}, u32[]{:S(2)}, u32[]{:S(2)}) %collective-permute-start.11) | collective-permute-done | bytes 10272 | tf_op jit(solution)/shard_map/ppermute | solution.py:742
  64.6 0.7 collective-permute-done.10.two
  65.5 10.3 %all_to_all.22.came = bf16[8,16,512]{2,1,0:T(8,128)(2,1)S(1)} all-to-all(bf16[8,16,512]{2,1,0:T(8,128)(2,1)S(1)} %shard_map.199), channel_id=1, replica_groups=mesh['req'=8,'head'=4] {'req'}, dimensions={0} | all-to-all | bytes 262144 | tf_op jit(solution)/shard_map/all_to_all | solution.py:84
  (15 shorter events, 1.7 us)
Async XLA Ops:
  0.6 13.0 %collective-permute-start = (bf16[160,512]{1,0:T(8,128)(2,1)}, bf16[160,512]{1,0:T(8,128)(2,1)S(1)}, u32[]{:S(2)}, u32[]{:S(2)}) collective-permute-start(bf16[160,512]{1,0:T(8,128)(2,1)} %param.24), channel_id=1, source_target_pairs={{0,0},{1,8},{2,16},{3,24},{4,4},{5,12},{6,20},{7,28},{8,1},{9,9},{... | collective-permute-start | bytes 491528 | tf_op jit(solution)/shard_map/ppermute | solution.py:757
  2.2 7.8 %collective-permute-start.2 = (bf16[16,512]{1,0:T(8,128)(2,1)}, bf16[16,512]{1,0:T(8,128)(2,1)S(1)}, u32[]{:S(2)}, u32[]{:S(2)}) collective-permute-start(bf16[16,512]{1,0:T(8,128)(2,1)} %hidden_far.1), channel_id=1, source_target_pairs={{0,2},{1,3},{2,0},{3,1},{4,6},{5,7},{6,4},{7,5},{8,10},{9,11},{10,... | collective-permute-start | bytes 49160 | tf_op jit(solution)/shard_map/ppermute | solution.py:742
  8.1 1.9 %collective-permute-start.1 = (bf16[16,512]{1,0:T(8,128)(2,1)}, bf16[16,512]{1,0:T(8,128)(2,1)S(1)}, u32[]{:S(2)}, u32[]{:S(2)}) collective-permute-start(bf16[16,512]{1,0:T(8,128)(2,1)} %hidden_far.1), channel_id=1, source_target_pairs={{0,1},{1,0},{2,3},{3,2},{4,5},{5,4},{6,7},{7,6},{8,9},{9,8},{10,11... | collective-permute-start | bytes 49160 | tf_op jit(solution)/shard_map/ppermute | solution.py:742
  9.0 3.4 %collective-permute-start.3 = (bf16[16,512]{1,0:T(8,128)(2,1)}, bf16[16,512]{1,0:T(8,128)(2,1)S(1)}, u32[]{:S(2)}, u32[]{:S(2)}) collective-permute-start(bf16[16,512]{1,0:T(8,128)(2,1)} %hidden_far.1), channel_id=1, source_target_pairs={{0,3},{1,2},{2,1},{3,0},{4,7},{5,6},{6,5},{7,4},{8,11},{9,10},{10,... | collective-permute-start | bytes 49160 | tf_op jit(solution)/shard_map/ppermute | solution.py:742
  18.0 14.2 %collective-permute-start.4 = (bf16[256,1280]{1,0:T(8,128)(2,1)S(1)}, bf16[256,1280]{1,0:T(8,128)(2,1)S(1)}, u32[]{:S(2)}, u32[]{:S(2)}) collective-permute-start(bf16[256,1280]{1,0:T(8,128)(2,1)S(1)} %get-tuple-element.23), channel_id=1, source_target_pairs={{0,1},{1,0},{2,3},{3,2},{4,5},{5,4},{6,7},{7,6},{8,9},{9,8},{10,11... | collective-permute-start | bytes 1966088 | tf_op jit(solution)/shard_map/ppermute | solution.py:742
  33.9 31.4 %copy-start = (bf16[640,512]{1,0:T(8,128)(2,1)S(1)}, bf16[640,512]{1,0:T(8,128)(2,1)}, u32[]{:S(2)}) copy-start(bf16[640,512]{1,0:T(8,128)(2,1)} %weight.1) | copy-start | bytes 1966084
  33.9 10.1 %all-to-all-start.1 = ((bf16[32,8,128]{2,1,0:T(8,128)(2,1)}), bf16[32,8,128]{2,1,0:T(8,128)(2,1)S(1)}, u32[]{:S(2)}, u32[]{:S(2)}) async-start(bf16[32,8,128]{2,1,0:T(8,128)(2,1)} %shard_map.195), calls=%async_computation.1 | async-start | bytes 131072 | tf_op jit(solution)/shard_map/all_to_all | solution.py:873
  36.6 4.9 %collective-permute-start.5 = (bf16[160,256]{1,0:T(8,128)(2,1)S(1)}, bf16[160,256]{1,0:T(8,128)(2,1)S(1)}, u32[]{:S(2)}, u32[]{:S(2)}) collective-permute-start(bf16[160,256]{1,0:T(8,128)(2,1)S(1)} %get-tuple-element.29), channel_id=1, source_target_pairs={{0,4},{4,0},{8,12},{12,8},{16,20},{20,16},{24,28},{28,24},{1,5},{5... | collective-permute-start | bytes 245768 | tf_op jit(solution)/shard_map/ppermute | solution.py:761
  45.0 3.2 %collective-permute-start.8 = (f32[16,256]{1,0:T(8,128)S(1)}, f32[16,256]{1,0:T(8,128)S(1)}, u32[]{:S(2)}, u32[]{:S(2)}) collective-permute-start(f32[16,256]{1,0:T(8,128)S(1)} %shard_map.196.own), channel_id=1, source_target_pairs={{0,3},{1,2},{2,1},{3,0},{4,7},{5,6},{6,5},{7,4},{8,11},{9,10},{10,... | collective-permute-start | bytes 49160 | tf_op jit(solution)/shard_map/ppermute | solution.py:742
  45.2 3.7 %collective-permute-start.7 = (f32[16,256]{1,0:T(8,128)S(1)}, f32[16,256]{1,0:T(8,128)S(1)}, u32[]{:S(2)}, u32[]{:S(2)}) collective-permute-start(f32[16,256]{1,0:T(8,128)S(1)} %shard_map.196.own), channel_id=1, source_target_pairs={{0,2},{1,3},{2,0},{3,1},{4,6},{5,7},{6,4},{7,5},{8,10},{9,11},{10,... | collective-permute-start | bytes 49160 | tf_op jit(solution)/shard_map/ppermute | solution.py:742
  46.8 2.1 %collective-permute-start.6 = (f32[16,256]{1,0:T(8,128)S(1)}, f32[16,256]{1,0:T(8,128)S(1)}, u32[]{:S(2)}, u32[]{:S(2)}) collective-permute-start(f32[16,256]{1,0:T(8,128)S(1)} %shard_map.196.own), channel_id=1, source_target_pairs={{0,1},{1,0},{2,3},{3,2},{4,5},{5,4},{6,7},{7,6},{8,9},{9,8},{10,11... | collective-permute-start | bytes 49160 | tf_op jit(solution)/shard_map/ppermute | solution.py:742
  61.5 3.2 %collective-permute-start.11 = (bf16[16,320]{1,0:T(8,128)(2,1)S(1)}, bf16[16,320]{1,0:T(8,128)(2,1)S(1)}, u32[]{:S(2)}, u32[]{:S(2)}) collective-permute-start(bf16[16,320]{1,0:T(8,128)(2,1)S(1)} %shard_map.198.own), channel_id=1, source_target_pairs={{0,3},{1,2},{2,1},{3,0},{4,7},{5,6},{6,5},{7,4},{8,11},{9,10},{10,... | collective-permute-start | bytes 30728 | tf_op jit(solution)/shard_map/ppermute | solution.py:742
  61.5 3.8 %collective-permute-start.10 = (bf16[16,320]{1,0:T(8,128)(2,1)S(1)}, bf16[16,320]{1,0:T(8,128)(2,1)S(1)}, u32[]{:S(2)}, u32[]{:S(2)}) collective-permute-start(bf16[16,320]{1,0:T(8,128)(2,1)S(1)} %shard_map.198.own), channel_id=1, source_target_pairs={{0,2},{1,3},{2,0},{3,1},{4,6},{5,7},{6,4},{7,5},{8,10},{9,11},{10,... | collective-permute-start | bytes 30728 | tf_op jit(solution)/shard_map/ppermute | solution.py:742
  62.3 3.0 %collective-permute-start.9 = (bf16[16,320]{1,0:T(8,128)(2,1)S(1)}, bf16[16,320]{1,0:T(8,128)(2,1)S(1)}, u32[]{:S(2)}, u32[]{:S(2)}) collective-permute-start(bf16[16,320]{1,0:T(8,128)(2,1)S(1)} %shard_map.198.own), channel_id=1, source_target_pairs={{0,1},{1,0},{2,3},{3,2},{4,5},{5,4},{6,7},{7,6},{8,9},{9,8},{10,11... | collective-permute-start | bytes 30728 | tf_op jit(solution)/shard_map/ppermute | solution.py:742

commit v15 on v12

--- a/solution.py
+++ b/solution.py
@@ -391,8 +391,11 @@
 def prepare_kernel(*refs):
     far, refs = refs[:12], refs[12:]
     (compact, summaries, kept, added, tables, mine, theirs), refs = refs[:7], refs[7:]
-    near, (ordered, plain, dealt, done) = refs[:12], refs[12:]
-    copies = fetch(far, near, done)
+    near, (ordered, plain, done) = refs[:12], refs[12:]
+    count = far[9].shape[0]
+    sources = [*far[:9], *[far[9].at[p] for p in range(count)], *far[10:]]
+    targets = [*near[:9], *[near[9].at[p] for p in range(count)], *near[10:]]
+    copies = fetch(sources, targets, done)
     (dest, lengths, source, table, keep, weights, query_gain, key_gain, turns) = near[:9]
     pages, gate, up = near[9:]
     group = lax.axis_index("req")
@@ -405,7 +408,7 @@
     for c in range(source.shape[1]):
         carried = carried + jnp.where(source[0, c] == group, c, 0)
     held_len = (lengths[0, group * R_DEV], lengths[0, carried * R_DEV + 1])
-    count, rows, _ = pages.shape
+    rows = pages.shape[1]
     owned = []
     for r in range(R_DEV):
         slots = []
@@ -444,9 +447,9 @@
     ]
     weight_columns = weights[...].T
     rows_of = iota((rows, KEEP), 0)
-    place = iota((rows, KEEP), 1)
-    copies[9].wait()
+    place = iota((rows, 16), 1)
     for p in range(count):
+        copies[9 + p].wait()
         picks = (keep[p : p + 1, :] == rows_of).astype(single)
         dropped = weight_columns[:, p : p + 1] * (1.0 - jnp.sum(picks, axis=1, keepdims=True))
         total = jnp.sum(dropped, axis=0, keepdims=True)
@@ -475,18 +478,23 @@
     kept[entries:, :] = plain[...].astype(bfloat)
     summaries[...] = ordered[...].astype(bfloat)
 
-    for copy in copies[10:]:
+    for copy in copies[9 + count :]:
         copy.wait()
     block = gate.shape[1] // 2
     piece = block // 2
-    for k in range(2):
+
+    def deal(target, k):
         for b in range(2):
             columns = slice(b * block + k * piece, b * block + (k + 1) * piece)
-            start = b * block
-            dealt[k, :, start : start + piece] = gate[:, columns].astype(single)
-            dealt[k, :, start + piece : start + block] = up[:, columns].astype(single)
-    mine[...] = dealt[lane & 1].astype(bfloat)
-    theirs[...] = dealt[1 - (lane & 1)].astype(bfloat)
+            parts = [gate[:, columns].astype(single), up[:, columns].astype(single)]
+            target[:, b * block : (b + 1) * block] = jnp.concatenate(parts, axis=1).astype(bfloat)
+
+    for core in range(2):
+
+        @pl.when((lane & 1) == core)
+        def _():
+            deal(mine, core)
+            deal(theirs, 1 - core)
 
 
 def attend_kernel(came, kept, added, tables, sent, x, extra_k, extra_v, out, logs):
@@ -789,9 +797,18 @@
     features = D // groups
     copies = pltpu.SemaphoreType.DMA
 
+    others = from_lanes(hidden_in)[1:]
+    blocks = run(
+        blocks_kernel,
+        [shaped((output_weight.shape[0], features), bfloat)] * 2,
+        [output_weight],
+        [],
+        [copies((2,))],
+    )
+    handed = [handed_over(block, turn) for turn, block in enumerate(blocks)]
+    holds = source[None, :]
     columns = input_weight.shape[1]
     padded = -(-columns // TILE) * TILE
-    holds = source[None, :]
     gain = attention_gain[None, :]
     weight = input_weight.T
     far = [holds, gain, weight, hidden_in]
@@ -802,7 +819,7 @@
             shaped((requests, features), bfloat),
         ],
         far,
-        from_lanes(hidden_in)[1:],
+        others,
         [
             *scalar_like(holds),
             *local_like(*far[1:]),
@@ -812,17 +829,11 @@
         ],
         2 * requests * features * columns,
     )
+    sent, *handed = lax.optimization_barrier((sent, *handed))
     came = lax.all_to_all(sent, both_axes, 0, 0, tiled=True)
-    blocks = run(
-        blocks_kernel,
-        [shaped((output_weight.shape[0], features), bfloat)] * 2,
-        [output_weight],
-        [],
-        [copies((2,))],
-    )
-    handed = [handed_over(block, turn) for turn, block in enumerate(blocks)]
-
-    scalars = [dest_slots, lengths[None, :], holds, page_table]
+
+    slots, _ = lax.optimization_barrier((dest_slots, sent))
+    scalars = [slots, lengths[None, :], source[None, :], page_table]
     arrays = [
         keep_rows,
         drop_weights,
@@ -853,12 +864,10 @@
             *local_like(*arrays),
             pltpu.VMEM((pages_here, KVW), single),
             pltpu.VMEM((extras, KVW), single),
-            pltpu.VMEM((2,) + gate_weight.shape, single),
-            copies((len(scalars + arrays),)),
+            copies((len(scalars + arrays) + pages_here - 1,)),
         ],
         2 * pages_here * TILE * PAGE * KVW,
     )
-    came, *handed = lax.optimization_barrier((came, *handed))
     span = -(-KVH * HD // TILE) * TILE
     (parts,) = run(
         attend_kernel,

time: 73.4 us -> 74.1 us (level)
  blocking collectives: 36.3 us -> 31.9 us
  Pallas kernels: 11.4 us -> 13.3 us
  waiting for transfers between devices: 7.37 us -> 9.24 us
  starting transfers between devices: 17 us -> 18.5 us
    all_to_all x1, blocking collectives: 15.5 us -> 11 us  [on_device(): came = lax.all_to_all(parts, both_axes, 0, 0, tiled=True)]
    pallas_call x9, Pallas kernels: 11.4 us -> 13.3 us  [run(): pl.pallas_call(kernel, out_shape=list(outs), in_specs=in_specs, out_specs...]
    all_to_all x1, waiting for transfers between devices: 0.29 us -> 1.95 us  [on_device(): came = lax.all_to_all(sent, both_axes, 0, 0, tiled=True)]
    ppermute x2, starting transfers between devices: 2.5 us -> 3.7 us  [handed_over(): return lax.ppermute(value, both_axes, pairs)]
    ppermute x10, starting transfers between devices: 9.45 us -> 10.3 us  [swapped_lanes(): return lax.ppermute(value, 'head', [(k, k ^ turn) for k in range(lanes)])]
  transfers between devices with their start and end apart: 13 -> 13, of which waited for: 7 -> 7; matrix products, arithmetic and copies ran while one was open for 0% -> 0% of each run, Pallas kernels for 7% -> 11%
where the time goes in v15:
time: 74.1 us; the launch traced here: 73.7 us
  blocking collectives  31.9 us (43%)
  starting transfers between devices  18.5 us (25%)
  Pallas kernels  13.3 us (18%)
  waiting for transfers between devices  9.24 us (12%)
    all_to_all x2, blocking collectives, exchange(): return lax.all_to_all(parts, 'req', split_axis=0, concat_axis=0, tiled=True)  20.9 us
    pallas_call x9, Pallas kernels, run(): pl.pallas_call(kernel, out_shape=list(outs), in_specs=in_specs, out_specs...  13.3 us
    all_to_all x1, blocking collectives, on_device(): came = lax.all_to_all(parts, both_axes, 0, 0, tiled=True)  11 us
    ppermute x10, starting transfers between devices, swapped_lanes(): return lax.ppermute(value, 'head', [(k, k ^ turn) for k in range(lanes)])  10.3 us
    ppermute x10, waiting for transfers between devices, swapped_lanes(): return lax.ppermute(value, 'head', [(k, k ^ turn) for k in range(lanes)])  7.28 us
    all_to_all x1, starting transfers between devices, on_device(): came = lax.all_to_all(sent, both_axes, 0, 0, tiled=True)  4.5 us
    ppermute x2, starting transfers between devices, handed_over(): return lax.ppermute(value, both_axes, pairs)  3.7 us
    all_to_all x1, waiting for transfers between devices, on_device(): came = lax.all_to_all(sent, both_axes, 0, 0, tiled=True)  1.95 us
  transfers between devices with their start and end apart: 13, of which 7 were waited for; matrix products, arithmetic and copies ran while one was open for 0% of the time, Pallas kernels for 11%

profile of v15, /device:TPU:0, one launch (start us, length us, event | category | flops | bytes accessed | tf_op | source)
XLA Modules:
  0.0 73.7 jit_solution(4864930540979215548)
XLA Ops:
  0.6 1.0 %shard_map.194 = (bf16[160,256]{1,0:T(8,128)(2,1)S(1)}, bf16[160,256]{1,0:T(8,128)(2,1)S(1)}) custom-call(bf16[160,512]{1,0:T(8,128)(2,1)} %weight_far.1), custom_call_target="tpu_custom_call" | custom-call | bytes 327680 | tf_op jit(solution)/shard_map/pallas_call | solution.py:298
  1.6 0.7 collective-permute-start.3
  2.3 3.0 %collective-permute-start.4 = (bf16[160,256]{1,0:T(8,128)(2,1)S(1)}, bf16[160,256]{1,0:T(8,128)(2,1)S(1)}, u32[]{:S(2)}, u32[]{:S(2)}) collective-permute-start(bf16[160,256]{1,0:T(8,128)(2,1)S(1)} %get-tuple-element.25), channel_id=1, source_target_pairs={{0,4},{1,12},{2,20},{3,28},{4,0},{5,8},{6,16},{7,24},{8,5},{9,13},... | collective-permute-start | bytes 245768 | tf_op jit(solution)/shard_map/ppermute | solution.py:770
  5.3 6.0 %collective-permute-start.1 = (bf16[16,512]{1,0:T(8,128)(2,1)}, bf16[16,512]{1,0:T(8,128)(2,1)S(1)}, u32[]{:S(2)}, u32[]{:S(2)}) collective-permute-start(bf16[16,512]{1,0:T(8,128)(2,1)} %hidden_far.1), channel_id=1, source_target_pairs={{0,2},{1,3},{2,0},{3,1},{4,6},{5,7},{6,4},{7,5},{8,10},{9,11},{10,... | collective-permute-start | bytes 49160 | tf_op jit(solution)/shard_map/ppermute | solution.py:754
  11.5 1.7 %collective-permute-done.1.two = bf16[16,512]{1,0:T(8,128)(2,1)S(1)} collective-permute-done((bf16[16,512]{1,0:T(8,128)(2,1)}, bf16[16,512]{1,0:T(8,128)(2,1)S(1)}, u32[]{:S(2)}, u32[]{:S(2)}) %collective-permute-start.1) | collective-permute-done | bytes 16416 | tf_op jit(solution)/shard_map/ppermute | solution.py:754
  13.2 1.6 %collective-permute-done.2.three = bf16[16,512]{1,0:T(8,128)(2,1)S(1)} collective-permute-done((bf16[16,512]{1,0:T(8,128)(2,1)}, bf16[16,512]{1,0:T(8,128)(2,1)S(1)}, u32[]{:S(2)}, u32[]{:S(2)}) %collective-permute-start.2) | collective-permute-done | bytes 16416 | tf_op jit(solution)/shard_map/ppermute | solution.py:754
  14.8 1.9 %shard_map.193 = (f32[32,8,128]{2,1,0:T(8,128)}, bf16[16,256]{1,0:T(8,128)(2,1)S(1)}) custom-call(s32[1,8]{1,0:T(1,128)} %bitcast.10, f32[1,2048]{1,0:T(1,128)} %bitcast.9, bf16[480,256]{1,0:T(8,128)(2,1)} %bitcast.7, bf16[16,512]{1,0:T(8,128)(2,1)} %hidden_far.1, bf16[16,512]{1,0:T(8,128)(2,1)S(1)} %collective-permute-done.one, ...), custom_call_target="tpu_custom_call" | custom-call | flops 3932160 | bytes 458784 | tf_op jit(solution)/shard_map/pallas_call | solution.py:298
  16.8 4.5 %all-to-all-start = ((f32[32,8,128]{2,1,0:T(8,128)}), f32[32,8,128]{2,1,0:T(8,128)S(1)}, u32[]{:S(2)}, u32[]{:S(2)}) async-start(f32[32,8,128]{2,1,0:T(8,128)} %get-tuple-element.26), calls=%async_computation | async-start | bytes 262144 | tf_op jit(solution)/shard_map/all_to_all | solution.py:833
  21.3 6.3 %shard_map.195 = (bf16[4,128,640]{2,1,0:T(8,128)(2,1)}, bf16[8,640]{1,0:T(8,128)(2,1)}, bf16[528,640]{1,0:T(8,128)(2,1)S(1)}, f32[8,640]{1,0:T(8,128)S(1)}, f32[...) custom-call(s32[1,8]{1,0:T(1,128)} %refs_0_, s32[1,16]{1,0:T(1,128)} %bitcast.13, ...), custom_call_target="tpu_custom_call" | custom-call | flops 167772160 | bytes 5374720 | tf_op jit(solution)/shard_map/pallas_call | solution.py:298
  27.6 2.0 %all-to-all-done.came = f32[32,8,128]{2,1,0:T(8,128)S(1)} async-done(((f32[32,8,128]{2,1,0:T(8,128)}), f32[32,8,128]{2,1,0:T(8,128)S(1)}, u32[]{:S(2)}, u32[]{:S(2)}) %all-to-all-start) | async-done | bytes 131104 | tf_op jit(solution)/shard_map/all_to_all | solution.py:833
  29.6 1.1 %shard_map.196 = bf16[32,8,128]{2,1,0:T(8,128)(2,1)S(1)} custom-call(f32[32,8,128]{2,1,0:T(8,128)S(1)} %all-to-all-done.came, bf16[528,640]{1,0:T(8,128)(2,1)S(1)} %get-tuple-element.30.kept, f32[8,640]{1,0:T(8,128)S(1)} %get-tuple-element.31.added, f32[96,128]{1,0:T(8,128)S(1)} %get-tuple-element.32.tables), custom_call_target="tpu_custom_call" | custom-call | flops 56623104 | bytes 942080 | tf_op jit(solution)/shard_map/pallas_call | solution.py:298
  30.7 0.3 collective-permute-start.5
  30.9 11.0 %all_to_all.20.came = bf16[32,8,128]{2,1,0:T(8,128)(2,1)S(1)} all-to-all(bf16[32,8,128]{2,1,0:T(8,128)(2,1)S(1)} %shard_map.196), channel_id=1, replica_groups=mesh['req'=8,'head'=4] {'req','head'}, dimensions={0} | all-to-all | bytes 131072 | tf_op jit(solution)/shard_map/all_to_all | solution.py:888
  42.0 1.0 %shard_map.197.own = f32[16,256]{1,0:T(8,128)S(1)} custom-call(s32[1,8]{1,0:T(1,128)} %bitcast.12, bf16[32,8,128]{2,1,0:T(8,128)(2,1)S(1)} %all_to_all.20.came, bf16[160,256]{1,0:T(8,128)(2,1)S(1)} %collective-permute-done.3.first, bf16[160,256]{1,0:T(8,128)(2,1)S(1)} %collective-permute-done.4.second), custom_call_target="tpu_custom_call" | custom-call | flops 2621440 | bytes 245792 | tf_op jit(solution)/shard_map/pallas_call | solution.py:298
  43.2 1.6 %collective-permute-start.7 = (f32[16,256]{1,0:T(8,128)S(1)}, f32[16,256]{1,0:T(8,128)S(1)}, u32[]{:S(2)}, u32[]{:S(2)}) collective-permute-start(f32[16,256]{1,0:T(8,128)S(1)} %shard_map.197.own), channel_id=1, source_target_pairs={{0,2},{1,3},{2,0},{3,1},{4,6},{5,7},{6,4},{7,5},{8,10},{9,11},{10,... | collective-permute-start | bytes 49160 | tf_op jit(solution)/shard_map/ppermute | solution.py:754
  45.0 1.3 %collective-permute-done.8.three = f32[16,256]{1,0:T(8,128)S(1)} collective-permute-done((f32[16,256]{1,0:T(8,128)S(1)}, f32[16,256]{1,0:T(8,128)S(1)}, u32[]{:S(2)}, u32[]{:S(2)}) %collective-permute-start.8) | collective-permute-done | bytes 16416 | tf_op jit(solution)/shard_map/ppermute | solution.py:754
  46.2 0.7 collective-permute-done.7.two
  47.0 1.0 %shard_map.198 = (bf16[8,16,768]{2,1,0:T(8,128)(2,1)S(1)}, bf16[16,256]{1,0:T(8,128)(2,1)S(1)}) custom-call(f32[1,2048]{1,0:T(1,128)} %bitcast.8, f32[16,256]{1,0:T(8,128)S(1)} %shard_map.197.own, f32[16,256]{1,0:T(8,128)S(1)} %collective-permute-done.6.one, f32[16,256]{1,0:T(8,128)S(1)} %collective-permute-done.7.two, ...), custom_call_target="tpu_custom_call" | custom-call | flops 20971520 | bytes 1597440 | tf_op jit(solution)/shard_map/pallas_call | solution.py:298
  48.0 10.3 %all_to_all.21.came = bf16[8,16,768]{2,1,0:T(8,128)(2,1)S(1)} all-to-all(bf16[8,16,768]{2,1,0:T(8,128)(2,1)S(1)} %get-tuple-element.41), channel_id=1, replica_groups=mesh['req'=8,'head'=4] {'req'}, dimensions={0} | all-to-all | bytes 393216 | tf_op jit(solution)/shard_map/all_to_all | solution.py:84
  58.5 1.6 %collective-permute-start.10 = (bf16[16,320]{1,0:T(8,128)(2,1)S(1)}, bf16[16,320]{1,0:T(8,128)(2,1)S(1)}, u32[]{:S(2)}, u32[]{:S(2)}) collective-permute-start(bf16[16,320]{1,0:T(8,128)(2,1)S(1)} %shard_map.199.own), channel_id=1, source_target_pairs={{0,2},{1,3},{2,0},{3,1},{4,6},{5,7},{6,4},{7,5},{8,10},{9,11},{10,... | collective-permute-start | bytes 30728 | tf_op jit(solution)/shard_map/ppermute | solution.py:754
  60.3 1.3 %collective-permute-done.11.three = bf16[16,320]{1,0:T(8,128)(2,1)S(1)} collective-permute-done((bf16[16,320]{1,0:T(8,128)(2,1)S(1)}, bf16[16,320]{1,0:T(8,128)(2,1)S(1)}, u32[]{:S(2)}, u32[]{:S(2)}) %collective-permute-start.11) | collective-permute-done | bytes 10272 | tf_op jit(solution)/shard_map/ppermute | solution.py:754
  61.6 0.6 collective-permute-done.10.two
  62.4 10.6 %all_to_all.22.came = bf16[8,16,512]{2,1,0:T(8,128)(2,1)S(1)} all-to-all(bf16[8,16,512]{2,1,0:T(8,128)(2,1)S(1)} %shard_map.200), channel_id=1, replica_groups=mesh['req'=8,'head'=4] {'req'}, dimensions={0} | all-to-all | bytes 262144 | tf_op jit(solution)/shard_map/all_to_all | solution.py:84
  73.1 0.6 shard_map.201
  (16 shorter events, 1.3 us)
Async XLA Ops:
  1.6 15.2 %collective-permute-start.3 = (bf16[160,256]{1,0:T(8,128)(2,1)S(1)}, bf16[160,256]{1,0:T(8,128)(2,1)S(1)}, u32[]{:S(2)}, u32[]{:S(2)}) collective-permute-start(bf16[160,256]{1,0:T(8,128)(2,1)S(1)} %get-tuple-element.24), channel_id=1, source_target_pairs={{0,0},{1,8},{2,16},{3,24},{4,4},{5,12},{6,20},{7,28},{8,1},{9,9},{... | collective-permute-start | bytes 245768 | tf_op jit(solution)/shard_map/ppermute | solution.py:770
  2.3 14.5 %collective-permute-start.4 = (bf16[160,256]{1,0:T(8,128)(2,1)S(1)}, bf16[160,256]{1,0:T(8,128)(2,1)S(1)}, u32[]{:S(2)}, u32[]{:S(2)}) collective-permute-start(bf16[160,256]{1,0:T(8,128)(2,1)S(1)} %get-tuple-element.25), channel_id=1, source_target_pairs={{0,4},{1,12},{2,20},{3,28},{4,0},{5,8},{6,16},{7,24},{8,5},{9,13},... | collective-permute-start | bytes 245768 | tf_op jit(solution)/shard_map/ppermute | solution.py:770
  5.3 7.9 %collective-permute-start.1 = (bf16[16,512]{1,0:T(8,128)(2,1)}, bf16[16,512]{1,0:T(8,128)(2,1)S(1)}, u32[]{:S(2)}, u32[]{:S(2)}) collective-permute-start(bf16[16,512]{1,0:T(8,128)(2,1)} %hidden_far.1), channel_id=1, source_target_pairs={{0,2},{1,3},{2,0},{3,1},{4,6},{5,7},{6,4},{7,5},{8,10},{9,11},{10,... | collective-permute-start | bytes 49160 | tf_op jit(solution)/shard_map/ppermute | solution.py:754
  11.3 1.9 %collective-permute-start = (bf16[16,512]{1,0:T(8,128)(2,1)}, bf16[16,512]{1,0:T(8,128)(2,1)S(1)}, u32[]{:S(2)}, u32[]{:S(2)}) collective-permute-start(bf16[16,512]{1,0:T(8,128)(2,1)} %hidden_far.1), channel_id=1, source_target_pairs={{0,1},{1,0},{2,3},{3,2},{4,5},{5,4},{6,7},{7,6},{8,9},{9,8},{10,11... | collective-permute-start | bytes 49160 | tf_op jit(solution)/shard_map/ppermute | solution.py:754
  11.5 3.4 %collective-permute-start.2 = (bf16[16,512]{1,0:T(8,128)(2,1)}, bf16[16,512]{1,0:T(8,128)(2,1)S(1)}, u32[]{:S(2)}, u32[]{:S(2)}) collective-permute-start(bf16[16,512]{1,0:T(8,128)(2,1)} %hidden_far.1), channel_id=1, source_target_pairs={{0,3},{1,2},{2,1},{3,0},{4,7},{5,6},{6,5},{7,4},{8,11},{9,10},{10,... | collective-permute-start | bytes 49160 | tf_op jit(solution)/shard_map/ppermute | solution.py:754
  16.8 12.7 %all-to-all-start = ((f32[32,8,128]{2,1,0:T(8,128)}), f32[32,8,128]{2,1,0:T(8,128)S(1)}, u32[]{:S(2)}, u32[]{:S(2)}) async-start(f32[32,8,128]{2,1,0:T(8,128)} %get-tuple-element.26), calls=%async_computation | async-start | bytes 262144 | tf_op jit(solution)/shard_map/all_to_all | solution.py:833
  30.6 31.6 %copy-start = (bf16[640,512]{1,0:T(8,128)(2,1)S(1)}, bf16[640,512]{1,0:T(8,128)(2,1)}, u32[]{:S(2)}) copy-start(bf16[640,512]{1,0:T(8,128)(2,1)} %weight.1) | copy-start | bytes 1966084
  30.7 11.3 %collective-permute-start.5 = (bf16[256,1280]{1,0:T(8,128)(2,1)S(1)}, bf16[256,1280]{1,0:T(8,128)(2,1)S(1)}, u32[]{:S(2)}, u32[]{:S(2)}) collective-permute-start(bf16[256,1280]{1,0:T(8,128)(2,1)S(1)} %get-tuple-element.34), channel_id=1, source_target_pairs={{0,1},{1,0},{2,3},{3,2},{4,5},{5,4},{6,7},{7,6},{8,9},{9,8},{10,11... | collective-permute-start | bytes 1966088 | tf_op jit(solution)/shard_map/ppermute | solution.py:754
  43.0 3.2 %collective-permute-start.8 = (f32[16,256]{1,0:T(8,128)S(1)}, f32[16,256]{1,0:T(8,128)S(1)}, u32[]{:S(2)}, u32[]{:S(2)}) collective-permute-start(f32[16,256]{1,0:T(8,128)S(1)} %shard_map.197.own), channel_id=1, source_target_pairs={{0,3},{1,2},{2,1},{3,0},{4,7},{5,6},{6,5},{7,4},{8,11},{9,10},{10,... | collective-permute-start | bytes 49160 | tf_op jit(solution)/shard_map/ppermute | solution.py:754
  43.2 3.7 %collective-permute-start.7 = (f32[16,256]{1,0:T(8,128)S(1)}, f32[16,256]{1,0:T(8,128)S(1)}, u32[]{:S(2)}, u32[]{:S(2)}) collective-permute-start(f32[16,256]{1,0:T(8,128)S(1)} %shard_map.197.own), channel_id=1, source_target_pairs={{0,2},{1,3},{2,0},{3,1},{4,6},{5,7},{6,4},{7,5},{8,10},{9,11},{10,... | collective-permute-start | bytes 49160 | tf_op jit(solution)/shard_map/ppermute | solution.py:754
  44.8 2.1 %collective-permute-start.6 = (f32[16,256]{1,0:T(8,128)S(1)}, f32[16,256]{1,0:T(8,128)S(1)}, u32[]{:S(2)}, u32[]{:S(2)}) collective-permute-start(f32[16,256]{1,0:T(8,128)S(1)} %shard_map.197.own), channel_id=1, source_target_pairs={{0,1},{1,0},{2,3},{3,2},{4,5},{5,4},{6,7},{7,6},{8,9},{9,8},{10,11... | collective-permute-start | bytes 49160 | tf_op jit(solution)/shard_map/ppermute | solution.py:754
  58.4 3.2 %collective-permute-start.11 = (bf16[16,320]{1,0:T(8,128)(2,1)S(1)}, bf16[16,320]{1,0:T(8,128)(2,1)S(1)}, u32[]{:S(2)}, u32[]{:S(2)}) collective-permute-start(bf16[16,320]{1,0:T(8,128)(2,1)S(1)} %shard_map.199.own), channel_id=1, source_target_pairs={{0,3},{1,2},{2,1},{3,0},{4,7},{5,6},{6,5},{7,4},{8,11},{9,10},{10,... | collective-permute-start | bytes 30728 | tf_op jit(solution)/shard_map/ppermute | solution.py:754
  58.5 3.8 %collective-permute-start.10 = (bf16[16,320]{1,0:T(8,128)(2,1)S(1)}, bf16[16,320]{1,0:T(8,128)(2,1)S(1)}, u32[]{:S(2)}, u32[]{:S(2)}) collective-permute-start(bf16[16,320]{1,0:T(8,128)(2,1)S(1)} %shard_map.199.own), channel_id=1, source_target_pairs={{0,2},{1,3},{2,0},{3,1},{4,6},{5,7},{6,4},{7,5},{8,10},{9,11},{10,... | collective-permute-start | bytes 30728 | tf_op jit(solution)/shard_map/ppermute | solution.py:754
  60.1 2.2 %collective-permute-start.9 = (bf16[16,320]{1,0:T(8,128)(2,1)S(1)}, bf16[16,320]{1,0:T(8,128)(2,1)S(1)}, u32[]{:S(2)}, u32[]{:S(2)}) collective-permute-start(bf16[16,320]{1,0:T(8,128)(2,1)S(1)} %shard_map.199.own), channel_id=1, source_target_pairs={{0,1},{1,0},{2,3},{3,2},{4,5},{5,4},{6,7},{7,6},{8,9},{9,8},{10,11... | collective-permute-start | bytes 30728 | tf_op jit(solution)/shard_map/ppermute | solution.py:754

commit v16 on v13

--- a/solution.py
+++ b/solution.py
@@ -389,12 +389,12 @@
 
 
 def prepare_kernel(*refs):
-    far, refs = refs[:12], refs[12:]
-    (compact, summaries, kept, added, tables, mine, theirs), refs = refs[:7], refs[7:]
-    near, (ordered, plain, dealt, done) = refs[:12], refs[12:]
+    far, refs = refs[:13], refs[13:]
+    (compact, summaries, kept, added, tables, mine, theirs, *handed), refs = refs[:9], refs[9:]
+    near, (ordered, plain, dealt, done) = refs[:13], refs[13:]
     copies = fetch(far, near, done)
     (dest, lengths, source, table, keep, weights, query_gain, key_gain, turns) = near[:9]
-    pages, gate, up = near[9:]
+    pages, gate, up, output = near[9:]
     group = lax.axis_index("req")
     lane = lax.axis_index("head")
     lanes = lax.axis_size("head")
@@ -487,6 +487,10 @@
             dealt[k, :, start + piece : start + block] = up[:, columns].astype(single)
     mine[...] = dealt[lane & 1].astype(bfloat)
     theirs[...] = dealt[1 - (lane & 1)].astype(bfloat)
+    width = handed[0].shape[1]
+    for turn, block in enumerate(handed):
+        start = pl.multiple_of(((group & 1) ^ turn) * width, width)
+        block[...] = output[:, pl.ds(start, width)]
 
 
 def attend_kernel(came, kept, added, tables, sent, x, extra_k, extra_v, out, logs):
@@ -608,15 +612,6 @@
         tile = jnp.concatenate(tile, axis=0).astype(bfloat)
         for g in range(groups):
             sent[g * lanes + k] = tile
-
-
-def blocks_kernel(weight_far, same, other, done):
-    width = same.shape[1]
-    group = lax.axis_index("req")
-    starts = [pl.multiple_of(((group & 1) ^ turn) * width, width) for turn in range(2)]
-    parts = [weight_far.at[:, pl.ds(start, width)] for start in starts]
-    for copy in fetch(parts, (same, other), done):
-        copy.wait()
 
 
 def project_kernel(source_far, came, first, second, sent, source, logs, rows, pieces, done):
@@ -790,14 +785,6 @@
     copies = pltpu.SemaphoreType.DMA
 
     others = from_lanes(hidden_in)[1:]
-    blocks = run(
-        blocks_kernel,
-        [shaped((output_weight.shape[0], features), bfloat)] * 2,
-        [output_weight],
-        [],
-        [copies((2,))],
-    )
-    handed = [handed_over(block, turn) for turn, block in enumerate(blocks)]
     scalars = [dest_slots, lengths[None, :], source[None, :], page_table]
     arrays = [
         keep_rows,
@@ -808,10 +795,11 @@
         old_cache,
         gate_weight,
         up_weight,
+        output_weight,
     ]
     entries = pages_here * KEEP
     extras = 16
-    compact, summaries, kept, added, tables, mine, theirs = run(
+    compact, summaries, kept, added, tables, mine, theirs, *handed = run(
         prepare_kernel,
         [
             shaped((pages_here // 2, PAGE, KVW), bfloat),
@@ -821,6 +809,8 @@
             shaped((96, TILE), single),
             shaped(gate_weight.shape, bfloat),
             shaped(gate_weight.shape, bfloat),
+            shaped((output_weight.shape[0], features), bfloat),
+            shaped((output_weight.shape[0], features), bfloat),
         ],
         scalars + arrays,
         [],
@@ -834,8 +824,7 @@
         ],
         2 * pages_here * TILE * PAGE * KVW,
     )
-    tables, *moved = lax.optimization_barrier((tables, *others, *handed))
-    others, handed = moved[: lanes - 1], moved[lanes - 1 :]
+    tables, *others = lax.optimization_barrier((tables, *others))
 
     holds = source[None, :]
     columns = input_weight.shape[1]
@@ -861,9 +850,9 @@
         2 * requests * features * columns,
     )
     came = lax.all_to_all(sent, both_axes, 0, 0, tiled=True)
-    theirs, _ = lax.optimization_barrier((theirs, sent))
     theirs = swapped_lanes(theirs, 1)
-    came, theirs = lax.optimization_barrier((came, theirs))
+    handed = [handed_over(block, turn) for turn, block in enumerate(handed)]
+    came, theirs, *handed = lax.optimization_barrier((came, theirs, *handed))
     span = -(-KVH * HD // TILE) * TILE
     (parts,) = run(
         attend_kernel,

time: 72.9 us -> 76.2 us (1.045)
  waiting for transfers between devices: 3.93 us -> 12.8 us
  blocking collectives: 42.9 us -> 37.2 us
    all_to_all x1 -> x0, blocking collectives: 12.8 us -> none  [on_device(): came = lax.all_to_all(sent, both_axes, 0, 0, tiled=True)]
    all_to_all x1, blocking collectives: 9.24 us -> 16.4 us  [on_device(): came = lax.all_to_all(parts, both_axes, 0, 0, tiled=True)]
    all_to_all x0 -> x1, starting transfers between devices: none -> 4.96 us  [on_device(): came = lax.all_to_all(sent, both_axes, 0, 0, tiled=True)]
    ppermute x10, starting transfers between devices: 10.5 us -> 7.16 us  [swapped_lanes(): return lax.ppermute(value, 'head', [(k, k ^ turn) for k in range(lanes)])]
    ppermute x10, waiting for transfers between devices: 3.92 us -> 7.04 us  [swapped_lanes(): return lax.ppermute(value, 'head', [(k, k ^ turn) for k in range(lanes)])]
    ppermute x2, waiting for transfers between devices: 0.01 us -> 3.11 us  [handed_over(): return lax.ppermute(value, both_axes, pairs)]
    all_to_all x0 -> x1, waiting for transfers between devices: none -> 2.65 us  [on_device(): came = lax.all_to_all(sent, both_axes, 0, 0, tiled=True)]
    ppermute x2, starting transfers between devices: 3.7 us -> 2.5 us  [handed_over(): return lax.ppermute(value, both_axes, pairs)]
  transfers between devices with their start and end apart: 12 -> 13, of which waited for: 4 -> 8; matrix products, arithmetic and copies ran while one was open for 0% -> 0% of each run, Pallas kernels for 6% -> 3%
where the time goes in v16:
time: 76.2 us; the launch traced here: 75.8 us
  blocking collectives  37.2 us (49%)
  starting transfers between devices  14.6 us (19%)
  waiting for transfers between devices  12.8 us (17%)
  Pallas kernels  10.4 us (14%)
    all_to_all x2, blocking collectives, exchange(): return lax.all_to_all(parts, 'req', split_axis=0, concat_axis=0, tiled=True)  20.9 us
    all_to_all x1, blocking collectives, on_device(): came = lax.all_to_all(parts, both_axes, 0, 0, tiled=True)  16.4 us
    pallas_call x8, Pallas kernels, run(): pl.pallas_call(kernel, out_shape=list(outs), in_specs=in_specs, out_specs...  10.4 us
    ppermute x10, starting transfers between devices, swapped_lanes(): return lax.ppermute(value, 'head', [(k, k ^ turn) for k in range(lanes)])  7.16 us
    ppermute x10, waiting for transfers between devices, swapped_lanes(): return lax.ppermute(value, 'head', [(k, k ^ turn) for k in range(lanes)])  7.04 us
    all_to_all x1, starting transfers between devices, on_device(): came = lax.all_to_all(sent, both_axes, 0, 0, tiled=True)  4.96 us
    ppermute x2, waiting for transfers between devices, handed_over(): return lax.ppermute(value, both_axes, pairs)  3.11 us
    all_to_all x1, waiting for transfers between devices, on_device(): came = lax.all_to_all(sent, both_axes, 0, 0, tiled=True)  2.65 us
  transfers between devices with their start and end apart: 13, of which 8 were waited for; matrix products, arithmetic and copies ran while one was open for 0% of the time, Pallas kernels for 3%

profile of v16, /device:TPU:0, one launch (start us, length us, event | category | flops | bytes accessed | tf_op | source)
XLA Modules:
  0.0 75.8 jit_solution(4572086694881211346)
XLA Ops:
  0.6 4.4 %shard_map.193 = (bf16[4,128,640]{2,1,0:T(8,128)(2,1)}, bf16[8,640]{1,0:T(8,128)(2,1)}, bf16[528,640]{1,0:T(8,128)(2,1)S(1)}, f32[8,640]{1,0:T(8,128)S(1)}, f32[...) custom-call(s32[1,8]{1,0:T(1,128)} %refs_0_.1, ...), custom_call_target="tpu_custom_call" | custom-call | flops 167772160 | bytes 5702400 | tf_op jit(solution)/shard_map/pallas_call | solution.py:298
  5.0 0.5 collective-permute-start.3
  5.5 2.6 %collective-permute-start.1 = (bf16[16,512]{1,0:T(8,128)(2,1)S(1)}, bf16[16,512]{1,0:T(8,128)(2,1)S(1)}, u32[]{:S(2)}, u32[]{:S(2)}) collective-permute-start(bf16[16,512]{1,0:T(8,128)(2,1)S(1)} %copy-done.1), channel_id=1, source_target_pairs={{0,2},{1,3},{2,0},{3,1},{4,6},{5,7},{6,4},{7,5},{8,10},{9,11},{10,... | collective-permute-start | bytes 49160 | tf_op jit(solution)/shard_map/ppermute | solution.py:741
  8.3 1.5 %collective-permute-done.1.two = bf16[16,512]{1,0:T(8,128)(2,1)S(1)} collective-permute-done((bf16[16,512]{1,0:T(8,128)(2,1)S(1)}, bf16[16,512]{1,0:T(8,128)(2,1)S(1)}, u32[]{:S(2)}, u32[]{:S(2)}) %collective-permute-start.1) | collective-permute-done | bytes 16416 | tf_op jit(solution)/shard_map/ppermute | solution.py:741
  9.8 1.6 %collective-permute-done.2.three = bf16[16,512]{1,0:T(8,128)(2,1)S(1)} collective-permute-done((bf16[16,512]{1,0:T(8,128)(2,1)S(1)}, bf16[16,512]{1,0:T(8,128)(2,1)S(1)}, u32[]{:S(2)}, u32[]{:S(2)}) %collective-permute-start.2) | collective-permute-done | bytes 16416 | tf_op jit(solution)/shard_map/ppermute | solution.py:741
  11.4 1.9 %shard_map.194 = (f32[32,8,128]{2,1,0:T(8,128)}, bf16[16,256]{1,0:T(8,128)(2,1)S(1)}) custom-call(s32[1,8]{1,0:T(1,128)} %bitcast.11, f32[1,2048]{1,0:T(1,128)} %bitcast.9, bf16[480,256]{1,0:T(8,128)(2,1)} %bitcast.7, bf16[16,512]{1,0:T(8,128)(2,1)} %hidden_far.1, bf16[16,512]{1,0:T(8,128)(2,1)S(1)} %collective-permute-done.one, ...), custom_call_target="tpu_custom_call" | custom-call | flops 3932160 | bytes 458784 | tf_op jit(solution)/shard_map/pallas_call | solution.py:298
  13.4 5.0 %all-to-all-start = ((f32[32,8,128]{2,1,0:T(8,128)}), f32[32,8,128]{2,1,0:T(8,128)S(1)}, u32[]{:S(2)}, u32[]{:S(2)}) async-start(f32[32,8,128]{2,1,0:T(8,128)} %get-tuple-element.30), calls=%async_computation | async-start | bytes 262144 | tf_op jit(solution)/shard_map/all_to_all | solution.py:852
  18.3 0.7 collective-permute-start.4
  19.0 1.8 %collective-permute-start.5 = (bf16[160,256]{1,0:T(8,128)(2,1)S(1)}, bf16[160,256]{1,0:T(8,128)(2,1)S(1)}, u32[]{:S(2)}, u32[]{:S(2)}) collective-permute-start(bf16[160,256]{1,0:T(8,128)(2,1)S(1)} %get-tuple-element.33), channel_id=1, source_target_pairs={{0,4},{1,12},{2,20},{3,28},{4,0},{5,8},{6,16},{7,24},{8,5},{9,13},... | collective-permute-start | bytes 245768 | tf_op jit(solution)/shard_map/ppermute | solution.py:757
  20.9 3.1 %collective-permute-done.5.second = bf16[160,256]{1,0:T(8,128)(2,1)S(1)} collective-permute-done((bf16[160,256]{1,0:T(8,128)(2,1)S(1)}, bf16[160,256]{1,0:T(8,128)(2,1)S(1)}, u32[]{:S(2)}, u32[]{:S(2)}) %collective-permute-start.5) | collective-permute-done | bytes 81952 | tf_op jit(solution)/shard_map/ppermute | solution.py:757
  24.0 2.6 %all-to-all-done.came = f32[32,8,128]{2,1,0:T(8,128)S(1)} async-done(((f32[32,8,128]{2,1,0:T(8,128)}), f32[32,8,128]{2,1,0:T(8,128)S(1)}, u32[]{:S(2)}, u32[]{:S(2)}) %all-to-all-start) | async-done | bytes 131104 | tf_op jit(solution)/shard_map/all_to_all | solution.py:852
  26.6 1.1 %shard_map.195 = bf16[32,8,128]{2,1,0:T(8,128)(2,1)S(1)} custom-call(f32[32,8,128]{2,1,0:T(8,128)S(1)} %all-to-all-done.came, bf16[528,640]{1,0:T(8,128)(2,1)S(1)} %get-tuple-element.35.kept, f32[8,640]{1,0:T(8,128)S(1)} %get-tuple-element.36.added, f32[96,128]{1,0:T(8,128)S(1)} %get-tuple-element.37.tables), custom_call_target="tpu_custom_call" | custom-call | flops 56623104 | bytes 942080 | tf_op jit(solution)/shard_map/pallas_call | solution.py:298
  27.7 16.4 %all_to_all.20.came = bf16[32,8,128]{2,1,0:T(8,128)(2,1)S(1)} all-to-all(bf16[32,8,128]{2,1,0:T(8,128)(2,1)S(1)} %shard_map.195), channel_id=1, replica_groups=mesh['req'=8,'head'=4] {'req','head'}, dimensions={0} | all-to-all | bytes 131072 | tf_op jit(solution)/shard_map/all_to_all | solution.py:871
  44.1 1.0 %shard_map.196.own = f32[16,256]{1,0:T(8,128)S(1)} custom-call(s32[1,8]{1,0:T(1,128)} %bitcast.12, bf16[32,8,128]{2,1,0:T(8,128)(2,1)S(1)} %all_to_all.20.came, bf16[160,256]{1,0:T(8,128)(2,1)S(1)} %collective-permute-done.4.first, bf16[160,256]{1,0:T(8,128)(2,1)S(1)} %collective-permute-done.5.second), custom_call_target="tpu_custom_call" | custom-call | flops 2621440 | bytes 245792 | tf_op jit(solution)/shard_map/pallas_call | solution.py:298
  45.3 1.6 %collective-permute-start.7 = (f32[16,256]{1,0:T(8,128)S(1)}, f32[16,256]{1,0:T(8,128)S(1)}, u32[]{:S(2)}, u32[]{:S(2)}) collective-permute-start(f32[16,256]{1,0:T(8,128)S(1)} %shard_map.196.own), channel_id=1, source_target_pairs={{0,2},{1,3},{2,0},{3,1},{4,6},{5,7},{6,4},{7,5},{8,10},{9,11},{10,... | collective-permute-start | bytes 49160 | tf_op jit(solution)/shard_map/ppermute | solution.py:741
  47.0 1.3 %collective-permute-done.8.three = f32[16,256]{1,0:T(8,128)S(1)} collective-permute-done((f32[16,256]{1,0:T(8,128)S(1)}, f32[16,256]{1,0:T(8,128)S(1)}, u32[]{:S(2)}, u32[]{:S(2)}) %collective-permute-start.8) | collective-permute-done | bytes 16416 | tf_op jit(solution)/shard_map/ppermute | solution.py:741
  48.3 0.7 collective-permute-done.7.two
  49.0 1.0 %shard_map.197 = (bf16[8,16,768]{2,1,0:T(8,128)(2,1)S(1)}, bf16[16,256]{1,0:T(8,128)(2,1)S(1)}) custom-call(f32[1,2048]{1,0:T(1,128)} %bitcast.8, f32[16,256]{1,0:T(8,128)S(1)} %shard_map.196.own, f32[16,256]{1,0:T(8,128)S(1)} %collective-permute-done.6.one, f32[16,256]{1,0:T(8,128)S(1)} %collective-permute-done.7.two, ...), custom_call_target="tpu_custom_call" | custom-call | flops 20971520 | bytes 1597440 | tf_op jit(solution)/shard_map/pallas_call | solution.py:298
  50.1 10.3 %all_to_all.21.came = bf16[8,16,768]{2,1,0:T(8,128)(2,1)S(1)} all-to-all(bf16[8,16,768]{2,1,0:T(8,128)(2,1)S(1)} %get-tuple-element.43), channel_id=1, replica_groups=mesh['req'=8,'head'=4] {'req'}, dimensions={0} | all-to-all | bytes 393216 | tf_op jit(solution)/shard_map/all_to_all | solution.py:84
  60.6 1.6 %collective-permute-start.10 = (bf16[16,320]{1,0:T(8,128)(2,1)S(1)}, bf16[16,320]{1,0:T(8,128)(2,1)S(1)}, u32[]{:S(2)}, u32[]{:S(2)}) collective-permute-start(bf16[16,320]{1,0:T(8,128)(2,1)S(1)} %shard_map.198.own), channel_id=1, source_target_pairs={{0,2},{1,3},{2,0},{3,1},{4,6},{5,7},{6,4},{7,5},{8,10},{9,11},{10,... | collective-permute-start | bytes 30728 | tf_op jit(solution)/shard_map/ppermute | solution.py:741
  62.4 1.3 %collective-permute-done.11.three = bf16[16,320]{1,0:T(8,128)(2,1)S(1)} collective-permute-done((bf16[16,320]{1,0:T(8,128)(2,1)S(1)}, bf16[16,320]{1,0:T(8,128)(2,1)S(1)}, u32[]{:S(2)}, u32[]{:S(2)}) %collective-permute-start.11) | collective-permute-done | bytes 10272 | tf_op jit(solution)/shard_map/ppermute | solution.py:741
  63.7 0.6 collective-permute-done.10.two
  64.5 10.6 %all_to_all.22.came = bf16[8,16,512]{2,1,0:T(8,128)(2,1)S(1)} all-to-all(bf16[8,16,512]{2,1,0:T(8,128)(2,1)S(1)} %shard_map.199), channel_id=1, replica_groups=mesh['req'=8,'head'=4] {'req'}, dimensions={0} | all-to-all | bytes 262144 | tf_op jit(solution)/shard_map/all_to_all | solution.py:84
  75.2 0.6 shard_map.200
  (17 shorter events, 1.3 us)
Async XLA Ops:
  0.6 4.9 %copy-start.1 = (bf16[16,512]{1,0:T(8,128)(2,1)S(1)}, bf16[16,512]{1,0:T(8,128)(2,1)}, u32[]{:S(2)}) copy-start(bf16[16,512]{1,0:T(8,128)(2,1)} %hidden_far.1) | copy-start | bytes 49156
  5.0 21.6 %collective-permute-start.3 = (bf16[256,1280]{1,0:T(8,128)(2,1)S(1)}, bf16[256,1280]{1,0:T(8,128)(2,1)S(1)}, u32[]{:S(2)}, u32[]{:S(2)}) collective-permute-start(bf16[256,1280]{1,0:T(8,128)(2,1)S(1)} %get-tuple-element.31), channel_id=1, source_target_pairs={{0,1},{1,0},{2,3},{3,2},{4,5},{5,4},{6,7},{7,6},{8,9},{9,8},{10,11... | collective-permute-start | bytes 1966088 | tf_op jit(solution)/shard_map/ppermute | solution.py:741
  5.5 4.3 %collective-permute-start.1 = (bf16[16,512]{1,0:T(8,128)(2,1)S(1)}, bf16[16,512]{1,0:T(8,128)(2,1)S(1)}, u32[]{:S(2)}, u32[]{:S(2)}) collective-permute-start(bf16[16,512]{1,0:T(8,128)(2,1)S(1)} %copy-done.1), channel_id=1, source_target_pairs={{0,2},{1,3},{2,0},{3,1},{4,6},{5,7},{6,4},{7,5},{8,10},{9,11},{10,... | collective-permute-start | bytes 49160 | tf_op jit(solution)/shard_map/ppermute | solution.py:741
  8.1 1.7 %collective-permute-start = (bf16[16,512]{1,0:T(8,128)(2,1)S(1)}, bf16[16,512]{1,0:T(8,128)(2,1)S(1)}, u32[]{:S(2)}, u32[]{:S(2)}) collective-permute-start(bf16[16,512]{1,0:T(8,128)(2,1)S(1)} %copy-done.1), channel_id=1, source_target_pairs={{0,1},{1,0},{2,3},{3,2},{4,5},{5,4},{6,7},{7,6},{8,9},{9,8},{10,11... | collective-permute-start | bytes 49160 | tf_op jit(solution)/shard_map/ppermute | solution.py:741
  8.3 3.2 %collective-permute-start.2 = (bf16[16,512]{1,0:T(8,128)(2,1)S(1)}, bf16[16,512]{1,0:T(8,128)(2,1)S(1)}, u32[]{:S(2)}, u32[]{:S(2)}) collective-permute-start(bf16[16,512]{1,0:T(8,128)(2,1)S(1)} %copy-done.1), channel_id=1, source_target_pairs={{0,3},{1,2},{2,1},{3,0},{4,7},{5,6},{6,5},{7,4},{8,11},{9,10},{10,... | collective-permute-start | bytes 49160 | tf_op jit(solution)/shard_map/ppermute | solution.py:741
  13.4 13.2 %all-to-all-start = ((f32[32,8,128]{2,1,0:T(8,128)}), f32[32,8,128]{2,1,0:T(8,128)S(1)}, u32[]{:S(2)}, u32[]{:S(2)}) async-start(f32[32,8,128]{2,1,0:T(8,128)} %get-tuple-element.30), calls=%async_computation | async-start | bytes 262144 | tf_op jit(solution)/shard_map/all_to_all | solution.py:852
  18.3 2.5 %collective-permute-start.4 = (bf16[160,256]{1,0:T(8,128)(2,1)S(1)}, bf16[160,256]{1,0:T(8,128)(2,1)S(1)}, u32[]{:S(2)}, u32[]{:S(2)}) collective-permute-start(bf16[160,256]{1,0:T(8,128)(2,1)S(1)} %get-tuple-element.32), channel_id=1, source_target_pairs={{0,0},{1,8},{2,16},{3,24},{4,4},{5,12},{6,20},{7,28},{8,1},{9,9},{... | collective-permute-start | bytes 245768 | tf_op jit(solution)/shard_map/ppermute | solution.py:757
  19.0 4.9 %collective-permute-start.5 = (bf16[160,256]{1,0:T(8,128)(2,1)S(1)}, bf16[160,256]{1,0:T(8,128)(2,1)S(1)}, u32[]{:S(2)}, u32[]{:S(2)}) collective-permute-start(bf16[160,256]{1,0:T(8,128)(2,1)S(1)} %get-tuple-element.33), channel_id=1, source_target_pairs={{0,4},{1,12},{2,20},{3,28},{4,0},{5,8},{6,16},{7,24},{8,5},{9,13},... | collective-permute-start | bytes 245768 | tf_op jit(solution)/shard_map/ppermute | solution.py:757
  27.7 36.6 %copy-start = (bf16[640,512]{1,0:T(8,128)(2,1)S(1)}, bf16[640,512]{1,0:T(8,128)(2,1)}, u32[]{:S(2)}) copy-start(bf16[640,512]{1,0:T(8,128)(2,1)} %weight.1) | copy-start | bytes 1966084
  45.1 3.2 %collective-permute-start.8 = (f32[16,256]{1,0:T(8,128)S(1)}, f32[16,256]{1,0:T(8,128)S(1)}, u32[]{:S(2)}, u32[]{:S(2)}) collective-permute-start(f32[16,256]{1,0:T(8,128)S(1)} %shard_map.196.own), channel_id=1, source_target_pairs={{0,3},{1,2},{2,1},{3,0},{4,7},{5,6},{6,5},{7,4},{8,11},{9,10},{10,... | collective-permute-start | bytes 49160 | tf_op jit(solution)/shard_map/ppermute | solution.py:741
  45.3 3.7 %collective-permute-start.7 = (f32[16,256]{1,0:T(8,128)S(1)}, f32[16,256]{1,0:T(8,128)S(1)}, u32[]{:S(2)}, u32[]{:S(2)}) collective-permute-start(f32[16,256]{1,0:T(8,128)S(1)} %shard_map.196.own), channel_id=1, source_target_pairs={{0,2},{1,3},{2,0},{3,1},{4,6},{5,7},{6,4},{7,5},{8,10},{9,11},{10,... | collective-permute-start | bytes 49160 | tf_op jit(solution)/shard_map/ppermute | solution.py:741
  46.9 2.1 %collective-permute-start.6 = (f32[16,256]{1,0:T(8,128)S(1)}, f32[16,256]{1,0:T(8,128)S(1)}, u32[]{:S(2)}, u32[]{:S(2)}) collective-permute-start(f32[16,256]{1,0:T(8,128)S(1)} %shard_map.196.own), channel_id=1, source_target_pairs={{0,1},{1,0},{2,3},{3,2},{4,5},{5,4},{6,7},{7,6},{8,9},{9,8},{10,11... | collective-permute-start | bytes 49160 | tf_op jit(solution)/shard_map/ppermute | solution.py:741
  60.5 3.2 %collective-permute-start.11 = (bf16[16,320]{1,0:T(8,128)(2,1)S(1)}, bf16[16,320]{1,0:T(8,128)(2,1)S(1)}, u32[]{:S(2)}, u32[]{:S(2)}) collective-permute-start(bf16[16,320]{1,0:T(8,128)(2,1)S(1)} %shard_map.198.own), channel_id=1, source_target_pairs={{0,3},{1,2},{2,1},{3,0},{4,7},{5,6},{6,5},{7,4},{8,11},{9,10},{10,... | collective-permute-start | bytes 30728 | tf_op jit(solution)/shard_map/ppermute | solution.py:741
  60.6 3.8 %collective-permute-start.10 = (bf16[16,320]{1,0:T(8,128)(2,1)S(1)}, bf16[16,320]{1,0:T(8,128)(2,1)S(1)}, u32[]{:S(2)}, u32[]{:S(2)}) collective-permute-start(bf16[16,320]{1,0:T(8,128)(2,1)S(1)} %shard_map.198.own), channel_id=1, source_target_pairs={{0,2},{1,3},{2,0},{3,1},{4,6},{5,7},{6,4},{7,5},{8,10},{9,11},{10,... | collective-permute-start | bytes 30728 | tf_op jit(solution)/shard_map/ppermute | solution.py:741
  62.1 2.2 %collective-permute-start.9 = (bf16[16,320]{1,0:T(8,128)(2,1)S(1)}, bf16[16,320]{1,0:T(8,128)(2,1)S(1)}, u32[]{:S(2)}, u32[]{:S(2)}) collective-permute-start(bf16[16,320]{1,0:T(8,128)(2,1)S(1)} %shard_map.198.own), channel_id=1, source_target_pairs={{0,1},{1,0},{2,3},{3,2},{4,5},{5,4},{6,7},{7,6},{8,9},{9,8},{10,11... | collective-permute-start | bytes 30728 | tf_op jit(solution)/shard_map/ppermute | solution.py:741

commit v17 on v13

--- a/solution.py
+++ b/solution.py
@@ -389,12 +389,12 @@
 
 
 def prepare_kernel(*refs):
-    far, refs = refs[:12], refs[12:]
-    (compact, summaries, kept, added, tables, mine, theirs), refs = refs[:7], refs[7:]
-    near, (ordered, plain, dealt, done) = refs[:12], refs[12:]
+    far, refs = refs[:10], refs[10:]
+    (compact, summaries, kept, added, tables), refs = refs[:5], refs[5:]
+    near, (ordered, plain, done) = refs[:10], refs[10:]
     copies = fetch(far, near, done)
     (dest, lengths, source, table, keep, weights, query_gain, key_gain, turns) = near[:9]
-    pages, gate, up = near[9:]
+    pages = near[9]
     group = lax.axis_index("req")
     lane = lax.axis_index("head")
     lanes = lax.axis_size("head")
@@ -475,7 +475,9 @@
     kept[entries:, :] = plain[...].astype(bfloat)
     summaries[...] = ordered[...].astype(bfloat)
 
-    for copy in copies[10:]:
+
+def deal_kernel(gate_far, up_far, mine, theirs, gate, up, dealt, done):
+    for copy in fetch((gate_far, up_far), (gate, up), done):
         copy.wait()
     block = gate.shape[1] // 2
     piece = block // 2
@@ -485,8 +487,9 @@
             start = b * block
             dealt[k, :, start : start + piece] = gate[:, columns].astype(single)
             dealt[k, :, start + piece : start + block] = up[:, columns].astype(single)
-    mine[...] = dealt[lane & 1].astype(bfloat)
-    theirs[...] = dealt[1 - (lane & 1)].astype(bfloat)
+    core = lax.axis_index("head") & 1
+    mine[...] = dealt[core].astype(bfloat)
+    theirs[...] = dealt[1 - core].astype(bfloat)
 
 
 def attend_kernel(came, kept, added, tables, sent, x, extra_k, extra_v, out, logs):
@@ -806,12 +809,10 @@
         key_gain[None, :],
         rotation_table(),
         old_cache,
-        gate_weight,
-        up_weight,
     ]
     entries = pages_here * KEEP
     extras = 16
-    compact, summaries, kept, added, tables, mine, theirs = run(
+    compact, summaries, kept, added, tables = run(
         prepare_kernel,
         [
             shaped((pages_here // 2, PAGE, KVW), bfloat),
@@ -819,8 +820,6 @@
             shaped((entries + extras, KVW), bfloat),
             shaped((8, entries + TILE), single),
             shaped((96, TILE), single),
-            shaped(gate_weight.shape, bfloat),
-            shaped(gate_weight.shape, bfloat),
         ],
         scalars + arrays,
         [],
@@ -829,7 +828,6 @@
             *local_like(*arrays),
             pltpu.VMEM((pages_here, KVW), single),
             pltpu.VMEM((extras, KVW), single),
-            pltpu.VMEM((2,) + gate_weight.shape, single),
             copies((len(scalars + arrays),)),
         ],
         2 * pages_here * TILE * PAGE * KVW,
@@ -861,9 +859,18 @@
         2 * requests * features * columns,
     )
     came = lax.all_to_all(sent, both_axes, 0, 0, tiled=True)
-    theirs, _ = lax.optimization_barrier((theirs, sent))
-    theirs = swapped_lanes(theirs, 1)
-    came, theirs = lax.optimization_barrier((came, theirs))
+    gates, _ = lax.optimization_barrier((gate_weight, sent))
+    mine, theirs = run(
+        deal_kernel,
+        [shaped(gate_weight.shape, bfloat)] * 2,
+        [gates, up_weight],
+        [],
+        [
+            *local_like(gate_weight, up_weight),
+            pltpu.VMEM((2,) + gate_weight.shape, single),
+            copies((2,)),
+        ],
+    )
     span = -(-KVH * HD // TILE) * TILE
     (parts,) = run(
         attend_kernel,
@@ -879,7 +886,10 @@
         ],
         6 * 48 * entries * span,
     )
+    theirs, _ = lax.optimization_barrier((theirs, parts))
+    theirs = swapped_lanes(theirs, 1)
     came = lax.all_to_all(parts, both_axes, 0, 0, tiled=True)
+    came, theirs = lax.optimization_barrier((came, theirs))
     (sent,) = run(
         project_kernel,
         [shaped((requests, features), single)],

time: 72.9 us -> 73.7 us (1.011)
  blocking collectives: 42.9 us -> 30 us
  waiting for transfers between devices: 3.93 us -> 10.1 us
  starting transfers between devices: 14.2 us -> 19.1 us
  Pallas kernels: 10.6 us -> 13.3 us
    all_to_all x1 -> x0, blocking collectives: 12.8 us -> none  [on_device(): came = lax.all_to_all(sent, both_axes, 0, 0, tiled=True)]
    all_to_all x0 -> x1, waiting for transfers between devices: none -> 6.19 us  [on_device(): came = lax.all_to_all(sent, both_axes, 0, 0, tiled=True)]
    all_to_all x0 -> x1, starting transfers between devices: none -> 5.07 us  [on_device(): came = lax.all_to_all(sent, both_axes, 0, 0, tiled=True)]
    pallas_call x9 -> x10, Pallas kernels: 10.6 us -> 13.3 us  [run(): pl.pallas_call(kernel, out_shape=list(outs), in_specs=in_specs, out_specs...]
  transfers between devices with their start and end apart: 12 -> 13, of which waited for: 4 -> 5; matrix products, arithmetic and copies ran while one was open for 0% -> 0% of each run, Pallas kernels for 6% -> 9%
where the time goes in v17:
time: 73.7 us; the launch traced here: 73.2 us
  blocking collectives  30 us (41%)
  starting transfers between devices  19.1 us (26%)
  Pallas kernels  13.3 us (18%)
  waiting for transfers between devices  10.1 us (14%)
  between operations  0.77 us (1%)
    all_to_all x2, blocking collectives, exchange(): return lax.all_to_all(parts, 'req', split_axis=0, concat_axis=0, tiled=True)  20.9 us
    pallas_call x10, Pallas kernels, run(): pl.pallas_call(kernel, out_shape=list(outs), in_specs=in_specs, out_specs...  13.3 us
    ppermute x10, starting transfers between devices, swapped_lanes(): return lax.ppermute(value, 'head', [(k, k ^ turn) for k in range(lanes)])  10.3 us
    all_to_all x1, blocking collectives, on_device(): came = lax.all_to_all(parts, both_axes, 0, 0, tiled=True)  9.09 us
    all_to_all x1, waiting for transfers between devices, on_device(): came = lax.all_to_all(sent, both_axes, 0, 0, tiled=True)  6.19 us
    all_to_all x1, starting transfers between devices, on_device(): came = lax.all_to_all(sent, both_axes, 0, 0, tiled=True)  5.07 us
    ppermute x10, waiting for transfers between devices, swapped_lanes(): return lax.ppermute(value, 'head', [(k, k ^ turn) for k in range(lanes)])  3.92 us
    ppermute x2, starting transfers between devices, handed_over(): return lax.ppermute(value, both_axes, pairs)  3.7 us
  transfers between devices with their start and end apart: 13, of which 5 were waited for; matrix products, arithmetic and copies ran while one was open for 0% of the time, Pallas kernels for 9%

profile of v17, /device:TPU:0, one launch (start us, length us, event | category | flops | bytes accessed | tf_op | source)
XLA Modules:
  0.0 73.2 jit_solution(14649287588508872510)
XLA Ops:
  0.6 1.0 %shard_map.194 = (bf16[160,256]{1,0:T(8,128)(2,1)S(1)}, bf16[160,256]{1,0:T(8,128)(2,1)S(1)}) custom-call(bf16[160,512]{1,0:T(8,128)(2,1)} %weight_far.1), custom_call_target="tpu_custom_call" | custom-call | bytes 327680 | tf_op jit(solution)/shard_map/pallas_call | solution.py:298
  1.6 0.7 collective-permute-start.3
  2.3 3.0 %collective-permute-start.4 = (bf16[160,256]{1,0:T(8,128)(2,1)S(1)}, bf16[160,256]{1,0:T(8,128)(2,1)S(1)}, u32[]{:S(2)}, u32[]{:S(2)}) collective-permute-start(bf16[160,256]{1,0:T(8,128)(2,1)S(1)} %get-tuple-element.30), channel_id=1, source_target_pairs={{0,4},{1,12},{2,20},{3,28},{4,0},{5,8},{6,16},{7,24},{8,5},{9,13},... | collective-permute-start | bytes 245768 | tf_op jit(solution)/shard_map/ppermute | solution.py:765
  5.3 6.0 %collective-permute-start.1 = (bf16[16,512]{1,0:T(8,128)(2,1)}, bf16[16,512]{1,0:T(8,128)(2,1)S(1)}, u32[]{:S(2)}, u32[]{:S(2)}) collective-permute-start(bf16[16,512]{1,0:T(8,128)(2,1)} %hidden_far.1), channel_id=1, source_target_pairs={{0,2},{1,3},{2,0},{3,1},{4,6},{5,7},{6,4},{7,5},{8,10},{9,11},{10,... | collective-permute-start | bytes 49160 | tf_op jit(solution)/shard_map/ppermute | solution.py:749
  11.5 4.3 %shard_map.193 = (bf16[4,128,640]{2,1,0:T(8,128)(2,1)}, bf16[8,640]{1,0:T(8,128)(2,1)}, bf16[528,640]{1,0:T(8,128)(2,1)S(1)}, f32[8,640]{1,0:T(8,128)S(1)}, f32[96,128]{1,0:T(8,128)S(1)}) custom-call(s32[1,8]{1,0:T(1,128)} %refs_0_.1, s32[1,16]{1,0:T(1,128)} %bitcast.13, s32[1,8]{1,0:T(1,128)} %bitcast.10, s32[2,16]{1,0:T(2,128)} %refs_3_.1, ...), custom_call_target="tpu_custom_call" | custom-call | flops 167772160 | bytes 2753280 | tf_op jit(solution)/shard_map/pallas_call | solution.py:298
  15.8 1.9 %shard_map.195 = (f32[32,8,128]{2,1,0:T(8,128)}, bf16[16,256]{1,0:T(8,128)(2,1)S(1)}) custom-call(s32[1,8]{1,0:T(1,128)} %bitcast.11, f32[1,2048]{1,0:T(1,128)} %bitcast.9, bf16[480,256]{1,0:T(8,128)(2,1)} %bitcast.7, bf16[16,512]{1,0:T(8,128)(2,1)} %hidden_far.1, bf16[16,512]{1,0:T(8,128)(2,1)S(1)} %collective-permute-done.one, ...), custom_call_target="tpu_custom_call" | custom-call | flops 3932160 | bytes 458784 | tf_op jit(solution)/shard_map/pallas_call | solution.py:298
  17.7 5.1 %all-to-all-start = ((f32[32,8,128]{2,1,0:T(8,128)}), f32[32,8,128]{2,1,0:T(8,128)S(1)}, u32[]{:S(2)}, u32[]{:S(2)}) async-start(f32[32,8,128]{2,1,0:T(8,128)} %get-tuple-element.34), calls=%async_computation | async-start | bytes 262144 | tf_op jit(solution)/shard_map/all_to_all | solution.py:861
  22.8 2.0 %shard_map.197 = (bf16[256,1280]{1,0:T(8,128)(2,1)S(1)}, bf16[256,1280]{1,0:T(8,128)(2,1)S(1)}) custom-call(bf16[256,1280]{1,0:T(8,128)(2,1)} %gate_far, bf16[256,1280]{1,0:T(8,128)(2,1)} %up_far.1), custom_call_target="tpu_custom_call" | custom-call | bytes 2621440 | tf_op jit(solution)/shard_map/pallas_call | solution.py:298
  24.9 6.2 %all-to-all-done.came = f32[32,8,128]{2,1,0:T(8,128)S(1)} async-done(((f32[32,8,128]{2,1,0:T(8,128)}), f32[32,8,128]{2,1,0:T(8,128)S(1)}, u32[]{:S(2)}, u32[]{:S(2)}) %all-to-all-start) | async-done | bytes 131104 | tf_op jit(solution)/shard_map/all_to_all | solution.py:861
  31.1 1.1 %shard_map.196 = bf16[32,8,128]{2,1,0:T(8,128)(2,1)S(1)} custom-call(f32[32,8,128]{2,1,0:T(8,128)S(1)} %all-to-all-done.came, bf16[528,640]{1,0:T(8,128)(2,1)S(1)} %get-tuple-element.35.kept, f32[8,640]{1,0:T(8,128)S(1)} %get-tuple-element.36.added, f32[96,128]{1,0:T(8,128)S(1)} %get-tuple-element.37.tables), custom_call_target="tpu_custom_call" | custom-call | flops 56623104 | bytes 942080 | tf_op jit(solution)/shard_map/pallas_call | solution.py:298
  32.2 0.3 collective-permute-start.5
  32.4 9.1 %all_to_all.20.came = bf16[32,8,128]{2,1,0:T(8,128)(2,1)S(1)} all-to-all(bf16[32,8,128]{2,1,0:T(8,128)(2,1)S(1)} %shard_map.196), channel_id=1, replica_groups=mesh['req'=8,'head'=4] {'req','head'}, dimensions={0} | all-to-all | bytes 131072 | tf_op jit(solution)/shard_map/all_to_all | solution.py:891
  41.5 1.0 %shard_map.198.own = f32[16,256]{1,0:T(8,128)S(1)} custom-call(s32[1,8]{1,0:T(1,128)} %bitcast.12, bf16[32,8,128]{2,1,0:T(8,128)(2,1)S(1)} %all_to_all.20.came, bf16[160,256]{1,0:T(8,128)(2,1)S(1)} %collective-permute-done.3.first, bf16[160,256]{1,0:T(8,128)(2,1)S(1)} %collective-permute-done.4.second), custom_call_target="tpu_custom_call" | custom-call | flops 2621440 | bytes 245792 | tf_op jit(solution)/shard_map/pallas_call | solution.py:298
  42.8 1.6 %collective-permute-start.7 = (f32[16,256]{1,0:T(8,128)S(1)}, f32[16,256]{1,0:T(8,128)S(1)}, u32[]{:S(2)}, u32[]{:S(2)}) collective-permute-start(f32[16,256]{1,0:T(8,128)S(1)} %shard_map.198.own), channel_id=1, source_target_pairs={{0,2},{1,3},{2,0},{3,1},{4,6},{5,7},{6,4},{7,5},{8,10},{9,11},{10,... | collective-permute-start | bytes 49160 | tf_op jit(solution)/shard_map/ppermute | solution.py:749
  44.5 1.3 %collective-permute-done.8.three = f32[16,256]{1,0:T(8,128)S(1)} collective-permute-done((f32[16,256]{1,0:T(8,128)S(1)}, f32[16,256]{1,0:T(8,128)S(1)}, u32[]{:S(2)}, u32[]{:S(2)}) %collective-permute-start.8) | collective-permute-done | bytes 16416 | tf_op jit(solution)/shard_map/ppermute | solution.py:749
  45.8 0.7 collective-permute-done.7.two
  46.5 1.0 %shard_map.199 = (bf16[8,16,768]{2,1,0:T(8,128)(2,1)S(1)}, bf16[16,256]{1,0:T(8,128)(2,1)S(1)}) custom-call(f32[1,2048]{1,0:T(1,128)} %bitcast.8, f32[16,256]{1,0:T(8,128)S(1)} %shard_map.198.own, f32[16,256]{1,0:T(8,128)S(1)} %collective-permute-done.6.one, f32[16,256]{1,0:T(8,128)S(1)} %collective-permute-done.7.two, ...), custom_call_target="tpu_custom_call" | custom-call | flops 20971520 | bytes 1597440 | tf_op jit(solution)/shard_map/pallas_call | solution.py:298
  47.5 10.3 %all_to_all.21.came = bf16[8,16,768]{2,1,0:T(8,128)(2,1)S(1)} all-to-all(bf16[8,16,768]{2,1,0:T(8,128)(2,1)S(1)} %get-tuple-element.47), channel_id=1, replica_groups=mesh['req'=8,'head'=4] {'req'}, dimensions={0} | all-to-all | bytes 393216 | tf_op jit(solution)/shard_map/all_to_all | solution.py:84
  58.0 1.6 %collective-permute-start.10 = (bf16[16,320]{1,0:T(8,128)(2,1)S(1)}, bf16[16,320]{1,0:T(8,128)(2,1)S(1)}, u32[]{:S(2)}, u32[]{:S(2)}) collective-permute-start(bf16[16,320]{1,0:T(8,128)(2,1)S(1)} %shard_map.200.own), channel_id=1, source_target_pairs={{0,2},{1,3},{2,0},{3,1},{4,6},{5,7},{6,4},{7,5},{8,10},{9,11},{10,... | collective-permute-start | bytes 30728 | tf_op jit(solution)/shard_map/ppermute | solution.py:749
  59.6 0.3 collective-permute-start.9
  59.8 1.3 %collective-permute-done.11.three = bf16[16,320]{1,0:T(8,128)(2,1)S(1)} collective-permute-done((bf16[16,320]{1,0:T(8,128)(2,1)S(1)}, bf16[16,320]{1,0:T(8,128)(2,1)S(1)}, u32[]{:S(2)}, u32[]{:S(2)}) %collective-permute-start.11) | collective-permute-done | bytes 10272 | tf_op jit(solution)/shard_map/ppermute | solution.py:749
  61.1 0.6 collective-permute-done.10.two
  62.0 10.6 %all_to_all.22.came = bf16[8,16,512]{2,1,0:T(8,128)(2,1)S(1)} all-to-all(bf16[8,16,512]{2,1,0:T(8,128)(2,1)S(1)} %shard_map.201), channel_id=1, replica_groups=mesh['req'=8,'head'=4] {'req'}, dimensions={0} | all-to-all | bytes 262144 | tf_op jit(solution)/shard_map/all_to_all | solution.py:84
  72.6 0.6 shard_map.202
  (17 shorter events, 1.0 us)
Async XLA Ops:
  1.6 14.2 %collective-permute-start.3 = (bf16[160,256]{1,0:T(8,128)(2,1)S(1)}, bf16[160,256]{1,0:T(8,128)(2,1)S(1)}, u32[]{:S(2)}, u32[]{:S(2)}) collective-permute-start(bf16[160,256]{1,0:T(8,128)(2,1)S(1)} %get-tuple-element.29), channel_id=1, source_target_pairs={{0,0},{1,8},{2,16},{3,24},{4,4},{5,12},{6,20},{7,28},{8,1},{9,9},{... | collective-permute-start | bytes 245768 | tf_op jit(solution)/shard_map/ppermute | solution.py:765
  2.3 13.5 %collective-permute-start.4 = (bf16[160,256]{1,0:T(8,128)(2,1)S(1)}, bf16[160,256]{1,0:T(8,128)(2,1)S(1)}, u32[]{:S(2)}, u32[]{:S(2)}) collective-permute-start(bf16[160,256]{1,0:T(8,128)(2,1)S(1)} %get-tuple-element.30), channel_id=1, source_target_pairs={{0,4},{1,12},{2,20},{3,28},{4,0},{5,8},{6,16},{7,24},{8,5},{9,13},... | collective-permute-start | bytes 245768 | tf_op jit(solution)/shard_map/ppermute | solution.py:765
  5.3 10.5 %collective-permute-start.1 = (bf16[16,512]{1,0:T(8,128)(2,1)}, bf16[16,512]{1,0:T(8,128)(2,1)S(1)}, u32[]{:S(2)}, u32[]{:S(2)}) collective-permute-start(bf16[16,512]{1,0:T(8,128)(2,1)} %hidden_far.1), channel_id=1, source_target_pairs={{0,2},{1,3},{2,0},{3,1},{4,6},{5,7},{6,4},{7,5},{8,10},{9,11},{10,... | collective-permute-start | bytes 49160 | tf_op jit(solution)/shard_map/ppermute | solution.py:749
  11.3 4.5 %collective-permute-start = (bf16[16,512]{1,0:T(8,128)(2,1)}, bf16[16,512]{1,0:T(8,128)(2,1)S(1)}, u32[]{:S(2)}, u32[]{:S(2)}) collective-permute-start(bf16[16,512]{1,0:T(8,128)(2,1)} %hidden_far.1), channel_id=1, source_target_pairs={{0,1},{1,0},{2,3},{3,2},{4,5},{5,4},{6,7},{7,6},{8,9},{9,8},{10,11... | collective-permute-start | bytes 49160 | tf_op jit(solution)/shard_map/ppermute | solution.py:749
  11.5 4.3 %collective-permute-start.2 = (bf16[16,512]{1,0:T(8,128)(2,1)}, bf16[16,512]{1,0:T(8,128)(2,1)S(1)}, u32[]{:S(2)}, u32[]{:S(2)}) collective-permute-start(bf16[16,512]{1,0:T(8,128)(2,1)} %hidden_far.1), channel_id=1, source_target_pairs={{0,3},{1,2},{2,1},{3,0},{4,7},{5,6},{6,5},{7,4},{8,11},{9,10},{10,... | collective-permute-start | bytes 49160 | tf_op jit(solution)/shard_map/ppermute | solution.py:749
  17.7 13.3 %all-to-all-start = ((f32[32,8,128]{2,1,0:T(8,128)}), f32[32,8,128]{2,1,0:T(8,128)S(1)}, u32[]{:S(2)}, u32[]{:S(2)}) async-start(f32[32,8,128]{2,1,0:T(8,128)} %get-tuple-element.34), calls=%async_computation | async-start | bytes 262144 | tf_op jit(solution)/shard_map/all_to_all | solution.py:861
  32.1 29.6 %copy-start = (bf16[640,512]{1,0:T(8,128)(2,1)S(1)}, bf16[640,512]{1,0:T(8,128)(2,1)}, u32[]{:S(2)}) copy-start(bf16[640,512]{1,0:T(8,128)(2,1)} %weight.1) | copy-start | bytes 1966084
  32.2 9.4 %collective-permute-start.5 = (bf16[256,1280]{1,0:T(8,128)(2,1)S(1)}, bf16[256,1280]{1,0:T(8,128)(2,1)S(1)}, u32[]{:S(2)}, u32[]{:S(2)}) collective-permute-start(bf16[256,1280]{1,0:T(8,128)(2,1)S(1)} %get-tuple-element.40), channel_id=1, source_target_pairs={{0,1},{1,0},{2,3},{3,2},{4,5},{5,4},{6,7},{7,6},{8,9},{9,8},{10,11... | collective-permute-start | bytes 1966088 | tf_op jit(solution)/shard_map/ppermute | solution.py:749
  42.5 3.2 %collective-permute-start.8 = (f32[16,256]{1,0:T(8,128)S(1)}, f32[16,256]{1,0:T(8,128)S(1)}, u32[]{:S(2)}, u32[]{:S(2)}) collective-permute-start(f32[16,256]{1,0:T(8,128)S(1)} %shard_map.198.own), channel_id=1, source_target_pairs={{0,3},{1,2},{2,1},{3,0},{4,7},{5,6},{6,5},{7,4},{8,11},{9,10},{10,... | collective-permute-start | bytes 49160 | tf_op jit(solution)/shard_map/ppermute | solution.py:749
  42.8 3.7 %collective-permute-start.7 = (f32[16,256]{1,0:T(8,128)S(1)}, f32[16,256]{1,0:T(8,128)S(1)}, u32[]{:S(2)}, u32[]{:S(2)}) collective-permute-start(f32[16,256]{1,0:T(8,128)S(1)} %shard_map.198.own), channel_id=1, source_target_pairs={{0,2},{1,3},{2,0},{3,1},{4,6},{5,7},{6,4},{7,5},{8,10},{9,11},{10,... | collective-permute-start | bytes 49160 | tf_op jit(solution)/shard_map/ppermute | solution.py:749
  44.3 2.1 %collective-permute-start.6 = (f32[16,256]{1,0:T(8,128)S(1)}, f32[16,256]{1,0:T(8,128)S(1)}, u32[]{:S(2)}, u32[]{:S(2)}) collective-permute-start(f32[16,256]{1,0:T(8,128)S(1)} %shard_map.198.own), channel_id=1, source_target_pairs={{0,1},{1,0},{2,3},{3,2},{4,5},{5,4},{6,7},{7,6},{8,9},{9,8},{10,11... | collective-permute-start | bytes 49160 | tf_op jit(solution)/shard_map/ppermute | solution.py:749
  57.9 3.2 %collective-permute-start.11 = (bf16[16,320]{1,0:T(8,128)(2,1)S(1)}, bf16[16,320]{1,0:T(8,128)(2,1)S(1)}, u32[]{:S(2)}, u32[]{:S(2)}) collective-permute-start(bf16[16,320]{1,0:T(8,128)(2,1)S(1)} %shard_map.200.own), channel_id=1, source_target_pairs={{0,3},{1,2},{2,1},{3,0},{4,7},{5,6},{6,5},{7,4},{8,11},{9,10},{10,... | collective-permute-start | bytes 30728 | tf_op jit(solution)/shard_map/ppermute | solution.py:749
  58.0 3.8 %collective-permute-start.10 = (bf16[16,320]{1,0:T(8,128)(2,1)S(1)}, bf16[16,320]{1,0:T(8,128)(2,1)S(1)}, u32[]{:S(2)}, u32[]{:S(2)}) collective-permute-start(bf16[16,320]{1,0:T(8,128)(2,1)S(1)} %shard_map.200.own), channel_id=1, source_target_pairs={{0,2},{1,3},{2,0},{3,1},{4,6},{5,7},{6,4},{7,5},{8,10},{9,11},{10,... | collective-permute-start | bytes 30728 | tf_op jit(solution)/shard_map/ppermute | solution.py:749
  59.6 2.2 %collective-permute-start.9 = (bf16[16,320]{1,0:T(8,128)(2,1)S(1)}, bf16[16,320]{1,0:T(8,128)(2,1)S(1)}, u32[]{:S(2)}, u32[]{:S(2)}) collective-permute-start(bf16[16,320]{1,0:T(8,128)(2,1)S(1)} %shard_map.200.own), channel_id=1, source_target_pairs={{0,1},{1,0},{2,3},{3,2},{4,5},{5,4},{6,7},{7,6},{8,9},{9,8},{10,11... | collective-permute-start | bytes 30728 | tf_op jit(solution)/shard_map/ppermute | solution.py:749

commit v18 on v14

--- a/solution.py
+++ b/solution.py
@@ -851,8 +851,6 @@
         ],
         2 * pages_here * TILE * PAGE * KVW,
     )
-    theirs = swapped_lanes(theirs, 1)
-    came, theirs = lax.optimization_barrier((came, theirs))
     span = -(-KVH * HD // TILE) * TILE
     (parts,) = run(
         attend_kernel,
@@ -868,9 +866,11 @@
         ],
         6 * 48 * entries * span,
     )
-    given, _ = lax.optimization_barrier((given, parts))
+    theirs, given, _ = lax.optimization_barrier((theirs, given, parts))
+    theirs = swapped_lanes(theirs, 1)
     given = swapped_y(given)
     came = lax.all_to_all(parts, both_axes, 0, 0, tiled=True)
+    came, theirs = lax.optimization_barrier((came, theirs))
     (sent,) = run(
         project_kernel,
         [shaped((requests, features), single)],

time: 76.9 us -> 78.4 us (1.020)
  blocking collectives: 35.6 us -> 21.6 us
  starting transfers between devices: 16.8 us -> 29.7 us
  waiting for transfers between devices: 12.9 us -> 15 us
    all_to_all x1 -> x0, blocking collectives: 14 us -> none  [on_device(): came = lax.all_to_all(sent, both_axes, 0, 0, tiled=True)]
    all_to_all x1, starting transfers between devices: 2.7 us -> 10.1 us  [on_device(): came = lax.all_to_all(parts, both_axes, 0, 0, tiled=True)]
    all_to_all x0 -> x1, starting transfers between devices: none -> 5.08 us  [on_device(): came = lax.all_to_all(sent, both_axes, 0, 0, tiled=True)]
    ppermute x1, waiting for transfers between devices: 3.14 us -> 0.01 us  [swapped_y(): lax.ppermute(value, 'req', [(g, g ^ 1) for g in range(lax.axis_size('req'...]
    all_to_all x1, waiting for transfers between devices: 2.55 us -> 5.57 us  [on_device(): came = lax.all_to_all(parts, both_axes, 0, 0, tiled=True)]
    all_to_all x0 -> x1, waiting for transfers between devices: none -> 2.31 us  [on_device(): came = lax.all_to_all(sent, both_axes, 0, 0, tiled=True)]
  transfers between devices with their start and end apart: 13 -> 14, of which waited for: 8 -> 8; matrix products, arithmetic and copies ran while one was open for 0% -> 0% of each run, Pallas kernels for 2% -> 6%
where the time goes in v18:
time: 78.4 us; the launch traced here: 78 us
  starting transfers between devices  29.7 us (38%)
  blocking collectives  21.6 us (28%)
  waiting for transfers between devices  15 us (19%)
  Pallas kernels  11 us (14%)
    all_to_all x2, blocking collectives, exchange(): return lax.all_to_all(parts, 'req', split_axis=0, concat_axis=0, tiled=True)  21.6 us
    ppermute x10, starting transfers between devices, swapped_lanes(): return lax.ppermute(value, 'head', [(k, k ^ turn) for k in range(lanes)])  11.1 us
    pallas_call x8, Pallas kernels, run(): pl.pallas_call(kernel, out_shape=list(outs), in_specs=in_specs, out_specs...  11 us
    all_to_all x1, starting transfers between devices, on_device(): came = lax.all_to_all(parts, both_axes, 0, 0, tiled=True)  10.1 us
    ppermute x10, waiting for transfers between devices, swapped_lanes(): return lax.ppermute(value, 'head', [(k, k ^ turn) for k in range(lanes)])  7.08 us
    all_to_all x1, waiting for transfers between devices, on_device(): came = lax.all_to_all(parts, both_axes, 0, 0, tiled=True)  5.57 us
    all_to_all x1, starting transfers between devices, on_device(): came = lax.all_to_all(sent, both_axes, 0, 0, tiled=True)  5.08 us
    all_to_all x1, waiting for transfers between devices, on_device(): came = lax.all_to_all(sent, both_axes, 0, 0, tiled=True)  2.31 us
  transfers between devices with their start and end apart: 14, of which 8 were waited for; matrix products, arithmetic and copies ran while one was open for 0% of the time, Pallas kernels for 6%

profile of v18, /device:TPU:0, one launch (start us, length us, event | category | flops | bytes accessed | tf_op | source)
XLA Modules:
  0.0 78.0 jit_solution(3191978250238424372)
XLA Ops:
  0.6 3.0 %collective-permute-start.2 = (bf16[16,512]{1,0:T(8,128)(2,1)}, bf16[16,512]{1,0:T(8,128)(2,1)S(1)}, u32[]{:S(2)}, u32[]{:S(2)}) collective-permute-start(bf16[16,512]{1,0:T(8,128)(2,1)} %hidden_far.1), channel_id=1, source_target_pairs={{0,2},{1,3},{2,0},{3,1},{4,6},{5,7},{6,4},{7,5},{8,10},{9,11},{10,... | collective-permute-start | bytes 49160 | tf_op jit(solution)/shard_map/ppermute | solution.py:742
  3.8 1.7 %collective-permute-done.2.two = bf16[16,512]{1,0:T(8,128)(2,1)S(1)} collective-permute-done((bf16[16,512]{1,0:T(8,128)(2,1)}, bf16[16,512]{1,0:T(8,128)(2,1)S(1)}, u32[]{:S(2)}, u32[]{:S(2)}) %collective-permute-start.2) | collective-permute-done | bytes 16416 | tf_op jit(solution)/shard_map/ppermute | solution.py:742
  5.6 1.4 %collective-permute-done.3.three = bf16[16,512]{1,0:T(8,128)(2,1)S(1)} collective-permute-done((bf16[16,512]{1,0:T(8,128)(2,1)}, bf16[16,512]{1,0:T(8,128)(2,1)S(1)}, u32[]{:S(2)}, u32[]{:S(2)}) %collective-permute-start.3) | collective-permute-done | bytes 16416 | tf_op jit(solution)/shard_map/ppermute | solution.py:742
  7.0 1.9 %shard_map.193 = (f32[32,8,128]{2,1,0:T(8,128)}, bf16[16,256]{1,0:T(8,128)(2,1)S(1)}) custom-call(s32[1,8]{1,0:T(1,128)} %bitcast.10, f32[1,2048]{1,0:T(1,128)} %bitcast.9, bf16[480,256]{1,0:T(8,128)(2,1)} %bitcast.7, bf16[16,512]{1,0:T(8,128)(2,1)} %hidden_far.1, bf16[16,512]{1,0:T(8,128)(2,1)S(1)} %collective-permute-done.1.one, ...), custom_call_target="tpu_custom_call" | custom-call | flops 3932160 | bytes 458784 | tf_op jit(solution)/shard_map/pallas_call | solution.py:298
  8.9 5.1 %all-to-all-start = ((f32[32,8,128]{2,1,0:T(8,128)}), f32[32,8,128]{2,1,0:T(8,128)S(1)}, u32[]{:S(2)}, u32[]{:S(2)}) async-start(f32[32,8,128]{2,1,0:T(8,128)} %get-tuple-element.20), calls=%async_computation | async-start | bytes 262144 | tf_op jit(solution)/shard_map/all_to_all | solution.py:815
  14.0 1.6 %collective-permute-start = (bf16[160,512]{1,0:T(8,128)(2,1)}, bf16[160,512]{1,0:T(8,128)(2,1)S(1)}, u32[]{:S(2)}, u32[]{:S(2)}) collective-permute-start(bf16[160,512]{1,0:T(8,128)(2,1)} %param.24), channel_id=1, source_target_pairs={{0,0},{1,8},{2,16},{3,24},{4,4},{5,12},{6,20},{7,28},{8,1},{9,9},{... | collective-permute-start | bytes 491528 | tf_op jit(solution)/shard_map/ppermute | solution.py:757
  15.6 4.3 %shard_map.194 = (bf16[4,128,640]{2,1,0:T(8,128)(2,1)}, bf16[8,640]{1,0:T(8,128)(2,1)}, bf16[528,640]{1,0:T(8,128)(2,1)S(1)}, f32[8,640]{1,0:T(8,128)S(1)}, f32[...) custom-call(s32[1,8]{1,0:T(1,128)} %refs_0_.1, ...), custom_call_target="tpu_custom_call" | custom-call | flops 167772160 | bytes 5620480 | tf_op jit(solution)/shard_map/pallas_call | solution.py:298
  20.0 2.3 %all-to-all-done.came = f32[32,8,128]{2,1,0:T(8,128)S(1)} async-done(((f32[32,8,128]{2,1,0:T(8,128)}), f32[32,8,128]{2,1,0:T(8,128)S(1)}, u32[]{:S(2)}, u32[]{:S(2)}) %all-to-all-start) | async-done | bytes 131104 | tf_op jit(solution)/shard_map/all_to_all | solution.py:815
  22.3 1.7 %shard_map.195 = bf16[32,8,128]{2,1,0:T(8,128)(2,1)} custom-call(f32[32,8,128]{2,1,0:T(8,128)S(1)} %all-to-all-done.came, bf16[528,640]{1,0:T(8,128)(2,1)S(1)} %get-tuple-element.24.kept, f32[8,640]{1,0:T(8,128)S(1)} %get-tuple-element.25.added, f32[96,128]{1,0:T(8,128)S(1)} %get-tuple-element.26.tables), custom_call_target="tpu_custom_call" | custom-call | flops 56623104 | bytes 942080 | tf_op jit(solution)/shard_map/pallas_call | solution.py:298
  24.0 4.1 %collective-permute-start.4 = (bf16[256,1280]{1,0:T(8,128)(2,1)S(1)}, bf16[256,1280]{1,0:T(8,128)(2,1)S(1)}, u32[]{:S(2)}, u32[]{:S(2)}) collective-permute-start(bf16[256,1280]{1,0:T(8,128)(2,1)S(1)} %get-tuple-element.29), channel_id=1, source_target_pairs={{0,1},{1,0},{2,3},{3,2},{4,5},{5,4},{6,7},{7,6},{8,9},{9,8},{10,11... | collective-permute-start | bytes 1966088 | tf_op jit(solution)/shard_map/ppermute | solution.py:742
  28.0 10.1 %all-to-all-start.1 = ((bf16[32,8,128]{2,1,0:T(8,128)(2,1)}), bf16[32,8,128]{2,1,0:T(8,128)(2,1)S(1)}, u32[]{:S(2)}, u32[]{:S(2)}) async-start(bf16[32,8,128]{2,1,0:T(8,128)(2,1)} %shard_map.195), calls=%async_computation.1 | async-start | bytes 131072 | tf_op jit(solution)/shard_map/all_to_all | solution.py:872
  38.1 1.8 %collective-permute-start.5 = (bf16[160,256]{1,0:T(8,128)(2,1)S(1)}, bf16[160,256]{1,0:T(8,128)(2,1)S(1)}, u32[]{:S(2)}, u32[]{:S(2)}) collective-permute-start(bf16[160,256]{1,0:T(8,128)(2,1)S(1)} %get-tuple-element.31), channel_id=1, source_target_pairs={{0,4},{4,0},{8,12},{12,8},{16,20},{20,16},{24,28},{28,24},{1,5},{5... | collective-permute-start | bytes 245768 | tf_op jit(solution)/shard_map/ppermute | solution.py:761
  40.0 5.6 %all-to-all-done.1.came = bf16[32,8,128]{2,1,0:T(8,128)(2,1)S(1)} async-done(((bf16[32,8,128]{2,1,0:T(8,128)(2,1)}), bf16[32,8,128]{2,1,0:T(8,128)(2,1)S(1)}, u32[]{:S(2)}, u32[]{:S(2)}) %all-to-all-start.1) | async-done | bytes 65568 | tf_op jit(solution)/shard_map/all_to_all | solution.py:872
  45.5 1.0 %shard_map.196.own = f32[16,256]{1,0:T(8,128)S(1)} custom-call(s32[1,8]{1,0:T(1,128)} %bitcast.12, bf16[32,8,128]{2,1,0:T(8,128)(2,1)S(1)} %all-to-all-done.1.came, bf16[160,512]{1,0:T(8,128)(2,1)S(1)} %collective-permute-done.refs_12_.first, bf16[160,256]{1,0:T(8,128)(2,1)S(1)} %collective-permute-done.5.second), custom_call_target="tpu_custom_call" | custom-call | flops 2621440 | bytes 327712 | tf_op jit(solution)/shard_map/pallas_call | solution.py:298
  46.8 1.6 %collective-permute-start.7 = (f32[16,256]{1,0:T(8,128)S(1)}, f32[16,256]{1,0:T(8,128)S(1)}, u32[]{:S(2)}, u32[]{:S(2)}) collective-permute-start(f32[16,256]{1,0:T(8,128)S(1)} %shard_map.196.own), channel_id=1, source_target_pairs={{0,2},{1,3},{2,0},{3,1},{4,6},{5,7},{6,4},{7,5},{8,10},{9,11},{10,... | collective-permute-start | bytes 49160 | tf_op jit(solution)/shard_map/ppermute | solution.py:742
  48.5 1.3 %collective-permute-done.8.three = f32[16,256]{1,0:T(8,128)S(1)} collective-permute-done((f32[16,256]{1,0:T(8,128)S(1)}, f32[16,256]{1,0:T(8,128)S(1)}, u32[]{:S(2)}, u32[]{:S(2)}) %collective-permute-start.8) | collective-permute-done | bytes 16416 | tf_op jit(solution)/shard_map/ppermute | solution.py:742
  49.8 0.7 collective-permute-done.7.two
  50.5 1.0 %shard_map.197 = (bf16[8,16,768]{2,1,0:T(8,128)(2,1)S(1)}, bf16[16,256]{1,0:T(8,128)(2,1)S(1)}) custom-call(f32[1,2048]{1,0:T(1,128)} %bitcast.8, f32[16,256]{1,0:T(8,128)S(1)} %shard_map.196.own, f32[16,256]{1,0:T(8,128)S(1)} %collective-permute-done.6.one, f32[16,256]{1,0:T(8,128)S(1)} %collective-permute-done.7.two, ...), custom_call_target="tpu_custom_call" | custom-call | flops 20971520 | bytes 1597440 | tf_op jit(solution)/shard_map/pallas_call | solution.py:298
  51.5 11.3 %all_to_all.20.came = bf16[8,16,768]{2,1,0:T(8,128)(2,1)S(1)} all-to-all(bf16[8,16,768]{2,1,0:T(8,128)(2,1)S(1)} %get-tuple-element.35), channel_id=1, replica_groups=mesh['req'=8,'head'=4] {'req'}, dimensions={0} | all-to-all | bytes 393216 | tf_op jit(solution)/shard_map/all_to_all | solution.py:84
  63.1 0.8 collective-permute-start.10
  63.8 1.1 %collective-permute-start.9 = (bf16[16,320]{1,0:T(8,128)(2,1)S(1)}, bf16[16,320]{1,0:T(8,128)(2,1)S(1)}, u32[]{:S(2)}, u32[]{:S(2)}) collective-permute-start(bf16[16,320]{1,0:T(8,128)(2,1)S(1)} %shard_map.198.own), channel_id=1, source_target_pairs={{0,1},{1,0},{2,3},{3,2},{4,5},{5,4},{6,7},{7,6},{8,9},{9,8},{10,11... | collective-permute-start | bytes 30728 | tf_op jit(solution)/shard_map/ppermute | solution.py:742
  64.9 1.3 %collective-permute-done.11.three = bf16[16,320]{1,0:T(8,128)(2,1)S(1)} collective-permute-done((bf16[16,320]{1,0:T(8,128)(2,1)S(1)}, bf16[16,320]{1,0:T(8,128)(2,1)S(1)}, u32[]{:S(2)}, u32[]{:S(2)}) %collective-permute-start.11) | collective-permute-done | bytes 10272 | tf_op jit(solution)/shard_map/ppermute | solution.py:742
  66.2 0.7 collective-permute-done.10.two
  67.1 10.3 %all_to_all.21.came = bf16[8,16,512]{2,1,0:T(8,128)(2,1)S(1)} all-to-all(bf16[8,16,512]{2,1,0:T(8,128)(2,1)S(1)} %shard_map.199), channel_id=1, replica_groups=mesh['req'=8,'head'=4] {'req'}, dimensions={0} | all-to-all | bytes 262144 | tf_op jit(solution)/shard_map/all_to_all | solution.py:84
  (16 shorter events, 1.7 us)
Async XLA Ops:
  0.6 4.9 %collective-permute-start.2 = (bf16[16,512]{1,0:T(8,128)(2,1)}, bf16[16,512]{1,0:T(8,128)(2,1)S(1)}, u32[]{:S(2)}, u32[]{:S(2)}) collective-permute-start(bf16[16,512]{1,0:T(8,128)(2,1)} %hidden_far.1), channel_id=1, source_target_pairs={{0,2},{1,3},{2,0},{3,1},{4,6},{5,7},{6,4},{7,5},{8,10},{9,11},{10,... | collective-permute-start | bytes 49160 | tf_op jit(solution)/shard_map/ppermute | solution.py:742
  3.6 1.9 %collective-permute-start.1 = (bf16[16,512]{1,0:T(8,128)(2,1)}, bf16[16,512]{1,0:T(8,128)(2,1)S(1)}, u32[]{:S(2)}, u32[]{:S(2)}) collective-permute-start(bf16[16,512]{1,0:T(8,128)(2,1)} %hidden_far.1), channel_id=1, source_target_pairs={{0,1},{1,0},{2,3},{3,2},{4,5},{5,4},{6,7},{7,6},{8,9},{9,8},{10,11... | collective-permute-start | bytes 49160 | tf_op jit(solution)/shard_map/ppermute | solution.py:742
  3.6 3.4 %collective-permute-start.3 = (bf16[16,512]{1,0:T(8,128)(2,1)}, bf16[16,512]{1,0:T(8,128)(2,1)S(1)}, u32[]{:S(2)}, u32[]{:S(2)}) collective-permute-start(bf16[16,512]{1,0:T(8,128)(2,1)} %hidden_far.1), channel_id=1, source_target_pairs={{0,3},{1,2},{2,1},{3,0},{4,7},{5,6},{6,5},{7,4},{8,11},{9,10},{10,... | collective-permute-start | bytes 49160 | tf_op jit(solution)/shard_map/ppermute | solution.py:742
  8.9 13.3 %all-to-all-start = ((f32[32,8,128]{2,1,0:T(8,128)}), f32[32,8,128]{2,1,0:T(8,128)S(1)}, u32[]{:S(2)}, u32[]{:S(2)}) async-start(f32[32,8,128]{2,1,0:T(8,128)} %get-tuple-element.20), calls=%async_computation | async-start | bytes 262144 | tf_op jit(solution)/shard_map/all_to_all | solution.py:815
  14.0 1.6 %collective-permute-start = (bf16[160,512]{1,0:T(8,128)(2,1)}, bf16[160,512]{1,0:T(8,128)(2,1)S(1)}, u32[]{:S(2)}, u32[]{:S(2)}) collective-permute-start(bf16[160,512]{1,0:T(8,128)(2,1)} %param.24), channel_id=1, source_target_pairs={{0,0},{1,8},{2,16},{3,24},{4,4},{5,12},{6,20},{7,28},{8,1},{9,9},{... | collective-permute-start | bytes 491528 | tf_op jit(solution)/shard_map/ppermute | solution.py:757
  24.0 42.8 %copy-start = (bf16[640,512]{1,0:T(8,128)(2,1)S(1)}, bf16[640,512]{1,0:T(8,128)(2,1)}, u32[]{:S(2)}) copy-start(bf16[640,512]{1,0:T(8,128)(2,1)} %weight.1) | copy-start | bytes 1966084
  24.0 21.6 %collective-permute-start.4 = (bf16[256,1280]{1,0:T(8,128)(2,1)S(1)}, bf16[256,1280]{1,0:T(8,128)(2,1)S(1)}, u32[]{:S(2)}, u32[]{:S(2)}) collective-permute-start(bf16[256,1280]{1,0:T(8,128)(2,1)S(1)} %get-tuple-element.29), channel_id=1, source_target_pairs={{0,1},{1,0},{2,3},{3,2},{4,5},{5,4},{6,7},{7,6},{8,9},{9,8},{10,11... | collective-permute-start | bytes 1966088 | tf_op jit(solution)/shard_map/ppermute | solution.py:742
  28.0 17.5 %all-to-all-start.1 = ((bf16[32,8,128]{2,1,0:T(8,128)(2,1)}), bf16[32,8,128]{2,1,0:T(8,128)(2,1)S(1)}, u32[]{:S(2)}, u32[]{:S(2)}) async-start(bf16[32,8,128]{2,1,0:T(8,128)(2,1)} %shard_map.195), calls=%async_computation.1 | async-start | bytes 131072 | tf_op jit(solution)/shard_map/all_to_all | solution.py:872
  38.1 7.4 %collective-permute-start.5 = (bf16[160,256]{1,0:T(8,128)(2,1)S(1)}, bf16[160,256]{1,0:T(8,128)(2,1)S(1)}, u32[]{:S(2)}, u32[]{:S(2)}) collective-permute-start(bf16[160,256]{1,0:T(8,128)(2,1)S(1)} %get-tuple-element.31), channel_id=1, source_target_pairs={{0,4},{4,0},{8,12},{12,8},{16,20},{20,16},{24,28},{28,24},{1,5},{5... | collective-permute-start | bytes 245768 | tf_op jit(solution)/shard_map/ppermute | solution.py:761
  46.6 3.2 %collective-permute-start.8 = (f32[16,256]{1,0:T(8,128)S(1)}, f32[16,256]{1,0:T(8,128)S(1)}, u32[]{:S(2)}, u32[]{:S(2)}) collective-permute-start(f32[16,256]{1,0:T(8,128)S(1)} %shard_map.196.own), channel_id=1, source_target_pairs={{0,3},{1,2},{2,1},{3,0},{4,7},{5,6},{6,5},{7,4},{8,11},{9,10},{10,... | collective-permute-start | bytes 49160 | tf_op jit(solution)/shard_map/ppermute | solution.py:742
  46.8 3.7 %collective-permute-start.7 = (f32[16,256]{1,0:T(8,128)S(1)}, f32[16,256]{1,0:T(8,128)S(1)}, u32[]{:S(2)}, u32[]{:S(2)}) collective-permute-start(f32[16,256]{1,0:T(8,128)S(1)} %shard_map.196.own), channel_id=1, source_target_pairs={{0,2},{1,3},{2,0},{3,1},{4,6},{5,7},{6,4},{7,5},{8,10},{9,11},{10,... | collective-permute-start | bytes 49160 | tf_op jit(solution)/shard_map/ppermute | solution.py:742
  48.4 2.1 %collective-permute-start.6 = (f32[16,256]{1,0:T(8,128)S(1)}, f32[16,256]{1,0:T(8,128)S(1)}, u32[]{:S(2)}, u32[]{:S(2)}) collective-permute-start(f32[16,256]{1,0:T(8,128)S(1)} %shard_map.196.own), channel_id=1, source_target_pairs={{0,1},{1,0},{2,3},{3,2},{4,5},{5,4},{6,7},{7,6},{8,9},{9,8},{10,11... | collective-permute-start | bytes 49160 | tf_op jit(solution)/shard_map/ppermute | solution.py:742
  63.0 3.2 %collective-permute-start.11 = (bf16[16,320]{1,0:T(8,128)(2,1)S(1)}, bf16[16,320]{1,0:T(8,128)(2,1)S(1)}, u32[]{:S(2)}, u32[]{:S(2)}) collective-permute-start(bf16[16,320]{1,0:T(8,128)(2,1)S(1)} %shard_map.198.own), channel_id=1, source_target_pairs={{0,3},{1,2},{2,1},{3,0},{4,7},{5,6},{6,5},{7,4},{8,11},{9,10},{10,... | collective-permute-start | bytes 30728 | tf_op jit(solution)/shard_map/ppermute | solution.py:742
  63.1 3.8 %collective-permute-start.10 = (bf16[16,320]{1,0:T(8,128)(2,1)S(1)}, bf16[16,320]{1,0:T(8,128)(2,1)S(1)}, u32[]{:S(2)}, u32[]{:S(2)}) collective-permute-start(bf16[16,320]{1,0:T(8,128)(2,1)S(1)} %shard_map.198.own), channel_id=1, source_target_pairs={{0,2},{1,3},{2,0},{3,1},{4,6},{5,7},{6,4},{7,5},{8,10},{9,11},{10,... | collective-permute-start | bytes 30728 | tf_op jit(solution)/shard_map/ppermute | solution.py:742
  63.8 3.0 %collective-permute-start.9 = (bf16[16,320]{1,0:T(8,128)(2,1)S(1)}, bf16[16,320]{1,0:T(8,128)(2,1)S(1)}, u32[]{:S(2)}, u32[]{:S(2)}) collective-permute-start(bf16[16,320]{1,0:T(8,128)(2,1)S(1)} %shard_map.198.own), channel_id=1, source_target_pairs={{0,1},{1,0},{2,3},{3,2},{4,5},{5,4},{6,7},{7,6},{8,9},{9,8},{10,11... | collective-permute-start | bytes 30728 | tf_op jit(solution)/shard_map/ppermute | solution.py:742

commit v19 on v13

--- a/solution.py
+++ b/solution.py
@@ -445,11 +445,13 @@
     weight_columns = weights[...].T
     rows_of = iota((rows, KEEP), 0)
     place = iota((rows, 16), 1)
+    ones = jnp.ones((KEEP, 16), bfloat)
     copies[9].wait()
     for p in range(count):
         picks = (keep[p : p + 1, :] == rows_of).astype(single)
-        dropped = weight_columns[:, p : p + 1] * (1.0 - jnp.sum(picks, axis=1, keepdims=True))
-        total = jnp.sum(dropped, axis=0, keepdims=True)
+        listed = jnp.dot(picks.astype(bfloat), ones, preferred_element_type=single)
+        dropped = weight_columns[:, p : p + 1] * (1.0 - listed)
+        total = jnp.sum(dropped, axis=0, keepdims=True)[:, :1]
         left = jnp.concatenate([picks, three_terms(dropped, place)], axis=1).astype(bfloat)
         both = lax.dot_general(
             left, pages[p], (((0,), (0,)), ((), ())), preferred_element_type=single

time: 72.9 us -> 73.4 us (level)
  transfers between devices with their start and end apart: 12 -> 12, of which waited for: 4 -> 4; matrix products, arithmetic and copies ran while one was open for 0% -> 0% of each run, Pallas kernels for 6% -> 7%
where the time goes in v19:
time: 73.4 us; the launch traced here: 73 us
  blocking collectives  42.9 us (58%)
  starting transfers between devices  14.2 us (19%)
  Pallas kernels  11.2 us (15%)
  waiting for transfers between devices  3.93 us (5%)
  between operations  0.76 us (1%)
    all_to_all x2, blocking collectives, exchange(): return lax.all_to_all(parts, 'req', split_axis=0, concat_axis=0, tiled=True)  20.9 us
    all_to_all x1, blocking collectives, on_device(): came = lax.all_to_all(sent, both_axes, 0, 0, tiled=True)  12.8 us
    pallas_call x9, Pallas kernels, run(): pl.pallas_call(kernel, out_shape=list(outs), in_specs=in_specs, out_specs...  11.2 us
    ppermute x10, starting transfers between devices, swapped_lanes(): return lax.ppermute(value, 'head', [(k, k ^ turn) for k in range(lanes)])  10.5 us
    all_to_all x1, blocking collectives, on_device(): came = lax.all_to_all(parts, both_axes, 0, 0, tiled=True)  9.24 us
    ppermute x10, waiting for transfers between devices, swapped_lanes(): return lax.ppermute(value, 'head', [(k, k ^ turn) for k in range(lanes)])  3.92 us
    ppermute x2, starting transfers between devices, handed_over(): return lax.ppermute(value, both_axes, pairs)  3.7 us
  transfers between devices with their start and end apart: 12, of which 4 were waited for; matrix products, arithmetic and copies ran while one was open for 0% of the time, Pallas kernels for 7%

profile of v19, /device:TPU:0, one launch (start us, length us, event | category | flops | bytes accessed | tf_op | source)
XLA Modules:
  0.0 73.0 jit_solution(7468099439779368719)
XLA Ops:
  0.6 1.0 %shard_map.194 = (bf16[160,256]{1,0:T(8,128)(2,1)S(1)}, bf16[160,256]{1,0:T(8,128)(2,1)S(1)}) custom-call(bf16[160,512]{1,0:T(8,128)(2,1)} %weight_far.1), custom_call_target="tpu_custom_call" | custom-call | bytes 327680 | tf_op jit(solution)/shard_map/pallas_call | solution.py:298
  1.6 0.7 collective-permute-start.3
  2.3 3.0 %collective-permute-start.4 = (bf16[160,256]{1,0:T(8,128)(2,1)S(1)}, bf16[160,256]{1,0:T(8,128)(2,1)S(1)}, u32[]{:S(2)}, u32[]{:S(2)}) collective-permute-start(bf16[160,256]{1,0:T(8,128)(2,1)S(1)} %get-tuple-element.29), channel_id=1, source_target_pairs={{0,4},{1,12},{2,20},{3,28},{4,0},{5,8},{6,16},{7,24},{8,5},{9,13},... | collective-permute-start | bytes 245768 | tf_op jit(solution)/shard_map/ppermute | solution.py:764
  5.3 6.0 %collective-permute-start.1 = (bf16[16,512]{1,0:T(8,128)(2,1)}, bf16[16,512]{1,0:T(8,128)(2,1)S(1)}, u32[]{:S(2)}, u32[]{:S(2)}) collective-permute-start(bf16[16,512]{1,0:T(8,128)(2,1)} %hidden_far.1), channel_id=1, source_target_pairs={{0,2},{1,3},{2,0},{3,1},{4,6},{5,7},{6,4},{7,5},{8,10},{9,11},{10,... | collective-permute-start | bytes 49160 | tf_op jit(solution)/shard_map/ppermute | solution.py:748
  11.5 4.9 %shard_map.193 = (bf16[4,128,640]{2,1,0:T(8,128)(2,1)}, bf16[8,640]{1,0:T(8,128)(2,1)}, bf16[528,640]{1,0:T(8,128)(2,1)S(1)}, f32[8,640]{1,0:T(8,128)S(1)}, f32[...) custom-call(s32[1,8]{1,0:T(1,128)} %refs_0_.1, s32[1,16]{1,0:T(1,128)} %bitcast.13, ...), custom_call_target="tpu_custom_call" | custom-call | flops 167772160 | bytes 5374720 | tf_op jit(solution)/shard_map/pallas_call | solution.py:298
  16.4 1.3 %shard_map.195 = (f32[32,8,128]{2,1,0:T(8,128)S(1)}, bf16[16,256]{1,0:T(8,128)(2,1)S(1)}) custom-call(s32[1,8]{1,0:T(1,128)} %bitcast.11, f32[1,2048]{1,0:T(1,128)} %bitcast.9, bf16[480,256]{1,0:T(8,128)(2,1)} %bitcast.7, bf16[16,512]{1,0:T(8,128)(2,1)} %hidden_far.1, bf16[16,512]{1,0:T(8,128)(2,1)S(1)} %collective-permute-done.one, ...), custom_call_target="tpu_custom_call" | custom-call | flops 3932160 | bytes 458784 | tf_op jit(solution)/shard_map/pallas_call | solution.py:298
  17.7 0.5 collective-permute-start.5
  18.2 12.8 %all_to_all.20.came = f32[32,8,128]{2,1,0:T(8,128)S(1)} all-to-all(f32[32,8,128]{2,1,0:T(8,128)S(1)} %get-tuple-element.33), channel_id=1, replica_groups=mesh['req'=8,'head'=4] {'req','head'}, dimensions={0} | all-to-all | bytes 262144 | tf_op jit(solution)/shard_map/all_to_all | solution.py:865
  31.0 1.1 %shard_map.196 = bf16[32,8,128]{2,1,0:T(8,128)(2,1)S(1)} custom-call(f32[32,8,128]{2,1,0:T(8,128)S(1)} %all_to_all.20.came, bf16[528,640]{1,0:T(8,128)(2,1)S(1)} %get-tuple-element.37.kept, f32[8,640]{1,0:T(8,128)S(1)} %get-tuple-element.38.added, f32[96,128]{1,0:T(8,128)S(1)} %get-tuple-element.39.tables), custom_call_target="tpu_custom_call" | custom-call | flops 56623104 | bytes 942080 | tf_op jit(solution)/shard_map/pallas_call | solution.py:298
  32.1 9.2 %all_to_all.21.came = bf16[32,8,128]{2,1,0:T(8,128)(2,1)S(1)} all-to-all(bf16[32,8,128]{2,1,0:T(8,128)(2,1)S(1)} %shard_map.196), channel_id=1, replica_groups=mesh['req'=8,'head'=4] {'req','head'}, dimensions={0} | all-to-all | bytes 131072 | tf_op jit(solution)/shard_map/all_to_all | solution.py:884
  41.3 1.0 %shard_map.197.own = f32[16,256]{1,0:T(8,128)S(1)} custom-call(s32[1,8]{1,0:T(1,128)} %bitcast.12, bf16[32,8,128]{2,1,0:T(8,128)(2,1)S(1)} %all_to_all.21.came, bf16[160,256]{1,0:T(8,128)(2,1)S(1)} %collective-permute-done.3.first, bf16[160,256]{1,0:T(8,128)(2,1)S(1)} %collective-permute-done.4.second), custom_call_target="tpu_custom_call" | custom-call | flops 2621440 | bytes 245792 | tf_op jit(solution)/shard_map/pallas_call | solution.py:298
  42.3 0.2 collective-permute-start.8
  42.5 1.6 %collective-permute-start.7 = (f32[16,256]{1,0:T(8,128)S(1)}, f32[16,256]{1,0:T(8,128)S(1)}, u32[]{:S(2)}, u32[]{:S(2)}) collective-permute-start(f32[16,256]{1,0:T(8,128)S(1)} %shard_map.197.own), channel_id=1, source_target_pairs={{0,2},{1,3},{2,0},{3,1},{4,6},{5,7},{6,4},{7,5},{8,10},{9,11},{10,... | collective-permute-start | bytes 49160 | tf_op jit(solution)/shard_map/ppermute | solution.py:748
  44.3 1.3 %collective-permute-done.8.three = f32[16,256]{1,0:T(8,128)S(1)} collective-permute-done((f32[16,256]{1,0:T(8,128)S(1)}, f32[16,256]{1,0:T(8,128)S(1)}, u32[]{:S(2)}, u32[]{:S(2)}) %collective-permute-start.8) | collective-permute-done | bytes 16416 | tf_op jit(solution)/shard_map/ppermute | solution.py:748
  45.5 0.7 collective-permute-done.7.two
  46.3 1.0 %shard_map.198 = (bf16[8,16,768]{2,1,0:T(8,128)(2,1)S(1)}, bf16[16,256]{1,0:T(8,128)(2,1)S(1)}) custom-call(f32[1,2048]{1,0:T(1,128)} %bitcast.8, f32[16,256]{1,0:T(8,128)S(1)} %shard_map.197.own, f32[16,256]{1,0:T(8,128)S(1)} %collective-permute-done.6.one, f32[16,256]{1,0:T(8,128)S(1)} %collective-permute-done.7.two, ...), custom_call_target="tpu_custom_call" | custom-call | flops 20971520 | bytes 1597440 | tf_op jit(solution)/shard_map/pallas_call | solution.py:298
  47.3 10.3 %all_to_all.22.came = bf16[8,16,768]{2,1,0:T(8,128)(2,1)S(1)} all-to-all(bf16[8,16,768]{2,1,0:T(8,128)(2,1)S(1)} %get-tuple-element.45), channel_id=1, replica_groups=mesh['req'=8,'head'=4] {'req'}, dimensions={0} | all-to-all | bytes 393216 | tf_op jit(solution)/shard_map/all_to_all | solution.py:84
  57.8 1.6 %collective-permute-start.10 = (bf16[16,320]{1,0:T(8,128)(2,1)S(1)}, bf16[16,320]{1,0:T(8,128)(2,1)S(1)}, u32[]{:S(2)}, u32[]{:S(2)}) collective-permute-start(bf16[16,320]{1,0:T(8,128)(2,1)S(1)} %shard_map.199.own), channel_id=1, source_target_pairs={{0,2},{1,3},{2,0},{3,1},{4,6},{5,7},{6,4},{7,5},{8,10},{9,11},{10,... | collective-permute-start | bytes 30728 | tf_op jit(solution)/shard_map/ppermute | solution.py:748
  59.4 0.3 collective-permute-start.9
  59.6 1.3 %collective-permute-done.11.three = bf16[16,320]{1,0:T(8,128)(2,1)S(1)} collective-permute-done((bf16[16,320]{1,0:T(8,128)(2,1)S(1)}, bf16[16,320]{1,0:T(8,128)(2,1)S(1)}, u32[]{:S(2)}, u32[]{:S(2)}) %collective-permute-start.11) | collective-permute-done | bytes 10272 | tf_op jit(solution)/shard_map/ppermute | solution.py:748
  60.9 0.6 collective-permute-done.10.two
  61.5 0.2 shard_map.200
  61.8 10.6 %all_to_all.23.came = bf16[8,16,512]{2,1,0:T(8,128)(2,1)S(1)} all-to-all(bf16[8,16,512]{2,1,0:T(8,128)(2,1)S(1)} %shard_map.200), channel_id=1, replica_groups=mesh['req'=8,'head'=4] {'req'}, dimensions={0} | all-to-all | bytes 262144 | tf_op jit(solution)/shard_map/all_to_all | solution.py:84
  72.4 0.6 shard_map.201
  (15 shorter events, 0.6 us)
Async XLA Ops:
  1.6 14.8 %collective-permute-start.3 = (bf16[160,256]{1,0:T(8,128)(2,1)S(1)}, bf16[160,256]{1,0:T(8,128)(2,1)S(1)}, u32[]{:S(2)}, u32[]{:S(2)}) collective-permute-start(bf16[160,256]{1,0:T(8,128)(2,1)S(1)} %get-tuple-element.28), channel_id=1, source_target_pairs={{0,0},{1,8},{2,16},{3,24},{4,4},{5,12},{6,20},{7,28},{8,1},{9,9},{... | collective-permute-start | bytes 245768 | tf_op jit(solution)/shard_map/ppermute | solution.py:764
  2.3 14.1 %collective-permute-start.4 = (bf16[160,256]{1,0:T(8,128)(2,1)S(1)}, bf16[160,256]{1,0:T(8,128)(2,1)S(1)}, u32[]{:S(2)}, u32[]{:S(2)}) collective-permute-start(bf16[160,256]{1,0:T(8,128)(2,1)S(1)} %get-tuple-element.29), channel_id=1, source_target_pairs={{0,4},{1,12},{2,20},{3,28},{4,0},{5,8},{6,16},{7,24},{8,5},{9,13},... | collective-permute-start | bytes 245768 | tf_op jit(solution)/shard_map/ppermute | solution.py:764
  5.3 11.1 %collective-permute-start.1 = (bf16[16,512]{1,0:T(8,128)(2,1)}, bf16[16,512]{1,0:T(8,128)(2,1)S(1)}, u32[]{:S(2)}, u32[]{:S(2)}) collective-permute-start(bf16[16,512]{1,0:T(8,128)(2,1)} %hidden_far.1), channel_id=1, source_target_pairs={{0,2},{1,3},{2,0},{3,1},{4,6},{5,7},{6,4},{7,5},{8,10},{9,11},{10,... | collective-permute-start | bytes 49160 | tf_op jit(solution)/shard_map/ppermute | solution.py:748
  11.3 5.1 %collective-permute-start = (bf16[16,512]{1,0:T(8,128)(2,1)}, bf16[16,512]{1,0:T(8,128)(2,1)S(1)}, u32[]{:S(2)}, u32[]{:S(2)}) collective-permute-start(bf16[16,512]{1,0:T(8,128)(2,1)} %hidden_far.1), channel_id=1, source_target_pairs={{0,1},{1,0},{2,3},{3,2},{4,5},{5,4},{6,7},{7,6},{8,9},{9,8},{10,11... | collective-permute-start | bytes 49160 | tf_op jit(solution)/shard_map/ppermute | solution.py:748
  11.5 4.9 %collective-permute-start.2 = (bf16[16,512]{1,0:T(8,128)(2,1)}, bf16[16,512]{1,0:T(8,128)(2,1)S(1)}, u32[]{:S(2)}, u32[]{:S(2)}) collective-permute-start(bf16[16,512]{1,0:T(8,128)(2,1)} %hidden_far.1), channel_id=1, source_target_pairs={{0,3},{1,2},{2,1},{3,0},{4,7},{5,6},{6,5},{7,4},{8,11},{9,10},{10,... | collective-permute-start | bytes 49160 | tf_op jit(solution)/shard_map/ppermute | solution.py:748
  17.7 13.3 %collective-permute-start.5 = (bf16[256,1280]{1,0:T(8,128)(2,1)S(1)}, bf16[256,1280]{1,0:T(8,128)(2,1)S(1)}, u32[]{:S(2)}, u32[]{:S(2)}) collective-permute-start(bf16[256,1280]{1,0:T(8,128)(2,1)S(1)} %get-tuple-element.35), channel_id=1, source_target_pairs={{0,1},{1,0},{2,3},{3,2},{4,5},{5,4},{6,7},{7,6},{8,9},{9,8},{10,11... | collective-permute-start | bytes 1966088 | tf_op jit(solution)/shard_map/ppermute | solution.py:748
  32.1 29.5 %copy-start = (bf16[640,512]{1,0:T(8,128)(2,1)S(1)}, bf16[640,512]{1,0:T(8,128)(2,1)}, u32[]{:S(2)}) copy-start(bf16[640,512]{1,0:T(8,128)(2,1)} %weight.1) | copy-start | bytes 1966084
  42.3 3.2 %collective-permute-start.8 = (f32[16,256]{1,0:T(8,128)S(1)}, f32[16,256]{1,0:T(8,128)S(1)}, u32[]{:S(2)}, u32[]{:S(2)}) collective-permute-start(f32[16,256]{1,0:T(8,128)S(1)} %shard_map.197.own), channel_id=1, source_target_pairs={{0,3},{1,2},{2,1},{3,0},{4,7},{5,6},{6,5},{7,4},{8,11},{9,10},{10,... | collective-permute-start | bytes 49160 | tf_op jit(solution)/shard_map/ppermute | solution.py:748
  42.5 3.7 %collective-permute-start.7 = (f32[16,256]{1,0:T(8,128)S(1)}, f32[16,256]{1,0:T(8,128)S(1)}, u32[]{:S(2)}, u32[]{:S(2)}) collective-permute-start(f32[16,256]{1,0:T(8,128)S(1)} %shard_map.197.own), channel_id=1, source_target_pairs={{0,2},{1,3},{2,0},{3,1},{4,6},{5,7},{6,4},{7,5},{8,10},{9,11},{10,... | collective-permute-start | bytes 49160 | tf_op jit(solution)/shard_map/ppermute | solution.py:748
  44.1 2.1 %collective-permute-start.6 = (f32[16,256]{1,0:T(8,128)S(1)}, f32[16,256]{1,0:T(8,128)S(1)}, u32[]{:S(2)}, u32[]{:S(2)}) collective-permute-start(f32[16,256]{1,0:T(8,128)S(1)} %shard_map.197.own), channel_id=1, source_target_pairs={{0,1},{1,0},{2,3},{3,2},{4,5},{5,4},{6,7},{7,6},{8,9},{9,8},{10,11... | collective-permute-start | bytes 49160 | tf_op jit(solution)/shard_map/ppermute | solution.py:748
  57.7 3.2 %collective-permute-start.11 = (bf16[16,320]{1,0:T(8,128)(2,1)S(1)}, bf16[16,320]{1,0:T(8,128)(2,1)S(1)}, u32[]{:S(2)}, u32[]{:S(2)}) collective-permute-start(bf16[16,320]{1,0:T(8,128)(2,1)S(1)} %shard_map.199.own), channel_id=1, source_target_pairs={{0,3},{1,2},{2,1},{3,0},{4,7},{5,6},{6,5},{7,4},{8,11},{9,10},{10,... | collective-permute-start | bytes 30728 | tf_op jit(solution)/shard_map/ppermute | solution.py:748
  57.8 3.8 %collective-permute-start.10 = (bf16[16,320]{1,0:T(8,128)(2,1)S(1)}, bf16[16,320]{1,0:T(8,128)(2,1)S(1)}, u32[]{:S(2)}, u32[]{:S(2)}) collective-permute-start(bf16[16,320]{1,0:T(8,128)(2,1)S(1)} %shard_map.199.own), channel_id=1, source_target_pairs={{0,2},{1,3},{2,0},{3,1},{4,6},{5,7},{6,4},{7,5},{8,10},{9,11},{10,... | collective-permute-start | bytes 30728 | tf_op jit(solution)/shard_map/ppermute | solution.py:748
  59.4 2.2 %collective-permute-start.9 = (bf16[16,320]{1,0:T(8,128)(2,1)S(1)}, bf16[16,320]{1,0:T(8,128)(2,1)S(1)}, u32[]{:S(2)}, u32[]{:S(2)}) collective-permute-start(bf16[16,320]{1,0:T(8,128)(2,1)S(1)} %shard_map.199.own), channel_id=1, source_target_pairs={{0,1},{1,0},{2,3},{3,2},{4,5},{5,4},{6,7},{7,6},{8,9},{9,8},{10,11... | collective-permute-start | bytes 30728 | tf_op jit(solution)/shard_map/ppermute | solution.py:748

commit v20 on v13

--- a/solution.py
+++ b/solution.py
@@ -445,14 +445,24 @@
     weight_columns = weights[...].T
     rows_of = iota((rows, KEEP), 0)
     place = iota((rows, 16), 1)
-    copies[9].wait()
+    lefts, totals = [], []
     for p in range(count):
         picks = (keep[p : p + 1, :] == rows_of).astype(single)
         dropped = weight_columns[:, p : p + 1] * (1.0 - jnp.sum(picks, axis=1, keepdims=True))
         total = jnp.sum(dropped, axis=0, keepdims=True)
         left = jnp.concatenate([picks, three_terms(dropped, place)], axis=1).astype(bfloat)
+        lefts.append(left)
+        totals.append(total)
+        live = jnp.where(keep[p : p + 1, :] >= 0, 0.0, negative)
+        for r in range(R_DEV):
+            here = owner(r, p)
+            added[r : r + 1, KEEP * p : KEEP * (p + 1)] = jnp.where(here, live, negative)
+            level = jnp.where(here, jnp.log(total), negative)
+            extra[r] = jnp.where(column == p, level, extra[r])
+    copies[9].wait()
+    for p in range(count):
         both = lax.dot_general(
-            left, pages[p], (((0,), (0,)), ((), ())), preferred_element_type=single
+            lefts[p], pages[p], (((0,), (0,)), ((), ())), preferred_element_type=single
         )
         rows_kept = both[:KEEP].astype(bfloat)
         kept[KEEP * p : KEEP * (p + 1), :] = rows_kept
@@ -460,15 +470,9 @@
         start = pl.multiple_of((slot & 1) * KEEP, KEEP)
         compact[slot >> 1, pl.ds(start, KEEP), :] = rows_kept
         mean = both[KEEP : KEEP + 1] + both[KEEP + 1 : KEEP + 2] + both[KEEP + 2 : KEEP + 3]
-        mean = mean / total
+        mean = mean / totals[p]
         plain[p : p + 1, :] = mean
         ordered[pl.ds(slot, 1), :] = mean
-        live = jnp.where(keep[p : p + 1, :] >= 0, 0.0, negative)
-        for r in range(R_DEV):
-            here = owner(r, p)
-            added[r : r + 1, KEEP * p : KEEP * (p + 1)] = jnp.where(here, live, negative)
-            level = jnp.where(here, jnp.log(total), negative)
-            extra[r] = jnp.where(column == p, level, extra[r])
     for r in range(R_DEV):
         added[r : r + 1, entries : entries + TILE] = extra[r]
     plain[count:, :] = jnp.zeros_like(plain[count:, :])

time: 72.9 us -> 72.6 us (level)
  no operation moved by 1% of the time
where the time goes in v20:
time: 72.6 us; the launch traced here: 72.2 us
  blocking collectives  42.9 us (59%)
  starting transfers between devices  14.2 us (20%)
  Pallas kernels  10.4 us (14%)
  waiting for transfers between devices  3.93 us (5%)
  between operations  0.76 us (1%)
    all_to_all x2, blocking collectives, exchange(): return lax.all_to_all(parts, 'req', split_axis=0, concat_axis=0, tiled=True)  20.9 us
    all_to_all x1, blocking collectives, on_device(): came = lax.all_to_all(sent, both_axes, 0, 0, tiled=True)  12.8 us
    ppermute x10, starting transfers between devices, swapped_lanes(): return lax.ppermute(value, 'head', [(k, k ^ turn) for k in range(lanes)])  10.5 us
    pallas_call x9, Pallas kernels, run(): pl.pallas_call(kernel, out_shape=list(outs), in_specs=in_specs, out_specs...  10.4 us
    all_to_all x1, blocking collectives, on_device(): came = lax.all_to_all(parts, both_axes, 0, 0, tiled=True)  9.24 us
    ppermute x10, waiting for transfers between devices, swapped_lanes(): return lax.ppermute(value, 'head', [(k, k ^ turn) for k in range(lanes)])  3.92 us
    ppermute x2, starting transfers between devices, handed_over(): return lax.ppermute(value, both_axes, pairs)  3.7 us
  transfers between devices with their start and end apart: 12, of which 4 were waited for; matrix products, arithmetic and copies ran while one was open for 0% of the time, Pallas kernels for 6%

profile of v20, /device:TPU:0, one launch (start us, length us, event | category | flops | bytes accessed | tf_op | source)
XLA Modules:
  0.0 72.2 jit_solution(14017196827786204014)
XLA Ops:
  0.6 1.0 %shard_map.194 = (bf16[160,256]{1,0:T(8,128)(2,1)S(1)}, bf16[160,256]{1,0:T(8,128)(2,1)S(1)}) custom-call(bf16[160,512]{1,0:T(8,128)(2,1)} %weight_far.1), custom_call_target="tpu_custom_call" | custom-call | bytes 327680 | tf_op jit(solution)/shard_map/pallas_call | solution.py:298
  1.6 0.7 collective-permute-start.3
  2.3 3.0 %collective-permute-start.4 = (bf16[160,256]{1,0:T(8,128)(2,1)S(1)}, bf16[160,256]{1,0:T(8,128)(2,1)S(1)}, u32[]{:S(2)}, u32[]{:S(2)}) collective-permute-start(bf16[160,256]{1,0:T(8,128)(2,1)S(1)} %get-tuple-element.29), channel_id=1, source_target_pairs={{0,4},{1,12},{2,20},{3,28},{4,0},{5,8},{6,16},{7,24},{8,5},{9,13},... | collective-permute-start | bytes 245768 | tf_op jit(solution)/shard_map/ppermute | solution.py:766
  5.3 6.0 %collective-permute-start.1 = (bf16[16,512]{1,0:T(8,128)(2,1)}, bf16[16,512]{1,0:T(8,128)(2,1)S(1)}, u32[]{:S(2)}, u32[]{:S(2)}) collective-permute-start(bf16[16,512]{1,0:T(8,128)(2,1)} %hidden_far.1), channel_id=1, source_target_pairs={{0,2},{1,3},{2,0},{3,1},{4,6},{5,7},{6,4},{7,5},{8,10},{9,11},{10,... | collective-permute-start | bytes 49160 | tf_op jit(solution)/shard_map/ppermute | solution.py:750
  11.5 4.1 %shard_map.193 = (bf16[4,128,640]{2,1,0:T(8,128)(2,1)}, bf16[8,640]{1,0:T(8,128)(2,1)}, bf16[528,640]{1,0:T(8,128)(2,1)S(1)}, f32[8,640]{1,0:T(8,128)S(1)}, f32[...) custom-call(s32[1,8]{1,0:T(1,128)} %refs_0_.1, s32[1,16]{1,0:T(1,128)} %bitcast.13, ...), custom_call_target="tpu_custom_call" | custom-call | flops 167772160 | bytes 5374720 | tf_op jit(solution)/shard_map/pallas_call | solution.py:298
  15.6 1.3 %shard_map.195 = (f32[32,8,128]{2,1,0:T(8,128)S(1)}, bf16[16,256]{1,0:T(8,128)(2,1)S(1)}) custom-call(s32[1,8]{1,0:T(1,128)} %bitcast.11, f32[1,2048]{1,0:T(1,128)} %bitcast.9, bf16[480,256]{1,0:T(8,128)(2,1)} %bitcast.7, bf16[16,512]{1,0:T(8,128)(2,1)} %hidden_far.1, bf16[16,512]{1,0:T(8,128)(2,1)S(1)} %collective-permute-done.one, ...), custom_call_target="tpu_custom_call" | custom-call | flops 3932160 | bytes 458784 | tf_op jit(solution)/shard_map/pallas_call | solution.py:298
  16.9 0.5 collective-permute-start.5
  17.4 12.8 %all_to_all.20.came = f32[32,8,128]{2,1,0:T(8,128)S(1)} all-to-all(f32[32,8,128]{2,1,0:T(8,128)S(1)} %get-tuple-element.33), channel_id=1, replica_groups=mesh['req'=8,'head'=4] {'req','head'}, dimensions={0} | all-to-all | bytes 262144 | tf_op jit(solution)/shard_map/all_to_all | solution.py:867
  30.2 1.1 %shard_map.196 = bf16[32,8,128]{2,1,0:T(8,128)(2,1)S(1)} custom-call(f32[32,8,128]{2,1,0:T(8,128)S(1)} %all_to_all.20.came, bf16[528,640]{1,0:T(8,128)(2,1)S(1)} %get-tuple-element.37.kept, f32[8,640]{1,0:T(8,128)S(1)} %get-tuple-element.38.added, f32[96,128]{1,0:T(8,128)S(1)} %get-tuple-element.39.tables), custom_call_target="tpu_custom_call" | custom-call | flops 56623104 | bytes 942080 | tf_op jit(solution)/shard_map/pallas_call | solution.py:298
  31.3 9.2 %all_to_all.21.came = bf16[32,8,128]{2,1,0:T(8,128)(2,1)S(1)} all-to-all(bf16[32,8,128]{2,1,0:T(8,128)(2,1)S(1)} %shard_map.196), channel_id=1, replica_groups=mesh['req'=8,'head'=4] {'req','head'}, dimensions={0} | all-to-all | bytes 131072 | tf_op jit(solution)/shard_map/all_to_all | solution.py:886
  40.5 1.0 %shard_map.197.own = f32[16,256]{1,0:T(8,128)S(1)} custom-call(s32[1,8]{1,0:T(1,128)} %bitcast.12, bf16[32,8,128]{2,1,0:T(8,128)(2,1)S(1)} %all_to_all.21.came, bf16[160,256]{1,0:T(8,128)(2,1)S(1)} %collective-permute-done.3.first, bf16[160,256]{1,0:T(8,128)(2,1)S(1)} %collective-permute-done.4.second), custom_call_target="tpu_custom_call" | custom-call | flops 2621440 | bytes 245792 | tf_op jit(solution)/shard_map/pallas_call | solution.py:298
  41.5 0.2 collective-permute-start.8
  41.7 1.6 %collective-permute-start.7 = (f32[16,256]{1,0:T(8,128)S(1)}, f32[16,256]{1,0:T(8,128)S(1)}, u32[]{:S(2)}, u32[]{:S(2)}) collective-permute-start(f32[16,256]{1,0:T(8,128)S(1)} %shard_map.197.own), channel_id=1, source_target_pairs={{0,2},{1,3},{2,0},{3,1},{4,6},{5,7},{6,4},{7,5},{8,10},{9,11},{10,... | collective-permute-start | bytes 49160 | tf_op jit(solution)/shard_map/ppermute | solution.py:750
  43.5 1.3 %collective-permute-done.8.three = f32[16,256]{1,0:T(8,128)S(1)} collective-permute-done((f32[16,256]{1,0:T(8,128)S(1)}, f32[16,256]{1,0:T(8,128)S(1)}, u32[]{:S(2)}, u32[]{:S(2)}) %collective-permute-start.8) | collective-permute-done | bytes 16416 | tf_op jit(solution)/shard_map/ppermute | solution.py:750
  44.7 0.7 %collective-permute-done.7.two = f32[16,256]{1,0:T(8,128)S(1)} collective-permute-done((f32[16,256]{1,0:T(8,128)S(1)}, f32[16,256]{1,0:T(8,128)S(1)}, u32[]{:S(2)}, u32[]{:S(2)}) %collective-permute-start.7) | collective-permute-done | bytes 16416 | tf_op jit(solution)/shard_map/ppermute | solution.py:750
  45.5 1.0 %shard_map.198 = (bf16[8,16,768]{2,1,0:T(8,128)(2,1)S(1)}, bf16[16,256]{1,0:T(8,128)(2,1)S(1)}) custom-call(f32[1,2048]{1,0:T(1,128)} %bitcast.8, f32[16,256]{1,0:T(8,128)S(1)} %shard_map.197.own, f32[16,256]{1,0:T(8,128)S(1)} %collective-permute-done.6.one, f32[16,256]{1,0:T(8,128)S(1)} %collective-permute-done.7.two, ...), custom_call_target="tpu_custom_call" | custom-call | flops 20971520 | bytes 1597440 | tf_op jit(solution)/shard_map/pallas_call | solution.py:298
  46.5 10.3 %all_to_all.22.came = bf16[8,16,768]{2,1,0:T(8,128)(2,1)S(1)} all-to-all(bf16[8,16,768]{2,1,0:T(8,128)(2,1)S(1)} %get-tuple-element.45), channel_id=1, replica_groups=mesh['req'=8,'head'=4] {'req'}, dimensions={0} | all-to-all | bytes 393216 | tf_op jit(solution)/shard_map/all_to_all | solution.py:84
  57.0 1.6 %collective-permute-start.10 = (bf16[16,320]{1,0:T(8,128)(2,1)S(1)}, bf16[16,320]{1,0:T(8,128)(2,1)S(1)}, u32[]{:S(2)}, u32[]{:S(2)}) collective-permute-start(bf16[16,320]{1,0:T(8,128)(2,1)S(1)} %shard_map.199.own), channel_id=1, source_target_pairs={{0,2},{1,3},{2,0},{3,1},{4,6},{5,7},{6,4},{7,5},{8,10},{9,11},{10,... | collective-permute-start | bytes 30728 | tf_op jit(solution)/shard_map/ppermute | solution.py:750
  58.6 0.3 collective-permute-start.9
  58.8 1.3 %collective-permute-done.11.three = bf16[16,320]{1,0:T(8,128)(2,1)S(1)} collective-permute-done((bf16[16,320]{1,0:T(8,128)(2,1)S(1)}, bf16[16,320]{1,0:T(8,128)(2,1)S(1)}, u32[]{:S(2)}, u32[]{:S(2)}) %collective-permute-start.11) | collective-permute-done | bytes 10272 | tf_op jit(solution)/shard_map/ppermute | solution.py:750
  60.1 0.6 collective-permute-done.10.two
  60.7 0.2 shard_map.200
  61.0 10.6 %all_to_all.23.came = bf16[8,16,512]{2,1,0:T(8,128)(2,1)S(1)} all-to-all(bf16[8,16,512]{2,1,0:T(8,128)(2,1)S(1)} %shard_map.200), channel_id=1, replica_groups=mesh['req'=8,'head'=4] {'req'}, dimensions={0} | all-to-all | bytes 262144 | tf_op jit(solution)/shard_map/all_to_all | solution.py:84
  71.6 0.6 shard_map.201
  (15 shorter events, 0.6 us)
Async XLA Ops:
  1.6 14.0 %collective-permute-start.3 = (bf16[160,256]{1,0:T(8,128)(2,1)S(1)}, bf16[160,256]{1,0:T(8,128)(2,1)S(1)}, u32[]{:S(2)}, u32[]{:S(2)}) collective-permute-start(bf16[160,256]{1,0:T(8,128)(2,1)S(1)} %get-tuple-element.28), channel_id=1, source_target_pairs={{0,0},{1,8},{2,16},{3,24},{4,4},{5,12},{6,20},{7,28},{8,1},{9,9},{... | collective-permute-start | bytes 245768 | tf_op jit(solution)/shard_map/ppermute | solution.py:766
  2.3 13.3 %collective-permute-start.4 = (bf16[160,256]{1,0:T(8,128)(2,1)S(1)}, bf16[160,256]{1,0:T(8,128)(2,1)S(1)}, u32[]{:S(2)}, u32[]{:S(2)}) collective-permute-start(bf16[160,256]{1,0:T(8,128)(2,1)S(1)} %get-tuple-element.29), channel_id=1, source_target_pairs={{0,4},{1,12},{2,20},{3,28},{4,0},{5,8},{6,16},{7,24},{8,5},{9,13},... | collective-permute-start | bytes 245768 | tf_op jit(solution)/shard_map/ppermute | solution.py:766
  5.3 10.3 %collective-permute-start.1 = (bf16[16,512]{1,0:T(8,128)(2,1)}, bf16[16,512]{1,0:T(8,128)(2,1)S(1)}, u32[]{:S(2)}, u32[]{:S(2)}) collective-permute-start(bf16[16,512]{1,0:T(8,128)(2,1)} %hidden_far.1), channel_id=1, source_target_pairs={{0,2},{1,3},{2,0},{3,1},{4,6},{5,7},{6,4},{7,5},{8,10},{9,11},{10,... | collective-permute-start | bytes 49160 | tf_op jit(solution)/shard_map/ppermute | solution.py:750
  11.3 4.3 %collective-permute-start = (bf16[16,512]{1,0:T(8,128)(2,1)}, bf16[16,512]{1,0:T(8,128)(2,1)S(1)}, u32[]{:S(2)}, u32[]{:S(2)}) collective-permute-start(bf16[16,512]{1,0:T(8,128)(2,1)} %hidden_far.1), channel_id=1, source_target_pairs={{0,1},{1,0},{2,3},{3,2},{4,5},{5,4},{6,7},{7,6},{8,9},{9,8},{10,11... | collective-permute-start | bytes 49160 | tf_op jit(solution)/shard_map/ppermute | solution.py:750
  11.5 4.1 %collective-permute-start.2 = (bf16[16,512]{1,0:T(8,128)(2,1)}, bf16[16,512]{1,0:T(8,128)(2,1)S(1)}, u32[]{:S(2)}, u32[]{:S(2)}) collective-permute-start(bf16[16,512]{1,0:T(8,128)(2,1)} %hidden_far.1), channel_id=1, source_target_pairs={{0,3},{1,2},{2,1},{3,0},{4,7},{5,6},{6,5},{7,4},{8,11},{9,10},{10,... | collective-permute-start | bytes 49160 | tf_op jit(solution)/shard_map/ppermute | solution.py:750
  16.9 13.3 %collective-permute-start.5 = (bf16[256,1280]{1,0:T(8,128)(2,1)S(1)}, bf16[256,1280]{1,0:T(8,128)(2,1)S(1)}, u32[]{:S(2)}, u32[]{:S(2)}) collective-permute-start(bf16[256,1280]{1,0:T(8,128)(2,1)S(1)} %get-tuple-element.35), channel_id=1, source_target_pairs={{0,1},{1,0},{2,3},{3,2},{4,5},{5,4},{6,7},{7,6},{8,9},{9,8},{10,11... | collective-permute-start | bytes 1966088 | tf_op jit(solution)/shard_map/ppermute | solution.py:750
  31.3 29.5 %copy-start = (bf16[640,512]{1,0:T(8,128)(2,1)S(1)}, bf16[640,512]{1,0:T(8,128)(2,1)}, u32[]{:S(2)}) copy-start(bf16[640,512]{1,0:T(8,128)(2,1)} %weight.1) | copy-start | bytes 1966084
  41.5 3.2 %collective-permute-start.8 = (f32[16,256]{1,0:T(8,128)S(1)}, f32[16,256]{1,0:T(8,128)S(1)}, u32[]{:S(2)}, u32[]{:S(2)}) collective-permute-start(f32[16,256]{1,0:T(8,128)S(1)} %shard_map.197.own), channel_id=1, source_target_pairs={{0,3},{1,2},{2,1},{3,0},{4,7},{5,6},{6,5},{7,4},{8,11},{9,10},{10,... | collective-permute-start | bytes 49160 | tf_op jit(solution)/shard_map/ppermute | solution.py:750
  41.7 3.7 %collective-permute-start.7 = (f32[16,256]{1,0:T(8,128)S(1)}, f32[16,256]{1,0:T(8,128)S(1)}, u32[]{:S(2)}, u32[]{:S(2)}) collective-permute-start(f32[16,256]{1,0:T(8,128)S(1)} %shard_map.197.own), channel_id=1, source_target_pairs={{0,2},{1,3},{2,0},{3,1},{4,6},{5,7},{6,4},{7,5},{8,10},{9,11},{10,... | collective-permute-start | bytes 49160 | tf_op jit(solution)/shard_map/ppermute | solution.py:750
  43.3 2.1 %collective-permute-start.6 = (f32[16,256]{1,0:T(8,128)S(1)}, f32[16,256]{1,0:T(8,128)S(1)}, u32[]{:S(2)}, u32[]{:S(2)}) collective-permute-start(f32[16,256]{1,0:T(8,128)S(1)} %shard_map.197.own), channel_id=1, source_target_pairs={{0,1},{1,0},{2,3},{3,2},{4,5},{5,4},{6,7},{7,6},{8,9},{9,8},{10,11... | collective-permute-start | bytes 49160 | tf_op jit(solution)/shard_map/ppermute | solution.py:750
  56.9 3.2 %collective-permute-start.11 = (bf16[16,320]{1,0:T(8,128)(2,1)S(1)}, bf16[16,320]{1,0:T(8,128)(2,1)S(1)}, u32[]{:S(2)}, u32[]{:S(2)}) collective-permute-start(bf16[16,320]{1,0:T(8,128)(2,1)S(1)} %shard_map.199.own), channel_id=1, source_target_pairs={{0,3},{1,2},{2,1},{3,0},{4,7},{5,6},{6,5},{7,4},{8,11},{9,10},{10,... | collective-permute-start | bytes 30728 | tf_op jit(solution)/shard_map/ppermute | solution.py:750
  57.0 3.8 %collective-permute-start.10 = (bf16[16,320]{1,0:T(8,128)(2,1)S(1)}, bf16[16,320]{1,0:T(8,128)(2,1)S(1)}, u32[]{:S(2)}, u32[]{:S(2)}) collective-permute-start(bf16[16,320]{1,0:T(8,128)(2,1)S(1)} %shard_map.199.own), channel_id=1, source_target_pairs={{0,2},{1,3},{2,0},{3,1},{4,6},{5,7},{6,4},{7,5},{8,10},{9,11},{10,... | collective-permute-start | bytes 30728 | tf_op jit(solution)/shard_map/ppermute | solution.py:750
  58.6 2.2 %collective-permute-start.9 = (bf16[16,320]{1,0:T(8,128)(2,1)S(1)}, bf16[16,320]{1,0:T(8,128)(2,1)S(1)}, u32[]{:S(2)}, u32[]{:S(2)}) collective-permute-start(bf16[16,320]{1,0:T(8,128)(2,1)S(1)} %shard_map.199.own), channel_id=1, source_target_pairs={{0,1},{1,0},{2,3},{3,2},{4,5},{5,4},{6,7},{7,6},{8,9},{9,8},{10,11... | collective-permute-start | bytes 30728 | tf_op jit(solution)/shard_map/ppermute | solution.py:750

commit v21 on v13

--- a/solution.py
+++ b/solution.py
@@ -608,15 +608,6 @@
         tile = jnp.concatenate(tile, axis=0).astype(bfloat)
         for g in range(groups):
             sent[g * lanes + k] = tile
-
-
-def blocks_kernel(weight_far, same, other, done):
-    width = same.shape[1]
-    group = lax.axis_index("req")
-    starts = [pl.multiple_of(((group & 1) ^ turn) * width, width) for turn in range(2)]
-    parts = [weight_far.at[:, pl.ds(start, width)] for start in starts]
-    for copy in fetch(parts, (same, other), done):
-        copy.wait()
 
 
 def project_kernel(source_far, came, first, second, sent, source, logs, rows, pieces, done):
@@ -658,9 +649,11 @@
     for b in range(2):
         pieces[b] = attention[:, features * b : features * (b + 1)]
     total = 0.0
+    width = sent.shape[1]
+    here = pl.ds(pl.multiple_of((group & 1) * width, width), width)
     for turn, weight in enumerate((first, second)):
         piece = pieces[(group & 1) ^ turn].astype(bfloat)
-        total = total + jnp.dot(piece, weight[...], preferred_element_type=single)
+        total = total + jnp.dot(piece, weight[:, here], preferred_element_type=single)
     sent[...] = total
 
 
@@ -750,16 +743,19 @@
     return [value] + [swapped_lanes(value, turn) for turn in range(1, lax.axis_size("head"))]
 
 
-def handed_over(value, turn):
+def transposed(value):
     groups = lax.axis_size("req")
     lanes = lax.axis_size("head")
-    share = groups // lanes
     pairs = [
-        (g * lanes + h, (share * h + ((g & 1) ^ turn)) * lanes + g // share)
+        (g * lanes + h, (2 * h + (g & 1)) * lanes + g // 2)
         for g in range(groups)
         for h in range(lanes)
     ]
     return lax.ppermute(value, both_axes, pairs)
+
+
+def swapped_y(value):
+    return lax.ppermute(value, "req", [(g, g ^ 1) for g in range(lax.axis_size("req"))])
 
 
 def on_device(
@@ -790,14 +786,7 @@
     copies = pltpu.SemaphoreType.DMA
 
     others = from_lanes(hidden_in)[1:]
-    blocks = run(
-        blocks_kernel,
-        [shaped((output_weight.shape[0], features), bfloat)] * 2,
-        [output_weight],
-        [],
-        [copies((2,))],
-    )
-    handed = [handed_over(block, turn) for turn, block in enumerate(blocks)]
+    handed = transposed(output_weight)
     scalars = [dest_slots, lengths[None, :], source[None, :], page_table]
     arrays = [
         keep_rows,
@@ -834,8 +823,7 @@
         ],
         2 * pages_here * TILE * PAGE * KVW,
     )
-    tables, *moved = lax.optimization_barrier((tables, *others, *handed))
-    others, handed = moved[: lanes - 1], moved[lanes - 1 :]
+    tables, handed, *others = lax.optimization_barrier((tables, handed, *others))
 
     holds = source[None, :]
     columns = input_weight.shape[1]
@@ -861,9 +849,10 @@
         2 * requests * features * columns,
     )
     came = lax.all_to_all(sent, both_axes, 0, 0, tiled=True)
-    theirs, _ = lax.optimization_barrier((theirs, sent))
+    theirs, given, _ = lax.optimization_barrier((theirs, handed, sent))
     theirs = swapped_lanes(theirs, 1)
-    came, theirs = lax.optimization_barrier((came, theirs))
+    given = swapped_y(given)
+    came, theirs, given = lax.optimization_barrier((came, theirs, given))
     span = -(-KVH * HD // TILE) * TILE
     (parts,) = run(
         attend_kernel,
@@ -884,7 +873,7 @@
         project_kernel,
         [shaped((requests, features), single)],
         [holds],
-        [came, *handed],
+        [came, handed, given],
         [
             *scalar_like(holds),
             pltpu.VMEM((lanes, 2 * groups, TILE), single),

time: 72.9 us -> 75.8 us (1.040)
  blocking collectives: 42.9 us -> 32.7 us
  waiting for transfers between devices: 3.93 us -> 10.9 us
  starting transfers between devices: 14.2 us -> 20.8 us
    all_to_all x1 -> x0, blocking collectives: 12.8 us -> none  [on_device(): came = lax.all_to_all(sent, both_axes, 0, 0, tiled=True)]
    all_to_all x0 -> x1, starting transfers between devices: none -> 5.97 us  [on_device(): came = lax.all_to_all(sent, both_axes, 0, 0, tiled=True)]
    ppermute x2, waiting for transfers between devices: 0.01 us -> 5.86 us  [the longest x1 5.86 us: swapped_y(): lax.ppermute(value, 'req', [(g, g ^ 1) for g in range(lax.axis_size('req'...]
    all_to_all x1, blocking collectives: 9.24 us -> 11.5 us  [on_device(): came = lax.all_to_all(parts, both_axes, 0, 0, tiled=True)]
    ppermute x10, starting transfers between devices: 10.5 us -> 11.4 us  [swapped_lanes(): return lax.ppermute(value, 'head', [(k, k ^ turn) for k in range(lanes)])]
    pallas_call x9 -> x8, Pallas kernels: 10.6 us -> 10.3 us  [run(): pl.pallas_call(kernel, out_shape=list(outs), in_specs=in_specs, out_specs...]
  transfers between devices with their start and end apart: 12 -> 13, of which waited for: 4 -> 5; matrix products, arithmetic and copies ran while one was open for 0% -> 0% of each run, Pallas kernels for 6% -> 6%
where the time goes in v21:
time: 75.8 us; the launch traced here: 75.4 us
  blocking collectives  32.7 us (43%)
  starting transfers between devices  20.8 us (27%)
  waiting for transfers between devices  10.9 us (14%)
  Pallas kernels  10.3 us (14%)
    all_to_all x2, blocking collectives, exchange(): return lax.all_to_all(parts, 'req', split_axis=0, concat_axis=0, tiled=True)  21.2 us
    all_to_all x1, blocking collectives, on_device(): came = lax.all_to_all(parts, both_axes, 0, 0, tiled=True)  11.5 us
    ppermute x10, starting transfers between devices, swapped_lanes(): return lax.ppermute(value, 'head', [(k, k ^ turn) for k in range(lanes)])  11.4 us
    pallas_call x8, Pallas kernels, run(): pl.pallas_call(kernel, out_shape=list(outs), in_specs=in_specs, out_specs...  10.3 us
    all_to_all x1, starting transfers between devices, on_device(): came = lax.all_to_all(sent, both_axes, 0, 0, tiled=True)  5.97 us
    ppermute x1, waiting for transfers between devices, swapped_y(): lax.ppermute(value, 'req', [(g, g ^ 1) for g in range(lax.axis_size('req'...  5.86 us
    ppermute x10, waiting for transfers between devices, swapped_lanes(): return lax.ppermute(value, 'head', [(k, k ^ turn) for k in range(lanes)])  4.47 us
    ppermute x1, starting transfers between devices, swapped_y(): lax.ppermute(value, 'req', [(g, g ^ 1) for g in range(lax.axis_size('req'...  1.83 us
  transfers between devices with their start and end apart: 13, of which 5 were waited for; matrix products, arithmetic and copies ran while one was open for 0% of the time, Pallas kernels for 6%

profile of v21, /device:TPU:0, one launch (start us, length us, event | category | flops | bytes accessed | tf_op | source)
XLA Modules:
  0.0 75.4 jit_solution(10385087406725213812)
XLA Ops:
  0.6 1.6 %collective-permute-start = (bf16[160,512]{1,0:T(8,128)(2,1)}, bf16[160,512]{1,0:T(8,128)(2,1)S(1)}, u32[]{:S(2)}, u32[]{:S(2)}) collective-permute-start(bf16[160,512]{1,0:T(8,128)(2,1)} %param.24), channel_id=1, source_target_pairs={{0,0},{1,8},{2,16},{3,24},{4,4},{5,12},{6,20},{7,28},{8,1},{9,9},{... | collective-permute-start | bytes 491528 | tf_op jit(solution)/shard_map/ppermute | solution.py:754
  2.2 3.5 %collective-permute-start.1 = (bf16[16,512]{1,0:T(8,128)(2,1)}, bf16[16,512]{1,0:T(8,128)(2,1)S(1)}, u32[]{:S(2)}, u32[]{:S(2)}) collective-permute-start(bf16[16,512]{1,0:T(8,128)(2,1)} %hidden_far.1), channel_id=1, source_target_pairs={{0,1},{1,0},{2,3},{3,2},{4,5},{5,4},{6,7},{7,6},{8,9},{9,8},{10,11... | collective-permute-start | bytes 49160 | tf_op jit(solution)/shard_map/ppermute | solution.py:739
  5.8 3.5 %collective-permute-start.2 = (bf16[16,512]{1,0:T(8,128)(2,1)}, bf16[16,512]{1,0:T(8,128)(2,1)S(1)}, u32[]{:S(2)}, u32[]{:S(2)}) collective-permute-start(bf16[16,512]{1,0:T(8,128)(2,1)} %hidden_far.1), channel_id=1, source_target_pairs={{0,2},{1,3},{2,0},{3,1},{4,6},{5,7},{6,4},{7,5},{8,10},{9,11},{10,... | collective-permute-start | bytes 49160 | tf_op jit(solution)/shard_map/ppermute | solution.py:739
  9.2 4.3 %shard_map.193 = (bf16[4,128,640]{2,1,0:T(8,128)(2,1)}, bf16[8,640]{1,0:T(8,128)(2,1)}, bf16[528,640]{1,0:T(8,128)(2,1)S(1)}, f32[8,640]{1,0:T(8,128)S(1)}, f32[...) custom-call(s32[1,8]{1,0:T(1,128)} %refs_0_.1, s32[1,16]{1,0:T(1,128)} %bitcast.13, ...), custom_call_target="tpu_custom_call" | custom-call | flops 167772160 | bytes 5374720 | tf_op jit(solution)/shard_map/pallas_call | solution.py:298
  13.6 1.9 %shard_map.194 = (f32[32,8,128]{2,1,0:T(8,128)}, bf16[16,256]{1,0:T(8,128)(2,1)S(1)}) custom-call(s32[1,8]{1,0:T(1,128)} %bitcast.11, f32[1,2048]{1,0:T(1,128)} %bitcast.9, bf16[480,256]{1,0:T(8,128)(2,1)} %bitcast.7, bf16[16,512]{1,0:T(8,128)(2,1)} %hidden_far.1, bf16[16,512]{1,0:T(8,128)(2,1)S(1)} %collective-permute-done.1.one, ...), custom_call_target="tpu_custom_call" | custom-call | flops 3932160 | bytes 458784 | tf_op jit(solution)/shard_map/pallas_call | solution.py:298
  15.8 6.0 %all-to-all-start = ((f32[32,8,128]{2,1,0:T(8,128)}), f32[32,8,128]{2,1,0:T(8,128)S(1)}, u32[]{:S(2)}, u32[]{:S(2)}) async-start(f32[32,8,128]{2,1,0:T(8,128)} %get-tuple-element.30), calls=%async_computation | async-start | bytes 262144 | tf_op jit(solution)/shard_map/all_to_all | solution.py:851
  21.7 1.8 %collective-permute-start.5 = (bf16[160,512]{1,0:T(8,128)(2,1)S(1)}, bf16[160,512]{1,0:T(8,128)(2,1)S(1)}, u32[]{:S(2)}, u32[]{:S(2)}) collective-permute-start(bf16[160,512]{1,0:T(8,128)(2,1)S(1)} %collective-permute-done.first), channel_id=1, source_target_pairs={{0,4},{4,0},{8,12},{12,8},{16,20},{20,16},{24,28},{28,24},{1,5},{5... | collective-permute-start | bytes 491528 | tf_op jit(solution)/shard_map/ppermute | solution.py:758
  23.6 5.9 %collective-permute-done.5.second = bf16[160,512]{1,0:T(8,128)(2,1)S(1)} collective-permute-done((bf16[160,512]{1,0:T(8,128)(2,1)S(1)}, bf16[160,512]{1,0:T(8,128)(2,1)S(1)}, u32[]{:S(2)}, u32[]{:S(2)}) %collective-permute-start.5) | collective-permute-done | bytes 163872 | tf_op jit(solution)/shard_map/ppermute | solution.py:758
  29.4 0.5 all-to-all-done.came
  30.0 1.1 %shard_map.195 = bf16[32,8,128]{2,1,0:T(8,128)(2,1)S(1)} custom-call(f32[32,8,128]{2,1,0:T(8,128)S(1)} %all-to-all-done.came, bf16[528,640]{1,0:T(8,128)(2,1)S(1)} %get-tuple-element.36.kept, f32[8,640]{1,0:T(8,128)S(1)} %get-tuple-element.37.added, f32[96,128]{1,0:T(8,128)S(1)} %get-tuple-element.38.tables), custom_call_target="tpu_custom_call" | custom-call | flops 56623104 | bytes 942080 | tf_op jit(solution)/shard_map/pallas_call | solution.py:298
  31.1 11.5 %all_to_all.20.came = bf16[32,8,128]{2,1,0:T(8,128)(2,1)S(1)} all-to-all(bf16[32,8,128]{2,1,0:T(8,128)(2,1)S(1)} %shard_map.195), channel_id=1, replica_groups=mesh['req'=8,'head'=4] {'req','head'}, dimensions={0} | all-to-all | bytes 131072 | tf_op jit(solution)/shard_map/all_to_all | solution.py:871
  42.6 1.0 %shard_map.196.own = f32[16,256]{1,0:T(8,128)S(1)} custom-call(s32[1,8]{1,0:T(1,128)} %bitcast.12, bf16[32,8,128]{2,1,0:T(8,128)(2,1)S(1)} %all_to_all.20.came, bf16[160,512]{1,0:T(8,128)(2,1)S(1)} %collective-permute-done.first, bf16[160,512]{1,0:T(8,128)(2,1)S(1)} %collective-permute-done.5.second), custom_call_target="tpu_custom_call" | custom-call | flops 2621440 | bytes 409632 | tf_op jit(solution)/shard_map/pallas_call | solution.py:298
  43.8 0.5 collective-permute-start.7
  44.2 1.3 %collective-permute-start.8 = (f32[16,256]{1,0:T(8,128)S(1)}, f32[16,256]{1,0:T(8,128)S(1)}, u32[]{:S(2)}, u32[]{:S(2)}) collective-permute-start(f32[16,256]{1,0:T(8,128)S(1)} %shard_map.196.own), channel_id=1, source_target_pairs={{0,3},{1,2},{2,1},{3,0},{4,7},{5,6},{6,5},{7,4},{8,11},{9,10},{10,... | collective-permute-start | bytes 49160 | tf_op jit(solution)/shard_map/ppermute | solution.py:739
  45.5 2.1 %collective-permute-done.7.two = f32[16,256]{1,0:T(8,128)S(1)} collective-permute-done((f32[16,256]{1,0:T(8,128)S(1)}, f32[16,256]{1,0:T(8,128)S(1)}, u32[]{:S(2)}, u32[]{:S(2)}) %collective-permute-start.7) | collective-permute-done | bytes 16416 | tf_op jit(solution)/shard_map/ppermute | solution.py:739
  47.6 1.0 %shard_map.197 = (bf16[8,16,768]{2,1,0:T(8,128)(2,1)S(1)}, bf16[16,256]{1,0:T(8,128)(2,1)S(1)}) custom-call(f32[1,2048]{1,0:T(1,128)} %bitcast.8, f32[16,256]{1,0:T(8,128)S(1)} %shard_map.196.own, f32[16,256]{1,0:T(8,128)S(1)} %collective-permute-done.6.one, f32[16,256]{1,0:T(8,128)S(1)} %collective-permute-done.7.two, ...), custom_call_target="tpu_custom_call" | custom-call | flops 20971520 | bytes 1597440 | tf_op jit(solution)/shard_map/pallas_call | solution.py:298
  48.6 10.9 %all_to_all.21.came = bf16[8,16,768]{2,1,0:T(8,128)(2,1)S(1)} all-to-all(bf16[8,16,768]{2,1,0:T(8,128)(2,1)S(1)} %get-tuple-element.43), channel_id=1, replica_groups=mesh['req'=8,'head'=4] {'req'}, dimensions={0} | all-to-all | bytes 393216 | tf_op jit(solution)/shard_map/all_to_all | solution.py:84
  59.7 1.5 %collective-permute-start.10 = (bf16[16,320]{1,0:T(8,128)(2,1)S(1)}, bf16[16,320]{1,0:T(8,128)(2,1)S(1)}, u32[]{:S(2)}, u32[]{:S(2)}) collective-permute-start(bf16[16,320]{1,0:T(8,128)(2,1)S(1)} %shard_map.198.own), channel_id=1, source_target_pairs={{0,2},{1,3},{2,0},{3,1},{4,6},{5,7},{6,4},{7,5},{8,10},{9,11},{10,... | collective-permute-start | bytes 30728 | tf_op jit(solution)/shard_map/ppermute | solution.py:739
  61.1 0.7 collective-permute-start.9
  61.9 1.6 %collective-permute-done.10.two = bf16[16,320]{1,0:T(8,128)(2,1)S(1)} collective-permute-done((bf16[16,320]{1,0:T(8,128)(2,1)S(1)}, bf16[16,320]{1,0:T(8,128)(2,1)S(1)}, u32[]{:S(2)}, u32[]{:S(2)}) %collective-permute-start.10) | collective-permute-done | bytes 10272 | tf_op jit(solution)/shard_map/ppermute | solution.py:739
  63.4 0.8 %collective-permute-done.11.three = bf16[16,320]{1,0:T(8,128)(2,1)S(1)} collective-permute-done((bf16[16,320]{1,0:T(8,128)(2,1)S(1)}, bf16[16,320]{1,0:T(8,128)(2,1)S(1)}, u32[]{:S(2)}, u32[]{:S(2)}) %collective-permute-start.11) | collective-permute-done | bytes 10272 | tf_op jit(solution)/shard_map/ppermute | solution.py:739
  64.3 0.2 shard_map.199
  64.5 10.3 %all_to_all.22.came = bf16[8,16,512]{2,1,0:T(8,128)(2,1)S(1)} all-to-all(bf16[8,16,512]{2,1,0:T(8,128)(2,1)S(1)} %shard_map.199), channel_id=1, replica_groups=mesh['req'=8,'head'=4] {'req'}, dimensions={0} | all-to-all | bytes 262144 | tf_op jit(solution)/shard_map/all_to_all | solution.py:84
  74.8 0.6 shard_map.200
  (15 shorter events, 0.6 us)
Async XLA Ops:
  0.6 13.0 %collective-permute-start = (bf16[160,512]{1,0:T(8,128)(2,1)}, bf16[160,512]{1,0:T(8,128)(2,1)S(1)}, u32[]{:S(2)}, u32[]{:S(2)}) collective-permute-start(bf16[160,512]{1,0:T(8,128)(2,1)} %param.24), channel_id=1, source_target_pairs={{0,0},{1,8},{2,16},{3,24},{4,4},{5,12},{6,20},{7,28},{8,1},{9,9},{... | collective-permute-start | bytes 491528 | tf_op jit(solution)/shard_map/ppermute | solution.py:754
  2.2 11.4 %collective-permute-start.1 = (bf16[16,512]{1,0:T(8,128)(2,1)}, bf16[16,512]{1,0:T(8,128)(2,1)S(1)}, u32[]{:S(2)}, u32[]{:S(2)}) collective-permute-start(bf16[16,512]{1,0:T(8,128)(2,1)} %hidden_far.1), channel_id=1, source_target_pairs={{0,1},{1,0},{2,3},{3,2},{4,5},{5,4},{6,7},{7,6},{8,9},{9,8},{10,11... | collective-permute-start | bytes 49160 | tf_op jit(solution)/shard_map/ppermute | solution.py:739
  5.8 7.8 %collective-permute-start.2 = (bf16[16,512]{1,0:T(8,128)(2,1)}, bf16[16,512]{1,0:T(8,128)(2,1)S(1)}, u32[]{:S(2)}, u32[]{:S(2)}) collective-permute-start(bf16[16,512]{1,0:T(8,128)(2,1)} %hidden_far.1), channel_id=1, source_target_pairs={{0,2},{1,3},{2,0},{3,1},{4,6},{5,7},{6,4},{7,5},{8,10},{9,11},{10,... | collective-permute-start | bytes 49160 | tf_op jit(solution)/shard_map/ppermute | solution.py:739
  9.2 4.4 %collective-permute-start.3 = (bf16[16,512]{1,0:T(8,128)(2,1)}, bf16[16,512]{1,0:T(8,128)(2,1)S(1)}, u32[]{:S(2)}, u32[]{:S(2)}) collective-permute-start(bf16[16,512]{1,0:T(8,128)(2,1)} %hidden_far.1), channel_id=1, source_target_pairs={{0,3},{1,2},{2,1},{3,0},{4,7},{5,6},{6,5},{7,4},{8,11},{9,10},{10,... | collective-permute-start | bytes 49160 | tf_op jit(solution)/shard_map/ppermute | solution.py:739
  15.6 14.4 %collective-permute-start.4 = (bf16[256,1280]{1,0:T(8,128)(2,1)S(1)}, bf16[256,1280]{1,0:T(8,128)(2,1)S(1)}, u32[]{:S(2)}, u32[]{:S(2)}) collective-permute-start(bf16[256,1280]{1,0:T(8,128)(2,1)S(1)} %get-tuple-element.33), channel_id=1, source_target_pairs={{0,1},{1,0},{2,3},{3,2},{4,5},{5,4},{6,7},{7,6},{8,9},{9,8},{10,11... | collective-permute-start | bytes 1966088 | tf_op jit(solution)/shard_map/ppermute | solution.py:739
  15.8 14.2 %all-to-all-start = ((f32[32,8,128]{2,1,0:T(8,128)}), f32[32,8,128]{2,1,0:T(8,128)S(1)}, u32[]{:S(2)}, u32[]{:S(2)}) async-start(f32[32,8,128]{2,1,0:T(8,128)} %get-tuple-element.30), calls=%async_computation | async-start | bytes 262144 | tf_op jit(solution)/shard_map/all_to_all | solution.py:851
  21.7 7.7 %collective-permute-start.5 = (bf16[160,512]{1,0:T(8,128)(2,1)S(1)}, bf16[160,512]{1,0:T(8,128)(2,1)S(1)}, u32[]{:S(2)}, u32[]{:S(2)}) collective-permute-start(bf16[160,512]{1,0:T(8,128)(2,1)S(1)} %collective-permute-done.first), channel_id=1, source_target_pairs={{0,4},{4,0},{8,12},{12,8},{16,20},{20,16},{24,28},{28,24},{1,5},{5... | collective-permute-start | bytes 491528 | tf_op jit(solution)/shard_map/ppermute | solution.py:758
  31.1 33.2 %copy-start = (bf16[640,512]{1,0:T(8,128)(2,1)S(1)}, bf16[640,512]{1,0:T(8,128)(2,1)}, u32[]{:S(2)}) copy-start(bf16[640,512]{1,0:T(8,128)(2,1)} %weight.1) | copy-start | bytes 1966084
  43.6 1.9 %collective-permute-start.6 = (f32[16,256]{1,0:T(8,128)S(1)}, f32[16,256]{1,0:T(8,128)S(1)}, u32[]{:S(2)}, u32[]{:S(2)}) collective-permute-start(f32[16,256]{1,0:T(8,128)S(1)} %shard_map.196.own), channel_id=1, source_target_pairs={{0,1},{1,0},{2,3},{3,2},{4,5},{5,4},{6,7},{7,6},{8,9},{9,8},{10,11... | collective-permute-start | bytes 49160 | tf_op jit(solution)/shard_map/ppermute | solution.py:739
  43.8 3.8 %collective-permute-start.7 = (f32[16,256]{1,0:T(8,128)S(1)}, f32[16,256]{1,0:T(8,128)S(1)}, u32[]{:S(2)}, u32[]{:S(2)}) collective-permute-start(f32[16,256]{1,0:T(8,128)S(1)} %shard_map.196.own), channel_id=1, source_target_pairs={{0,2},{1,3},{2,0},{3,1},{4,6},{5,7},{6,4},{7,5},{8,10},{9,11},{10,... | collective-permute-start | bytes 49160 | tf_op jit(solution)/shard_map/ppermute | solution.py:739
  44.2 3.3 %collective-permute-start.8 = (f32[16,256]{1,0:T(8,128)S(1)}, f32[16,256]{1,0:T(8,128)S(1)}, u32[]{:S(2)}, u32[]{:S(2)}) collective-permute-start(f32[16,256]{1,0:T(8,128)S(1)} %shard_map.196.own), channel_id=1, source_target_pairs={{0,3},{1,2},{2,1},{3,0},{4,7},{5,6},{6,5},{7,4},{8,11},{9,10},{10,... | collective-permute-start | bytes 49160 | tf_op jit(solution)/shard_map/ppermute | solution.py:739
  59.7 3.8 %collective-permute-start.10 = (bf16[16,320]{1,0:T(8,128)(2,1)S(1)}, bf16[16,320]{1,0:T(8,128)(2,1)S(1)}, u32[]{:S(2)}, u32[]{:S(2)}) collective-permute-start(bf16[16,320]{1,0:T(8,128)(2,1)S(1)} %shard_map.198.own), channel_id=1, source_target_pairs={{0,2},{1,3},{2,0},{3,1},{4,6},{5,7},{6,4},{7,5},{8,10},{9,11},{10,... | collective-permute-start | bytes 30728 | tf_op jit(solution)/shard_map/ppermute | solution.py:739
  61.1 3.1 %collective-permute-start.11 = (bf16[16,320]{1,0:T(8,128)(2,1)S(1)}, bf16[16,320]{1,0:T(8,128)(2,1)S(1)}, u32[]{:S(2)}, u32[]{:S(2)}) collective-permute-start(bf16[16,320]{1,0:T(8,128)(2,1)S(1)} %shard_map.198.own), channel_id=1, source_target_pairs={{0,3},{1,2},{2,1},{3,0},{4,7},{5,6},{6,5},{7,4},{8,11},{9,10},{10,... | collective-permute-start | bytes 30728 | tf_op jit(solution)/shard_map/ppermute | solution.py:739
  61.1 3.1 %collective-permute-start.9 = (bf16[16,320]{1,0:T(8,128)(2,1)S(1)}, bf16[16,320]{1,0:T(8,128)(2,1)S(1)}, u32[]{:S(2)}, u32[]{:S(2)}) collective-permute-start(bf16[16,320]{1,0:T(8,128)(2,1)S(1)} %shard_map.198.own), channel_id=1, source_target_pairs={{0,1},{1,0},{2,3},{3,2},{4,5},{5,4},{6,7},{7,6},{8,9},{9,8},{10,11... | collective-permute-start | bytes 30728 | tf_op jit(solution)/shard_map/ppermute | solution.py:739

commit v22 on v20

--- a/solution.py
+++ b/solution.py
@@ -865,9 +865,6 @@
         2 * requests * features * columns,
     )
     came = lax.all_to_all(sent, both_axes, 0, 0, tiled=True)
-    theirs, _ = lax.optimization_barrier((theirs, sent))
-    theirs = swapped_lanes(theirs, 1)
-    came, theirs = lax.optimization_barrier((came, theirs))
     span = -(-KVH * HD // TILE) * TILE
     (parts,) = run(
         attend_kernel,
@@ -883,7 +880,10 @@
         ],
         6 * 48 * entries * span,
     )
+    theirs, _ = lax.optimization_barrier((theirs, parts))
+    theirs = swapped_lanes(theirs, 1)
     came = lax.all_to_all(parts, both_axes, 0, 0, tiled=True)
+    came, theirs = lax.optimization_barrier((came, theirs))
     (sent,) = run(
         project_kernel,
         [shaped((requests, features), single)],

time: 72.6 us -> 72.6 us (level)
  no operation moved by 1% of the time
where the time goes in v22:
time: 72.6 us; the launch traced here: 72.2 us
  blocking collectives  43.1 us (59%)
  starting transfers between devices  14 us (19%)
  Pallas kernels  10.4 us (14%)
  waiting for transfers between devices  3.93 us (5%)
  between operations  0.76 us (1%)
    all_to_all x2, blocking collectives, exchange(): return lax.all_to_all(parts, 'req', split_axis=0, concat_axis=0, tiled=True)  20.9 us
    all_to_all x1, blocking collectives, on_device(): came = lax.all_to_all(sent, both_axes, 0, 0, tiled=True)  13.1 us
    pallas_call x9, Pallas kernels, run(): pl.pallas_call(kernel, out_shape=list(outs), in_specs=in_specs, out_specs...  10.4 us
    ppermute x10, starting transfers between devices, swapped_lanes(): return lax.ppermute(value, 'head', [(k, k ^ turn) for k in range(lanes)])  10.3 us
    all_to_all x1, blocking collectives, on_device(): came = lax.all_to_all(parts, both_axes, 0, 0, tiled=True)  9.09 us
    ppermute x10, waiting for transfers between devices, swapped_lanes(): return lax.ppermute(value, 'head', [(k, k ^ turn) for k in range(lanes)])  3.92 us
    ppermute x2, starting transfers between devices, handed_over(): return lax.ppermute(value, both_axes, pairs)  3.7 us
  transfers between devices with their start and end apart: 12, of which 4 were waited for; matrix products, arithmetic and copies ran while one was open for 0% of the time, Pallas kernels for 6%

profile of v22, /device:TPU:0, one launch (start us, length us, event | category | flops | bytes accessed | tf_op | source)
XLA Modules:
  0.0 72.2 jit_solution(11642151547787825417)
XLA Ops:
  0.6 1.0 %shard_map.194 = (bf16[160,256]{1,0:T(8,128)(2,1)S(1)}, bf16[160,256]{1,0:T(8,128)(2,1)S(1)}) custom-call(bf16[160,512]{1,0:T(8,128)(2,1)} %weight_far.1), custom_call_target="tpu_custom_call" | custom-call | bytes 327680 | tf_op jit(solution)/shard_map/pallas_call | solution.py:298
  1.6 0.7 collective-permute-start.3
  2.3 3.0 %collective-permute-start.4 = (bf16[160,256]{1,0:T(8,128)(2,1)S(1)}, bf16[160,256]{1,0:T(8,128)(2,1)S(1)}, u32[]{:S(2)}, u32[]{:S(2)}) collective-permute-start(bf16[160,256]{1,0:T(8,128)(2,1)S(1)} %get-tuple-element.29), channel_id=1, source_target_pairs={{0,4},{1,12},{2,20},{3,28},{4,0},{5,8},{6,16},{7,24},{8,5},{9,13},... | collective-permute-start | bytes 245768 | tf_op jit(solution)/shard_map/ppermute | solution.py:766
  5.3 6.0 %collective-permute-start.1 = (bf16[16,512]{1,0:T(8,128)(2,1)}, bf16[16,512]{1,0:T(8,128)(2,1)S(1)}, u32[]{:S(2)}, u32[]{:S(2)}) collective-permute-start(bf16[16,512]{1,0:T(8,128)(2,1)} %hidden_far.1), channel_id=1, source_target_pairs={{0,2},{1,3},{2,0},{3,1},{4,6},{5,7},{6,4},{7,5},{8,10},{9,11},{10,... | collective-permute-start | bytes 49160 | tf_op jit(solution)/shard_map/ppermute | solution.py:750
  11.5 4.1 %shard_map.193 = (bf16[4,128,640]{2,1,0:T(8,128)(2,1)}, bf16[8,640]{1,0:T(8,128)(2,1)}, bf16[528,640]{1,0:T(8,128)(2,1)S(1)}, f32[8,640]{1,0:T(8,128)S(1)}, f32[...) custom-call(s32[1,8]{1,0:T(1,128)} %refs_0_.1, s32[1,16]{1,0:T(1,128)} %bitcast.13, ...), custom_call_target="tpu_custom_call" | custom-call | flops 167772160 | bytes 5374720 | tf_op jit(solution)/shard_map/pallas_call | solution.py:298
  15.6 1.3 %shard_map.195 = (f32[32,8,128]{2,1,0:T(8,128)S(1)}, bf16[16,256]{1,0:T(8,128)(2,1)S(1)}) custom-call(s32[1,8]{1,0:T(1,128)} %bitcast.11, f32[1,2048]{1,0:T(1,128)} %bitcast.9, bf16[480,256]{1,0:T(8,128)(2,1)} %bitcast.7, bf16[16,512]{1,0:T(8,128)(2,1)} %hidden_far.1, bf16[16,512]{1,0:T(8,128)(2,1)S(1)} %collective-permute-done.one, ...), custom_call_target="tpu_custom_call" | custom-call | flops 3932160 | bytes 458784 | tf_op jit(solution)/shard_map/pallas_call | solution.py:298
  16.9 13.1 %all_to_all.20.came = f32[32,8,128]{2,1,0:T(8,128)S(1)} all-to-all(f32[32,8,128]{2,1,0:T(8,128)S(1)} %get-tuple-element.33), channel_id=1, replica_groups=mesh['req'=8,'head'=4] {'req','head'}, dimensions={0} | all-to-all | bytes 262144 | tf_op jit(solution)/shard_map/all_to_all | solution.py:867
  30.0 1.1 %shard_map.196 = bf16[32,8,128]{2,1,0:T(8,128)(2,1)S(1)} custom-call(f32[32,8,128]{2,1,0:T(8,128)S(1)} %all_to_all.20.came, bf16[528,640]{1,0:T(8,128)(2,1)S(1)} %get-tuple-element.34.kept, f32[8,640]{1,0:T(8,128)S(1)} %get-tuple-element.35.added, f32[96,128]{1,0:T(8,128)S(1)} %get-tuple-element.36.tables), custom_call_target="tpu_custom_call" | custom-call | flops 56623104 | bytes 942080 | tf_op jit(solution)/shard_map/pallas_call | solution.py:298
  31.1 0.3 collective-permute-start.5
  31.4 9.1 %all_to_all.21.came = bf16[32,8,128]{2,1,0:T(8,128)(2,1)S(1)} all-to-all(bf16[32,8,128]{2,1,0:T(8,128)(2,1)S(1)} %shard_map.196), channel_id=1, replica_groups=mesh['req'=8,'head'=4] {'req','head'}, dimensions={0} | all-to-all | bytes 131072 | tf_op jit(solution)/shard_map/all_to_all | solution.py:885
  40.5 1.0 %shard_map.197.own = f32[16,256]{1,0:T(8,128)S(1)} custom-call(s32[1,8]{1,0:T(1,128)} %bitcast.12, bf16[32,8,128]{2,1,0:T(8,128)(2,1)S(1)} %all_to_all.21.came, bf16[160,256]{1,0:T(8,128)(2,1)S(1)} %collective-permute-done.3.first, bf16[160,256]{1,0:T(8,128)(2,1)S(1)} %collective-permute-done.4.second), custom_call_target="tpu_custom_call" | custom-call | flops 2621440 | bytes 245792 | tf_op jit(solution)/shard_map/pallas_call | solution.py:298
  41.5 0.2 collective-permute-start.8
  41.7 1.6 %collective-permute-start.7 = (f32[16,256]{1,0:T(8,128)S(1)}, f32[16,256]{1,0:T(8,128)S(1)}, u32[]{:S(2)}, u32[]{:S(2)}) collective-permute-start(f32[16,256]{1,0:T(8,128)S(1)} %shard_map.197.own), channel_id=1, source_target_pairs={{0,2},{1,3},{2,0},{3,1},{4,6},{5,7},{6,4},{7,5},{8,10},{9,11},{10,... | collective-permute-start | bytes 49160 | tf_op jit(solution)/shard_map/ppermute | solution.py:750
  43.4 1.3 %collective-permute-done.8.three = f32[16,256]{1,0:T(8,128)S(1)} collective-permute-done((f32[16,256]{1,0:T(8,128)S(1)}, f32[16,256]{1,0:T(8,128)S(1)}, u32[]{:S(2)}, u32[]{:S(2)}) %collective-permute-start.8) | collective-permute-done | bytes 16416 | tf_op jit(solution)/shard_map/ppermute | solution.py:750
  44.7 0.7 %collective-permute-done.7.two = f32[16,256]{1,0:T(8,128)S(1)} collective-permute-done((f32[16,256]{1,0:T(8,128)S(1)}, f32[16,256]{1,0:T(8,128)S(1)}, u32[]{:S(2)}, u32[]{:S(2)}) %collective-permute-start.7) | collective-permute-done | bytes 16416 | tf_op jit(solution)/shard_map/ppermute | solution.py:750
  45.4 1.0 %shard_map.198 = (bf16[8,16,768]{2,1,0:T(8,128)(2,1)S(1)}, bf16[16,256]{1,0:T(8,128)(2,1)S(1)}) custom-call(f32[1,2048]{1,0:T(1,128)} %bitcast.8, f32[16,256]{1,0:T(8,128)S(1)} %shard_map.197.own, f32[16,256]{1,0:T(8,128)S(1)} %collective-permute-done.6.one, f32[16,256]{1,0:T(8,128)S(1)} %collective-permute-done.7.two, ...), custom_call_target="tpu_custom_call" | custom-call | flops 20971520 | bytes 1597440 | tf_op jit(solution)/shard_map/pallas_call | solution.py:298
  46.4 10.3 %all_to_all.22.came = bf16[8,16,768]{2,1,0:T(8,128)(2,1)S(1)} all-to-all(bf16[8,16,768]{2,1,0:T(8,128)(2,1)S(1)} %get-tuple-element.45), channel_id=1, replica_groups=mesh['req'=8,'head'=4] {'req'}, dimensions={0} | all-to-all | bytes 393216 | tf_op jit(solution)/shard_map/all_to_all | solution.py:84
  56.9 1.6 %collective-permute-start.10 = (bf16[16,320]{1,0:T(8,128)(2,1)S(1)}, bf16[16,320]{1,0:T(8,128)(2,1)S(1)}, u32[]{:S(2)}, u32[]{:S(2)}) collective-permute-start(bf16[16,320]{1,0:T(8,128)(2,1)S(1)} %shard_map.199.own), channel_id=1, source_target_pairs={{0,2},{1,3},{2,0},{3,1},{4,6},{5,7},{6,4},{7,5},{8,10},{9,11},{10,... | collective-permute-start | bytes 30728 | tf_op jit(solution)/shard_map/ppermute | solution.py:750
  58.5 0.3 collective-permute-start.9
  58.8 1.3 %collective-permute-done.11.three = bf16[16,320]{1,0:T(8,128)(2,1)S(1)} collective-permute-done((bf16[16,320]{1,0:T(8,128)(2,1)S(1)}, bf16[16,320]{1,0:T(8,128)(2,1)S(1)}, u32[]{:S(2)}, u32[]{:S(2)}) %collective-permute-start.11) | collective-permute-done | bytes 10272 | tf_op jit(solution)/shard_map/ppermute | solution.py:750
  60.1 0.6 collective-permute-done.10.two
  60.7 0.2 shard_map.200
  60.9 10.6 %all_to_all.23.came = bf16[8,16,512]{2,1,0:T(8,128)(2,1)S(1)} all-to-all(bf16[8,16,512]{2,1,0:T(8,128)(2,1)S(1)} %shard_map.200), channel_id=1, replica_groups=mesh['req'=8,'head'=4] {'req'}, dimensions={0} | all-to-all | bytes 262144 | tf_op jit(solution)/shard_map/all_to_all | solution.py:84
  71.6 0.6 shard_map.201
  (15 shorter events, 0.6 us)
Async XLA Ops:
  1.6 14.0 %collective-permute-start.3 = (bf16[160,256]{1,0:T(8,128)(2,1)S(1)}, bf16[160,256]{1,0:T(8,128)(2,1)S(1)}, u32[]{:S(2)}, u32[]{:S(2)}) collective-permute-start(bf16[160,256]{1,0:T(8,128)(2,1)S(1)} %get-tuple-element.28), channel_id=1, source_target_pairs={{0,0},{1,8},{2,16},{3,24},{4,4},{5,12},{6,20},{7,28},{8,1},{9,9},{... | collective-permute-start | bytes 245768 | tf_op jit(solution)/shard_map/ppermute | solution.py:766
  2.3 13.3 %collective-permute-start.4 = (bf16[160,256]{1,0:T(8,128)(2,1)S(1)}, bf16[160,256]{1,0:T(8,128)(2,1)S(1)}, u32[]{:S(2)}, u32[]{:S(2)}) collective-permute-start(bf16[160,256]{1,0:T(8,128)(2,1)S(1)} %get-tuple-element.29), channel_id=1, source_target_pairs={{0,4},{1,12},{2,20},{3,28},{4,0},{5,8},{6,16},{7,24},{8,5},{9,13},... | collective-permute-start | bytes 245768 | tf_op jit(solution)/shard_map/ppermute | solution.py:766
  5.3 10.3 %collective-permute-start.1 = (bf16[16,512]{1,0:T(8,128)(2,1)}, bf16[16,512]{1,0:T(8,128)(2,1)S(1)}, u32[]{:S(2)}, u32[]{:S(2)}) collective-permute-start(bf16[16,512]{1,0:T(8,128)(2,1)} %hidden_far.1), channel_id=1, source_target_pairs={{0,2},{1,3},{2,0},{3,1},{4,6},{5,7},{6,4},{7,5},{8,10},{9,11},{10,... | collective-permute-start | bytes 49160 | tf_op jit(solution)/shard_map/ppermute | solution.py:750
  11.3 4.3 %collective-permute-start = (bf16[16,512]{1,0:T(8,128)(2,1)}, bf16[16,512]{1,0:T(8,128)(2,1)S(1)}, u32[]{:S(2)}, u32[]{:S(2)}) collective-permute-start(bf16[16,512]{1,0:T(8,128)(2,1)} %hidden_far.1), channel_id=1, source_target_pairs={{0,1},{1,0},{2,3},{3,2},{4,5},{5,4},{6,7},{7,6},{8,9},{9,8},{10,11... | collective-permute-start | bytes 49160 | tf_op jit(solution)/shard_map/ppermute | solution.py:750
  11.5 4.1 %collective-permute-start.2 = (bf16[16,512]{1,0:T(8,128)(2,1)}, bf16[16,512]{1,0:T(8,128)(2,1)S(1)}, u32[]{:S(2)}, u32[]{:S(2)}) collective-permute-start(bf16[16,512]{1,0:T(8,128)(2,1)} %hidden_far.1), channel_id=1, source_target_pairs={{0,3},{1,2},{2,1},{3,0},{4,7},{5,6},{6,5},{7,4},{8,11},{9,10},{10,... | collective-permute-start | bytes 49160 | tf_op jit(solution)/shard_map/ppermute | solution.py:750
  31.1 29.6 %copy-start = (bf16[640,512]{1,0:T(8,128)(2,1)S(1)}, bf16[640,512]{1,0:T(8,128)(2,1)}, u32[]{:S(2)}) copy-start(bf16[640,512]{1,0:T(8,128)(2,1)} %weight.1) | copy-start | bytes 1966084
  31.1 9.4 %collective-permute-start.5 = (bf16[256,1280]{1,0:T(8,128)(2,1)S(1)}, bf16[256,1280]{1,0:T(8,128)(2,1)S(1)}, u32[]{:S(2)}, u32[]{:S(2)}) collective-permute-start(bf16[256,1280]{1,0:T(8,128)(2,1)S(1)} %get-tuple-element.38), channel_id=1, source_target_pairs={{0,1},{1,0},{2,3},{3,2},{4,5},{5,4},{6,7},{7,6},{8,9},{9,8},{10,11... | collective-permute-start | bytes 1966088 | tf_op jit(solution)/shard_map/ppermute | solution.py:750
  41.5 3.2 %collective-permute-start.8 = (f32[16,256]{1,0:T(8,128)S(1)}, f32[16,256]{1,0:T(8,128)S(1)}, u32[]{:S(2)}, u32[]{:S(2)}) collective-permute-start(f32[16,256]{1,0:T(8,128)S(1)} %shard_map.197.own), channel_id=1, source_target_pairs={{0,3},{1,2},{2,1},{3,0},{4,7},{5,6},{6,5},{7,4},{8,11},{9,10},{10,... | collective-permute-start | bytes 49160 | tf_op jit(solution)/shard_map/ppermute | solution.py:750
  41.7 3.7 %collective-permute-start.7 = (f32[16,256]{1,0:T(8,128)S(1)}, f32[16,256]{1,0:T(8,128)S(1)}, u32[]{:S(2)}, u32[]{:S(2)}) collective-permute-start(f32[16,256]{1,0:T(8,128)S(1)} %shard_map.197.own), channel_id=1, source_target_pairs={{0,2},{1,3},{2,0},{3,1},{4,6},{5,7},{6,4},{7,5},{8,10},{9,11},{10,... | collective-permute-start | bytes 49160 | tf_op jit(solution)/shard_map/ppermute | solution.py:750
  43.3 2.1 %collective-permute-start.6 = (f32[16,256]{1,0:T(8,128)S(1)}, f32[16,256]{1,0:T(8,128)S(1)}, u32[]{:S(2)}, u32[]{:S(2)}) collective-permute-start(f32[16,256]{1,0:T(8,128)S(1)} %shard_map.197.own), channel_id=1, source_target_pairs={{0,1},{1,0},{2,3},{3,2},{4,5},{5,4},{6,7},{7,6},{8,9},{9,8},{10,11... | collective-permute-start | bytes 49160 | tf_op jit(solution)/shard_map/ppermute | solution.py:750
  56.9 3.2 %collective-permute-start.11 = (bf16[16,320]{1,0:T(8,128)(2,1)S(1)}, bf16[16,320]{1,0:T(8,128)(2,1)S(1)}, u32[]{:S(2)}, u32[]{:S(2)}) collective-permute-start(bf16[16,320]{1,0:T(8,128)(2,1)S(1)} %shard_map.199.own), channel_id=1, source_target_pairs={{0,3},{1,2},{2,1},{3,0},{4,7},{5,6},{6,5},{7,4},{8,11},{9,10},{10,... | collective-permute-start | bytes 30728 | tf_op jit(solution)/shard_map/ppermute | solution.py:750
  56.9 3.8 %collective-permute-start.10 = (bf16[16,320]{1,0:T(8,128)(2,1)S(1)}, bf16[16,320]{1,0:T(8,128)(2,1)S(1)}, u32[]{:S(2)}, u32[]{:S(2)}) collective-permute-start(bf16[16,320]{1,0:T(8,128)(2,1)S(1)} %shard_map.199.own), channel_id=1, source_target_pairs={{0,2},{1,3},{2,0},{3,1},{4,6},{5,7},{6,4},{7,5},{8,10},{9,11},{10,... | collective-permute-start | bytes 30728 | tf_op jit(solution)/shard_map/ppermute | solution.py:750
  58.5 2.2 %collective-permute-start.9 = (bf16[16,320]{1,0:T(8,128)(2,1)S(1)}, bf16[16,320]{1,0:T(8,128)(2,1)S(1)}, u32[]{:S(2)}, u32[]{:S(2)}) collective-permute-start(bf16[16,320]{1,0:T(8,128)(2,1)S(1)} %shard_map.199.own), channel_id=1, source_target_pairs={{0,1},{1,0},{2,3},{3,2},{4,5},{5,4},{6,7},{7,6},{8,9},{9,8},{10,11... | collective-permute-start | bytes 30728 | tf_op jit(solution)/shard_map/ppermute | solution.py:750
